TPU v7x, 32 devices: a whole 2x2x4 slice. The times are simulated.
32 devices in a mesh: fsdp: 8 (over z, core), seq: 4 (over y, x).
Axes of the slice: x: 2, y: 2, z: 4, core: 2. Of those that a mesh axis runs over, the one named last changes fastest.
Arguments:
- tokens: bfloat16 [3, 32, 320, 1024], P(None, ('fsdp', 'seq')), may hold values from -6 to 6
- counts: int32 [3, 32], P(None, 'fsdp'), may hold values from 64 to 320, as said below
- ln1_gain: bfloat16 [1024], P('fsdp'), may hold values from 0.5 to 1.5
- ln1_shift: bfloat16 [1024], P('fsdp'), may hold values from -1.75 to 1.75
- w_qkv: bfloat16 [1024, 3072], P('fsdp'), may hold values from -0.1875 to 0.1875
- b_qv: bfloat16 [2048], P('fsdp'), may hold values from -1.75 to 1.75
- w_out: bfloat16 [1024, 1024], P('fsdp'), may hold values from -1.5 to 1.5
- b_out: bfloat16 [1024], P('fsdp'), may hold values from -1.75 to 1.75
- ln2_gain: bfloat16 [1024], P('fsdp'), may hold values from 0.5 to 1.5
- ln2_shift: bfloat16 [1024], P('fsdp'), may hold values from -1.75 to 1.75
- w_up: bfloat16 [1024, 4096], P('fsdp'), may hold values from -0.1875 to 0.1875
- b_up: bfloat16 [4096], P('fsdp'), may hold values from -3 to 3
- w_down: bfloat16 [4096, 1024], P('fsdp'), may hold values from -0.09375 to 0.09375
- b_down: bfloat16 [1024], P('fsdp'), may hold values from -1.75 to 1.75
- cotangent: bfloat16 [3, 32, 320, 1024], P(None, ('fsdp', 'seq')), may hold values from -6 to 6
Outputs:
- activations: bfloat16 [3, 32, 320, 1024], P(None, ('fsdp', 'seq'))
- input_grad: bfloat16 [3, 32, 320, 1024], P(None, ('fsdp', 'seq'))
- grad_ln1_gain: float32 [1024], P('fsdp')
- grad_ln1_shift: float32 [1024], P('fsdp')
- grad_w_qkv: float32 [1024, 3072], P('fsdp')
- grad_b_qv: float32 [2048], P('fsdp')
- grad_w_out: float32 [1024, 1024], P('fsdp')
- grad_b_out: float32 [1024], P('fsdp')
- grad_ln2_gain: float32 [1024], P('fsdp')
- grad_ln2_shift: float32 [1024], P('fsdp')
- grad_w_up: float32 [1024, 4096], P('fsdp')
- grad_b_up: float32 [4096], P('fsdp')
- grad_w_down: float32 [4096, 1024], P('fsdp')
- grad_b_down: float32 [1024], P('fsdp')
Inputs may be any that keep to these rules, and one draw needn't show every extreme that they name: counts[m, i] is 64 plus the image's kept slots; slots at and after it are padding; in every micro-batch each index of fsdp holds an image with all 320 slots live and one with only the 64 buffer slots.
All inputs are finite; a program needn't handle non-finite values.
Results may differ from a plain program's by a relative error of at most 0.018.
Values may be sent and summed in bfloat16 or wider, within the bound.
No kernel may reach another device: no remote copies, remote signals or barrier semaphores. Data moves between devices by JAX's collectives and lax.ppermute only.
A program may use at most 256 MiB of HBM per device.

v0:
```python
import jax
import jax.numpy as jnp
from jax import lax
from jax.sharding import PartitionSpec as P

HEADS = 16
HD = 64


epsilon = 1e-05


def as_sent(value):

    def short(part):
        return part.astype(jnp.bfloat16) if part.dtype == jnp.float32 else part

    return jax.tree.map(short, value)


def layer_norm(values, gain_vector, shift_vector):
    center = values - jnp.mean(values, axis=-1, keepdims=True)
    spread = jnp.mean(center * center, axis=-1, keepdims=True)
    return center * lax.rsqrt(spread + epsilon) * gain_vector + shift_vector


def times_transposed(left, right):
    return lax.dot_general(
        left, right, (((1,), (1,)), ((), ())), preferred_element_type=jnp.float32
    )


def transposed_times(left, right):
    return lax.dot_general(
        left, right, (((0,), (0,)), ((), ())), preferred_element_type=jnp.float32
    )


def masked_scores(query_part, key_part, live_keys, score_scale):
    scores = (
        jnp.einsum("bshd,bthd->bhst", query_part, key_part, preferred_element_type=jnp.float32)
        * score_scale
    )
    return jnp.where(live_keys, scores, -1e30)


def on_device(
    tokens,
    counts,
    ln1_gain,
    ln1_shift,
    w_qkv,
    b_qv,
    w_out,
    b_out,
    ln2_gain,
    ln2_shift,
    w_up,
    b_up,
    w_down,
    b_down,
    cotangent,
):
    gathered = (
        lax.all_gather(ln1_gain, "fsdp", axis=0, tiled=True),
        lax.all_gather(ln1_shift, "fsdp", axis=0, tiled=True),
        lax.all_gather(w_qkv, "fsdp", axis=0, tiled=True),
        lax.all_gather(b_qv, "fsdp", axis=0, tiled=True),
        lax.all_gather(w_out, "fsdp", axis=0, tiled=True),
        lax.all_gather(b_out, "fsdp", axis=0, tiled=True),
        lax.all_gather(ln2_gain, "fsdp", axis=0, tiled=True),
        lax.all_gather(ln2_shift, "fsdp", axis=0, tiled=True),
        lax.all_gather(w_up, "fsdp", axis=0, tiled=True),
        lax.all_gather(b_up, "fsdp", axis=0, tiled=True),
        lax.all_gather(w_down, "fsdp", axis=0, tiled=True),
        lax.all_gather(b_down, "fsdp", axis=0, tiled=True),
    )
    (
        gain_one,
        shift_one,
        qkv_weight,
        qkv_half,
        out_weight,
        out_bias,
        gain_two,
        shift_two,
        up_weight,
        up_bias,
        down_weight,
        down_bias,
    ) = gathered
    gain_one = gain_one.astype(jnp.float32)
    shift_one = shift_one.astype(jnp.float32)
    qkv_half = qkv_half.astype(jnp.float32)
    out_bias = out_bias.astype(jnp.float32)
    gain_two = gain_two.astype(jnp.float32)
    shift_two = shift_two.astype(jnp.float32)
    up_bias = up_bias.astype(jnp.float32)
    down_bias = down_bias.astype(jnp.float32)
    micro_count, images, slot_count, model_width = tokens.shape
    head_size = HD
    row_count = images * slot_count
    score_scale = head_size ** (-0.5)
    qkv_bias = jnp.concatenate(
        [qkv_half[:model_width], jnp.zeros((model_width,), jnp.float32), qkv_half[model_width:]]
    )
    positions = jnp.arange(slot_count, dtype=jnp.int32)
    own_start = lax.axis_index("seq") * images
    totals = [jnp.zeros(weight.shape, jnp.float32) for weight in gathered]
    output_blocks = []
    input_blocks = []
    for micro_index in range(micro_count):
        own_counts = lax.dynamic_slice_in_dim(counts[micro_index], own_start, images)
        live_keys = (positions[None, :] < own_counts[:, None])[:, None, None, :]
        flat_rows = tokens[micro_index].reshape(row_count, model_width).astype(jnp.float32)
        normed_one, norm_back_one = jax.vjp(layer_norm, flat_rows, gain_one, shift_one)
        normed_low = normed_one.astype(jnp.bfloat16)
        projected = (
            jnp.dot(normed_low, qkv_weight, preferred_element_type=jnp.float32) + qkv_bias
        ).astype(jnp.bfloat16)
        grouped = projected.reshape(images, slot_count, 3, HEADS, head_size)
        query_part = grouped[:, :, 0]
        key_part = grouped[:, :, 1]
        value_part = grouped[:, :, 2]
        scores = masked_scores(query_part, key_part, live_keys, score_scale)
        maximum = jnp.max(scores, axis=-1, keepdims=True)
        log_total = maximum + jnp.log(jnp.sum(jnp.exp(scores - maximum), axis=-1, keepdims=True))
        attention_low = jnp.exp(scores - log_total).astype(jnp.bfloat16)
        mixed = jnp.einsum(
            "bhst,bthd->bshd", attention_low, value_part, preferred_element_type=jnp.float32
        )
        mixed_rows = mixed.astype(jnp.bfloat16).reshape(row_count, model_width)
        middle = (
            flat_rows
            + jnp.dot(mixed_rows, out_weight, preferred_element_type=jnp.float32)
            + out_bias
        )
        normed_two, norm_back_two = jax.vjp(layer_norm, middle, gain_two, shift_two)
        normed_two_low = normed_two.astype(jnp.bfloat16)
        upper_in = jnp.dot(normed_two_low, up_weight, preferred_element_type=jnp.float32) + up_bias
        activated, gelu_back = jax.vjp(jax.nn.gelu, upper_in)
        hidden_low = activated.astype(jnp.bfloat16)
        result = (
            middle
            + jnp.dot(hidden_low, down_weight, preferred_element_type=jnp.float32)
            + down_bias
        )
        output_blocks.append(result.astype(jnp.bfloat16).reshape(images, slot_count, model_width))
        grad_out = cotangent[micro_index].reshape(row_count, model_width).astype(jnp.float32)
        grad_low = grad_out.astype(jnp.bfloat16)
        d_down_weight = transposed_times(hidden_low, grad_low)
        d_down_bias = jnp.sum(grad_low.astype(jnp.float32), axis=0)
        grad_hidden = times_transposed(grad_low, down_weight)
        grad_upper = gelu_back(grad_hidden)[0].astype(jnp.bfloat16)
        d_up_weight = transposed_times(normed_two_low, grad_upper)
        d_up_bias = jnp.sum(grad_upper.astype(jnp.float32), axis=0)
        grad_normed_two = times_transposed(grad_upper, up_weight)
        grad_from_norm, d_gain_two, d_shift_two = norm_back_two(grad_normed_two)
        grad_middle = grad_out + grad_from_norm
        grad_middle_low = grad_middle.astype(jnp.bfloat16)
        d_out_weight = transposed_times(mixed_rows, grad_middle_low)
        d_out_bias = jnp.sum(grad_middle_low.astype(jnp.float32), axis=0)
        grad_mixed = times_transposed(grad_middle_low, out_weight).astype(jnp.bfloat16)
        grad_grouped = grad_mixed.reshape(images, slot_count, HEADS, head_size)
        attention = jnp.exp(masked_scores(query_part, key_part, live_keys, score_scale) - log_total)
        attention_again = attention.astype(jnp.bfloat16)
        grad_attention = jnp.einsum(
            "bshd,bthd->bhst", grad_grouped, value_part, preferred_element_type=jnp.float32
        )
        grad_value = jnp.einsum(
            "bhst,bshd->bthd", attention_again, grad_grouped, preferred_element_type=jnp.float32
        )
        row_dot = jnp.sum(grad_attention * attention, axis=-1, keepdims=True)
        grad_scores = (attention * (grad_attention - row_dot)).astype(jnp.bfloat16)
        grad_query = (
            jnp.einsum("bhst,bthd->bshd", grad_scores, key_part, preferred_element_type=jnp.float32)
            * score_scale
        )
        grad_key = (
            jnp.einsum(
                "bhst,bshd->bthd", grad_scores, query_part, preferred_element_type=jnp.float32
            )
            * score_scale
        )
        grad_stacked = jnp.stack([grad_query, grad_key, grad_value], axis=2).astype(jnp.bfloat16)
        grad_projected = grad_stacked.reshape(row_count, 3 * model_width)
        d_qkv_weight = transposed_times(normed_low, grad_projected)
        column_sums = jnp.sum(grad_projected.astype(jnp.float32), axis=0)
        d_qkv_bias = jnp.concatenate([column_sums[:model_width], column_sums[2 * model_width :]])
        grad_normed_one = times_transposed(grad_projected, qkv_weight)
        grad_from_first, d_gain_one, d_shift_one = norm_back_one(grad_normed_one)
        input_blocks.append(
            (grad_middle + grad_from_first)
            .astype(jnp.bfloat16)
            .reshape(images, slot_count, model_width)
        )
        updates = (
            d_gain_one,
            d_shift_one,
            d_qkv_weight,
            d_qkv_bias,
            d_out_weight,
            d_out_bias,
            d_gain_two,
            d_shift_two,
            d_up_weight,
            d_up_bias,
            d_down_weight,
            d_down_bias,
        )
        totals = [before + update for before, update in zip(totals, updates)]
    partials = tuple(totals)
    shared = jax.tree.map(
        lambda part: part.astype(jnp.float32),
        lax.psum_scatter(as_sent(partials), "fsdp", scatter_dimension=0, tiled=True),
    )
    summed = jax.tree.map(lambda part: part.astype(jnp.float32), lax.psum(as_sent(shared), "seq"))
    activations = jnp.stack(output_blocks, axis=0)
    input_grad = jnp.stack(input_blocks, axis=0)
    return (
        activations,
        input_grad,
        summed[0],
        summed[1],
        summed[2],
        summed[3],
        summed[4],
        summed[5],
        summed[6],
        summed[7],
        summed[8],
        summed[9],
        summed[10],
        summed[11],
    )


def solution(mesh):
    in_specs = (
        P(None, ("fsdp", "seq"), None, None),
        P(None, "fsdp"),
        P("fsdp"),
        P("fsdp"),
        P("fsdp", None),
        P("fsdp"),
        P("fsdp", None),
        P("fsdp"),
        P("fsdp"),
        P("fsdp"),
        P("fsdp", None),
        P("fsdp"),
        P("fsdp", None),
        P("fsdp"),
        P(None, ("fsdp", "seq"), None, None),
    )
    out_specs = (
        P(None, ("fsdp", "seq"), None, None),
        P(None, ("fsdp", "seq"), None, None),
        P("fsdp"),
        P("fsdp"),
        P("fsdp", None),
        P("fsdp"),
        P("fsdp", None),
        P("fsdp"),
        P("fsdp"),
        P("fsdp"),
        P("fsdp", None),
        P("fsdp"),
        P("fsdp", None),
        P("fsdp"),
    )
    return jax.shard_map(
        on_device, mesh=mesh, in_specs=in_specs, out_specs=out_specs, check_vma=False
    )
```

profile of v0, /device:TPU:8, one launch (start us, length us, event | category | flops | bytes accessed | tf_op | source)
XLA Modules:
  0.0 815.0 jit_solution(212791826634680455)
XLA Ops:
  10.1 9.0 %all-gather.3 = bf16[8,1,128]{2,1,0:T(2,128)(2,1)S(1)} all-gather(bf16[1,1,128]{2,1,0:T(2,128)(2,1)S(1)} %bitcast.462), channel_id=1, replica_groups=mesh['fsdp'=8,'seq'=4] {'fsdp'}, dimensions={0}, use_global_device_ids=true | all-gather | bytes 2304 | tf_op jit(solution)/shard_map/all_gather | solution.py:70
  19.2 11.8 %all-gather.1 = bf16[8,1,128]{2,1,0:T(2,128)(2,1)S(1)} all-gather(bf16[1,1,128]{2,1,0:T(2,128)(2,1)S(1)} %bitcast.463), channel_id=1, replica_groups=mesh['fsdp'=8,'seq'=4] {'fsdp'}, dimensions={0}, use_global_device_ids=true | all-gather | bytes 2304 | tf_op jit(solution)/shard_map/all_gather | solution.py:66
  31.0 8.6 %all-gather = bf16[8,1,128]{2,1,0:T(2,128)(2,1)S(1)} all-gather(bf16[1,1,128]{2,1,0:T(2,128)(2,1)S(1)} %bitcast.464), channel_id=1, replica_groups=mesh['fsdp'=8,'seq'=4] {'fsdp'}, dimensions={0}, use_global_device_ids=true | all-gather | bytes 2304 | tf_op jit(solution)/shard_map/all_gather | solution.py:65
  39.6 11.9 %all-gather.6 = bf16[8,1,512]{2,1,0:T(2,128)(2,1)S(1)} all-gather(bf16[1,1,512]{2,1,0:T(2,128)(2,1)S(1)} %reshape.876), channel_id=1, replica_groups=mesh['fsdp'=8,'seq'=4] {'fsdp'}, dimensions={0}, use_global_device_ids=true | all-gather | bytes 9216 | tf_op jit(solution)/shard_map/all_gather | solution.py:74
  51.6 11.7 %all-gather.5 = bf16[8,1,128]{2,1,0:T(2,128)(2,1)S(1)} all-gather(bf16[1,1,128]{2,1,0:T(2,128)(2,1)S(1)} %bitcast.465), channel_id=1, replica_groups=mesh['fsdp'=8,'seq'=4] {'fsdp'}, dimensions={0}, use_global_device_ids=true | all-gather | bytes 2304 | tf_op jit(solution)/shard_map/all_gather | solution.py:72
  63.3 8.9 %all-gather.4 = bf16[8,1,128]{2,1,0:T(2,128)(2,1)S(1)} all-gather(bf16[1,1,128]{2,1,0:T(2,128)(2,1)S(1)} %bitcast.466), channel_id=1, replica_groups=mesh['fsdp'=8,'seq'=4] {'fsdp'}, dimensions={0}, use_global_device_ids=true | all-gather | bytes 2304 | tf_op jit(solution)/shard_map/all_gather | solution.py:71
  73.4 9.9 %all-gather.2 = bf16[8,1,256]{2,1,0:T(2,128)(2,1)S(1)} all-gather(bf16[1,1,256]{2,1,0:T(2,128)(2,1)S(1)} %reshape.868), channel_id=1, replica_groups=mesh['fsdp'=8,'seq'=4] {'fsdp'}, dimensions={0}, use_global_device_ids=true | all-gather | bytes 4608 | tf_op jit(solution)/shard_map/all_gather | solution.py:68
  87.9 6.4 fusion.29
  94.3 4.2 copy.78
  98.5 6.5 fusion.28
  104.9 4.3 copy.76
  109.2 3.5 fusion.2
  116.4 3.3 convolution_convert_fusion
  119.8 2.9 fusion.199
  129.0 2.4 convolution_convert_fusion.1
  132.8 53.1 %all-gather.17.cloned.1.call-done = bf16[1024,4096]{1,0:T(8,128)(2,1)} async-done(((bf16[128,4096]{1,0:T(8,128)(2,1)}), bf16[1024,4096]{1,0:T(8,128)(2,1)}) %all-gather.17.cloned.1.call-update) | async-done | bytes 8388624 | tf_op jit(solution)/shard_map/all_gather | solution.py:73
  185.8 9.3 %convolution_add_fusion = f32[320,4096]{1,0:T(8,128)} fusion(bf16[1024,4096]{1,0:T(8,128)(2,1)} %all-gather.17.cloned.1.call-done, f32[4096]{0:T(1024)S(1)} %bitcast.454, f32[320,1024]{1,0:T(8,128)} %copy-done.14, f32[320]{0:T(512)S(1)} %fusion.176, f32[320]{0:T(512)S(1)} %broadcast_multiply_fusion, f32[1024]{0:T(1024)S(1)} %bitcast.429, f32[1024]{0:T(1024)S(1)} %bitcast.419), kind=kOutput, calls=%fused_computation.27 | convolution fusion | flops 2687303680 | bytes 14969344 | tf_op jit(solution)/shard_map/dot_general | solution.py:140
  195.2 4.8 convolution_add_fusion.1
  199.9 68.0 %all-gather.19.cloned.1.call-done = bf16[4096,1024]{1,0:T(8,128)(2,1)} async-done(((bf16[512,1024]{1,0:T(8,128)(2,1)}), bf16[4096,1024]{1,0:T(8,128)(2,1)}) %all-gather.19.cloned.1.call-update) | async-done | bytes 8388624 | tf_op jit(solution)/shard_map/all_gather | solution.py:75
  267.9 9.8 %convert_reduce_fusion.1 = (f32[4096]{0:T(1024)}, bf16[320,4096]{1,0:T(8,128)(2,1)S(1)}) fusion(f32[320,4096]{1,0:T(8,128)} %convolution_add_fusion.1, bf16[4096,1024]{1,0:T(8,128)(2,1)} %all-gather.19.cloned.1.call-done, bf16[3,1,320,1024]{3,2,1,0:T(8,128)(2,1)} %param.29), kind=kOutput, calls=%fused_computation.52 | convolution fusion | flops 2713186304 | bytes 16924672 | tf_op jit(solution)/shard_map/dot_general | solution.py:28
  277.7 6.3 fusion.202
  284.2 9.0 %convert_reduce_fusion = (f32[4096]{0:T(1024)}, bf16[320,4096]{1,0:T(8,128)(2,1)S(1)}) fusion(f32[320,4096]{1,0:T(8,128)S(1)} %copy-done.35, bf16[4096,1024]{1,0:T(8,128)(2,1)} %all-gather.19.cloned.1.call-done, bf16[3,1,320,1024]{3,2,1,0:T(8,128)(2,1)S(1)} %copy-done.4), kind=kOutput, calls=%fused_computation.51 | convolution fusion | flops 2713186304 | bytes 16924672 | tf_op jit(solution)/shard_map/dot_general | solution.py:28
  293.2 7.8 multiply_reduce_fusion.3
  306.1 6.2 convolution_bitcast_fusion
  312.2 5.4 multiply_reduce_fusion
  317.7 2.4 multiply_convert_fusion
  326.4 5.3 convolution_bitcast_fusion.1
  331.8 5.4 multiply_reduce_fusion.1
  337.2 2.8 multiply_convert_fusion.1
  342.7 3.3 fusion.205
  348.6 3.0 fusion.203
  351.6 4.9 fusion.75
  356.5 3.7 fusion.27
  360.1 4.3 copy.74
  364.4 3.5 fusion
  369.7 2.2 copy-done.2
  371.9 3.3 convolution_convert_fusion.2
  376.6 3.0 convolution_add_fusion.2
  379.6 10.7 %convert_reduce_fusion.2 = (f32[4096]{0:T(1024)}, bf16[320,4096]{1,0:T(8,128)(2,1)S(1)}) fusion(f32[320,4096]{1,0:T(8,128)S(1)} %convolution_add_fusion.2, bf16[4096,1024]{1,0:T(8,128)(2,1)} %all-gather.19.cloned.1.call-done, bf16[3,1,320,1024]{3,2,1,0:T(8,128)(2,1)S(1)} %copy-done.5), kind=kOutput, calls=%fused_computation.53 | convolution fusion | flops 2713186304 | bytes 16924672 | tf_op jit(solution)/shard_map/dot_general | solution.py:28
  390.4 7.2 multiply_reduce_fusion.5
  399.1 3.2 fusion.204
  403.6 9.6 %multiply_reduce_fusion.2 = (f32[16,320]{1,0:T(8,128)S(1)}, f32[16,320,320]{1,2,0:T(8,128)}) fusion(f32[16,320,320]{1,2,0:T(8,128)} %copy-done.2, f32[16,320]{1,0:T(8,128)S(1)} %log_add_fusion.2, pred[320]{0:T(512)(128)(4,1)S(1)} %copy-done.117, bf16[320,16,64]{0,2,1:T(8,128)(2,1)S(1)} %bitcast.411, bf16[1,320,3,16,64]{1,4,3,2,0:T(8,128)(2,1)} %bitcast.398), kind=kOutput, calls=%fused_computation.8 | convolution fusion | flops 217902080 | bytes 15900992 | tf_op jit(solution)/shard_map/bshd,bthd->bhst/dot_general | solution.py:167
  413.2 2.6 add_convert_fusion.3
  415.9 7.3 multiply_convert_fusion.2
  425.5 5.2 convolution_bitcast_fusion.2
  432.4 6.9 fusion.108
  439.3 6.8 fusion.111
  446.1 13.8 %add_convert_fusion.2 = bf16[1024,3072]{1,0:T(8,128)(2,1)} fusion(f32[1024,3072]{1,0:T(8,128)} %fusion.111, f32[1024,3072]{1,0:T(8,128)} %fusion.108, bf16[320,3072]{0,1:T(8,128)(2,1)} %bitcast.402, f32[320]{0:T(512)S(1)} %copy-done.102, f32[320]{0:T(512)S(1)} %copy-done.92, f32[1024]{0:T(1024)S(1)} %bitcast.450, f32[1024]{0:T(1024)S(1)} %bitcast.441, ...), kind=kOutput, calls=%fused_computation.2 | convolution fusion | flops 2024669184 | bytes 34091008 | tf_op jit(solution)/shard_map/dot_general | solution.py:34
  460.6 12.8 %fusion.180 = f32[1024,4096]{1,0:T(8,128)} fusion(bf16[320,4096]{1,0:T(8,128)(2,1)} %copy-done.48, f32[320,1024]{1,0:T(8,128)} %copy-done.12, f32[1024]{0:T(1024)S(1)} %bitcast.432, f32[1024]{0:T(1024)S(1)} %bitcast.426, f32[320]{0:T(512)S(1)} %copy-done.76, f32[320]{0:T(512)S(1)} %copy-done.69), kind=kOutput, calls=%fused_computation.321 | convolution fusion | flops 2685992960 | bytes 20720128 | tf_op jit(solution)/shard_map/dot_general | solution.py:34
  473.4 8.5 %fusion.181 = f32[1024,4096]{1,0:T(8,128)} fusion(bf16[320,4096]{1,0:T(8,128)(2,1)S(1)} %copy-done.47, f32[320,1024]{1,0:T(8,128)S(1)} %copy-done.11, f32[320]{0:T(512)S(1)} %copy-done.74, f32[320]{0:T(512)S(1)} %copy-done.67, f32[1024]{0:T(1024)S(1)} %bitcast.433, f32[1024]{0:T(1024)S(1)} %bitcast.427), kind=kOutput, calls=%fused_computation.322 | convolution fusion | flops 2685992960 | bytes 20720128 | tf_op jit(solution)/shard_map/dot_general | solution.py:34
  481.9 16.7 %add_convert_fusion.1 = bf16[1024,4096]{1,0:T(8,128)(2,1)} fusion(f32[1024,4096]{1,0:T(8,128)} %fusion.180, f32[1024,4096]{1,0:T(8,128)} %fusion.181, bf16[320,4096]{1,0:T(8,128)(2,1)} %copy-done.43, f32[320,1024]{1,0:T(8,128)} %copy-done.14, f32[320]{0:T(512)S(1)} %copy-done.94, f32[320]{0:T(512)S(1)} %copy-done.86, f32[1024]{0:T(1024)S(1)} %bitcast.434, ...), kind=kOutput, calls=%fused_computation.1 | convolution fusion | flops 2698575872 | bytes 45885952 | tf_op jit(solution)/shard_map/dot_general | solution.py:34
  499.1 13.4 %fusion.127 = f32[4096,1024]{1,0:T(8,128)} fusion(bf16[3,1,320,1024]{3,2,1,0:T(8,128)(2,1)} %param.29, f32[320,4096]{1,0:T(8,128)} %copy-done.34), kind=kOutput, calls=%fused_computation.228 | convolution fusion | flops 2696151040 | bytes 22675456 | tf_op jit(solution)/shard_map/dot_general | solution.py:34
  512.5 13.4 %fusion.121 = f32[4096,1024]{1,0:T(8,128)} fusion(bf16[3,1,320,1024]{3,2,1,0:T(8,128)(2,1)} %param.29, f32[320,4096]{1,0:T(8,128)} %convolution_add_fusion.1), kind=kOutput, calls=%fused_computation.224 | convolution fusion | flops 2696151040 | bytes 22675456 | tf_op jit(solution)/shard_map/dot_general | solution.py:34
  526.0 17.2 %add_convert_fusion = bf16[4096,1024]{1,0:T(8,128)(2,1)} fusion(f32[4096,1024]{1,0:T(8,128)} %fusion.127, f32[4096,1024]{1,0:T(8,128)} %fusion.121, bf16[3,1,320,1024]{3,2,1,0:T(8,128)(2,1)} %param.29, f32[320,4096]{1,0:T(8,128)} %convolution_add_fusion), kind=kOutput, calls=%fused_computation | convolution fusion | flops 2708733952 | bytes 47841280 | tf_op jit(solution)/shard_map/dot_general | solution.py:34
  543.9 12.8 %all-gather.7 = bf16[8,1,128]{2,1,0:T(2,128)(2,1)S(1)} all-gather(bf16[1,1,128]{2,1,0:T(2,128)(2,1)S(1)} %bitcast.467), channel_id=1, replica_groups=mesh['fsdp'=8,'seq'=4] {'fsdp'}, dimensions={0}, use_global_device_ids=true | all-gather | bytes 2304 | tf_op jit(solution)/shard_map/all_gather | solution.py:76
  559.8 8.3 %fusion.71 = (f32[1024]{0:T(1024)S(1)}, f32[320]{0:T(512)S(1)}, f32[320]{0:T(512)S(1)}, f32[1024]{0:T(1024)S(1)}, f32[320]{0:T(512)S(1)}, /*index=5*/f32[1024]{0...) fusion(f32[320,1024]{1,0:T(8,128)} %copy-done.52, f32[320]{0:T(512)S(1)} %copy-done.102, f32[320]{0:T(512)S(1)} %copy-done.92, ...), kind=kOutput, calls=%fused_computation.155 | convolution fusion | flops 2022763520 | bytes 14189056 | tf_op jit(solution)/shard_map/dot_general | solution.py:28
  570.7 25.5 %all-reduce.8 = (bf16[1024]{0:T(1024)(128)(2,1)S(1)}, bf16[1024]{0:T(1024)(128)(2,1)S(1)}, bf16[2048]{0:T(1024)(128)(2,1)S(1)}, bf16[1024]{0:T(1024)(128)(2,1)S(...) all-reduce(bf16[1024]{0:T(1024)(128)(2,1)S(1)} %add_convert_fusion., ...), channel_id=2, replica_groups=mesh['fsdp'=8,'seq'=4] {'fsdp'}, use_global_device_ids=true, to_apply=%region_36.37.clone | all-reduce | flops 12288 | bytes 49152
  596.7 10.5 %all-reduce.9 = (bf16[128]{0:T(256)(128)(2,1)S(1)}, bf16[128]{0:T(256)(128)(2,1)S(1)}, bf16[256]{0:T(256)(128)(2,1)S(1)}, bf16[128]{0:T(256)(128)(2,1)S(1)}, bf1...) all-reduce(bf16[128]{0:T(256)(128)(2,1)S(1)} %dynamic-slice.4, ...), channel_id=1, replica_groups=mesh['fsdp'=8,'seq'=4] {'seq'}, use_global_device_ids=true, to_apply=%region_37.38 | all-reduce | flops 1536 | bytes 6144 | tf_op jit(solution)/shard_map/psum | solution.py:217
  611.4 9.6 %fusion.92 = bf16[1,1,320,1024]{3,2,1,0:T(8,128)(2,1)} fusion(f32[320,1024]{1,0:T(8,128)} %copy-done.14, bf16[4096,1024]{1,0:T(8,128)(2,1)} %all-gather.19.cloned.1.call-done, f32[1024]{0:T(1024)S(1)} %bitcast.459, f32[320,4096]{1,0:T(8,128)} %convolution_add_fusion), kind=kOutput, calls=%fused_computation.194 | convolution fusion | flops 2697134080 | bytes 15601664 | tf_op jit(solution)/shard_map/dot_general | solution.py:145
  621.0 88.4 %reduce-scatter.11.cloned.1.call-done = bf16[512,1024]{1,0:T(8,128)(2,1)} async-done(((bf16[4096,1024]{1,0:T(8,128)(2,1)}), bf16[512,1024]{1,0:T(8,128)(2,1)}) %reduce-scatter.11.cloned.1.call-update) | async-done | bytes 1048592 | tf_op jit(solution)/shard_map/reduce_scatter | solution.py:215
  709.4 8.4 %fusion.91 = bf16[1,1,320,1024]{3,2,1,0:T(8,128)(2,1)S(1)} fusion(f32[320,1024]{1,0:T(8,128)S(1)} %copy-done.11, bf16[4096,1024]{1,0:T(8,128)(2,1)} %all-gather.19.cloned.1.call-done, f32[1024]{0:T(1024)S(1)} %bitcast.460, f32[320,4096]{1,0:T(8,128)} %convolution_add_fusion.1), kind=kOutput, calls=%fused_computation.193 | convolution fusion | flops 2697134080 | bytes 15601664 | tf_op jit(solution)/shard_map/dot_general | solution.py:145
  717.9 9.5 %fusion.90 = bf16[1,1,320,1024]{3,2,1,0:T(8,128)(2,1)S(1)} fusion(f32[320,1024]{1,0:T(8,128)S(1)} %copy-done.13, bf16[4096,1024]{1,0:T(8,128)(2,1)} %all-gather.19.cloned.1.call-done, f32[1024]{0:T(1024)S(1)} %bitcast.461, f32[320,4096]{1,0:T(8,128)} %copy-done.34), kind=kOutput, calls=%fused_computation.192 | convolution fusion | flops 2697134080 | bytes 15601664 | tf_op jit(solution)/shard_map/dot_general | solution.py:145
  732.9 68.9 %all-reduce.13.cloned.1.call-done = (bf16[128,3072]{1,0:T(8,128)(2,1)}, bf16[128,1024]{1,0:T(8,128)(2,1)}, bf16[128,4096]{1,0:T(8,128)(2,1)}, bf16[512,1024]{1,0:T(8,128)(2,1)}) async-done(((bf16[128,3072]{1,0:T(8,128)(2,1)}, bf16[128,1024]{1,0:T(8,128)(2,1)}, bf16[128,4096]{1,0:T(8,128)(2,1)}, bf16[512,1024]{1,0:T(8,128)(2,1)}), (bf16[128,3072]{1,0:T(8,128)(2,1)}, bf16[128,1024]{1,0:T(8,128)(2,1)}, ...) | async-done | bytes 3145744 | tf_op jit(solution)/shard_map/psum | solution.py:217
  801.8 2.5 convert_element_type.508
  (447 shorter events, 65.2 us)
Async XLA Ops:
  7.2 11.9 %copy-start.143 = (bf16[256]{0:T(256)(128)(2,1)S(1)}, bf16[256]{0:T(256)(128)(2,1)}, u32[]{:S(2)}) copy-start(bf16[256]{0:T(256)(128)(2,1)} %param.20) | copy-start | bytes 1540
  7.2 12.0 %copy-start.137 = (bf16[128]{0:T(256)(128)(2,1)S(1)}, bf16[128]{0:T(256)(128)(2,1)}, u32[]{:S(2)}) copy-start(bf16[128]{0:T(256)(128)(2,1)} %param.18) | copy-start | bytes 772
  7.2 23.8 %copy-start.138 = (bf16[128]{0:T(256)(128)(2,1)S(1)}, bf16[128]{0:T(256)(128)(2,1)}, u32[]{:S(2)}) copy-start(bf16[128]{0:T(256)(128)(2,1)} %param.17) | copy-start | bytes 772
  7.2 32.4 %copy-start.135 = (bf16[512]{0:T(512)(128)(2,1)S(1)}, bf16[512]{0:T(512)(128)(2,1)}, u32[]{:S(2)}) copy-start(bf16[512]{0:T(512)(128)(2,1)} %param.26) | copy-start | bytes 3076
  7.2 44.4 %copy-start.139 = (bf16[128]{0:T(256)(128)(2,1)S(1)}, bf16[128]{0:T(256)(128)(2,1)}, u32[]{:S(2)}) copy-start(bf16[128]{0:T(256)(128)(2,1)} %param.24) | copy-start | bytes 772
  7.2 56.1 %copy-start.140 = (bf16[128]{0:T(256)(128)(2,1)S(1)}, bf16[128]{0:T(256)(128)(2,1)}, u32[]{:S(2)}) copy-start(bf16[128]{0:T(256)(128)(2,1)} %param.23) | copy-start | bytes 772
  7.3 65.0 %copy-start.134 = (s32[3,4]{1,0:T(4,128)S(1)}, s32[3,4]{1,0:T(4,128)}, u32[]{:S(2)}) copy-start(s32[3,4]{1,0:T(4,128)} %param.16) | copy-start | bytes 148
  7.3 78.6 %copy-start.3 = (bf16[3,1,320,1024]{3,2,1,0:T(8,128)(2,1)S(1)}, bf16[3,1,320,1024]{3,2,1,0:T(8,128)(2,1)}, u32[]{:S(2)}) copy-start(bf16[3,1,320,1024]{3,2,1,0:T(8,128)(2,1)} %param.15) | copy-start | bytes 5898244
  7.3 80.6 %all-gather.13.cloned.1.call-start = ((), (), s32[]{:S(2)}) async-start(), calls=%async_computation.4 | async-start | bytes 7077888 | tf_op jit(solution)/shard_map/all_gather | solution.py:67
  8.0 111.7 %all-gather.15.cloned.1.call-start = ((), (), s32[]{:S(2)}) async-start(), calls=%async_computation.5 | async-start | bytes 2359296 | tf_op jit(solution)/shard_map/all_gather | solution.py:69
  8.8 177.1 %all-gather.17.cloned.1.call-start = ((), (), s32[]{:S(2)}) async-start(), calls=%async_computation.6 | async-start | bytes 9437184 | tf_op jit(solution)/shard_map/all_gather | solution.py:73
  9.5 258.4 %all-gather.19.cloned.1.call-start = ((), (), s32[]{:S(2)}) async-start(), calls=%async_computation.7 | async-start | bytes 9437184 | tf_op jit(solution)/shard_map/all_gather | solution.py:75
  10.1 610.9 %reduce-scatter.7.cloned.1.call-start = ((), (), s32[]{:S(2)}) async-start(), calls=%async_computation.9 | async-start | bytes 2359296 | tf_op jit(solution)/shard_map/reduce_scatter | solution.py:215
  19.1 112.3 %copy-start.59 = (f32[8,1,128]{2,1,0:T(1,128)}, f32[8,1,128]{2,1,0:T(1,128)S(1)}, u32[]{:S(2)}) copy-start(f32[8,1,128]{2,1,0:T(1,128)S(1)} %convert_element_type.539) | copy-start | bytes 12292
  51.6 143.6 %copy-start.111 = (f32[8,1,512]{2,1,0:T(1,128)}, f32[8,1,512]{2,1,0:T(1,128)S(1)}, u32[]{:S(2)}) copy-start(f32[8,1,512]{2,1,0:T(1,128)S(1)} %convert_element_type.542) | copy-start | bytes 49156
  84.0 30.5 %copy-start.121 = (pred[320]{0:T(512)(128)(4,1)}, pred[320]{0:T(512)(128)(4,1)S(1)}, u32[]{:S(2)}) copy-start(pred[320]{0:T(512)(128)(4,1)S(1)} %iota_compare_fusion) | copy-start | bytes 964
  84.6 43.0 %copy-start.119 = (pred[320]{0:T(512)(128)(4,1)}, pred[320]{0:T(512)(128)(4,1)S(1)}, u32[]{:S(2)}) copy-start(pred[320]{0:T(512)(128)(4,1)S(1)} %iota_compare_fusion.1) | copy-start | bytes 964
  85.9 12.6 %copy-start.115 = (f32[3072]{0:T(1024)}, f32[3072]{0:T(1024)S(1)}, u32[]{:S(2)}) copy-start(f32[3072]{0:T(1024)S(1)} %pad_maximum_fusion.2) | copy-start | bytes 36868
  86.2 12.2 %copy-start.77 = (f32[320]{0:T(512)}, f32[320]{0:T(512)S(1)}, u32[]{:S(2)}) copy-start(f32[320]{0:T(512)S(1)} %get-tuple-element.137) | copy-start | bytes 3844
  87.3 11.2 %copy-start.87 = (f32[320]{0:T(512)}, f32[320]{0:T(512)S(1)}, u32[]{:S(2)}) copy-start(f32[320]{0:T(512)S(1)} %fusion.173) | copy-start | bytes 3844
  122.6 178.4 %copy-start.85 = (f32[320]{0:T(512)}, f32[320]{0:T(512)S(1)}, u32[]{:S(2)}) copy-start(f32[320]{0:T(512)S(1)} %broadcast_multiply_fusion) | copy-start | bytes 3844
  132.4 168.7 %copy-start.10 = (f32[320,1024]{1,0:T(8,128)}, f32[320,1024]{1,0:T(8,128)S(1)}, u32[]{:S(2)}) copy-start(f32[320,1024]{1,0:T(8,128)S(1)} %get-tuple-element.115) | copy-start | bytes 3932164
  132.4 168.6 %copy-start.66 = (f32[320]{0:T(512)}, f32[320]{0:T(512)S(1)}, u32[]{:S(2)}) copy-start(f32[320]{0:T(512)S(1)} %broadcast_multiply_fusion.2) | copy-start | bytes 3844
  132.7 168.3 %copy-start.93 = (f32[320]{0:T(512)}, f32[320]{0:T(512)S(1)}, u32[]{:S(2)}) copy-start(f32[320]{0:T(512)S(1)} %fusion.176) | copy-start | bytes 3844
  132.8 168.3 %copy-start.73 = (f32[320]{0:T(512)}, f32[320]{0:T(512)S(1)}, u32[]{:S(2)}) copy-start(f32[320]{0:T(512)S(1)} %fusion.174) | copy-start | bytes 3844
  185.8 9.3 %copy-start.142 = (bf16[1024,4096]{1,0:T(8,128)(2,1)S(1)}, bf16[1024,4096]{1,0:T(8,128)(2,1)}, u32[]{:S(2)}) copy-start(bf16[1024,4096]{1,0:T(8,128)(2,1)} %all-gather.17.cloned.1.call-done) | copy-start | bytes 25165828
  284.2 9.1 %copy-start.15 = (f32[320,1024]{1,0:T(8,128)S(1)}, f32[320,1024]{1,0:T(8,128)}, u32[]{:S(2)}) copy-start(f32[320,1024]{1,0:T(8,128)} %copy-done.14) | copy-start | bytes 3932164
  306.1 11.6 %slice-start = ((s8[7864320]{0:T(1024)(128)(4,1)}), s8[4194304]{0:T(1024)(128)(4,1)S(1)}, s32[]{:S(2)}) async-start(s8[7864320]{0:T(1024)(128)(4,1)} %bitcast.382), calls=%async_computation.13 | async-start | bytes 8388608
  326.4 10.8 %slice-start.2 = ((s8[7864320]{0:T(1024)(128)(4,1)}), s8[4194304]{0:T(1024)(128)(4,1)S(1)}, s32[]{:S(2)}) async-start(s8[7864320]{0:T(1024)(128)(4,1)} %bitcast.384), calls=%async_computation.15 | async-start | bytes 8388608
  368.0 8.6 %slice-start.4 = ((s8[8388608]{0:T(1024)(128)(4,1)}), s8[4194304]{0:T(1024)(128)(4,1)S(1)}, s32[]{:S(2)}) async-start(s8[8388608]{0:T(1024)(128)(4,1)} %bitcast.468), calls=%async_computation.17 | async-start | bytes 8388608
  371.9 43.9 %copy-start.64 = (f32[16,320]{1,0:T(8,128)}, f32[16,320]{1,0:T(8,128)S(1)}, u32[]{:S(2)}) copy-start(f32[16,320]{1,0:T(8,128)S(1)} %log_add_fusion.2) | copy-start | bytes 61444
  376.2 21.4 %copy-start.12 = (f32[320,1024]{1,0:T(8,128)}, f32[320,1024]{1,0:T(8,128)S(1)}, u32[]{:S(2)}) copy-start(f32[320,1024]{1,0:T(8,128)S(1)} %get-tuple-element.125) | copy-start | bytes 3932164
  376.3 21.4 %copy-start.68 = (f32[320]{0:T(512)}, f32[320]{0:T(512)S(1)}, u32[]{:S(2)}) copy-start(f32[320]{0:T(512)S(1)} %broadcast_multiply_fusion.4) | copy-start | bytes 3844
  376.6 21.0 %copy-start.75 = (f32[320]{0:T(512)}, f32[320]{0:T(512)S(1)}, u32[]{:S(2)}) copy-start(f32[320]{0:T(512)S(1)} %fusion.172) | copy-start | bytes 3844
  379.6 10.8 %copy-start.34 = (f32[320,4096]{1,0:T(8,128)}, f32[320,4096]{1,0:T(8,128)S(1)}, u32[]{:S(2)}) copy-start(f32[320,4096]{1,0:T(8,128)S(1)} %convolution_add_fusion.2) | copy-start | bytes 15728644
  403.6 9.6 %copy-start.8 = (f32[1024,1024]{1,0:T(8,128)S(1)}, f32[1024,1024]{1,0:T(8,128)}, u32[]{:S(2)}) copy-start(f32[1024,1024]{1,0:T(8,128)} %fusion.205) | copy-start | bytes 12582916
  403.6 9.6 %copy-start.9 = (f32[1024,1024]{1,0:T(8,128)S(1)}, f32[1024,1024]{1,0:T(8,128)}, u32[]{:S(2)}) copy-start(f32[1024,1024]{1,0:T(8,128)} %fusion.204) | copy-start | bytes 12582916
  403.6 9.6 %copy-start.41 = (bf16[16,64,320]{2,1,0:T(8,128)(2,1)S(1)}, bf16[16,64,320]{2,1,0:T(8,128)(2,1)}, u32[]{:S(2)}) copy-start(bf16[16,64,320]{2,1,0:T(8,128)(2,1)} %copy-done.40) | copy-start | bytes 1966084
  403.6 9.6 %copy-start.45 = (bf16[320,1024]{1,0:T(8,128)(2,1)S(1)}, bf16[320,1024]{1,0:T(8,128)(2,1)}, u32[]{:S(2)}) copy-start(bf16[320,1024]{1,0:T(8,128)(2,1)} %copy-done.44) | copy-start | bytes 1966084
  415.8 205.2 %reduce-scatter.5.cloned.1.call-start = ((), (), s32[]{:S(2)}) async-start(), calls=%async_computation.8 | async-start | bytes 7077888 | tf_op jit(solution)/shard_map/reduce_scatter | solution.py:215
  460.0 13.4 %copy-start.11 = (f32[320,1024]{1,0:T(8,128)S(1)}, f32[320,1024]{1,0:T(8,128)}, u32[]{:S(2)}) copy-start(f32[320,1024]{1,0:T(8,128)} %copy-done.10) | copy-start | bytes 3932164
  460.0 13.4 %copy-start.67 = (f32[320]{0:T(512)S(1)}, f32[320]{0:T(512)}, u32[]{:S(2)}) copy-start(f32[320]{0:T(512)} %copy-done.66) | copy-start | bytes 3844
  460.0 13.4 %copy-start.74 = (f32[320]{0:T(512)S(1)}, f32[320]{0:T(512)}, u32[]{:S(2)}) copy-start(f32[320]{0:T(512)} %copy-done.73) | copy-start | bytes 3844
  460.0 161.0 %reduce-scatter.9.cloned.1.call-start = ((), (), s32[]{:S(2)}) async-start(), calls=%async_computation.10 | async-start | bytes 9437184 | tf_op jit(solution)/shard_map/reduce_scatter | solution.py:215
  460.6 12.8 %copy-start.47 = (bf16[320,4096]{1,0:T(8,128)(2,1)S(1)}, bf16[320,4096]{1,0:T(8,128)(2,1)}, u32[]{:S(2)}) copy-start(bf16[320,4096]{1,0:T(8,128)(2,1)} %copy-done.46) | copy-start | bytes 7864324
  473.4 8.5 %copy-start.86 = (f32[320]{0:T(512)S(1)}, f32[320]{0:T(512)}, u32[]{:S(2)}) copy-start(f32[320]{0:T(512)} %copy-done.85) | copy-start | bytes 3844
  473.4 8.5 %copy-start.94 = (f32[320]{0:T(512)S(1)}, f32[320]{0:T(512)}, u32[]{:S(2)}) copy-start(f32[320]{0:T(512)} %copy-done.93) | copy-start | bytes 3844
  498.6 210.8 %reduce-scatter.11.cloned.1.call-start = ((), (), s32[]{:S(2)}) async-start(), calls=%async_computation.11 | async-start | bytes 9437184 | tf_op jit(solution)/shard_map/reduce_scatter | solution.py:215
  543.2 13.5 %copy-start.144 = (u32[32]{0:T(128)S(1)}, u32[32]{0:T(128)}, u32[]{:S(2)}) copy-start(u32[32]{0:T(128)} %constant.70) | copy-start | bytes 388
  543.2 16.0 %copy-start.72 = (f32[3,16,64]{2,1,0:T(8,128)S(1)}, f32[3,16,64]{2,1,0:T(8,128)}, u32[]{:S(2)}) copy-start(f32[3,16,64]{2,1,0:T(8,128)} %get-tuple-element.76) | copy-start | bytes 36868
  543.2 16.2 %copy-start.71 = (f32[3,16,64]{2,1,0:T(8,128)S(1)}, f32[3,16,64]{2,1,0:T(8,128)}, u32[]{:S(2)}) copy-start(f32[3,16,64]{2,1,0:T(8,128)} %get-tuple-element.74) | copy-start | bytes 36868
  543.2 16.3 %copy-start.70 = (f32[3,16,64]{2,1,0:T(8,128)S(1)}, f32[3,16,64]{2,1,0:T(8,128)}, u32[]{:S(2)}) copy-start(f32[3,16,64]{2,1,0:T(8,128)} %get-tuple-element.72) | copy-start | bytes 36868
  543.2 16.5 %copy-start.98 = (f32[320]{0:T(512)S(1)}, f32[320]{0:T(512)}, u32[]{:S(2)}) copy-start(f32[320]{0:T(512)} %copy-done.97) | copy-start | bytes 3844
  543.2 16.5 %copy-start.133 = (f32[320]{0:T(512)S(1)}, f32[320]{0:T(512)}, u32[]{:S(2)}) copy-start(f32[320]{0:T(512)} %get-tuple-element.30) | copy-start | bytes 3844
  543.3 16.5 %copy-start.96 = (f32[320]{0:T(512)S(1)}, f32[320]{0:T(512)}, u32[]{:S(2)}) copy-start(f32[320]{0:T(512)} %copy-done.95) | copy-start | bytes 3844
  543.3 16.5 %copy-start.132 = (f32[320]{0:T(512)S(1)}, f32[320]{0:T(512)}, u32[]{:S(2)}) copy-start(f32[320]{0:T(512)} %get-tuple-element.29) | copy-start | bytes 3844
  543.3 16.5 %copy-start.80 = (f32[320]{0:T(512)S(1)}, f32[320]{0:T(512)}, u32[]{:S(2)}) copy-start(f32[320]{0:T(512)} %copy-done.77) | copy-start | bytes 3844
  543.3 16.5 %copy-start.89 = (f32[320]{0:T(512)S(1)}, f32[320]{0:T(512)}, u32[]{:S(2)}) copy-start(f32[320]{0:T(512)} %copy-done.87) | copy-start | bytes 3844
  543.3 258.5 %all-reduce.13.cloned.1.call-start = ((), (), s32[]{:S(2)}) async-start(), calls=%async_computation.12 | async-start | bytes 6291456 | tf_op jit(solution)/shard_map/psum | solution.py:217
  709.4 8.4 %copy-start.13 = (f32[320,1024]{1,0:T(8,128)S(1)}, f32[320,1024]{1,0:T(8,128)}, u32[]{:S(2)}) copy-start(f32[320,1024]{1,0:T(8,128)} %copy-done.12) | copy-start | bytes 3932164
  717.9 9.6 %copy-start.58 = (bf16[1,1,320,1024]{3,2,1,0:T(8,128)(2,1)S(1)}, bf16[1,1,320,1024]{3,2,1,0:T(8,128)(2,1)}, u32[]{:S(2)}) copy-start(bf16[1,1,320,1024]{3,2,1,0:T(8,128)(2,1)} %fusion.92) | copy-start | bytes 1966084
  717.9 11.1 %copy-start.29 = (f32[320,1024]{1,0:T(8,128)S(1)}, f32[320,1024]{1,0:T(8,128)}, u32[]{:S(2)}) copy-start(f32[320,1024]{1,0:T(8,128)} %copy-done.28) | copy-start | bytes 3932164
  717.9 11.1 %copy-start.37 = (f32[320,1024]{1,0:T(8,128)S(1)}, f32[320,1024]{1,0:T(8,128)}, u32[]{:S(2)}) copy-start(f32[320,1024]{1,0:T(8,128)} %copy-done.36) | copy-start | bytes 3932164
  717.9 11.1 %copy-start.54 = (f32[320,1024]{1,0:T(8,128)S(1)}, f32[320,1024]{1,0:T(8,128)}, u32[]{:S(2)}) copy-start(f32[320,1024]{1,0:T(8,128)} %get-tuple-element.121) | copy-start | bytes 3932164
  (98 other events, 354.2 us)
Sparse Core Ops, SparseCore 0:
  9.7 63.8 all-gather.12
  75.2 29.9 all-gather.14
  106.9 78.9 all-gather.16
  187.3 80.5 all-gather.18
  415.9 33.2 reduce-scatter.6
  460.1 68.0 reduce-scatter.4
  530.5 88.5 reduce-scatter.8
  621.4 87.9 reduce-scatter.10
  712.8 88.9 all-reduce.12
where the time goes:
time: 823 us; the launch traced here: 815 us
  matrix products  318 us (39%)
  waiting for transfers between devices  281 us (34%)
  blocking collectives  121 us (15%)
  other arithmetic  47.7 us (6%)
  local copies, waits for them, and re-layouts  28.8 us (3%)
  between operations  18.1 us (2%)
    dot_general x12, matrix products, transposed_times(): lax.dot_general(left, right, (((0,), (0,)), ((), ())), preferred_element_...  119 us
    reduce_scatter x4, waiting for transfers between devices, on_device(): lax.psum_scatter(as_sent(partials), 'fsdp', scatter_dimension=0, tiled=True)  88.4 us
    dot_general x12, matrix products, times_transposed(): lax.dot_general(left, right, (((1,), (1,)), ((), ())), preferred_element_...  70.5 us
    psum x1, waiting for transfers between devices, on_device(): lax.psum(as_sent(shared), 'seq')  68.9 us
    all_gather x1, waiting for transfers between devices, on_device(): lax.all_gather(w_down, 'fsdp', axis=0, tiled=True)  68 us
    all_gather x1, waiting for transfers between devices, on_device(): lax.all_gather(w_up, 'fsdp', axis=0, tiled=True)  53.1 us
    dot_general x3, matrix products, on_device(): jnp.dot(hidden_low, down_weight, preferred_element_type=jnp.float32)  27.5 us
    unnamed x1, blocking collectives  25.5 us
  transfers between devices with their start and end apart: 9, of which 4 were waited for; matrix products, arithmetic and copies ran while one was open for 29% of the time, Pallas kernels for 0%

commit v1 on v0

v1 whole, which is shorter than its diff:
```python
import jax
import jax.numpy as jnp
from jax import lax
from jax.experimental import pallas as pl
from jax.experimental.pallas import tpu as pltpu
from jax.sharding import PartitionSpec as P

HEADS = 16
HD = 64
LANES = 256
PER = LANES // HD
SCALE = HD ** (-0.5)
epsilon = 1e-05
BF = jnp.bfloat16
F32 = jnp.float32


def nt(a, b):
    return lax.dot_general(a, b, (((1,), (1,)), ((), ())), preferred_element_type=F32)


def tn(a, b):
    return lax.dot_general(a, b, (((0,), (0,)), ((), ())), preferred_element_type=F32)


def nn(a, b):
    return jnp.dot(a, b, preferred_element_type=F32)


def head_masks(rows):
    lane = lax.broadcasted_iota(jnp.int32, (rows, LANES), 1) // HD
    return [lane == h for h in range(PER)]


def attention_forward(counts_ref, qkv_ref, out_ref):
    slots, wide = qkv_ref.shape
    width = wide // 3
    live = counts_ref[pl.program_id(0)]
    masks = head_masks(slots)
    alive = lax.broadcasted_iota(jnp.int32, (slots, slots), 1) < live
    for g in range(width // LANES):
        q = qkv_ref[:, pl.ds(g * LANES, LANES)] * jnp.asarray(SCALE, BF)
        k = qkv_ref[:, pl.ds(width + g * LANES, LANES)]
        v = qkv_ref[:, pl.ds(2 * width + g * LANES, LANES)]
        zero = jnp.zeros_like(q)
        total = jnp.zeros((slots, LANES), F32)
        for mask in masks:
            s = jnp.where(alive, nt(jnp.where(mask, q, zero), k), -1e30)
            e = jnp.exp(s - jnp.max(s, axis=1, keepdims=True))
            p = e * (1.0 / jnp.sum(e, axis=1, keepdims=True))
            total += nn(p.astype(BF), jnp.where(mask, v, zero))
        out_ref[:, pl.ds(g * LANES, LANES)] = total.astype(BF)


def attention_backward(counts_ref, qkv_ref, do_ref, out_ref):
    slots, wide = qkv_ref.shape
    width = wide // 3
    live = counts_ref[pl.program_id(0)]
    masks = head_masks(slots)
    alive = lax.broadcasted_iota(jnp.int32, (slots, slots), 0) < live
    for g in range(width // LANES):
        q = qkv_ref[:, pl.ds(g * LANES, LANES)] * jnp.asarray(SCALE, BF)
        k = qkv_ref[:, pl.ds(width + g * LANES, LANES)]
        v = qkv_ref[:, pl.ds(2 * width + g * LANES, LANES)]
        do = do_ref[:, pl.ds(g * LANES, LANES)]
        zero = jnp.zeros_like(q)
        dq = jnp.zeros((slots, LANES), F32)
        dk = jnp.zeros((slots, LANES), F32)
        dv = jnp.zeros((slots, LANES), F32)
        for mask in masks:
            qh = jnp.where(mask, q, zero)
            doh = jnp.where(mask, do, zero)
            s = jnp.where(alive, nt(k, qh), -1e30)
            e = jnp.exp(s - jnp.max(s, axis=0, keepdims=True))
            p = e * (1.0 / jnp.sum(e, axis=0, keepdims=True))
            dp = nt(v, doh)
            ds = (p * (dp - jnp.sum(p * dp, axis=0, keepdims=True))).astype(BF)
            dv += nn(p.astype(BF), doh)
            dk += nn(ds, qh)
            dq += tn(ds, jnp.where(mask, k, zero))
        out_ref[:, pl.ds(g * LANES, LANES)] = (dq * SCALE).astype(BF)
        out_ref[:, pl.ds(width + g * LANES, LANES)] = dk.astype(BF)
        out_ref[:, pl.ds(2 * width + g * LANES, LANES)] = dv.astype(BF)


def per_image(kernel, counts, slots, arrays, out_width):
    rows = arrays[0].shape[0]
    return pl.pallas_call(
        kernel,
        grid_spec=pltpu.PrefetchScalarGridSpec(
            num_scalar_prefetch=1,
            grid=(rows // slots,),
            in_specs=[pl.BlockSpec((slots, a.shape[1]), lambda i, c: (i, 0)) for a in arrays],
            out_specs=pl.BlockSpec((slots, out_width), lambda i, c: (i, 0)),
        ),
        out_shape=jax.ShapeDtypeStruct((rows, out_width), BF),
        compiler_params=pltpu.CompilerParams(vmem_limit_bytes=48 * 2**20),
    )(counts, *arrays)


def packed_rows(parts):
    rows = [part.reshape(part.shape[:-1] + (-1, 128)) for part in parts]
    total, start = 0, 0
    count = sum(part.shape[-2] for part in rows)
    for part in rows:
        size = part.shape[-2]
        edges = [(0, 0)] * (part.ndim - 2) + [(start, count - start - size), (0, 0)]
        total = total + jnp.pad(part, edges)
        start += size
    return total


def gather_small(where, parts):
    if by_hand():
        planes = lax.axis_size("fsdp") // 2
        packed = packed_rows(parts)
        column = jnp.stack([packed] + [send(packed, step, 0, 0) for step in range(1, planes)])
        both = jnp.stack([column, send(column, 0, 1, 0)])
        steps = (where[0] - jnp.arange(planes)) % planes
        flips = (where[1] + jnp.arange(2)) % 2
        whole = both[flips][:, steps].transpose(1, 0, 2, 3).reshape(2 * planes, -1)
    else:
        packed = jnp.concatenate(parts)
        whole = lax.all_gather(packed, "fsdp", axis=0, tiled=False)
    result, start = [], 0
    for part in parts:
        size = part.shape[0]
        result.append(whole[:, start : start + size].reshape(-1).astype(F32))
        start += size
    return result


def reduce_small(where, parts):
    shards = lax.axis_size("fsdp")
    if by_hand():
        planes = shards // 2
        packed = packed_rows([part.reshape(planes, 2, -1) for part in parts])
        chip = pick(packed, where[1], 1) + send(pick(packed, 1 - where[1], 1), 0, 1, 0)
        pair = chip + send(chip, 0, 0, 1)
        plane = pair + send(pair, 0, 0, 2)
        own = pick(plane, where[0])
        for step in range(1, planes):
            own += send(pick(plane, (where[0] + step) % planes), step, 0, 0)
        own = own.reshape(-1)
    else:
        packed = jnp.concatenate([part.reshape(shards, -1) for part in parts], axis=1)
        total = lax.psum(packed, ("fsdp", "seq"))
        own = lax.dynamic_index_in_dim(total, lax.axis_index("fsdp"), axis=0, keepdims=False)
    result, start = [], 0
    for part in parts:
        size = part.shape[0] // shards
        result.append(own[start : start + size])
        start += size
    return result


def send(value, step, flip_core, flip_seq):
    shards, others = lax.axis_size("fsdp"), lax.axis_size("seq")
    pairs = [
        (i * others + j, ((i + 2 * step) % shards ^ flip_core) * others + (j ^ flip_seq))
        for i in range(shards)
        for j in range(others)
    ]
    return lax.ppermute(value, ("fsdp", "seq"), pairs)


def after(value, *earlier):
    return lax.optimization_barrier((value, earlier))[0]


def pick(value, index, axis=0):
    return lax.dynamic_index_in_dim(value, index, axis=axis, keepdims=False)


def place():
    shard = lax.axis_index("fsdp")
    return jnp.stack([shard // 2, shard % 2, lax.axis_index("seq")]).astype(jnp.int32)


def by_hand():
    return lax.axis_size("seq") == 4 and lax.axis_size("fsdp") == 8


def assemble(where, parts, shapes, by_rows):
    planes, depth, wide = parts[0][-5].shape
    planes += 1
    half = depth // 2
    each = len(parts[0])
    flat = list(parts[0]) + list(parts[1])
    total = 2 * (4 + (planes - 1) * 5)

    def kernel(place_ref, *refs):
        ins, outs = refs[: len(flat)], refs[len(flat) : -3]
        held, in_sems, out_sems = refs[-3:]
        z, core, me = place_ref[0], place_ref[1], place_ref[2]
        places = [me, me + 1 - 2 * (me % 2), (me + 2) % 4, 3 - me, 3 - me]

        moves = []
        for flip_core in range(2):
            own = ins[flip_core * each : (flip_core + 1) * each - 5]
            shard = 2 * z + (core + flip_core) % 2
            for unit in range(4):
                if by_rows:
                    source = own[0].at[pl.ds(unit * depth, depth), :]
                elif unit * wide < own[0].shape[1]:
                    source = own[0].at[:, pl.ds(unit * wide, wide)]
                else:
                    source = own[1]
                moves.append((source, shard, jnp.int32(unit), 0, depth))
        for flip_core in range(2):
            others = ins[(flip_core + 1) * each - 5 : (flip_core + 1) * each]
            for step in range(1, planes):
                shard = 2 * ((z + planes - step) % planes) + (core + flip_core) % 2
                for n, spot in enumerate(places):
                    first, size = ((0, depth), (0, depth), (0, depth), (0, half), (half, half))[n]
                    moves.append((others[n].at[step - 1], shard, spot, first, size))

        def bring(n):
            source, _, _, _, size = moves[n]
            return pltpu.make_async_copy(source, held.at[n, pl.ds(0, size)], in_sems.at[n])

        def put(n, act):
            _, shard, unit, first, size = moves[n]
            if by_rows:
                row, column = shard * (4 * depth) + unit * depth + first, 0
            else:
                row, column = shard * depth + first, pl.multiple_of(unit * wide, wide)
            row = pl.multiple_of(row, half)

            def to(target, column):
                spot = outs[target].at[pl.ds(row, size), pl.ds(column, wide)]
                act(pltpu.make_async_copy(held.at[n, pl.ds(0, size)], spot, out_sems.at[n]))

            if len(outs) == 1:
                to(0, column)
            else:
                pl.when(unit < 3)(lambda: to(0, column))
                pl.when(unit == 3)(lambda: to(1, 0))

        for n in range(total):
            bring(n).start()
        for n in range(total):
            bring(n).wait()
            put(n, lambda copy: copy.start())
        for n in range(total):
            put(n, lambda copy: copy.wait())

    return pl.pallas_call(
        kernel,
        in_specs=[pl.BlockSpec(memory_space=pltpu.SMEM)]
        + [pl.BlockSpec(memory_space=pl.ANY)] * len(flat),
        out_specs=[pl.BlockSpec(memory_space=pl.ANY)] * len(shapes),
        out_shape=[jax.ShapeDtypeStruct(shape, BF) for shape in shapes],
        scratch_shapes=[
            pltpu.VMEM((total, depth, wide), BF),
            pltpu.SemaphoreType.DMA((total,)),
            pltpu.SemaphoreType.DMA((total,)),
        ],
        compiler_params=pltpu.CompilerParams(vmem_limit_bytes=24 * 2**20),
    )(where, *flat)


def wgrad_kernel(by_rows, mixed):
    def kernel(place_ref, *refs):
        mine_ref, far_ref = refs[-2:]

        def store(total):
            depth = total.shape[0] // 2
            first = place_ref[1] == 0
            low, high = total[:depth].astype(BF), total[depth:].astype(BF)
            mine_ref[...] = jnp.where(first, low, high)
            far_ref[...] = jnp.where(first, high, low)

        if by_rows:
            left = jnp.concatenate([refs[0][...], refs[1][...]], axis=1)
            store(tn(left, refs[2][...]))
        elif mixed:
            pl.when(pl.program_id(0) < 3)(lambda: store(tn(refs[0][...], refs[1][...])))
            pl.when(pl.program_id(0) == 3)(lambda: store(tn(refs[2][...], refs[3][...])))
        else:
            store(tn(refs[0][...], refs[1][...]))

    return kernel


def wgrad(where, left, right, extra=None, by_rows=False):
    rows = left.shape[0]
    shards = lax.axis_size("fsdp")
    planes = shards // 2
    if by_rows:
        depth, wide = left.shape[1] // (4 * shards), right.shape[1]
        arrays = [left, left, right]
        specs = [
            pl.BlockSpec((rows, depth), lambda j, z, c: (0, 8 * z + j)),
            pl.BlockSpec((rows, depth), lambda j, z, c: (0, 8 * z + 4 + j)),
            pl.BlockSpec((rows, wide), lambda j, z, c: (0, 0)),
        ]
    else:
        depth = left.shape[1] // shards
        wide = right.shape[1] // (3 if extra else 4)
        arrays = [left, right]
        specs = [
            pl.BlockSpec((rows, 2 * depth), lambda j, z, c: (0, z)),
            pl.BlockSpec((rows, wide), lambda j, z, c: (0, j)),
        ]
        if extra:
            arrays += list(extra)
            specs = [
                pl.BlockSpec((rows, 2 * depth), lambda j, z, c: (0, jnp.where(j < 3, z, planes - 1))),
                pl.BlockSpec((rows, wide), lambda j, z, c: (0, jnp.minimum(j, 2))),
                pl.BlockSpec((rows, 2 * depth), lambda j, z, c: (0, jnp.where(j < 3, 0, z))),
                pl.BlockSpec((rows, wide), lambda j, z, c: (0, 0)),
            ]
    out = pl.BlockSpec((None, None, depth, wide), lambda j, z, c: (j, z, 0, 0))
    shape = jax.ShapeDtypeStruct((4, planes, depth, wide), BF)
    return pl.pallas_call(
        wgrad_kernel(by_rows, extra is not None),
        grid_spec=pltpu.PrefetchScalarGridSpec(
            num_scalar_prefetch=1,
            grid=(4, planes),
            in_specs=specs,
            out_specs=[out, out],
        ),
        out_shape=[shape, shape],
        compiler_params=pltpu.CompilerParams(vmem_limit_bytes=48 * 2**20),
    )(where, *arrays)


def add(*parts):
    total = parts[0].astype(F32)
    for part in parts[1:]:
        total += part.astype(F32)
    return total.astype(BF)


def chip_sum(where, mine, far):
    planes, depth, wide = mine.shape[1:]

    def kernel(place_ref, mine_ref, far_ref, *outs):
        for flip in range(4):

            @pl.when(pl.program_id(0) == flip)
            def _():
                outs[flip][...] = add(mine_ref[...], far_ref[...])

    return pl.pallas_call(
        kernel,
        grid_spec=pltpu.PrefetchScalarGridSpec(
            num_scalar_prefetch=1,
            grid=(4, planes),
            in_specs=[
                pl.BlockSpec((None, None, depth, wide), lambda f, z, c: (c[2] ^ f, z, 0, 0))
            ]
            * 2,
            out_specs=[
                pl.BlockSpec(
                    (None, depth, wide),
                    lambda f, z, c, n=n: (jnp.where(f < n, 0, jnp.where(f > n, planes - 1, z)), 0, 0),
                )
                for n in range(4)
            ],
        ),
        out_shape=[jax.ShapeDtypeStruct((planes, depth, wide), BF)] * 4,
    )(where, mine, far)


def plane_parts(chip):
    return [chip[0]] + [send(chip[flip], 0, 0, flip) for flip in (1, 2, 3)]


def plane_sum(where, parts):
    planes, depth, wide = parts[0].shape

    def kernel(place_ref, *refs):
        ins, outs = refs[: len(parts)], refs[len(parts) :]
        for step in range(planes):
            at = (place_ref[0] + step) % planes
            outs[step][...] = add(*[ref[at] for ref in ins])

    return pl.pallas_call(
        kernel,
        in_specs=[pl.BlockSpec(memory_space=pltpu.SMEM)]
        + [pl.BlockSpec(memory_space=pltpu.VMEM)] * len(parts),
        out_shape=[jax.ShapeDtypeStruct((depth, wide), BF)] * planes,
        compiler_params=pltpu.CompilerParams(vmem_limit_bytes=24 * 2**20),
    )(where, *parts)


def column_parts(parts):
    return [parts[0]] + [send(part, step, 0, 0) for step, part in enumerate(parts) if step]


def shares(total):
    return [total] + over_plane(total)


def spread(where, parts, shapes, by_rows=False):
    depth, wide = parts[0].shape

    def kernel(place_ref, *refs):
        ins, outs = refs[: len(parts)], refs[len(parts) :]
        me = place_ref[2]
        for spot, ref in zip([me, me + 1 - 2 * (me % 2), (me + 2) % 4, 3 - me], ins):
            value = ref[...].astype(F32)
            if by_rows:
                outs[0][pl.ds(pl.multiple_of(spot * depth, depth), depth), :] = value
            elif len(outs) == 1:
                outs[0][:, pl.ds(pl.multiple_of(spot * wide, wide), wide)] = value
            else:

                @pl.when(spot < 3)
                def _():
                    outs[0][:, pl.ds(pl.multiple_of(spot * wide, wide), wide)] = value

                @pl.when(spot == 3)
                def _():
                    outs[1][...] = value

    return pl.pallas_call(
        kernel,
        in_specs=[pl.BlockSpec(memory_space=pltpu.SMEM)]
        + [pl.BlockSpec(memory_space=pltpu.VMEM)] * len(parts),
        out_shape=[jax.ShapeDtypeStruct(shape, F32) for shape in shapes],
        compiler_params=pltpu.CompilerParams(vmem_limit_bytes=24 * 2**20),
    )(where, *parts)


def along_z(mine):
    return [send(mine, step, 0, 0) for step in range(1, lax.axis_size("fsdp") // 2)]


def over_plane(value):
    return [send(value, 0, 0, flip) for flip in (1, 2, 3)]


def to_partner(values):
    return [send(value, 0, 1, 0) for value in values]


def across(along_x, along_y):
    half = along_x.shape[1] // 2
    return [send(along_x[:, :half], 0, 0, 2), send(along_y[:, half:], 0, 0, 1)]


def plain_sum(left, right):
    share = lax.psum_scatter(tn(left, right).astype(BF), "fsdp", scatter_dimension=0, tiled=True)
    return lax.psum(share, "seq").astype(F32)


def normal(values):
    center = values - jnp.mean(values, axis=-1, keepdims=True)
    inverse = lax.rsqrt(jnp.mean(center * center, axis=-1, keepdims=True) + epsilon)
    return center * inverse, inverse


def norm_back(grad, unit, inverse, gain):
    e = grad * gain
    return inverse * (
        e
        - jnp.mean(e, axis=-1, keepdims=True)
        - unit * jnp.mean(e * unit, axis=-1, keepdims=True)
    )


def gelu_and_slope(u):
    c = 0.7978845608
    t = jnp.tanh(c * (u + 0.044715 * u * u * u))
    half = 0.5 * (1.0 + t)
    slope = half + 0.5 * u * (1.0 - t * t) * (c + (3 * 0.044715 * c) * u * u)
    return u * half, slope


def plainly(
    tokens, live, x, g_low, small, w_qkv, w_out, w_up, w_down
):
    gain1, shift1, bias_qkv, bias_out, gain2, shift2, bias_up, bias_down = small
    slots, width = tokens.shape[2:]
    qkv_w, out_w, up_w, down_w = [
        lax.all_gather(w, "fsdp", axis=0, tiled=True) for w in (w_qkv, w_out, w_up, w_down)
    ]
    g = g_low.astype(F32)
    unit1, inverse1 = normal(x)
    a1 = (unit1 * gain1 + shift1).astype(BF)
    qkv = (nn(a1, qkv_w) + bias_qkv).astype(BF)
    o = per_image(attention_forward, live, slots, [qkv], width)
    y1 = x + nn(o, out_w) + bias_out
    unit2, inverse2 = normal(y1)
    a2 = (unit2 * gain2 + shift2).astype(BF)
    hid, slope = gelu_and_slope(nn(a2, up_w) + bias_up)
    hid = hid.astype(BF)
    s_down = plain_sum(hid, g_low)
    du = (nt(g_low, down_w) * slope).astype(BF)
    s_up = plain_sum(a2, du)
    activations = (y1 + nn(hid, down_w) + bias_down).astype(BF)
    da2 = nt(du, up_w)
    dy1 = g + norm_back(da2, unit2, inverse2, gain2)
    d1 = dy1.astype(BF)
    s_out = plain_sum(o, d1)
    do = nt(d1, out_w).astype(BF)
    dqkv = per_image(attention_backward, live, slots, [qkv, do], 3 * width)
    s_qkv = plain_sum(a1, dqkv)
    da1 = nt(dqkv, qkv_w)
    input_grad = (dy1 + norm_back(da1, unit1, inverse1, gain1)).astype(BF)
    sums = column_sums(da1, unit1, dqkv, d1, da2, unit2, du, g)
    return activations, input_grad, s_qkv, s_out, s_up, s_down, sums


def column_sums(da1, unit1, dqkv, d1, da2, unit2, du, g):
    width = da1.shape[1]
    sums_qkv = jnp.sum(dqkv.astype(F32), axis=0)
    return (
        jnp.sum(da1 * unit1, axis=0),
        jnp.sum(da1, axis=0),
        jnp.concatenate([sums_qkv[:width], sums_qkv[2 * width :]]),
        jnp.sum(d1.astype(F32), axis=0),
        jnp.sum(da2 * unit2, axis=0),
        jnp.sum(da2, axis=0),
        jnp.sum(du.astype(F32), axis=0),
        jnp.sum(g, axis=0),
    )


def by_parts(
    where, tokens, live, x, g_low, small, w_qkv, w_out, w_up, w_down
):
    gain1, shift1, bias_qkv, bias_out, gain2, shift2, bias_up, bias_down = small
    slots, width = tokens.shape[2:]
    wide = w_up.shape[1]
    me = where[2]
    g = g_low.astype(F32)

    rows_in = w_qkv.shape[0]
    unit = lax.dynamic_slice(w_qkv, (0, jnp.minimum(me, 2) * width), (rows_in, width))
    z_first = along_z(jnp.where(me < 3, unit, w_out))
    z_second = along_z(lax.dynamic_slice(w_up, (0, me * width), (rows_in, width)))
    z_third = along_z(lax.dynamic_slice(w_down, (me * rows_in, 0), (rows_in, width)))
    unit1, inverse1 = normal(x)

    col_first = jnp.stack(z_first)
    two_first = [send(col_first, 0, 0, flip) for flip in (1, 2)]
    own_far_first = to_partner(after([w_qkv, w_out, col_first], col_first))
    col_second = jnp.stack(after(z_second, col_first))
    two_second = [send(col_second, 0, 0, flip) for flip in (1, 2)]
    a1 = (unit1 * gain1 + shift1).astype(BF)
    two_first = after(two_first, col_second, a1)
    cross_first = across(*two_first)
    two_far_first = to_partner(two_first)
    col_third = jnp.stack(after(z_third, two_first))
    two_third = [send(col_third, 0, 0, flip) for flip in (1, 2)]
    cross_first = after(cross_first, col_third)
    near_first = [w_qkv, w_out, col_first] + two_first + cross_first
    far_first = own_far_first + two_far_first + to_partner(cross_first)
    own_far_second = to_partner(after([w_up, col_second], cross_first))
    two_second = after(two_second, cross_first)
    cross_second = across(*two_second)
    two_far_second = to_partner(two_second)
    qkv_w, out_w = assemble(
        where, [near_first, far_first], [(width, 3 * width), (width, width)], False
    )
    qkv = (nn(a1, qkv_w) + bias_qkv).astype(BF)
    cross_second = after(cross_second, qkv)
    near_second = [w_up, col_second] + two_second + cross_second
    far_second = own_far_second + two_far_second + to_partner(cross_second)
    own_far_third = to_partner(after([w_down, col_third], cross_second))
    two_third = after(two_third, qkv)
    cross_third = across(*two_third)
    two_far_third = to_partner(two_third)
    o = per_image(attention_forward, live, slots, [after(qkv, two_third)], width)
    cross_third = after(cross_third, o)
    near_third = [w_down, col_third] + two_third + cross_third
    far_third = own_far_third + two_far_third + to_partner(cross_third)
    y1 = x + nn(o, out_w) + bias_out
    unit2, inverse2 = normal(y1)
    a2 = (unit2 * gain2 + shift2).astype(BF)
    (up_w,) = assemble(where, after([near_second, far_second], a2), [(width, wide)], False)
    hid, slope = gelu_and_slope(nn(a2, up_w) + bias_up)
    hid = hid.astype(BF)
    slope = slope.astype(BF)

    mine_down, far_down = wgrad(where, hid, g_low, by_rows=True)
    got_down = send(far_down, 0, 1, 0)
    (down_w,) = assemble(where, after([near_third, far_third], mine_down), [(wide, width)], True)
    du = (nt(g_low, down_w) * slope.astype(F32)).astype(BF)
    chip_down = chip_sum(where, *after((mine_down, got_down), du))
    plane_down = plane_parts(chip_down)
    mine_up, far_up = wgrad(where, a2, after(du, chip_down))
    got_up = send(far_up, 0, 1, 0)
    da2 = nt(after(du, mine_up), up_w)
    dy1 = g + norm_back(da2, unit2, inverse2, gain2)
    d1 = dy1.astype(BF)
    chip_up = chip_sum(where, *after((mine_up, got_up), d1))
    plane_up = plane_parts(chip_up)
    do = nt(after(d1, chip_up), out_w).astype(BF)
    dqkv = per_image(attention_backward, live, slots, [qkv, do], 3 * width)
    column_down = column_parts(plane_sum(where, after(plane_down, dqkv)))
    mine_qkv, far_qkv = wgrad(where, a1, after(dqkv, column_down[0]), extra=(o, d1))
    got_qkv = send(far_qkv, 0, 1, 0)
    da1 = nt(after(dqkv, mine_qkv), qkv_w)
    dx = norm_back(da1, unit1, inverse1, gain1)
    input_grad = (dy1 + dx).astype(BF)
    chip_qkv = chip_sum(where, *after((mine_qkv, got_qkv), input_grad))
    plane_qkv = plane_parts(chip_qkv)
    column_up = column_parts(plane_sum(where, after(plane_up, chip_qkv)))
    share_down = shares(add(*after(column_down, column_up[0])))
    activations = (y1 + nn(after(hid, share_down[0]), down_w) + bias_down).astype(BF)
    share_up = shares(add(*after(column_up, activations)))
    (s_down,) = spread(where, after(share_down, share_up[0]), [w_down.shape], True)
    column_qkv = column_parts(plane_sum(where, after(plane_qkv, s_down)))
    (s_up,) = spread(where, after(share_up, column_qkv[0]), [w_up.shape])
    share_qkv = shares(add(*after(column_qkv, s_up)))
    s_qkv, s_out = spread(where, share_qkv, [w_qkv.shape, w_out.shape])
    sums = column_sums(da1, unit1, dqkv, d1, da2, unit2, du, g)
    return (
        activations,
        input_grad,
        s_qkv,
        s_out,
        s_up,
        s_down,
        sums,
    )


def on_device(
    tokens,
    counts,
    ln1_gain,
    ln1_shift,
    w_qkv,
    b_qv,
    w_out,
    b_out,
    ln2_gain,
    ln2_shift,
    w_up,
    b_up,
    w_down,
    b_down,
    cotangent,
):
    where = place()
    small = gather_small(
        where, (ln1_gain, ln1_shift, b_qv, b_out, ln2_gain, ln2_shift, b_up, b_down)
    )
    micro, images, slots, width = tokens.shape
    rows = micro * images * slots
    half = small[2]
    small[2] = jnp.concatenate([half[:width], jnp.zeros((width,), F32), half[width:]])
    own_start = lax.axis_index("seq") * images
    live = lax.dynamic_slice_in_dim(counts, own_start, images, axis=1).reshape(-1)
    x = tokens.reshape(rows, width).astype(F32)
    g_low = cotangent.reshape(rows, width)
    weights = (w_qkv, w_out, w_up, w_down)
    if by_hand():
        found = by_parts(where, tokens, live, x, g_low, small, *weights)
    else:
        found = plainly(tokens, live, x, g_low, small, *weights)
    activations, input_grad, s_qkv, s_out, s_up, s_down, sums = found
    sums = reduce_small(where, sums)
    return (
        activations.reshape(tokens.shape),
        input_grad.reshape(tokens.shape),
        sums[0],
        sums[1],
        s_qkv,
        sums[2],
        s_out,
        sums[3],
        sums[4],
        sums[5],
        s_up,
        sums[6],
        s_down,
        sums[7],
    )


def solution(mesh):
    row = P(None, ("fsdp", "seq"), None, None)
    one, two = P("fsdp"), P("fsdp", None)
    params = (one, one, two, one, two, one, one, one, two, one, two, one)
    return jax.shard_map(
        on_device,
        mesh=mesh,
        in_specs=(row, P(None, "fsdp")) + params + (row,),
        out_specs=(row, row) + params,
        check_vma=False,
    )
```

time: 823 us -> 563 us (0.68)
  matrix products: 318 us -> 96.9 us
  Pallas kernels: 0 us -> 166 us
  waiting for transfers between devices: 281 us -> 148 us
  blocking collectives: 121 us -> 0 us
  starting transfers between devices: 0.94 us -> 79.5 us
  other arithmetic: 47.7 us -> 30.6 us
  between operations: 18.1 us -> 2.07 us
    dot_general x54 -> x8, matrix products: 318 us -> 96.9 us  [the longest x4 55.8 us: nt(): lax.dot_general(a, b, (((1,), (1,)), ((), ())), preferred_element_type=F32)]
    pallas_call x0 -> x17, Pallas kernels: none -> 166 us  [the longest x3 54.6 us: wgrad(): pl.pallas_call(wgrad_kernel(by_rows, extra is not None), grid_spec=pltpu....]
    ppermute x0 -> x80, waiting for transfers between devices: none -> 148 us  [send(): return lax.ppermute(value, ('fsdp', 'seq'), pairs)]
    all_gather x4 -> x0, waiting for transfers between devices: 121 us -> none  [the longest x1 68 us: on_device(): lax.all_gather(w_down, 'fsdp', axis=0, tiled=True)]
    reduce_scatter x4 -> x0, waiting for transfers between devices: 88.4 us -> none  [on_device(): lax.psum_scatter(as_sent(partials), 'fsdp', scatter_dimension=0, tiled=True)]
    all_gather x8 -> x0, blocking collectives: 84.7 us -> none  [the longest x1 12.8 us: on_device(): lax.all_gather(b_down, 'fsdp', axis=0, tiled=True)]
    ppermute x0 -> x80, starting transfers between devices: none -> 79.5 us  [send(): return lax.ppermute(value, ('fsdp', 'seq'), pairs)]
    psum x1 -> x0, waiting for transfers between devices: 68.9 us -> none  [on_device(): lax.psum(as_sent(shared), 'seq')]
  transfers between devices with their start and end apart: 9 -> 80, of which waited for: 4 -> 28; matrix products, arithmetic and copies ran while one was open for 29% -> 25% of each run, Pallas kernels for 0% -> 20%
where the time goes in v1:
time: 563 us; the launch traced here: 555 us
  Pallas kernels  166 us (29%)
  waiting for transfers between devices  148 us (26%)
  matrix products  96.9 us (17%)
  starting transfers between devices  79.5 us (14%)
  local copies, waits for them, and re-layouts  31.3 us (6%)
  other arithmetic  30.6 us (5%)
    ppermute x80, waiting for transfers between devices, send(): return lax.ppermute(value, ('fsdp', 'seq'), pairs)  148 us
    ppermute x80, starting transfers between devices, send(): return lax.ppermute(value, ('fsdp', 'seq'), pairs)  79.5 us
    dot_general x4, matrix products, nt(): lax.dot_general(a, b, (((1,), (1,)), ((), ())), preferred_element_type=F32)  55.8 us
    pallas_call x3, Pallas kernels, wgrad(): pl.pallas_call(wgrad_kernel(by_rows, extra is not None), grid_spec=pltpu....  54.6 us
    pallas_call x2, Pallas kernels, per_image(): pl.pallas_call(kernel, grid_spec=pltpu.PrefetchScalarGridSpec(num_scalar_...  45.8 us
    dot_general x4, matrix products, nn(): return jnp.dot(a, b, preferred_element_type=F32)  41 us
    pallas_call x3, Pallas kernels, chip_sum(): pl.pallas_call(kernel, grid_spec=pltpu.PrefetchScalarGridSpec(num_scalar_...  37 us
    unnamed x154, local copies, waits for them, and re-layouts  18.8 us
  transfers between devices with their start and end apart: 80, of which 28 were waited for; matrix products, arithmetic and copies ran while one was open for 25% of the time, Pallas kernels for 20%

profile of v1, /device:TPU:8, one launch (start us, length us, event | category | flops | bytes accessed | tf_op | source)
XLA Modules:
  0.0 554.9 jit_solution(6279923238862129274)
XLA Ops:
  1.7 3.0 collective-permute-start.1
  6.8 2.9 collective-permute-start.5
  10.2 2.0 convert_reduce_fusion.2
  17.5 9.3 %collective-permute-done.6 = bf16[128,1024]{1,0:T(8,128)(2,1)S(1)} collective-permute-done((bf16[128,1024]{1,0:T(8,128)(2,1)S(1)}, bf16[128,1024]{1,0:T(8,128)(2,1)S(1)}, u32[]{:S(2)}, u32[]{:S(2)}) %collective-permute-start.6) | collective-permute-done | bytes 262176 | tf_op jit(solution)/shard_map/ppermute | solution.py:164
  26.8 2.1 collective-permute-done.4
  34.0 2.6 collective-permute-start.9
  36.6 3.3 collective-permute-start.10
  43.0 10.7 %collective-permute-done.9 = bf16[128,1024]{1,0:T(8,128)(2,1)S(1)} collective-permute-done((bf16[128,1024]{1,0:T(8,128)(2,1)S(1)}, bf16[128,1024]{1,0:T(8,128)(2,1)S(1)}, u32[]{:S(2)}, u32[]{:S(2)}) %collective-permute-start.9) | collective-permute-done | bytes 262176 | tf_op jit(solution)/shard_map/ppermute | solution.py:164
  53.7 3.0 collective-permute-start.14
  56.7 6.3 %collective-permute-done.10 = bf16[128,1024]{1,0:T(8,128)(2,1)S(1)} collective-permute-done((bf16[128,1024]{1,0:T(8,128)(2,1)S(1)}, bf16[128,1024]{1,0:T(8,128)(2,1)S(1)}, u32[]{:S(2)}, u32[]{:S(2)}) %collective-permute-start.10) | collective-permute-done | bytes 262176 | tf_op jit(solution)/shard_map/ppermute | solution.py:164
  63.0 3.4 collective-permute-start.15
  67.0 5.4 collective-permute-done.11
  72.5 4.6 collective-permute-done.14
  77.7 3.5 collective-permute-done.15
  82.2 4.4 fusion.9
  86.5 2.1 slice.130
  93.4 14.2 %collective-permute-done.12.refs_5_ = bf16[3,64,1024]{2,1,0:T(8,128)(2,1)} collective-permute-done((bf16[3,64,1024]{2,1,0:T(8,128)(2,1)}, bf16[3,64,1024]{2,1,0:T(8,128)(2,1)}, u32[]{:S(2)}, u32[]{:S(2)}) %collective-permute-start.12) | collective-permute-done | bytes 393248 | tf_op jit(solution)/shard_map/ppermute | solution.py:164
  120.3 5.6 %shard_map.254 = (bf16[1024,3072]{1,0:T(8,128)(2,1)S(1)}, bf16[1024,1024]{1,0:T(8,128)(2,1)S(1)}) custom-call(s32[3]{0:T(128)S(1)} %pad_add_fusion.2.place_ref, bf16[128,3072]{1,0:T(8,128)(2,1)S(1)} %copy-done.22, bf16[128,1024]{1,0:T(8,128)(2,1)} %refs_1_.1, bf16[3,128,1024]{2,1,0:T(8,128)(2,1)} %pad_maximum_fusion.refs_2_, ...), custom_call_target="tpu_custom_call" | custom-call | tf_op jit(solution)/shard_map/pallas_call | solution.py:248
  126.0 8.4 %add_convert_fusion.qkv_ref = bf16[960,3072]{1,0:T(8,128)(2,1)} fusion(f32[3072]{0:T(1024)S(1)} %pad_maximum_fusion.5, bf16[960,1024]{1,0:T(8,128)(2,1)S(1)} %get-tuple-element.312.refs_0_, bf16[1024,3072]{1,0:T(8,128)(2,1)S(1)} %get-tuple-element.155), kind=kOutput, calls=%fused_computation.16 | convolution fusion | flops 6045696000 | bytes 14168064 | tf_op jit(solution)/shard_map/dot_general | solution.py:27
  135.1 14.9 %shard_map.255.refs_2_ = bf16[960,1024]{1,0:T(8,128)(2,1)S(1)} custom-call(s32[3]{0:T(128)S(1)} %fusion.17.counts_ref, bf16[960,3072]{1,0:T(8,128)(2,1)} %add_convert_fusion.qkv_ref), custom_call_target="tpu_custom_call" | custom-call | tf_op jit(solution)/shard_map/pallas_call | solution.py:88
  150.0 2.2 bitcast_add_fusion
  155.8 8.5 %collective-permute-done.37.refs_4_ = bf16[3,64,1024]{2,1,0:T(8,128)(2,1)} collective-permute-done((bf16[3,64,1024]{2,1,0:T(8,128)(2,1)S(1)}, bf16[3,64,1024]{2,1,0:T(8,128)(2,1)}, u32[]{:S(2)}, u32[]{:S(2)}) %collective-permute-start.37) | collective-permute-done | bytes 393248 | tf_op jit(solution)/shard_map/ppermute | solution.py:164
  169.1 5.0 shard_map.256
  175.2 16.4 %multiply_convert_fusion = (bf16[960,4096]{1,0:T(8,128)(2,1)}, f32[960,4096]{1,0:T(8,128)}) fusion(f32[4096]{0:T(1024)} %bitcast.179, bf16[960,1024]{1,0:T(8,128)(2,1)S(1)} %add_convert_fusion.3.refs_0_, bf16[1024,4096]{1,0:T(8,128)(2,1)S(1)} %shard_map.256), kind=kOutput, calls=%fused_computation.13 | convolution fusion | flops 8092385280 | bytes 33964032 | tf_op jit(solution)/shard_map/dot_general | solution.py:27
  191.6 17.7 %shard_map.257 = (bf16[4,4,128,1024]{3,2,1,0:T(8,128)(2,1)S(1)}, bf16[4,4,128,1024]{3,2,1,0:T(8,128)(2,1)}) custom-call(s32[3]{0:T(128)S(1)} %pad_add_fusion.2.place_ref, bf16[960,4096]{1,0:T(8,128)(2,1)} %get-tuple-element.240.refs_0_.refs_1_, bf16[960,4096]{1,0:T(8,128)(2,1)} %get-tuple-element.240.refs_0_.refs_1_, bf16[960,1024]{1,0:T(8,128)(2,1)S(1)} %bitcast.157), custom_call_target="tpu_custom_call" | custom-call | tf_op jit(solution)/shard_map/pallas_call | solution.py:316
  217.9 4.9 shard_map.258
  222.8 23.2 %convert_reduce_fusion = (f32[4096]{0:T(1024)S(1)}, bf16[960,4096]{1,0:T(8,128)(2,1)}) fusion(f32[960,4096]{1,0:T(8,128)} %get-tuple-element.338, f32[4096]{0:T(1024)S(1)} %bitcast.180, bf16[4096,1024]{1,0:T(8,128)(2,1)S(1)} %shard_map.258, bf16[960,1024]{1,0:T(8,128)(2,1)S(1)} %bitcast.158), kind=kOutput, calls=%fused_computation.12 | convolution fusion | flops 8143499264 | bytes 33980416 | tf_op jit(solution)/shard_map/dot_general | solution.py:19
  246.1 12.4 %shard_map.259 = (bf16[4,128,1024]{2,1,0:T(8,128)(2,1)}, bf16[4,128,1024]{2,1,0:T(8,128)(2,1)}, bf16[4,128,1024]{2,1,0:T(8,128)(2,1)}, bf16[4,128,1024]{2,1,0:T(8,128)(2,1)}) custom-call(s32[3]{0:T(128)} %copy-done.42, bf16[4,4,128,1024]{3,2,1,0:T(8,128)(2,1)} %copy-done.13, bf16[4,4,128,1024]{3,2,1,0:T(8,128)(2,1)} %collective-permute-done.36.far_ref), custom_call_target="tpu_custom_call" | custom-call | tf_op jit(solution)/shard_map/pallas_call | solution.py:346
  260.0 18.6 %shard_map.260 = (bf16[4,4,128,1024]{3,2,1,0:T(8,128)(2,1)S(1)}, bf16[4,4,128,1024]{3,2,1,0:T(8,128)(2,1)}) custom-call(s32[3]{0:T(128)S(1)} %copy-done.43, bf16[960,1024]{1,0:T(8,128)(2,1)S(1)} %copy-done.6, bf16[960,4096]{1,0:T(8,128)(2,1)} %get-tuple-element.204.refs_1_), custom_call_target="tpu_custom_call" | custom-call | tf_op jit(solution)/shard_map/pallas_call | solution.py:316
  282.3 15.6 %multiply_reduce_fusion = (f32[1024]{0:T(1024)S(1)}, f32[960]{0:T(1024)S(1)}, f32[960]{0:T(1024)S(1)}, f32[1024]{0:T(1024)S(1)}, f32[960,1024]{1,0:T(8,128)}) fusion(f32[960]{0:T(1024)S(1)} %copy-done.67, f32[960]{0:T(1024)S(1)} %broadcast_multiply_fusion.5, f32[960,1024]{1,0:T(8,128)S(1)} %copy-done.49, f32[1024]{0:T(1024)S(1)} %get-tuple-element.322, ...), kind=kOutput, calls=%fused_computation.25 | convolution fusion | flops 8062889984 | bytes 24148992 | tf_op jit(solution)/shard_map/dot_general | solution.py:19
  297.9 5.0 convert_reduce_fusion.4
  302.9 12.2 %shard_map.261 = (bf16[4,128,1024]{2,1,0:T(8,128)(2,1)}, bf16[4,128,1024]{2,1,0:T(8,128)(2,1)}, bf16[4,128,1024]{2,1,0:T(8,128)(2,1)}, bf16[4,128,1024]{2,1,0:T(8,128)(2,1)}) custom-call(s32[3]{0:T(128)} %copy-done.42, bf16[4,4,128,1024]{3,2,1,0:T(8,128)(2,1)} %copy-done.12, bf16[4,4,128,1024]{3,2,1,0:T(8,128)(2,1)} %collective-permute-done.48.far_ref), custom_call_target="tpu_custom_call" | custom-call | tf_op jit(solution)/shard_map/pallas_call | solution.py:346
  315.1 4.4 convolution_convert_fusion.do_ref
  319.6 31.0 %shard_map.262.refs_1_ = bf16[960,3072]{1,0:T(8,128)(2,1)} custom-call(s32[3]{0:T(128)S(1)} %fusion.17.counts_ref, bf16[960,3072]{1,0:T(8,128)(2,1)} %add_convert_fusion.qkv_ref, bf16[960,1024]{1,0:T(8,128)(2,1)S(1)} %convolution_convert_fusion.do_ref), custom_call_target="tpu_custom_call" | custom-call | tf_op jit(solution)/shard_map/pallas_call | solution.py:88
  350.6 2.9 shard_map.263
  353.5 18.2 %shard_map.264 = (bf16[4,4,128,1024]{3,2,1,0:T(8,128)(2,1)}, bf16[4,4,128,1024]{3,2,1,0:T(8,128)(2,1)}) custom-call(s32[3]{0:T(128)S(1)} %copy-done.44, bf16[960,1024]{1,0:T(8,128)(2,1)S(1)} %copy-done.9, bf16[960,3072]{1,0:T(8,128)(2,1)} %shard_map.262.refs_1_, bf16[960,1024]{1,0:T(8,128)(2,1)S(1)} %copy-done.11, bf16[960,1024]{1,0:T(8,128)(2,1)S(1)} %copy-done.7), custom_call_target="tpu_custom_call" | custom-call | tf_op jit(solution)/shard_map/pallas_call | solution.py:316
  375.7 12.6 %multiply_reduce_fusion.1 = (f32[1024]{0:T(1024)S(1)}, f32[1024]{0:T(1024)S(1)}, f32[960]{0:T(1024)S(1)}, f32[960]{0:T(1024)S(1)}, f32[960,1024]{1,0:T(8,128)S(1)}) fusion(f32[960]{0:T(1024)S(1)} %copy-done.65, f32[960]{0:T(1024)S(1)} %copy-done.63, bf16[3,1,320,1024]{3,2,1,0:T(8,128)(2,1)} %param.15, f32[960,1024]{1,0:T(8,128)} %get-tuple-element.311, ...), kind=kOutput, calls=%fused_computation.27 | convolution fusion | flops 6049624064 | bytes 22047744 | tf_op jit(solution)/shard_map/dot_general | solution.py:19
  390.6 7.7 %collective-permute-done.52.refs_1_ = bf16[4,128,1024]{2,1,0:T(8,128)(2,1)S(1)} collective-permute-done((bf16[4,128,1024]{2,1,0:T(8,128)(2,1)}, bf16[4,128,1024]{2,1,0:T(8,128)(2,1)S(1)}, u32[]{:S(2)}, u32[]{:S(2)}) %collective-permute-start.52) | collective-permute-done | bytes 1048608 | tf_op jit(solution)/shard_map/ppermute | solution.py:164
  398.3 3.3 collective-permute-start.50
  401.6 20.1 %collective-permute-done.53.refs_2_ = bf16[4,128,1024]{2,1,0:T(8,128)(2,1)S(1)} collective-permute-done((bf16[4,128,1024]{2,1,0:T(8,128)(2,1)}, bf16[4,128,1024]{2,1,0:T(8,128)(2,1)S(1)}, u32[]{:S(2)}, u32[]{:S(2)}) %collective-permute-start.53) | collective-permute-done | bytes 1048608 | tf_op jit(solution)/shard_map/ppermute | solution.py:164
  421.7 2.8 add_convert_fusion.2
  424.5 12.4 %shard_map.265 = (bf16[4,128,1024]{2,1,0:T(8,128)(2,1)}, bf16[4,128,1024]{2,1,0:T(8,128)(2,1)}, bf16[4,128,1024]{2,1,0:T(8,128)(2,1)}, bf16[4,128,1024]{2,1,0:T(8,128)(2,1)}) custom-call(s32[3]{0:T(128)} %copy-done.42, bf16[4,4,128,1024]{3,2,1,0:T(8,128)(2,1)} %get-tuple-element.225.mine_ref, bf16[4,4,128,1024]{3,2,1,0:T(8,128)(2,1)} %collective-permute-done.55.far_ref), custom_call_target="tpu_custom_call" | custom-call | tf_op jit(solution)/shard_map/pallas_call | solution.py:346
  438.8 2.1 collective-permute-start.68
  440.9 5.1 collective-permute-start.69
  447.4 2.0 collective-permute-start.62
  449.4 2.0 add_convert_fusion.7.refs_0_
  453.6 8.0 %collective-permute-done.69 = bf16[128,1024]{1,0:T(8,128)(2,1)S(1)} collective-permute-done((bf16[128,1024]{1,0:T(8,128)(2,1)S(1)}, bf16[128,1024]{1,0:T(8,128)(2,1)S(1)}, u32[]{:S(2)}, u32[]{:S(2)}) %collective-permute-start.69) | collective-permute-done | bytes 262176 | tf_op jit(solution)/shard_map/ppermute | solution.py:164
  461.6 2.0 collective-permute-start.65
  463.6 2.6 collective-permute-done.70
  466.2 2.5 collective-permute-start.66
  468.7 14.0 %add_convert_fusion.1 = bf16[960,1024]{1,0:T(8,128)(2,1)} fusion(f32[960,1024]{1,0:T(8,128)S(1)} %copy-done.50, f32[1024]{0:T(1024)S(1)} %copy-done.70, f32[1024]{0:T(1024)S(1)} %get-tuple-element.322, bf16[960,4096]{1,0:T(8,128)(2,1)} %get-tuple-element.240.refs_0_.refs_1_, bf16[4096,1024]{1,0:T(8,128)(2,1)} %copy-done.3), kind=kOutput, calls=%fused_computation.28 | convolution fusion | flops 8056995840 | bytes 22159360 | tf_op jit(solution)/shard_map/dot_general | solution.py:27
  482.7 16.4 %collective-permute-done.65.refs_1_ = bf16[128,1024]{1,0:T(8,128)(2,1)S(1)} collective-permute-done((bf16[128,1024]{1,0:T(8,128)(2,1)}, bf16[128,1024]{1,0:T(8,128)(2,1)S(1)}, u32[]{:S(2)}, u32[]{:S(2)}) %collective-permute-start.65) | collective-permute-done | bytes 262176 | tf_op jit(solution)/shard_map/ppermute | solution.py:164
  500.8 5.9 %collective-permute-done.66.refs_2_ = bf16[128,1024]{1,0:T(8,128)(2,1)S(1)} collective-permute-done((bf16[128,1024]{1,0:T(8,128)(2,1)}, bf16[128,1024]{1,0:T(8,128)(2,1)S(1)}, u32[]{:S(2)}, u32[]{:S(2)}) %collective-permute-start.66) | collective-permute-done | bytes 262176 | tf_op jit(solution)/shard_map/ppermute | solution.py:164
  514.2 2.5 shard_map.267
  519.5 2.1 collective-permute-start.76
  523.0 2.3 collective-permute-start.72
  526.9 2.4 shard_map.269
  529.3 6.4 %collective-permute-done.71 = bf16[128,1024]{1,0:T(8,128)(2,1)S(1)} collective-permute-done((bf16[128,1024]{1,0:T(8,128)(2,1)S(1)}, bf16[128,1024]{1,0:T(8,128)(2,1)S(1)}, u32[]{:S(2)}, u32[]{:S(2)}) %collective-permute-start.71) | collective-permute-done | bytes 262176 | tf_op jit(solution)/shard_map/ppermute | solution.py:164
  535.7 2.8 collective-permute-done.72
  538.5 2.3 collective-permute-done.73
  541.9 2.6 collective-permute-start.79
  545.6 3.8 collective-permute-done.77.refs_1_
  549.4 3.0 collective-permute-done.78.refs_2_
  552.4 2.1 shard_map.270
  (340 shorter events, 89.2 us)
Async XLA Ops:
  1.6 32.4 %collective-permute-start.2 = (bf16[12,128]{1,0:T(8,128)(2,1)S(1)}, bf16[12,128]{1,0:T(8,128)(2,1)}, u32[]{:S(2)}, u32[]{:S(2)}) collective-permute-start(bf16[12,128]{1,0:T(8,128)(2,1)S(1)} %pad_add_fusion.1), channel_id=1, source_target_pairs={{0,24},{1,25},{2,26},{3,27},{4,28},{5,29},{6,30},{7,31},{8,0},{9,1... | collective-permute-start | bytes 9224 | tf_op jit(solution)/shard_map/ppermute | solution.py:164
  1.7 34.9 %collective-permute-start.1 = (bf16[12,128]{1,0:T(8,128)(2,1)S(1)}, bf16[12,128]{1,0:T(8,128)(2,1)}, u32[]{:S(2)}, u32[]{:S(2)}) collective-permute-start(bf16[12,128]{1,0:T(8,128)(2,1)S(1)} %pad_add_fusion.1), channel_id=1, source_target_pairs={{0,16},{1,17},{2,18},{3,19},{4,20},{5,21},{6,22},{7,23},{8,24},{9,... | collective-permute-start | bytes 9224 | tf_op jit(solution)/shard_map/ppermute | solution.py:164
  5.7 21.1 %collective-permute-start.6 = (bf16[128,1024]{1,0:T(8,128)(2,1)S(1)}, bf16[128,1024]{1,0:T(8,128)(2,1)S(1)}, u32[]{:S(2)}, u32[]{:S(2)}) collective-permute-start(bf16[128,1024]{1,0:T(8,128)(2,1)S(1)} %dynamic-slice_select_fusion), channel_id=1, source_target_pairs={{0,24},{1,25},{2,26},{3,27},{4,28},{5,29},{6,30},{7,31},{8,0},{9,1... | collective-permute-start | bytes 786440 | tf_op jit(solution)/shard_map/ppermute | solution.py:164
  6.8 20.0 %collective-permute-start.5 = (bf16[128,1024]{1,0:T(8,128)(2,1)S(1)}, bf16[128,1024]{1,0:T(8,128)(2,1)S(1)}, u32[]{:S(2)}, u32[]{:S(2)}) collective-permute-start(bf16[128,1024]{1,0:T(8,128)(2,1)S(1)} %dynamic-slice_select_fusion), channel_id=1, source_target_pairs={{0,16},{1,17},{2,18},{3,19},{4,20},{5,21},{6,22},{7,23},{8,24},{9,... | collective-permute-start | bytes 786440 | tf_op jit(solution)/shard_map/ppermute | solution.py:164
  9.7 19.2 %collective-permute-start.4 = (bf16[128,1024]{1,0:T(8,128)(2,1)S(1)}, bf16[128,1024]{1,0:T(8,128)(2,1)}, u32[]{:S(2)}, u32[]{:S(2)}) collective-permute-start(bf16[128,1024]{1,0:T(8,128)(2,1)S(1)} %dynamic-slice_select_fusion), channel_id=1, source_target_pairs={{0,8},{1,9},{2,10},{3,11},{4,12},{5,13},{6,14},{7,15},{8,16},{9,17... | collective-permute-start | bytes 786440 | tf_op jit(solution)/shard_map/ppermute | solution.py:164
  26.8 13.1 %collective-permute-start = (bf16[12,128]{1,0:T(8,128)(2,1)S(1)}, bf16[12,128]{1,0:T(8,128)(2,1)S(1)}, u32[]{:S(2)}, u32[]{:S(2)}) collective-permute-start(bf16[12,128]{1,0:T(8,128)(2,1)S(1)} %pad_add_fusion.1), channel_id=1, source_target_pairs={{0,8},{1,9},{2,10},{3,11},{4,12},{5,13},{6,14},{7,15},{8,16},{9,17... | collective-permute-start | bytes 9224 | tf_op jit(solution)/shard_map/ppermute | solution.py:164
  30.8 50.8 %collective-permute-start.7 = (bf16[3,128,1024]{2,1,0:T(8,128)(2,1)}, bf16[3,128,1024]{2,1,0:T(8,128)(2,1)}, u32[]{:S(2)}, u32[]{:S(2)}) collective-permute-start(bf16[3,128,1024]{2,1,0:T(8,128)(2,1)} %pad_maximum_fusion.refs_2_), channel_id=1, source_target_pairs={{0,1},{1,0},{2,3},{3,2},{4,5},{5,4},{6,7},{7,6},{8,9},{9,8},{10,11... | collective-permute-start | bytes 2359304 | tf_op jit(solution)/shard_map/ppermute | solution.py:164
  32.4 49.2 %collective-permute-start.8 = (bf16[3,128,1024]{2,1,0:T(8,128)(2,1)}, bf16[3,128,1024]{2,1,0:T(8,128)(2,1)}, u32[]{:S(2)}, u32[]{:S(2)}) collective-permute-start(bf16[3,128,1024]{2,1,0:T(8,128)(2,1)} %pad_maximum_fusion.refs_2_), channel_id=1, source_target_pairs={{0,2},{1,3},{2,0},{3,1},{4,6},{5,7},{6,4},{7,5},{8,10},{9,11},{10,... | collective-permute-start | bytes 2359304 | tf_op jit(solution)/shard_map/ppermute | solution.py:164
  34.0 19.7 %collective-permute-start.9 = (bf16[128,1024]{1,0:T(8,128)(2,1)S(1)}, bf16[128,1024]{1,0:T(8,128)(2,1)S(1)}, u32[]{:S(2)}, u32[]{:S(2)}) collective-permute-start(bf16[128,1024]{1,0:T(8,128)(2,1)S(1)} %constant_dynamic-slice_fusion.7), channel_id=1, source_target_pairs={{0,8},{1,9},{2,10},{3,11},{4,12},{5,13},{6,14},{7,15},{8,16},{9,17... | collective-permute-start | bytes 786440 | tf_op jit(solution)/shard_map/ppermute | solution.py:164
  36.6 26.4 %collective-permute-start.10 = (bf16[128,1024]{1,0:T(8,128)(2,1)S(1)}, bf16[128,1024]{1,0:T(8,128)(2,1)S(1)}, u32[]{:S(2)}, u32[]{:S(2)}) collective-permute-start(bf16[128,1024]{1,0:T(8,128)(2,1)S(1)} %constant_dynamic-slice_fusion.7), channel_id=1, source_target_pairs={{0,16},{1,17},{2,18},{3,19},{4,20},{5,21},{6,22},{7,23},{8,24},{9,... | collective-permute-start | bytes 786440 | tf_op jit(solution)/shard_map/ppermute | solution.py:164
  41.8 30.6 %collective-permute-start.11 = (bf16[128,1024]{1,0:T(8,128)(2,1)S(1)}, bf16[128,1024]{1,0:T(8,128)(2,1)S(1)}, u32[]{:S(2)}, u32[]{:S(2)}) collective-permute-start(bf16[128,1024]{1,0:T(8,128)(2,1)S(1)} %constant_dynamic-slice_fusion.7), channel_id=1, source_target_pairs={{0,24},{1,25},{2,26},{3,27},{4,28},{5,29},{6,30},{7,31},{8,0},{9,1... | collective-permute-start | bytes 786440 | tf_op jit(solution)/shard_map/ppermute | solution.py:164
  53.7 23.5 %collective-permute-start.14 = (bf16[128,1024]{1,0:T(8,128)(2,1)}, bf16[128,1024]{1,0:T(8,128)(2,1)S(1)}, u32[]{:S(2)}, u32[]{:S(2)}) collective-permute-start(bf16[128,1024]{1,0:T(8,128)(2,1)} %constant_dynamic-slice_fusion.6), channel_id=1, source_target_pairs={{0,8},{1,9},{2,10},{3,11},{4,12},{5,13},{6,14},{7,15},{8,16},{9,17... | collective-permute-start | bytes 786440 | tf_op jit(solution)/shard_map/ppermute | solution.py:164
  63.0 18.1 %collective-permute-start.15 = (bf16[128,1024]{1,0:T(8,128)(2,1)}, bf16[128,1024]{1,0:T(8,128)(2,1)S(1)}, u32[]{:S(2)}, u32[]{:S(2)}) collective-permute-start(bf16[128,1024]{1,0:T(8,128)(2,1)} %constant_dynamic-slice_fusion.6), channel_id=1, source_target_pairs={{0,16},{1,17},{2,18},{3,19},{4,20},{5,21},{6,22},{7,23},{8,24},{9,... | collective-permute-start | bytes 786440 | tf_op jit(solution)/shard_map/ppermute | solution.py:164
  72.5 17.9 %collective-permute-start.16 = (bf16[128,1024]{1,0:T(8,128)(2,1)}, bf16[128,1024]{1,0:T(8,128)(2,1)S(1)}, u32[]{:S(2)}, u32[]{:S(2)}) collective-permute-start(bf16[128,1024]{1,0:T(8,128)(2,1)} %constant_dynamic-slice_fusion.6), channel_id=1, source_target_pairs={{0,24},{1,25},{2,26},{3,27},{4,28},{5,29},{6,30},{7,31},{8,0},{9,1... | collective-permute-start | bytes 786440 | tf_op jit(solution)/shard_map/ppermute | solution.py:164
  77.2 32.9 %collective-permute-start.26 = (bf16[3,128,1024]{2,1,0:T(8,128)(2,1)S(1)}, bf16[3,128,1024]{2,1,0:T(8,128)(2,1)}, u32[]{:S(2)}, u32[]{:S(2)}) collective-permute-start(bf16[3,128,1024]{2,1,0:T(8,128)(2,1)S(1)} %pad_maximum_fusion.1.refs_1_), channel_id=1, source_target_pairs={{0,1},{1,0},{2,3},{3,2},{4,5},{5,4},{6,7},{7,6},{8,9},{9,8},{10,11... | collective-permute-start | bytes 2359304 | tf_op jit(solution)/shard_map/ppermute | solution.py:164
  81.2 28.9 %collective-permute-start.27 = (bf16[3,128,1024]{2,1,0:T(8,128)(2,1)S(1)}, bf16[3,128,1024]{2,1,0:T(8,128)(2,1)}, u32[]{:S(2)}, u32[]{:S(2)}) collective-permute-start(bf16[3,128,1024]{2,1,0:T(8,128)(2,1)S(1)} %pad_maximum_fusion.1.refs_1_), channel_id=1, source_target_pairs={{0,2},{1,3},{2,0},{3,1},{4,6},{5,7},{6,4},{7,5},{8,10},{9,11},{10,... | collective-permute-start | bytes 2359304 | tf_op jit(solution)/shard_map/ppermute | solution.py:164
  81.6 11.8 %collective-permute-start.17 = (bf16[128,3072]{1,0:T(8,128)(2,1)S(1)}, bf16[128,3072]{1,0:T(8,128)(2,1)}, u32[]{:S(2)}, u32[]{:S(2)}) collective-permute-start(bf16[128,3072]{1,0:T(8,128)(2,1)S(1)} %copy-done.21), channel_id=1, source_target_pairs={{0,4},{1,5},{2,6},{3,7},{4,0},{5,1},{6,2},{7,3},{8,12},{9,13},{10,... | collective-permute-start | bytes 2359304 | tf_op jit(solution)/shard_map/ppermute | solution.py:164
  90.4 17.3 %collective-permute-start.12 = (bf16[3,64,1024]{2,1,0:T(8,128)(2,1)}, bf16[3,64,1024]{2,1,0:T(8,128)(2,1)}, u32[]{:S(2)}, u32[]{:S(2)}) collective-permute-start(bf16[3,64,1024]{2,1,0:T(8,128)(2,1)} %slice.130), channel_id=1, source_target_pairs={{0,2},{1,3},{2,0},{3,1},{4,6},{5,7},{6,4},{7,5},{8,10},{9,11},{10,... | collective-permute-start | bytes 1179656 | tf_op jit(solution)/shard_map/ppermute | solution.py:164
  92.7 15.0 %collective-permute-start.13 = (bf16[3,64,1024]{2,1,0:T(8,128)(2,1)}, bf16[3,64,1024]{2,1,0:T(8,128)(2,1)}, u32[]{:S(2)}, u32[]{:S(2)}) collective-permute-start(bf16[3,64,1024]{2,1,0:T(8,128)(2,1)} %slice.131), channel_id=1, source_target_pairs={{0,1},{1,0},{2,3},{3,2},{4,5},{5,4},{6,7},{7,6},{8,9},{9,8},{10,11... | collective-permute-start | bytes 1179656 | tf_op jit(solution)/shard_map/ppermute | solution.py:164
  93.4 20.6 %collective-permute-start.19 = (bf16[3,128,1024]{2,1,0:T(8,128)(2,1)}, bf16[3,128,1024]{2,1,0:T(8,128)(2,1)S(1)}, u32[]{:S(2)}, u32[]{:S(2)}) collective-permute-start(bf16[3,128,1024]{2,1,0:T(8,128)(2,1)} %pad_maximum_fusion.refs_2_), channel_id=1, source_target_pairs={{0,4},{1,5},{2,6},{3,7},{4,0},{5,1},{6,2},{7,3},{8,12},{9,13},{10,... | collective-permute-start | bytes 2359304 | tf_op jit(solution)/shard_map/ppermute | solution.py:164
  114.0 20.5 %collective-permute-start.24 = (bf16[3,128,1024]{2,1,0:T(8,128)(2,1)S(1)}, bf16[3,128,1024]{2,1,0:T(8,128)(2,1)S(1)}, u32[]{:S(2)}, u32[]{:S(2)}) collective-permute-start(bf16[3,128,1024]{2,1,0:T(8,128)(2,1)S(1)} %pad_maximum_fusion.2.refs_1_), channel_id=1, source_target_pairs={{0,1},{1,0},{2,3},{3,2},{4,5},{5,4},{6,7},{7,6},{8,9},{9,8},{10,11... | collective-permute-start | bytes 2359304 | tf_op jit(solution)/shard_map/ppermute | solution.py:164
  114.6 20.4 %collective-permute-start.25 = (bf16[3,128,1024]{2,1,0:T(8,128)(2,1)S(1)}, bf16[3,128,1024]{2,1,0:T(8,128)(2,1)S(1)}, u32[]{:S(2)}, u32[]{:S(2)}) collective-permute-start(bf16[3,128,1024]{2,1,0:T(8,128)(2,1)S(1)} %pad_maximum_fusion.2.refs_1_), channel_id=1, source_target_pairs={{0,2},{1,3},{2,0},{3,1},{4,6},{5,7},{6,4},{7,5},{8,10},{9,11},{10,... | collective-permute-start | bytes 2359304 | tf_op jit(solution)/shard_map/ppermute | solution.py:164
  115.0 39.6 %collective-permute-start.32 = (bf16[3,128,1024]{2,1,0:T(8,128)(2,1)}, bf16[3,128,1024]{2,1,0:T(8,128)(2,1)S(1)}, u32[]{:S(2)}, u32[]{:S(2)}) collective-permute-start(bf16[3,128,1024]{2,1,0:T(8,128)(2,1)} %collective-permute-done.26.refs_2_), channel_id=1, source_target_pairs={{0,4},{1,5},{2,6},{3,7},{4,0},{5,1},{6,2},{7,3},{8,12},{9,13},{10,... | collective-permute-start | bytes 2359304 | tf_op jit(solution)/shard_map/ppermute | solution.py:164
  115.0 37.6 %collective-permute-start.28 = (bf16[3,64,1024]{2,1,0:T(8,128)(2,1)S(1)}, bf16[3,64,1024]{2,1,0:T(8,128)(2,1)S(1)}, u32[]{:S(2)}, u32[]{:S(2)}) collective-permute-start(bf16[3,64,1024]{2,1,0:T(8,128)(2,1)S(1)} %slice.140), channel_id=1, source_target_pairs={{0,2},{1,3},{2,0},{3,1},{4,6},{5,7},{6,4},{7,5},{8,10},{9,11},{10,... | collective-permute-start | bytes 1179656 | tf_op jit(solution)/shard_map/ppermute | solution.py:164
  116.7 36.4 %collective-permute-start.29 = (bf16[3,64,1024]{2,1,0:T(8,128)(2,1)S(1)}, bf16[3,64,1024]{2,1,0:T(8,128)(2,1)S(1)}, u32[]{:S(2)}, u32[]{:S(2)}) collective-permute-start(bf16[3,64,1024]{2,1,0:T(8,128)(2,1)S(1)} %slice.141), channel_id=1, source_target_pairs={{0,1},{1,0},{2,3},{3,2},{4,5},{5,4},{6,7},{7,6},{8,9},{9,8},{10,11... | collective-permute-start | bytes 1179656 | tf_op jit(solution)/shard_map/ppermute | solution.py:164
  134.5 32.2 %collective-permute-start.30 = (bf16[128,4096]{1,0:T(8,128)(2,1)S(1)}, bf16[128,4096]{1,0:T(8,128)(2,1)S(1)}, u32[]{:S(2)}, u32[]{:S(2)}) collective-permute-start(bf16[128,4096]{1,0:T(8,128)(2,1)S(1)} %copy-done.18), channel_id=1, source_target_pairs={{0,4},{1,5},{2,6},{3,7},{4,0},{5,1},{6,2},{7,3},{8,12},{9,13},{10,... | collective-permute-start | bytes 3145736 | tf_op jit(solution)/shard_map/ppermute | solution.py:164
  135.0 19.6 %collective-permute-start.31 = (bf16[3,128,1024]{2,1,0:T(8,128)(2,1)S(1)}, bf16[3,128,1024]{2,1,0:T(8,128)(2,1)S(1)}, u32[]{:S(2)}, u32[]{:S(2)}) collective-permute-start(bf16[3,128,1024]{2,1,0:T(8,128)(2,1)S(1)} %pad_maximum_fusion.1.refs_1_), channel_id=1, source_target_pairs={{0,4},{1,5},{2,6},{3,7},{4,0},{5,1},{6,2},{7,3},{8,12},{9,13},{10,... | collective-permute-start | bytes 2359304 | tf_op jit(solution)/shard_map/ppermute | solution.py:164
  152.7 11.6 %collective-permute-start.37 = (bf16[3,64,1024]{2,1,0:T(8,128)(2,1)S(1)}, bf16[3,64,1024]{2,1,0:T(8,128)(2,1)}, u32[]{:S(2)}, u32[]{:S(2)}) collective-permute-start(bf16[3,64,1024]{2,1,0:T(8,128)(2,1)S(1)} %slice.143), channel_id=1, source_target_pairs={{0,2},{1,3},{2,0},{3,1},{4,6},{5,7},{6,4},{7,5},{8,10},{9,11},{10,... | collective-permute-start | bytes 1179656 | tf_op jit(solution)/shard_map/ppermute | solution.py:164
  153.1 11.3 %collective-permute-start.38 = (bf16[3,64,1024]{2,1,0:T(8,128)(2,1)S(1)}, bf16[3,64,1024]{2,1,0:T(8,128)(2,1)}, u32[]{:S(2)}, u32[]{:S(2)}) collective-permute-start(bf16[3,64,1024]{2,1,0:T(8,128)(2,1)S(1)} %slice.144), channel_id=1, source_target_pairs={{0,1},{1,0},{2,3},{3,2},{4,5},{5,4},{6,7},{7,6},{8,9},{9,8},{10,11... | collective-permute-start | bytes 1179656 | tf_op jit(solution)/shard_map/ppermute | solution.py:164
  154.6 11.0 %collective-permute-start.33 = (bf16[3,128,1024]{2,1,0:T(8,128)(2,1)}, bf16[3,128,1024]{2,1,0:T(8,128)(2,1)S(1)}, u32[]{:S(2)}, u32[]{:S(2)}) collective-permute-start(bf16[3,128,1024]{2,1,0:T(8,128)(2,1)} %collective-permute-done.27.refs_3_), channel_id=1, source_target_pairs={{0,4},{1,5},{2,6},{3,7},{4,0},{5,1},{6,2},{7,3},{8,12},{9,13},{10,... | collective-permute-start | bytes 2359304 | tf_op jit(solution)/shard_map/ppermute | solution.py:164
  154.6 19.5 %collective-permute-start.40 = (bf16[3,128,1024]{2,1,0:T(8,128)(2,1)S(1)}, bf16[3,128,1024]{2,1,0:T(8,128)(2,1)S(1)}, u32[]{:S(2)}, u32[]{:S(2)}) collective-permute-start(bf16[3,128,1024]{2,1,0:T(8,128)(2,1)S(1)} %pad_maximum_fusion.2.refs_1_), channel_id=1, source_target_pairs={{0,4},{1,5},{2,6},{3,7},{4,0},{5,1},{6,2},{7,3},{8,12},{9,13},{10,... | collective-permute-start | bytes 2359304 | tf_op jit(solution)/shard_map/ppermute | solution.py:164
  165.7 45.6 %collective-permute-start.41 = (bf16[3,128,1024]{2,1,0:T(8,128)(2,1)S(1)}, bf16[3,128,1024]{2,1,0:T(8,128)(2,1)}, u32[]{:S(2)}, u32[]{:S(2)}) collective-permute-start(bf16[3,128,1024]{2,1,0:T(8,128)(2,1)S(1)} %collective-permute-done.24.refs_2_), channel_id=1, source_target_pairs={{0,4},{1,5},{2,6},{3,7},{4,0},{5,1},{6,2},{7,3},{8,12},{9,13},{10,... | collective-permute-start | bytes 2359304 | tf_op jit(solution)/shard_map/ppermute | solution.py:164
  166.0 45.7 %collective-permute-start.42 = (bf16[3,128,1024]{2,1,0:T(8,128)(2,1)S(1)}, bf16[3,128,1024]{2,1,0:T(8,128)(2,1)}, u32[]{:S(2)}, u32[]{:S(2)}) collective-permute-start(bf16[3,128,1024]{2,1,0:T(8,128)(2,1)S(1)} %collective-permute-done.25.refs_3_), channel_id=1, source_target_pairs={{0,4},{1,5},{2,6},{3,7},{4,0},{5,1},{6,2},{7,3},{8,12},{9,13},{10,... | collective-permute-start | bytes 2359304 | tf_op jit(solution)/shard_map/ppermute | solution.py:164
  166.6 45.9 %collective-permute-start.39 = (bf16[512,1024]{1,0:T(8,128)(2,1)S(1)}, bf16[512,1024]{1,0:T(8,128)(2,1)S(1)}, u32[]{:S(2)}, u32[]{:S(2)}) collective-permute-start(bf16[512,1024]{1,0:T(8,128)(2,1)S(1)} %copy-done.19), channel_id=1, source_target_pairs={{0,4},{1,5},{2,6},{3,7},{4,0},{5,1},{6,2},{7,3},{8,12},{9,13},{10,... | collective-permute-start | bytes 3145736 | tf_op jit(solution)/shard_map/ppermute | solution.py:164
  166.7 45.0 %collective-permute-start.43 = (bf16[3,64,1024]{2,1,0:T(8,128)(2,1)}, bf16[3,64,1024]{2,1,0:T(8,128)(2,1)}, u32[]{:S(2)}, u32[]{:S(2)}) collective-permute-start(bf16[3,64,1024]{2,1,0:T(8,128)(2,1)} %collective-permute-done.37.refs_4_), channel_id=1, source_target_pairs={{0,4},{1,5},{2,6},{3,7},{4,0},{5,1},{6,2},{7,3},{8,12},{9,13},{10,... | collective-permute-start | bytes 1179656 | tf_op jit(solution)/shard_map/ppermute | solution.py:164
  175.0 36.6 %collective-permute-start.44 = (bf16[3,64,1024]{2,1,0:T(8,128)(2,1)}, bf16[3,64,1024]{2,1,0:T(8,128)(2,1)S(1)}, u32[]{:S(2)}, u32[]{:S(2)}) collective-permute-start(bf16[3,64,1024]{2,1,0:T(8,128)(2,1)} %collective-permute-done.38.refs_5_), channel_id=1, source_target_pairs={{0,4},{1,5},{2,6},{3,7},{4,0},{5,1},{6,2},{7,3},{8,12},{9,13},{10,... | collective-permute-start | bytes 1179656 | tf_op jit(solution)/shard_map/ppermute | solution.py:164
  211.3 34.7 %collective-permute-start.36 = (bf16[4,4,128,1024]{3,2,1,0:T(8,128)(2,1)}, bf16[4,4,128,1024]{3,2,1,0:T(8,128)(2,1)}, u32[]{:S(2)}, u32[]{:S(2)}) collective-permute-start(bf16[4,4,128,1024]{3,2,1,0:T(8,128)(2,1)} %get-tuple-element.179), channel_id=1, source_target_pairs={{0,4},{1,5},{2,6},{3,7},{4,0},{5,1},{6,2},{7,3},{8,12},{9,13},{10,... | collective-permute-start | bytes 12582920 | tf_op jit(solution)/shard_map/ppermute | solution.py:164
  278.6 24.3 %collective-permute-start.48 = (bf16[4,4,128,1024]{3,2,1,0:T(8,128)(2,1)}, bf16[4,4,128,1024]{3,2,1,0:T(8,128)(2,1)}, u32[]{:S(2)}, u32[]{:S(2)}) collective-permute-start(bf16[4,4,128,1024]{3,2,1,0:T(8,128)(2,1)} %get-tuple-element.205), channel_id=1, source_target_pairs={{0,4},{1,5},{2,6},{3,7},{4,0},{5,1},{6,2},{7,3},{8,12},{9,13},{10,... | collective-permute-start | bytes 12582920 | tf_op jit(solution)/shard_map/ppermute | solution.py:164
  278.8 71.8 %collective-permute-start.45 = (bf16[4,128,1024]{2,1,0:T(8,128)(2,1)}, bf16[4,128,1024]{2,1,0:T(8,128)(2,1)S(1)}, u32[]{:S(2)}, u32[]{:S(2)}) collective-permute-start(bf16[4,128,1024]{2,1,0:T(8,128)(2,1)} %get-tuple-element.199), channel_id=1, source_target_pairs={{0,1},{1,0},{2,3},{3,2},{4,5},{5,4},{6,7},{7,6},{8,9},{9,8},{10,11... | collective-permute-start | bytes 3145736 | tf_op jit(solution)/shard_map/ppermute | solution.py:164
  280.3 70.2 %collective-permute-start.46 = (bf16[4,128,1024]{2,1,0:T(8,128)(2,1)}, bf16[4,128,1024]{2,1,0:T(8,128)(2,1)}, u32[]{:S(2)}, u32[]{:S(2)}) collective-permute-start(bf16[4,128,1024]{2,1,0:T(8,128)(2,1)} %get-tuple-element.200), channel_id=1, source_target_pairs={{0,2},{1,3},{2,0},{3,1},{4,6},{5,7},{6,4},{7,5},{8,10},{9,11},{10,... | collective-permute-start | bytes 3145736 | tf_op jit(solution)/shard_map/ppermute | solution.py:164
  281.7 68.9 %collective-permute-start.47 = (bf16[4,128,1024]{2,1,0:T(8,128)(2,1)}, bf16[4,128,1024]{2,1,0:T(8,128)(2,1)}, u32[]{:S(2)}, u32[]{:S(2)}) collective-permute-start(bf16[4,128,1024]{2,1,0:T(8,128)(2,1)} %get-tuple-element.201), channel_id=1, source_target_pairs={{0,3},{1,2},{2,1},{3,0},{4,7},{5,6},{6,5},{7,4},{8,11},{9,10},{10,... | collective-permute-start | bytes 3145736 | tf_op jit(solution)/shard_map/ppermute | solution.py:164
  371.7 50.0 %collective-permute-start.55 = (bf16[4,4,128,1024]{3,2,1,0:T(8,128)(2,1)}, bf16[4,4,128,1024]{3,2,1,0:T(8,128)(2,1)}, u32[]{:S(2)}, u32[]{:S(2)}) collective-permute-start(bf16[4,4,128,1024]{3,2,1,0:T(8,128)(2,1)} %get-tuple-element.223), channel_id=1, source_target_pairs={{0,4},{1,5},{2,6},{3,7},{4,0},{5,1},{6,2},{7,3},{8,12},{9,13},{10,... | collective-permute-start | bytes 12582920 | tf_op jit(solution)/shard_map/ppermute | solution.py:164
  372.1 26.2 %collective-permute-start.52 = (bf16[4,128,1024]{2,1,0:T(8,128)(2,1)}, bf16[4,128,1024]{2,1,0:T(8,128)(2,1)S(1)}, u32[]{:S(2)}, u32[]{:S(2)}) collective-permute-start(bf16[4,128,1024]{2,1,0:T(8,128)(2,1)} %get-tuple-element.209), channel_id=1, source_target_pairs={{0,1},{1,0},{2,3},{3,2},{4,5},{5,4},{6,7},{7,6},{8,9},{9,8},{10,11... | collective-permute-start | bytes 3145736 | tf_op jit(solution)/shard_map/ppermute | solution.py:164
  373.7 48.0 %collective-permute-start.53 = (bf16[4,128,1024]{2,1,0:T(8,128)(2,1)}, bf16[4,128,1024]{2,1,0:T(8,128)(2,1)S(1)}, u32[]{:S(2)}, u32[]{:S(2)}) collective-permute-start(bf16[4,128,1024]{2,1,0:T(8,128)(2,1)} %get-tuple-element.210), channel_id=1, source_target_pairs={{0,2},{1,3},{2,0},{3,1},{4,6},{5,7},{6,4},{7,5},{8,10},{9,11},{10,... | collective-permute-start | bytes 3145736 | tf_op jit(solution)/shard_map/ppermute | solution.py:164
  375.1 61.8 %collective-permute-start.54 = (bf16[4,128,1024]{2,1,0:T(8,128)(2,1)}, bf16[4,128,1024]{2,1,0:T(8,128)(2,1)}, u32[]{:S(2)}, u32[]{:S(2)}) collective-permute-start(bf16[4,128,1024]{2,1,0:T(8,128)(2,1)} %get-tuple-element.211), channel_id=1, source_target_pairs={{0,3},{1,2},{2,1},{3,0},{4,7},{5,6},{6,5},{7,4},{8,11},{9,10},{10,... | collective-permute-start | bytes 3145736 | tf_op jit(solution)/shard_map/ppermute | solution.py:164
  390.6 55.4 %collective-permute-start.49 = (bf16[128,1024]{1,0:T(8,128)(2,1)}, bf16[128,1024]{1,0:T(8,128)(2,1)}, u32[]{:S(2)}, u32[]{:S(2)}) collective-permute-start(bf16[128,1024]{1,0:T(8,128)(2,1)} %get-tuple-element.218), channel_id=1, source_target_pairs={{0,8},{1,9},{2,10},{3,11},{4,12},{5,13},{6,14},{7,15},{8,16},{9,17... | collective-permute-start | bytes 786440 | tf_op jit(solution)/shard_map/ppermute | solution.py:164
  398.3 47.6 %collective-permute-start.50 = (bf16[128,1024]{1,0:T(8,128)(2,1)}, bf16[128,1024]{1,0:T(8,128)(2,1)}, u32[]{:S(2)}, u32[]{:S(2)}) collective-permute-start(bf16[128,1024]{1,0:T(8,128)(2,1)} %get-tuple-element.219), channel_id=1, source_target_pairs={{0,16},{1,17},{2,18},{3,19},{4,20},{5,21},{6,22},{7,23},{8,24},{9,... | collective-permute-start | bytes 786440 | tf_op jit(solution)/shard_map/ppermute | solution.py:164
  421.7 25.7 %collective-permute-start.51 = (bf16[128,1024]{1,0:T(8,128)(2,1)}, bf16[128,1024]{1,0:T(8,128)(2,1)}, u32[]{:S(2)}, u32[]{:S(2)}) collective-permute-start(bf16[128,1024]{1,0:T(8,128)(2,1)} %get-tuple-element.220), channel_id=1, source_target_pairs={{0,24},{1,25},{2,26},{3,27},{4,28},{5,29},{6,30},{7,31},{8,0},{9,1... | collective-permute-start | bytes 786440 | tf_op jit(solution)/shard_map/ppermute | solution.py:164
  421.7 19.2 %collective-permute-start.57 = (f32[4,12,128]{2,0,1:T(4,128)S(1)}, f32[4,12,128]{2,0,1:T(4,128)S(1)}, u32[]{:S(2)}, u32[]{:S(2)}) collective-permute-start(f32[4,12,128]{2,0,1:T(4,128)S(1)} %add.375), channel_id=1, source_target_pairs={{0,1},{1,0},{2,3},{3,2},{4,5},{5,4},{6,7},{7,6},{8,9},{9,8},{10,11... | collective-permute-start | bytes 73736 | tf_op jit(solution)/shard_map/ppermute | solution.py:164
  438.8 13.2 %collective-permute-start.68 = (bf16[128,1024]{1,0:T(8,128)(2,1)S(1)}, bf16[128,1024]{1,0:T(8,128)(2,1)S(1)}, u32[]{:S(2)}, u32[]{:S(2)}) collective-permute-start(bf16[128,1024]{1,0:T(8,128)(2,1)S(1)} %get-tuple-element.241), channel_id=1, source_target_pairs={{0,8},{1,9},{2,10},{3,11},{4,12},{5,13},{6,14},{7,15},{8,16},{9,17... | collective-permute-start | bytes 786440 | tf_op jit(solution)/shard_map/ppermute | solution.py:164
  440.9 20.7 %collective-permute-start.69 = (bf16[128,1024]{1,0:T(8,128)(2,1)S(1)}, bf16[128,1024]{1,0:T(8,128)(2,1)S(1)}, u32[]{:S(2)}, u32[]{:S(2)}) collective-permute-start(bf16[128,1024]{1,0:T(8,128)(2,1)S(1)} %get-tuple-element.242), channel_id=1, source_target_pairs={{0,16},{1,17},{2,18},{3,19},{4,20},{5,21},{6,22},{7,23},{8,24},{9,... | collective-permute-start | bytes 786440 | tf_op jit(solution)/shard_map/ppermute | solution.py:164
  446.0 20.2 %collective-permute-start.70 = (bf16[128,1024]{1,0:T(8,128)(2,1)S(1)}, bf16[128,1024]{1,0:T(8,128)(2,1)S(1)}, u32[]{:S(2)}, u32[]{:S(2)}) collective-permute-start(bf16[128,1024]{1,0:T(8,128)(2,1)S(1)} %get-tuple-element.243), channel_id=1, source_target_pairs={{0,24},{1,25},{2,26},{3,27},{4,28},{5,29},{6,30},{7,31},{8,0},{9,1... | collective-permute-start | bytes 786440 | tf_op jit(solution)/shard_map/ppermute | solution.py:164
  447.4 62.9 %collective-permute-start.62 = (bf16[4,128,1024]{2,1,0:T(8,128)(2,1)}, bf16[4,128,1024]{2,1,0:T(8,128)(2,1)S(1)}, u32[]{:S(2)}, u32[]{:S(2)}) collective-permute-start(bf16[4,128,1024]{2,1,0:T(8,128)(2,1)} %get-tuple-element.228), channel_id=1, source_target_pairs={{0,1},{1,0},{2,3},{3,2},{4,5},{5,4},{6,7},{7,6},{8,9},{9,8},{10,11... | collective-permute-start | bytes 3145736 | tf_op jit(solution)/shard_map/ppermute | solution.py:164
  451.4 60.4 %collective-permute-start.63 = (bf16[4,128,1024]{2,1,0:T(8,128)(2,1)}, bf16[4,128,1024]{2,1,0:T(8,128)(2,1)S(1)}, u32[]{:S(2)}, u32[]{:S(2)}) collective-permute-start(bf16[4,128,1024]{2,1,0:T(8,128)(2,1)} %get-tuple-element.229), channel_id=1, source_target_pairs={{0,2},{1,3},{2,0},{3,1},{4,6},{5,7},{6,4},{7,5},{8,10},{9,11},{10,... | collective-permute-start | bytes 3145736 | tf_op jit(solution)/shard_map/ppermute | solution.py:164
  452.1 64.7 %collective-permute-start.64 = (bf16[4,128,1024]{2,1,0:T(8,128)(2,1)}, bf16[4,128,1024]{2,1,0:T(8,128)(2,1)}, u32[]{:S(2)}, u32[]{:S(2)}) collective-permute-start(bf16[4,128,1024]{2,1,0:T(8,128)(2,1)} %get-tuple-element.230), channel_id=1, source_target_pairs={{0,3},{1,2},{2,1},{3,0},{4,7},{5,6},{6,5},{7,4},{8,11},{9,10},{10,... | collective-permute-start | bytes 3145736 | tf_op jit(solution)/shard_map/ppermute | solution.py:164
  461.6 37.5 %collective-permute-start.65 = (bf16[128,1024]{1,0:T(8,128)(2,1)}, bf16[128,1024]{1,0:T(8,128)(2,1)S(1)}, u32[]{:S(2)}, u32[]{:S(2)}) collective-permute-start(bf16[128,1024]{1,0:T(8,128)(2,1)} %add_convert_fusion.7.refs_0_), channel_id=1, source_target_pairs={{0,1},{1,0},{2,3},{3,2},{4,5},{5,4},{6,7},{7,6},{8,9},{9,8},{10,11... | collective-permute-start | bytes 786440 | tf_op jit(solution)/shard_map/ppermute | solution.py:164
  466.2 40.5 %collective-permute-start.66 = (bf16[128,1024]{1,0:T(8,128)(2,1)}, bf16[128,1024]{1,0:T(8,128)(2,1)S(1)}, u32[]{:S(2)}, u32[]{:S(2)}) collective-permute-start(bf16[128,1024]{1,0:T(8,128)(2,1)} %add_convert_fusion.7.refs_0_), channel_id=1, source_target_pairs={{0,2},{1,3},{2,0},{3,1},{4,6},{5,7},{6,4},{7,5},{8,10},{9,11},{10,... | collective-permute-start | bytes 786440 | tf_op jit(solution)/shard_map/ppermute | solution.py:164
  507.4 17.9 %collective-permute-start.74 = (bf16[128,1024]{1,0:T(8,128)(2,1)S(1)}, bf16[128,1024]{1,0:T(8,128)(2,1)}, u32[]{:S(2)}, u32[]{:S(2)}) collective-permute-start(bf16[128,1024]{1,0:T(8,128)(2,1)S(1)} %add_convert_fusion.6.refs_0_), channel_id=1, source_target_pairs={{0,1},{1,0},{2,3},{3,2},{4,5},{5,4},{6,7},{7,6},{8,9},{9,8},{10,11... | collective-permute-start | bytes 786440 | tf_op jit(solution)/shard_map/ppermute | solution.py:164
  510.3 11.3 %collective-permute-start.60 = (f32[12,128]{1,0:T(8,128)S(1)}, f32[12,128]{1,0:T(8,128)S(1)}, u32[]{:S(2)}, u32[]{:S(2)}) collective-permute-start(f32[12,128]{1,0:T(8,128)S(1)} %bitcast.188), channel_id=1, source_target_pairs={{0,16},{1,17},{2,18},{3,19},{4,20},{5,21},{6,22},{7,23},{8,24},{9,... | collective-permute-start | bytes 18440 | tf_op jit(solution)/shard_map/ppermute | solution.py:164
  511.8 11.2 %collective-permute-start.59 = (f32[12,128]{1,0:T(8,128)S(1)}, f32[12,128]{1,0:T(8,128)S(1)}, u32[]{:S(2)}, u32[]{:S(2)}) collective-permute-start(f32[12,128]{1,0:T(8,128)S(1)} %bitcast.187), channel_id=1, source_target_pairs={{0,8},{1,9},{2,10},{3,11},{4,12},{5,13},{6,14},{7,15},{8,16},{9,17... | collective-permute-start | bytes 18440 | tf_op jit(solution)/shard_map/ppermute | solution.py:164
  521.6 14.1 %collective-permute-start.71 = (bf16[128,1024]{1,0:T(8,128)(2,1)S(1)}, bf16[128,1024]{1,0:T(8,128)(2,1)S(1)}, u32[]{:S(2)}, u32[]{:S(2)}) collective-permute-start(bf16[128,1024]{1,0:T(8,128)(2,1)S(1)} %get-tuple-element.257), channel_id=1, source_target_pairs={{0,8},{1,9},{2,10},{3,11},{4,12},{5,13},{6,14},{7,15},{8,16},{9,17... | collective-permute-start | bytes 786440 | tf_op jit(solution)/shard_map/ppermute | solution.py:164
  523.0 15.4 %collective-permute-start.72 = (bf16[128,1024]{1,0:T(8,128)(2,1)S(1)}, bf16[128,1024]{1,0:T(8,128)(2,1)S(1)}, u32[]{:S(2)}, u32[]{:S(2)}) collective-permute-start(bf16[128,1024]{1,0:T(8,128)(2,1)S(1)} %get-tuple-element.258), channel_id=1, source_target_pairs={{0,16},{1,17},{2,18},{3,19},{4,20},{5,21},{6,22},{7,23},{8,24},{9,... | collective-permute-start | bytes 786440 | tf_op jit(solution)/shard_map/ppermute | solution.py:164
  525.3 15.5 %collective-permute-start.73 = (bf16[128,1024]{1,0:T(8,128)(2,1)S(1)}, bf16[128,1024]{1,0:T(8,128)(2,1)S(1)}, u32[]{:S(2)}, u32[]{:S(2)}) collective-permute-start(bf16[128,1024]{1,0:T(8,128)(2,1)S(1)} %get-tuple-element.259), channel_id=1, source_target_pairs={{0,24},{1,25},{2,26},{3,27},{4,28},{5,29},{6,30},{7,31},{8,0},{9,1... | collective-permute-start | bytes 786440 | tf_op jit(solution)/shard_map/ppermute | solution.py:164
  541.5 10.9 %collective-permute-start.78 = (bf16[128,1024]{1,0:T(8,128)(2,1)S(1)}, bf16[128,1024]{1,0:T(8,128)(2,1)S(1)}, u32[]{:S(2)}, u32[]{:S(2)}) collective-permute-start(bf16[128,1024]{1,0:T(8,128)(2,1)S(1)} %add_convert_fusion.5.refs_0_), channel_id=1, source_target_pairs={{0,2},{1,3},{2,0},{3,1},{4,6},{5,7},{6,4},{7,5},{8,10},{9,11},{10,... | collective-permute-start | bytes 786440 | tf_op jit(solution)/shard_map/ppermute | solution.py:164
  (89 other events, 1408.1 us)

commit v2 on v1

v2 whole, which is shorter than its diff:
```python
import jax
import jax.numpy as jnp
from jax import lax
from jax.experimental import pallas as pl
from jax.experimental.pallas import tpu as pltpu
from jax.sharding import PartitionSpec as P

HEADS = 16
HD = 64
LANES = 256
PER = LANES // HD
TILE = 1024
HEIGHTS = 3
WIDE = 512
PARTS = 2
SCALE = HD ** (-0.5)
epsilon = 1e-05
BF = jnp.bfloat16
F32 = jnp.float32


def nt(a, b):
    return lax.dot_general(a, b, (((1,), (1,)), ((), ())), preferred_element_type=F32)


def tn(a, b):
    return lax.dot_general(a, b, (((0,), (0,)), ((), ())), preferred_element_type=F32)


def nn(a, b):
    return jnp.dot(a, b, preferred_element_type=F32)


def by_head(value):
    lane = lax.broadcasted_iota(jnp.int32, value.shape, 1) // HD
    zero = jnp.zeros_like(value)
    return jnp.concatenate([jnp.where(lane == h, value, zero) for h in range(PER)])


def own_lanes(value):
    slots = value.shape[0] // PER
    lane = lax.broadcasted_iota(jnp.int32, (slots, LANES), 1) // HD
    total = value[:slots]
    for h in range(1, PER):
        total = jnp.where(lane == h, value[h * slots : (h + 1) * slots], total)
    return total


def probabilities(k, heads, live):
    s = nt(k, heads)
    s = jnp.where(lax.broadcasted_iota(jnp.int32, s.shape, 0) < live, s, -1e30)
    e = jnp.exp(s - jnp.max(s, axis=0, keepdims=True))
    return e * (1.0 / jnp.sum(e, axis=0, keepdims=True))


def attention_forward(counts_ref, qkv_ref, out_ref):
    width = qkv_ref.shape[1] // 3
    live = counts_ref[pl.program_id(0)]
    for g in range(width // LANES):
        q = qkv_ref[:, pl.ds(g * LANES, LANES)] * jnp.asarray(SCALE, BF)
        k = qkv_ref[:, pl.ds(width + g * LANES, LANES)]
        v = qkv_ref[:, pl.ds(2 * width + g * LANES, LANES)]
        p = probabilities(k, by_head(q), live)
        out_ref[:, pl.ds(g * LANES, LANES)] = own_lanes(tn(p.astype(BF), v)).astype(BF)


def attention_backward(counts_ref, qkv_ref, do_ref, out_ref):
    width = qkv_ref.shape[1] // 3
    live = counts_ref[pl.program_id(0)]
    for g in range(width // LANES):
        q = qkv_ref[:, pl.ds(g * LANES, LANES)] * jnp.asarray(SCALE, BF)
        k = qkv_ref[:, pl.ds(width + g * LANES, LANES)]
        v = qkv_ref[:, pl.ds(2 * width + g * LANES, LANES)]
        heads, do_heads = by_head(q), by_head(do_ref[:, pl.ds(g * LANES, LANES)])
        p = probabilities(k, heads, live)
        dp = nt(v, do_heads)
        ds = (p * (dp - jnp.sum(p * dp, axis=0, keepdims=True))).astype(BF)
        out_ref[:, pl.ds(g * LANES, LANES)] = (own_lanes(tn(ds, k)) * SCALE).astype(BF)
        out_ref[:, pl.ds(width + g * LANES, LANES)] = nn(ds, heads).astype(BF)
        out_ref[:, pl.ds(2 * width + g * LANES, LANES)] = nn(p.astype(BF), do_heads).astype(BF)


def per_image(kernel, counts, slots, arrays, out_width):
    rows = arrays[0].shape[0]
    return pl.pallas_call(
        kernel,
        grid_spec=pltpu.PrefetchScalarGridSpec(
            num_scalar_prefetch=1,
            grid=(rows // slots,),
            in_specs=[pl.BlockSpec((slots, a.shape[1]), lambda i, c: (i, 0)) for a in arrays],
            out_specs=pl.BlockSpec((slots, out_width), lambda i, c: (i, 0)),
        ),
        out_shape=jax.ShapeDtypeStruct((rows, out_width), BF),
        compiler_params=pltpu.CompilerParams(vmem_limit_bytes=48 * 2**20),
    )(counts, *arrays)


def packed_rows(parts):
    rows = [part.reshape(part.shape[:-1] + (-1, 128)) for part in parts]
    total, start = 0, 0
    count = sum(part.shape[-2] for part in rows)
    for part in rows:
        size = part.shape[-2]
        edges = [(0, 0)] * (part.ndim - 2) + [(start, count - start - size), (0, 0)]
        total = total + jnp.pad(part, edges)
        start += size
    return total


def small_table(where, column, parts):
    planes = column.shape[0]
    both = jnp.stack([column, send(column, 0, 1, 0)])
    flips = (where[1] + jnp.arange(2)) % 2
    whole = both[flips].transpose(1, 0, 2, 3).reshape(2 * planes, -1)
    return cut(whole, parts)


def cut(whole, parts):
    result, start = [], 0
    for part in parts:
        size = part.shape[0]
        result.append(whole[:, start : start + size].reshape(-1).astype(F32))
        start += size
    return result


def complete(small, width):
    half = small[2]
    middle = jnp.zeros((width,), F32)
    return small[:2] + [jnp.concatenate([half[:width], middle, half[width:]])] + small[3:]


def own_parts(own, parts):
    result, start = [], 0
    for part in parts:
        size = part.shape[0] // lax.axis_size("fsdp")
        result.append(own[start : start + size])
        start += size
    return result


def send(value, step, flip_core, flip_seq):
    shards, others = lax.axis_size("fsdp"), lax.axis_size("seq")
    pairs = [
        (i * others + j, ((i + 2 * step) % shards ^ flip_core) * others + (j ^ flip_seq))
        for i in range(shards)
        for j in range(others)
    ]
    return lax.ppermute(value, ("fsdp", "seq"), pairs)


def after(value, *earlier):
    return lax.optimization_barrier((value, earlier))[0]


def pick(value, index, axis=0):
    return lax.dynamic_index_in_dim(value, index, axis=axis, keepdims=False)


def place():
    shard = lax.axis_index("fsdp")
    return jnp.stack([shard // 2, shard % 2, lax.axis_index("seq")]).astype(jnp.int32)


def by_hand():
    return lax.axis_size("seq") == 4 and lax.axis_size("fsdp") == 8


def assemble(where, owns, pieces, targets):
    planes, depth = pieces[0][0].shape[:2]
    planes += 1
    half = depth // 2
    flat = [*owns[0], *pieces[0], *owns[1], *pieces[1]]
    each = len(flat) // 2
    widths = [own.shape[1] // 4 for own in owns[0]]
    total = len(targets) * 2 * (4 + (planes - 1) * 5)

    def kernel(place_ref, *refs):
        ins, outs = refs[: len(flat)], refs[len(flat) : -3]
        held, in_sems, out_sems = refs[-3:]
        z, core, me = place_ref[0], place_ref[1], place_ref[2]
        places = [me, me + 1 - 2 * (me % 2), (me + 2) % 4, 3 - me, 3 - me]
        parts = [(0, depth), (0, depth), (0, depth), (0, half), (half, half)]

        moves = []
        for flip_core in range(2):
            for target, wide in enumerate(widths):
                shard = 2 * z + (core + flip_core) % 2
                own = ins[flip_core * each + target]
                for unit in range(4):
                    source = own.at[:, pl.ds(unit * wide, wide)]
                    moves.append((source, shard, jnp.int32(unit), 0, depth, target))
        for flip_core in range(2):
            others = ins[(flip_core + 1) * each - 5 : (flip_core + 1) * each]
            for step in range(1, planes):
                shard = 2 * ((z + planes - step) % planes) + (core + flip_core) % 2
                for n, spot in enumerate(places):
                    for target, wide in enumerate(widths):
                        source = others[n].at[step - 1, :, pl.ds(sum(widths[:target]), wide)]
                        moves.append((source, shard, spot, *parts[n], target))

        def bring(n):
            source, _, _, _, size, target = moves[n]
            spot = held.at[n, pl.ds(0, size), pl.ds(0, widths[target])]
            return pltpu.make_async_copy(source, spot, in_sems.at[n])

        def put(n):
            _, shard, unit, first, size, target = moves[n]
            wide = widths[target]
            row = pl.multiple_of(shard * depth + first, half)
            column = pl.multiple_of(unit * wide, wide)
            return pltpu.make_async_copy(
                held.at[n, pl.ds(0, size), pl.ds(0, wide)],
                outs[target].at[pl.ds(row, size), pl.ds(column, wide)],
                out_sems.at[n],
            )

        for n in range(total):
            bring(n).start()
        for n in range(total):
            bring(n).wait()
            put(n).start()
        for n in range(total):
            put(n).wait()

    return pl.pallas_call(
        kernel,
        in_specs=[pl.BlockSpec(memory_space=pltpu.SMEM)]
        + [pl.BlockSpec(memory_space=pl.ANY)] * len(flat),
        out_specs=[pl.BlockSpec(memory_space=pltpu.HBM)] * len(targets),
        out_shape=[jax.ShapeDtypeStruct(shape, BF) for shape in targets],
        scratch_shapes=[
            pltpu.VMEM((total, depth, max(widths)), BF),
            pltpu.SemaphoreType.DMA((total,)),
            pltpu.SemaphoreType.DMA((total,)),
        ],
        compiler_params=pltpu.CompilerParams(vmem_limit_bytes=48 * 2**20),
    )(where, *flat)


def halves(place_ref, total, depth):
    first = place_ref[1] == 0
    for n in range(total.shape[0] // (2 * depth)):
        low = total[2 * n * depth : (2 * n + 1) * depth].astype(BF)
        high = total[(2 * n + 1) * depth : (2 * n + 2) * depth].astype(BF)
        yield n, jnp.where(first, low, high), jnp.where(first, high, low)


def wgrad_call(kernel, where, grid, specs, out, shape, arrays):
    return pl.pallas_call(
        kernel,
        grid_spec=pltpu.PrefetchScalarGridSpec(
            num_scalar_prefetch=1, grid=grid, in_specs=specs, out_specs=[out, out]
        ),
        out_shape=[jax.ShapeDtypeStruct(shape, BF)] * 2,
        compiler_params=pltpu.CompilerParams(vmem_limit_bytes=56 * 2**20),
    )(where, *arrays)


def wgrad_units(where, left, right, extra=None):
    rows, width = left.shape
    shards = lax.axis_size("fsdp")
    depth, wide = width // shards, right.shape[1] // (3 if extra else 4)

    def kernel(place_ref, *refs):
        mine_ref, far_ref = refs[-2:]

        def store(left_ref, right_ref):
            total = tn(left_ref[...], right_ref[...])
            for n, mine, far in halves(place_ref, total, depth):
                mine_ref[n] = mine
                far_ref[n] = far

        if extra:
            pl.when(pl.program_id(0) < 3)(lambda: store(refs[0], refs[1]))
            pl.when(pl.program_id(0) == 3)(lambda: store(refs[2], refs[3]))
        else:
            store(refs[0], refs[1])

    one = pl.Buffered(1)
    arrays = [left, right]
    specs = [
        pl.BlockSpec((rows, width), lambda j, c: (0, 0), pipeline_mode=one),
        pl.BlockSpec((rows, wide), lambda j, c: (0, jnp.minimum(j, 2) if extra else j)),
    ]
    if extra:
        arrays += list(extra)
        specs.append(pl.BlockSpec((rows, width), lambda j, c: (0, 0), pipeline_mode=one))
        specs.append(pl.BlockSpec((rows, wide), lambda j, c: (0, 0), pipeline_mode=one))
    out = pl.BlockSpec((None, shards // 2, depth, wide), lambda j, c: (j, 0, 0, 0))
    shape = (4, shards // 2, depth, wide)
    return wgrad_call(kernel, where, (4,), specs, out, shape, arrays)


def wgrad_planes(where, left, right):
    rows, width = right.shape
    planes = lax.axis_size("fsdp") // 2
    depth, wide = left.shape[1] // (2 * planes), width // 4

    def kernel(place_ref, left_ref, right_ref, mine_ref, far_ref):
        total = tn(left_ref[...], right_ref[...])
        for _, mine, far in halves(place_ref, total, depth):
            for j in range(4):
                mine_ref[j] = mine[:, j * wide : (j + 1) * wide]
                far_ref[j] = far[:, j * wide : (j + 1) * wide]

    specs = [
        pl.BlockSpec((rows, 2 * depth), lambda z, c: (0, z)),
        pl.BlockSpec((rows, width), lambda z, c: (0, 0), pipeline_mode=pl.Buffered(1)),
    ]
    out = pl.BlockSpec((4, None, depth, wide), lambda z, c: (0, z, 0, 0))
    shape = (4, planes, depth, wide)
    return wgrad_call(kernel, where, (planes,), specs, out, shape, (left, right))


def add(*parts):
    total = parts[0].astype(F32)
    for part in parts[1:]:
        total += part.astype(F32)
    return total.astype(BF)


def chip_sum(where, mine, far):
    planes, depth, wide = mine.shape[1:]
    half = planes // 2

    def kernel(place_ref, mine_ref, far_ref, *outs):
        for flip, (first, second) in enumerate(((0, 2), (1, 2), (0, 3), (1, 3))):

            @pl.when(pl.program_id(0) == flip)
            def _():
                total = add(mine_ref[...], far_ref[...])
                outs[first][flip // 2] = total[:half]
                outs[second][flip % 2] = total[half:]

    piece = (2, half, depth, wide)
    return pl.pallas_call(
        kernel,
        grid_spec=pltpu.PrefetchScalarGridSpec(
            num_scalar_prefetch=1,
            grid=(4,),
            in_specs=[pl.BlockSpec((None, planes, depth, wide), lambda f, c: (c[2] ^ f, 0, 0, 0))] * 2,
            out_specs=[pl.BlockSpec(piece, lambda f, c: (0, 0, 0, 0))] * 4,
        ),
        out_shape=[jax.ShapeDtypeStruct(piece, BF)] * 4,
        compiler_params=pltpu.CompilerParams(vmem_limit_bytes=32 * 2**20),
    )(where, mine, far)


def sides(chip):
    return [send(chip[1], 0, 0, 1), send(chip[3], 0, 0, 2)]


def side_sum(chip, got):
    half, depth, wide = chip[0].shape[1:]

    def kernel(a_ref, ga_ref, b_ref, gb_ref, *outs):
        for own, other, outs_of in ((a_ref, ga_ref, outs[:2]), (b_ref, gb_ref, outs[2:])):
            for n in range(2):

                @pl.when(pl.program_id(0) == n)
                def _():
                    outs_of[n][...] = add(own[...], other[...])

    return pl.pallas_call(
        kernel,
        grid=(2,),
        in_specs=[pl.BlockSpec((None, half, depth, wide), lambda n: (n, 0, 0, 0))] * 4,
        out_specs=[pl.BlockSpec((half, depth, wide), lambda n: (0, 0, 0))] * 4,
        out_shape=[jax.ShapeDtypeStruct((half, depth, wide), BF)] * 4,
        compiler_params=pltpu.CompilerParams(vmem_limit_bytes=32 * 2**20),
    )(chip[0], got[0], chip[2], got[1])


def ends(side):
    return [send(side[1], 0, 0, 2), send(side[3], 0, 0, 1)]


def plane_sum(side, got):
    half, depth, wide = side[0].shape
    parts = [side[0], got[0], side[2], got[1]]

    def kernel(*refs):
        out = refs[-1]
        for n in range(half):
            out[n] = add(refs[0][n], refs[1][n])
            out[half + n] = add(refs[2][n], refs[3][n])

    return pl.pallas_call(
        kernel,
        in_specs=[pl.BlockSpec(memory_space=pltpu.VMEM)] * 4,
        out_shape=jax.ShapeDtypeStruct((2 * half, depth, wide), BF),
        compiler_params=pltpu.CompilerParams(vmem_limit_bytes=24 * 2**20),
    )(*parts)


def plane_columns(where, side, got, last):
    half, depth, wide = side[0].shape
    planes, more = 2 * half, 16
    parts = [side[0], got[0], side[2], got[1], last]

    def kernel(place_ref, *refs):
        ins, outs = refs[:5], refs[5:]
        for step in range(planes):
            at = (place_ref[0] + step) % planes

            @pl.when(at < half)
            def _():
                outs[step][pl.ds(0, depth), :] = add(ins[0][at], ins[1][at])

            @pl.when(at >= half)
            def _():
                outs[step][pl.ds(0, depth), :] = add(ins[2][at - half], ins[3][at - half])

            outs[step][pl.ds(depth, more), :] = ins[4][at]

    return pl.pallas_call(
        kernel,
        in_specs=[pl.BlockSpec(memory_space=pltpu.SMEM)]
        + [pl.BlockSpec(memory_space=pltpu.VMEM)] * 5,
        out_shape=[jax.ShapeDtypeStruct((depth + more, wide), BF)] * planes,
        compiler_params=pltpu.CompilerParams(vmem_limit_bytes=24 * 2**20),
    )(where, *parts)


def column_parts(parts):
    return [parts[0]] + [send(part, step, 0, 0) for step, part in enumerate(parts) if step]


def column_groups():
    shards = lax.axis_size("fsdp")
    return [list(range(c, shards, 2)) for c in range(2)]


def column_sum(total):
    return lax.psum_scatter(
        total, "fsdp", scatter_dimension=0, tiled=False, axis_index_groups=column_groups()
    )


def from_plane(share):
    return lax.all_gather(share, "seq", axis=0, tiled=False)


def joined(units):
    count, depth, wide = units.shape

    def kernel(in_ref, out_ref):
        for j in range(count):
            out_ref[:, pl.ds(j * wide, wide)] = in_ref[j].astype(F32)

    return pl.pallas_call(
        kernel,
        in_specs=[pl.BlockSpec(memory_space=pltpu.VMEM)],
        out_specs=pl.BlockSpec(memory_space=pltpu.VMEM),
        out_shape=jax.ShapeDtypeStruct((depth, count * wide), F32),
        compiler_params=pltpu.CompilerParams(vmem_limit_bytes=24 * 2**20),
    )(units)


def shares(total):
    return [total] + over_plane(total)


def spread(where, parts, shapes, more=0):
    wide = parts[0].shape[1]
    depth = shapes[0][0]

    def kernel(place_ref, *refs):
        ins, outs = refs[: len(parts)], refs[len(parts) :]
        me = place_ref[2]
        for spot, ref in zip([me, me + 1 - 2 * (me % 2), (me + 2) % 4, 3 - me], ins):
            value = ref[pl.ds(0, depth), :].astype(F32)
            column = pl.ds(pl.multiple_of(spot * wide, wide), wide)
            if len(shapes) == 1:
                outs[0][:, column] = value
            else:

                @pl.when(spot < 3)
                def _():
                    outs[0][:, column] = value

                @pl.when(spot == 3)
                def _():
                    outs[1][...] = value

        if more:
            rows = [ref[pl.ds(depth, 16), :].astype(F32) for ref in ins]
            outs[-1][...] = (rows[0] + rows[1] + rows[2] + rows[3])[:more]

    out = [jax.ShapeDtypeStruct(shape, F32) for shape in shapes]
    return pl.pallas_call(
        kernel,
        in_specs=[pl.BlockSpec(memory_space=pltpu.SMEM)]
        + [pl.BlockSpec(memory_space=pltpu.VMEM)] * len(parts),
        out_shape=out + ([jax.ShapeDtypeStruct((more, wide), F32)] if more else []),
        compiler_params=pltpu.CompilerParams(vmem_limit_bytes=24 * 2**20),
    )(where, *parts)


def along_z(mine):
    return [send(mine, step, 0, 0) for step in range(1, lax.axis_size("fsdp") // 2)]


def over_plane(value):
    return [send(value, 0, 0, flip) for flip in (1, 2, 3)]


def to_partner(values):
    return [send(value, 0, 1, 0) for value in values]


def column(mine):
    return lax.all_gather(
        mine, "fsdp", axis=0, tiled=False, axis_index_groups=column_groups()
    )


def others(where, whole, depth):
    planes = whole.shape[0]
    return jnp.stack(
        [pick(whole, (where[0] + planes - step) % planes)[:depth] for step in range(1, planes)]
    )


def across(along_x, along_y):
    half = along_x.shape[1] // 2
    return [send(along_x[:, :half], 0, 0, 2), send(along_y[:, half:], 0, 0, 1)]


def plain_sum(left, right):
    share = lax.psum_scatter(tn(left, right).astype(BF), "fsdp", scatter_dimension=0, tiled=True)
    return lax.psum(share, "seq").astype(F32)


def normal(values):
    center = values - jnp.mean(values, axis=-1, keepdims=True)
    inverse = lax.rsqrt(jnp.mean(center * center, axis=-1, keepdims=True) + epsilon)
    return center * inverse, inverse


def norm_back(grad, unit, inverse, gain):
    e = grad * gain
    return inverse * (
        e
        - jnp.mean(e, axis=-1, keepdims=True)
        - unit * jnp.mean(e * unit, axis=-1, keepdims=True)
    )


def gelu_and_slope(u):
    c = 0.7978845608
    square = u * u
    t = jnp.tanh(u * (c + (0.044715 * c) * square))
    half = 0.5 + 0.5 * t
    hid = u * half
    return hid, half + hid * (1.0 - t) * (c + (3 * 0.044715 * c) * square)


def call(kernel, grid, in_specs, out_specs, out_shape, scratch, args):
    return pl.pallas_call(
        kernel,
        grid=grid,
        in_specs=in_specs,
        out_specs=out_specs,
        out_shape=out_shape,
        scratch_shapes=scratch,
        compiler_params=pltpu.CompilerParams(vmem_limit_bytes=56 * 2**20),
    )(*args)


def whole(array):
    return pl.BlockSpec(array.shape, lambda *i: (0,) * array.ndim, pipeline_mode=pl.Buffered(1))


def rows_of(height, width):
    return pl.BlockSpec((height, width), lambda i: (i, 0))


def columns_of(height, width):
    return pl.BlockSpec((height, width), lambda i: (0, i))


def struct(*shape, dtype=BF):
    return jax.ShapeDtypeStruct(shape, dtype)


def project(a, w, bias):
    rows, wide = a.shape[0], w.shape[1]

    def kernel(a_ref, w_ref, b_ref, out_ref):
        out_ref[...] = (nn(a_ref[...], w_ref[...]) + b_ref[...]).astype(BF)

    return call(
        kernel,
        (wide // TILE,),
        [whole(a), columns_of(w.shape[0], TILE), columns_of(1, TILE)],
        columns_of(rows, TILE),
        struct(rows, wide),
        [],
        (a, w, bias[None]),
    )


def middle(o, w, x, bias, gain, shift):
    rows, width = x.shape
    height = rows // 4

    def kernel(o_ref, w_ref, x_ref, b_ref, gain_ref, shift_ref, y_ref, a_ref):
        y = nn(o_ref[...], w_ref[...]) + x_ref[...].astype(F32) + b_ref[...]
        y_ref[...] = y
        unit, _ = normal(y)
        a_ref[...] = (unit * gain_ref[...] + shift_ref[...]).astype(BF)

    tile = rows_of(height, width)
    vectors = [bias[None], gain[None], shift[None]]
    return call(
        kernel,
        (rows // height,),
        [tile, whole(w), tile] + [whole(v) for v in vectors],
        [tile, tile],
        [struct(rows, width, dtype=F32), struct(rows, width)],
        [],
        (o, w, x, *vectors),
    )


def expand(a, w, bias):
    rows, wide = a.shape[0], w.shape[1]

    def kernel(a_ref, w_ref, b_ref, hid_ref, slope_ref):
        for part in range(PARTS):
            at = pl.ds(part * (rows // PARTS), rows // PARTS)
            hid, slope = gelu_and_slope(nn(a_ref[at, :], w_ref[...]) + b_ref[...])
            hid_ref[at, :] = hid.astype(BF)
            slope_ref[at, :] = slope.astype(BF)

    tile = columns_of(rows, WIDE)
    return call(
        kernel,
        (wide // WIDE,),
        [whole(a), columns_of(w.shape[0], WIDE), columns_of(1, WIDE)],
        [tile, tile],
        [struct(rows, wide)] * 2,
        [],
        (a, w, bias[None]),
    )


def back_down(g, w, slope):
    rows, wide = slope.shape

    def kernel(g_ref, w_ref, slope_ref, du_ref, sum_ref):
        du = (nt(g_ref[...], w_ref[...]) * slope_ref[...].astype(F32)).astype(BF)
        du_ref[...] = du
        sum_ref[...] = jnp.sum(du.astype(F32), axis=0, keepdims=True)

    tile = columns_of(rows, TILE)
    return call(
        kernel,
        (wide // TILE,),
        [whole(g), rows_of(TILE, w.shape[1]), tile],
        [tile, columns_of(1, TILE)],
        [struct(rows, wide), struct(1, wide, dtype=F32)],
        [],
        (g, w, slope),
    )


def back_norm(total, values, gain):
    unit, inverse = normal(values)
    sums = (
        jnp.sum(total * unit, axis=0, keepdims=True),
        jnp.sum(total, axis=0, keepdims=True),
    )
    return norm_back(total, unit, inverse, gain), sums


def gather_sums(refs, sums):
    @pl.when(pl.program_id(0) == 0)
    def _():
        for ref, value in zip(refs, sums):
            ref[...] = value

    @pl.when(pl.program_id(0) > 0)
    def _():
        for ref, value in zip(refs, sums):
            ref[...] += value


def back_up(du, w, y1, g, gain):
    rows, wide = du.shape
    width = y1.shape[1]
    height = rows // HEIGHTS

    def kernel(du_ref, w_ref, y_ref, g_ref, gain_ref, dy_ref, d1_ref, s1_ref, s2_ref, s3_ref):
        back, sums = back_norm(nt(du_ref[...], w_ref[...]), y_ref[...], gain_ref[...])
        dy = g_ref[...].astype(F32) + back
        dy_ref[...] = dy
        d1 = dy.astype(BF)
        d1_ref[...] = d1
        sums += (jnp.sum(d1.astype(F32), axis=0, keepdims=True),)
        gather_sums((s1_ref, s2_ref, s3_ref), sums)

    row, tile = pl.BlockSpec((1, width), lambda i: (0, 0)), rows_of(height, width)
    vector = struct(1, width, dtype=F32)
    return call(
        kernel,
        (rows // height,),
        [rows_of(height, wide), whole(w), tile, tile, whole(gain[None])],
        [tile, tile, row, row, row],
        [struct(rows, width, dtype=F32), struct(rows, width), vector, vector, vector],
        [],
        (du, w, y1, g, gain[None]),
    )


def back_out(d1, w):
    rows, width = d1.shape

    def kernel(d_ref, w_ref, out_ref):
        out_ref[...] = nt(d_ref[...], w_ref[...]).astype(BF)

    return call(
        kernel,
        (width // TILE,),
        [whole(d1), rows_of(TILE, width)],
        columns_of(rows, TILE),
        struct(rows, width),
        [],
        (d1, w),
    )


def back_qkv(dqkv, w, x, dy1, gain):
    rows, wide = dqkv.shape
    width = x.shape[1]
    height = rows // HEIGHTS

    def kernel(d_ref, w_ref, x_ref, dy_ref, gain_ref, dx_ref, s1_ref, s2_ref, s3_ref):
        back, sums = back_norm(
            nt(d_ref[...], w_ref[...]), x_ref[...].astype(F32), gain_ref[...]
        )
        dx_ref[...] = (dy_ref[...] + back).astype(BF)
        sums += (jnp.sum(d_ref[...].astype(F32), axis=0, keepdims=True),)
        gather_sums((s1_ref, s2_ref, s3_ref), sums)

    row, tile = pl.BlockSpec((1, width), lambda i: (0, 0)), rows_of(height, width)
    long = pl.BlockSpec((1, wide), lambda i: (0, 0))
    vector = struct(1, width, dtype=F32)
    return call(
        kernel,
        (rows // height,),
        [rows_of(height, wide), whole(w), tile, tile, whole(gain[None])],
        [tile, row, row, long],
        [struct(rows, width), vector, vector, struct(1, wide, dtype=F32)],
        [],
        (dqkv, w, x, dy1, gain[None]),
    )


def contract(hid, w, y1, bias):
    rows, wide = hid.shape
    width = w.shape[1]
    height = rows // HEIGHTS

    def kernel(h_ref, w_ref, y_ref, b_ref, out_ref):
        out_ref[...] = (nn(h_ref[...], w_ref[...]) + y_ref[...] + b_ref[...]).astype(BF)

    tile = rows_of(height, width)
    return call(
        kernel,
        (rows // height,),
        [rows_of(height, wide), whole(w), tile, whole(bias[None])],
        tile,
        struct(rows, width),
        [],
        (hid, w, y1, bias[None]),
    )


def plainly(
    tokens, live, x, g_low, small, w_qkv, w_out, w_up, w_down
):
    gain1, shift1, bias_qkv, bias_out, gain2, shift2, bias_up, bias_down = small
    slots, width = tokens.shape[2:]
    qkv_w, out_w, up_w, down_w = [
        lax.all_gather(w, "fsdp", axis=0, tiled=True) for w in (w_qkv, w_out, w_up, w_down)
    ]
    g = g_low.astype(F32)
    unit1, inverse1 = normal(x)
    a1 = (unit1 * gain1 + shift1).astype(BF)
    qkv = (nn(a1, qkv_w) + bias_qkv).astype(BF)
    o = per_image(attention_forward, live, slots, [qkv], width)
    y1 = x + nn(o, out_w) + bias_out
    unit2, inverse2 = normal(y1)
    a2 = (unit2 * gain2 + shift2).astype(BF)
    hid, slope = gelu_and_slope(nn(a2, up_w) + bias_up)
    hid = hid.astype(BF)
    s_down = plain_sum(hid, g_low)
    du = (nt(g_low, down_w) * slope).astype(BF)
    s_up = plain_sum(a2, du)
    activations = (y1 + nn(hid, down_w) + bias_down).astype(BF)
    da2 = nt(du, up_w)
    dy1 = g + norm_back(da2, unit2, inverse2, gain2)
    d1 = dy1.astype(BF)
    s_out = plain_sum(o, d1)
    do = nt(d1, out_w).astype(BF)
    dqkv = per_image(attention_backward, live, slots, [qkv, do], 3 * width)
    s_qkv = plain_sum(a1, dqkv)
    da1 = nt(dqkv, qkv_w)
    input_grad = (dy1 + norm_back(da1, unit1, inverse1, gain1)).astype(BF)
    sums = column_sums(da1, unit1, dqkv, d1, da2, unit2, du, g)
    shards = lax.axis_size("fsdp")
    packed = jnp.concatenate([part.reshape(shards, -1) for part in sums], axis=1)
    own = pick(lax.psum(packed, ("fsdp", "seq")), lax.axis_index("fsdp"))
    return activations, input_grad, s_qkv, s_out, s_up, s_down, own_parts(own, sums)


def column_sums(da1, unit1, dqkv, d1, da2, unit2, du, g):
    width = da1.shape[1]
    sums_qkv = jnp.sum(dqkv.astype(F32), axis=0)
    return (
        jnp.sum(da1 * unit1, axis=0),
        jnp.sum(da1, axis=0),
        jnp.concatenate([sums_qkv[:width], sums_qkv[2 * width :]]),
        jnp.sum(d1.astype(F32), axis=0),
        jnp.sum(da2 * unit2, axis=0),
        jnp.sum(da2, axis=0),
        jnp.sum(du.astype(F32), axis=0),
        jnp.sum(g, axis=0),
    )


def by_parts(where, tokens, live, x, g_low, vectors, w_qkv, w_out, w_up, w_down):
    slots, width = tokens.shape[2:]
    wide = w_up.shape[1]
    me = where[2]
    x_low = tokens.reshape(x.shape)

    def unit(w):
        return lax.dynamic_slice_in_dim(w, me * (w.shape[1] // 4), w.shape[1] // 4, axis=1)

    depth = w_qkv.shape[0]
    first = unit(w_qkv)
    z_first = along_z(first)
    w_up, w_out, w_down, vectors = after((w_up, w_out, w_down, vectors), first)
    packed = jnp.pad(packed_rows(vectors), ((0, 4), (0, 0))).reshape(2, width)
    packed = jnp.pad(packed, ((0, 14), (0, width // 4)))
    z_second = column(
        jnp.concatenate([jnp.concatenate([unit(w_up), unit(w_out)], axis=1), packed])
    )
    z_third = column(unit(w_down))
    unit1, _ = normal(x)
    sum_down = jnp.sum(g_low.astype(F32), axis=0)

    col_first = jnp.stack(after(z_first, unit1))
    two_first = [send(col_first, 0, 0, flip) for flip in (1, 2)]
    far_own_first = to_partner(after([w_qkv, w_out], col_first))
    far_first = to_partner([col_first])
    two_first = after(two_first, unit1)
    cross_first = across(*two_first)
    far_first += to_partner(two_first)
    z_second = after(z_second, two_first)
    small = complete(small_table(where, z_second[:, depth : depth + 2, :width], vectors), width)
    gain1, shift1, bias_qkv, bias_out, gain2, shift2, bias_up, bias_down = small
    a1 = (unit1 * gain1 + shift1).astype(BF)
    col_second = others(where, z_second, depth)
    two_second = [send(col_second, 0, 0, flip) for flip in (1, 2)]
    cross_first = after(cross_first, col_second, a1)
    near_first = [col_first] + two_first + cross_first
    far_first += to_partner(cross_first)
    (qkv_w,) = assemble(
        where,
        [[w_qkv], far_own_first[:1]],
        [near_first, far_first],
        [(width, 3 * width)],
    )
    qkv = project(a1, qkv_w, bias_qkv)
    two_second = after(two_second, qkv)
    cross_second = across(*two_second)
    col_third = others(where, after(z_third, two_second), w_down.shape[0])
    two_third = [send(col_third, 0, 0, flip) for flip in (1, 2)]
    far_own_second = to_partner(after([w_up], qkv_w)) + far_own_first[1:]
    far_second = to_partner(after([col_second], qkv_w)) + to_partner(two_second)
    o = per_image(attention_forward, live, slots, [after(qkv, col_third)], width)
    cross_second = after(cross_second, o)
    near_second = [col_second] + two_second + cross_second
    far_second += to_partner(cross_second)
    up_w, out_w = assemble(
        where,
        [[w_up, w_out], far_own_second],
        [near_second, far_second],
        [(width, wide), (width, width)],
    )
    y1, a2 = middle(o, out_w, x_low, bias_out, gain2, shift2)
    far_own_third = to_partner(after([w_down], cross_second))
    far_third = to_partner(after([col_third], cross_second))
    two_third, far_own_third, far_third = after((two_third, far_own_third, far_third), a2)
    cross_third = across(*two_third)
    far_third = far_third + to_partner(two_third)
    hid, slope = expand(a2, after(up_w, two_third), bias_up)
    far_third, cross_third = after((far_third, cross_third), hid)
    near_third = [col_third] + two_third + cross_third
    far_third = far_third + to_partner(cross_third)

    mine_down, far_down = wgrad_planes(where, after(hid, far_third[:3]), g_low)
    far_third = after(far_third, mine_down)
    got_down = send(after(far_down, far_third), 0, 1, 0)
    (down_w,) = assemble(
        where,
        [[w_down], far_own_third],
        [near_third, far_third],
        [(wide, width)],
    )
    du, sum_up = back_down(g_low, down_w, slope)
    chip_down = chip_sum(where, *after((mine_down, got_down), du))
    sides_down = sides(chip_down)
    mine_up, far_up = wgrad_units(where, a2, after(du, chip_down))
    got_up = send(far_up, 0, 1, 0)
    dy1, d1, sum_gain2, sum_shift2, sum_out = back_up(after(du, mine_up), up_w, y1, g_low, gain2)
    side_down = side_sum(chip_down, after(sides_down, dy1))
    ends_down = ends(side_down)
    do = back_out(after(d1, side_down), out_w)
    total_down = plane_sum(side_down, after(ends_down, do))
    share_down = column_sum(total_down)
    chip_up = chip_sum(where, *after((mine_up, got_up), total_down))
    sides_up = sides(chip_up)
    dqkv = per_image(attention_backward, live, slots, [qkv, after(do, chip_up)], 3 * width)
    share_down = after(share_down, dqkv)
    side_up = side_sum(chip_up, after(sides_up, share_down))
    ends_up = ends(side_up)
    mine_qkv, far_qkv = wgrad_units(where, a1, after(dqkv, side_up), extra=(o, d1))
    total_up = plane_sum(side_up, after(ends_up, mine_qkv))
    got_qkv = send(after(far_qkv, total_up), 0, 1, 0)
    share_up = column_sum(total_up)
    from_down = from_plane(share_down)
    chip_qkv = chip_sum(where, *after((mine_qkv, got_qkv), total_up))
    sides_qkv = sides(chip_qkv)
    input_grad, sum_gain1, sum_shift1, sum_qkv = back_qkv(
        after(dqkv, chip_qkv), qkv_w, x_low, dy1, gain1
    )
    s_down = joined(after(from_down, input_grad))
    side_qkv = side_sum(chip_qkv, after(sides_qkv, s_down))
    ends_qkv = ends(side_qkv)

    sum_qv = jnp.concatenate([sum_qkv[0, :width], sum_qkv[0, 2 * width :]])
    sums = (
        sum_gain1[0],
        sum_shift1[0],
        sum_qv,
        sum_out[0],
        sum_gain2[0],
        sum_shift2[0],
        sum_up[0],
        sum_down,
    )
    planes = lax.axis_size("fsdp") // 2
    rows = packed_rows([part.reshape(planes, 2, -1) for part in sums])
    rows = pick(rows, where[1], 1) + send(pick(rows, 1 - where[1], 1), 0, 1, 0)
    rows = jnp.pad(rows, ((0, 0), (0, 4), (0, 0))).reshape(planes, 2, width).astype(BF)
    rows = jnp.pad(rows, ((0, 0), (0, 14), (0, 0)))

    activations = contract(after(hid, side_qkv), down_w, y1, bias_down)
    column_qkv = column_parts(
        plane_columns(where, side_qkv, after(ends_qkv, activations), rows)
    )
    from_up = from_plane(after(share_up, activations))
    share_qkv = add(*after(column_qkv, column_qkv[0]))
    s_up = joined(after(from_up, share_qkv))
    s_qkv, s_out, own = spread(where, shares(share_qkv), [w_qkv.shape, w_out.shape], more=2)
    own = own.reshape(-1)
    return activations, input_grad, s_qkv, s_out, s_up, s_down, own_parts(own, sums)


def on_device(
    tokens,
    counts,
    ln1_gain,
    ln1_shift,
    w_qkv,
    b_qv,
    w_out,
    b_out,
    ln2_gain,
    ln2_shift,
    w_up,
    b_up,
    w_down,
    b_down,
    cotangent,
):
    where = place()
    vectors = (ln1_gain, ln1_shift, b_qv, b_out, ln2_gain, ln2_shift, b_up, b_down)
    micro, images, slots, width = tokens.shape
    rows = micro * images * slots
    own_start = lax.axis_index("seq") * images
    live = lax.dynamic_slice_in_dim(counts, own_start, images, axis=1).reshape(-1)
    x = tokens.reshape(rows, width).astype(F32)
    g_low = cotangent.reshape(rows, width)
    weights = (w_qkv, w_out, w_up, w_down)
    if by_hand():
        found = by_parts(where, tokens, live, x, g_low, vectors, *weights)
    else:
        packed = lax.all_gather(jnp.concatenate(vectors), "fsdp", axis=0, tiled=False)
        small = complete(cut(packed, vectors), width)
        found = plainly(tokens, live, x, g_low, small, *weights)
    activations, input_grad, s_qkv, s_out, s_up, s_down, sums = found
    return (
        activations.reshape(tokens.shape),
        input_grad.reshape(tokens.shape),
        sums[0],
        sums[1],
        s_qkv,
        sums[2],
        s_out,
        sums[3],
        sums[4],
        sums[5],
        s_up,
        sums[6],
        s_down,
        sums[7],
    )


def solution(mesh):
    row = P(None, ("fsdp", "seq"), None, None)
    one, two = P("fsdp"), P("fsdp", None)
    params = (one, one, two, one, two, one, one, one, two, one, two, one)
    return jax.shard_map(
        on_device,
        mesh=mesh,
        in_specs=(row, P(None, "fsdp")) + params + (row,),
        out_specs=(row, row) + params,
        check_vma=False,
    )
```

time: 563 us -> 469 us (0.83)
  matrix products: 96.9 us -> 0 us
  Pallas kernels: 166 us -> 235 us
  starting transfers between devices: 79.5 us -> 39.3 us
  other arithmetic: 30.6 us -> 12.4 us
  waiting for transfers between devices: 148 us -> 131 us
  between operations: 2.07 us -> 15.2 us
    pallas_call x6 -> x19, Pallas kernels: 61.1 us -> 159 us  [the longest x8 105 us: call(): pl.pallas_call(kernel, grid=grid, in_specs=in_specs, out_specs=out_specs,...]
    dot_general x8 -> x0, matrix products: 96.9 us -> none  [the longest x4 55.8 us: nt(): lax.dot_general(a, b, (((1,), (1,)), ((), ())), preferred_element_type=F32)]
    ppermute x80 -> x57, starting transfers between devices: 79.5 us -> 39.1 us  [send(): return lax.ppermute(value, ('fsdp', 'seq'), pairs)]
    pallas_call x3, Pallas kernels: 37 us -> 15.4 us  [chip_sum(): pl.pallas_call(kernel, grid_spec=pltpu.PrefetchScalarGridSpec(num_scalar_...]
    ppermute x80 -> x57, waiting for transfers between devices: 148 us -> 131 us  [send(): return lax.ppermute(value, ('fsdp', 'seq'), pairs)]
    pallas_call x2, Pallas kernels: 45.8 us -> 36.6 us  [per_image(): pl.pallas_call(kernel, grid_spec=pltpu.PrefetchScalarGridSpec(num_scalar_...]
    pallas_call x3, Pallas kernels: 15.5 us -> 21.8 us  [assemble(): pl.pallas_call(kernel, in_specs=[pl.BlockSpec(memory_space=pltpu.SMEM)] +...]
    unnamed x154 -> x80, local copies, waits for them, and re-layouts: 18.8 us -> 15.5 us
  transfers between devices with their start and end apart: 80 -> 63, of which waited for: 28 -> 28; matrix products, arithmetic and copies ran while one was open for 25% -> 5% of each run, Pallas kernels for 20% -> 46%
where the time goes in v2:
time: 469 us; the launch traced here: 463 us
  Pallas kernels  235 us (50%)
  waiting for transfers between devices  131 us (28%)
  starting transfers between devices  39.3 us (8%)
  local copies, waits for them, and re-layouts  29.7 us (6%)
  between operations  15.2 us (3%)
  other arithmetic  12.4 us (3%)
    ppermute x57, waiting for transfers between devices, send(): return lax.ppermute(value, ('fsdp', 'seq'), pairs)  131 us
    pallas_call x8, Pallas kernels, call(): pl.pallas_call(kernel, grid=grid, in_specs=in_specs, out_specs=out_specs,...  105 us
    pallas_call x3, Pallas kernels, wgrad_call(): pl.pallas_call(kernel, grid_spec=pltpu.PrefetchScalarGridSpec(num_scalar_...  43.3 us
    ppermute x57, starting transfers between devices, send(): return lax.ppermute(value, ('fsdp', 'seq'), pairs)  39.1 us
    pallas_call x2, Pallas kernels, per_image(): pl.pallas_call(kernel, grid_spec=pltpu.PrefetchScalarGridSpec(num_scalar_...  36.6 us
    pallas_call x3, Pallas kernels, assemble(): pl.pallas_call(kernel, in_specs=[pl.BlockSpec(memory_space=pltpu.SMEM)] +...  21.8 us
    unnamed x80, local copies, waits for them, and re-layouts  15.5 us
    pallas_call x3, Pallas kernels, chip_sum(): pl.pallas_call(kernel, grid_spec=pltpu.PrefetchScalarGridSpec(num_scalar_...  15.4 us
  transfers between devices with their start and end apart: 63, of which 28 were waited for; matrix products, arithmetic and copies ran while one was open for 5% of the time, Pallas kernels for 46%

profile of v2, /device:TPU:8, one launch (start us, length us, event | category | flops | bytes accessed | tf_op | source)
XLA Modules:
  0.0 463.0 jit_solution(9321935005009485308)
XLA Ops:
  11.8 1.6 collective-permute-start
  14.5 1.9 collective-permute-start.2
  16.5 1.9 convert_reduce_fusion
  19.3 9.3 %collective-permute-done = bf16[128,768]{1,0:T(8,128)(2,1)S(1)} collective-permute-done((bf16[128,768]{1,0:T(8,128)(2,1)S(1)}, bf16[128,768]{1,0:T(8,128)(2,1)S(1)}, u32[]{:S(2)}, u32[]{:S(2)}) %collective-permute-start) | collective-permute-done | bytes 196640 | tf_op jit(solution)/shard_map/ppermute | solution.py:149
  28.5 15.6 %collective-permute-done.1 = bf16[128,768]{1,0:T(8,128)(2,1)S(1)} collective-permute-done((bf16[128,768]{1,0:T(8,128)(2,1)S(1)}, bf16[128,768]{1,0:T(8,128)(2,1)S(1)}, u32[]{:S(2)}, u32[]{:S(2)}) %collective-permute-start.1) | collective-permute-done | bytes 196640 | tf_op jit(solution)/shard_map/ppermute | solution.py:149
  44.1 4.9 %collective-permute-done.2 = bf16[128,768]{1,0:T(8,128)(2,1)S(1)} collective-permute-done((bf16[128,768]{1,0:T(8,128)(2,1)S(1)}, bf16[128,768]{1,0:T(8,128)(2,1)S(1)}, u32[]{:S(2)}, u32[]{:S(2)}) %collective-permute-start.2) | collective-permute-done | bytes 196640 | tf_op jit(solution)/shard_map/ppermute | solution.py:149
  49.1 1.4 collective-permute-start.3
  50.5 1.5 collective-permute-start.4
  52.0 1.7 constant_dynamic-slice_fusion.3
  54.5 9.8 %collective-permute-done.3.refs_2_ = bf16[3,128,768]{2,1,0:T(8,128)(2,1)} collective-permute-done((bf16[3,128,768]{2,1,0:T(8,128)(2,1)S(1)}, bf16[3,128,768]{2,1,0:T(8,128)(2,1)}, u32[]{:S(2)}, u32[]{:S(2)}) %collective-permute-start.3) | collective-permute-done | bytes 589856 | tf_op jit(solution)/shard_map/ppermute | solution.py:149
  66.5 1.6 collective-permute-start.6
  73.5 1.5 collective-permute-start.14
  76.1 1.6 collective-permute-start.15
  78.2 3.3 collective-permute-done.7.refs_5_
  81.6 3.6 add_convert_fusion.a_ref.refs_0_
  87.5 7.9 %shard_map.254.w_ref = bf16[1024,3072]{1,0:T(8,128)(2,1)} custom-call(s32[3]{0:T(128)S(1)} %pad_add_fusion.1.place_ref, bf16[128,3072]{1,0:T(8,128)(2,1)} %refs_0_.1, bf16[3,128,768]{2,1,0:T(8,128)(2,1)S(1)} %pad_maximum_fusion.2.refs_1_, bf16[3,128,768]{2,1,0:T(8,128)(2,1)} %collective-permute-done.3.refs_2_, bf16[3,128,768]{2,1,0:T(8,128)(2,1)S(1)} %copy-done.8, ...), custom_call_target="tpu_custom_call" | custom-call | tf_op jit(solution)/shard_map/pallas_call | solution.py:226
  95.4 11.1 %shard_map.255.qkv_ref = bf16[960,3072]{1,0:T(8,128)(2,1)} custom-call(bf16[960,1024]{1,0:T(8,128)(2,1)} %add_convert_fusion.a_ref.refs_0_, bf16[1024,3072]{1,0:T(8,128)(2,1)} %shard_map.254.w_ref, f32[1,3072]{1,0:T(1,128)} %bitcast.115), custom_call_target="tpu_custom_call" | custom-call | tf_op jit(solution)/shard_map/pallas_call | solution.py:561
  110.0 11.0 %collective-permute-done.16.refs_5_ = bf16[3,64,1280]{2,1,0:T(8,128)(2,1)S(1)} collective-permute-done((bf16[3,64,1280]{2,1,0:T(8,128)(2,1)}, bf16[3,64,1280]{2,1,0:T(8,128)(2,1)S(1)}, u32[]{:S(2)}, u32[]{:S(2)}) %collective-permute-start.16) | collective-permute-done | bytes 491552 | tf_op jit(solution)/shard_map/ppermute | solution.py:149
  122.3 12.6 %shard_map.256.o_ref.refs_2_ = bf16[960,1024]{1,0:T(8,128)(2,1)S(1)} custom-call(s32[3]{0:T(128)S(1)} %fusion.12.counts_ref, bf16[960,3072]{1,0:T(8,128)(2,1)} %shard_map.255.qkv_ref), custom_call_target="tpu_custom_call" | custom-call | tf_op jit(solution)/shard_map/pallas_call | solution.py:85
  134.9 1.3 copy-done.2
  138.8 1.8 collective-permute-done.24.refs_13_
  142.7 7.1 %shard_map.257 = (bf16[1024,4096]{1,0:T(8,128)(2,1)}, bf16[1024,1024]{1,0:T(8,128)(2,1)}) custom-call(s32[3]{0:T(128)S(1)} %pad_add_fusion.1.place_ref, bf16[128,4096]{1,0:T(8,128)(2,1)} %refs_0_.2, bf16[128,1024]{1,0:T(8,128)(2,1)S(1)} %copy-done.19, bf16[3,128,1280]{2,1,0:T(8,128)(2,1)S(1)} %pad_maximum_fusion.refs_2_, ...), custom_call_target="tpu_custom_call" | custom-call | tf_op jit(solution)/shard_map/pallas_call | solution.py:226
  149.8 7.2 %shard_map.258 = (f32[960,1024]{1,0:T(8,128)}, bf16[960,1024]{1,0:T(8,128)(2,1)}) custom-call(bf16[960,1024]{1,0:T(8,128)(2,1)} %copy-done.2, bf16[1024,1024]{1,0:T(8,128)(2,1)} %get-tuple-element.179.w_ref, bf16[960,1024]{1,0:T(8,128)(2,1)} %bitcast.95, f32[1,1024]{1,0:T(1,128)} %bitcast.124, f32[1,1024]{1,0:T(1,128)} %bitcast.116, f32[1,1024]{1,0:T(1,128)} %bitcast.123), custom_call_target="tpu_custom_call" | custom-call | tf_op jit(solution)/shard_map/pallas_call | solution.py:561
  158.0 2.3 collective-permute-done.26.refs_3_
  163.5 19.3 %shard_map.259 = (bf16[960,4096]{1,0:T(8,128)(2,1)}, bf16[960,4096]{1,0:T(8,128)(2,1)}) custom-call(bf16[960,1024]{1,0:T(8,128)(2,1)} %get-tuple-element.180.a_ref.refs_0_, bf16[1024,4096]{1,0:T(8,128)(2,1)} %get-tuple-element.186.w_ref, f32[1,4096]{1,0:T(1,128)} %bitcast.114), custom_call_target="tpu_custom_call" | custom-call | tf_op jit(solution)/shard_map/pallas_call | solution.py:561
  183.4 14.3 %shard_map.260 = (bf16[4,4,512,256]{3,2,1,0:T(8,128)(2,1)}, bf16[4,4,512,256]{3,2,1,0:T(8,128)(2,1)}) custom-call(s32[3]{0:T(128)} %copy-done.20, bf16[960,4096]{1,0:T(8,128)(2,1)} %get-tuple-element.263.left_ref.h_ref, bf16[960,1024]{1,0:T(8,128)(2,1)} %bitcast.97), custom_call_target="tpu_custom_call" | custom-call | tf_op jit(solution)/shard_map/pallas_call | solution.py:250
  197.8 6.8 %shard_map.261.w_ref = bf16[4096,1024]{1,0:T(8,128)(2,1)} custom-call(s32[3]{0:T(128)S(1)} %copy-done.21, bf16[512,1024]{1,0:T(8,128)(2,1)} %refs_0_.3, bf16[3,512,256]{2,1,0:T(8,128)(2,1)S(1)} %pad_maximum_fusion.1.refs_1_, bf16[3,512,256]{2,1,0:T(8,128)(2,1)S(1)} %collective-permute-done.25.refs_2_, ...), custom_call_target="tpu_custom_call" | custom-call | tf_op jit(solution)/shard_map/pallas_call | solution.py:226
  204.7 15.0 %shard_map.262 = (bf16[960,4096]{1,0:T(8,128)(2,1)}, f32[1,4096]{1,0:T(1,128)}) custom-call(bf16[960,1024]{1,0:T(8,128)(2,1)} %bitcast.98, bf16[4096,1024]{1,0:T(8,128)(2,1)} %shard_map.261.w_ref, bf16[960,4096]{1,0:T(8,128)(2,1)} %get-tuple-element.202.slope_ref), custom_call_target="tpu_custom_call" | custom-call | tf_op jit(solution)/shard_map/pallas_call | solution.py:561
  219.7 4.2 shard_map.263
  224.8 13.8 %shard_map.264 = (bf16[4,4,128,1024]{3,2,1,0:T(8,128)(2,1)}, bf16[4,4,128,1024]{3,2,1,0:T(8,128)(2,1)}) custom-call(s32[3]{0:T(128)} %copy-done.20, bf16[960,1024]{1,0:T(8,128)(2,1)} %get-tuple-element.180.a_ref.refs_0_, bf16[960,4096]{1,0:T(8,128)(2,1)} %get-tuple-element.214.refs_1_.du_ref), custom_call_target="tpu_custom_call" | custom-call | tf_op jit(solution)/shard_map/pallas_call | solution.py:250
  239.0 1.3 collective-permute-start.36
  240.3 1.5 collective-permute-start.37
  241.9 17.4 %shard_map.265 = (f32[960,1024]{1,0:T(8,128)}, bf16[960,1024]{1,0:T(8,128)(2,1)}, f32[1,1024]{1,0:T(1,128)}, f32[1,1024]{1,0:T(1,128)}, f32[1,1024]{1,0:T(1,128)}) custom-call(bf16[960,4096]{1,0:T(8,128)(2,1)} %get-tuple-element.214.refs_1_.du_ref, bf16[1024,4096]{1,0:T(8,128)(2,1)} %get-tuple-element.186.w_ref, f32[960,1024]{1,0:T(8,128)} %get-tuple-element.215.y_ref, ...), custom_call_target="tpu_custom_call" | custom-call | tf_op jit(solution)/shard_map/pallas_call | solution.py:561
  259.2 5.0 %collective-permute-done.36.ga_ref = bf16[2,2,512,256]{3,2,1,0:T(8,128)(2,1)S(1)} collective-permute-done((bf16[2,2,512,256]{3,2,1,0:T(8,128)(2,1)S(1)}, bf16[2,2,512,256]{3,2,1,0:T(8,128)(2,1)S(1)}, u32[]{:S(2)}, u32[]{:S(2)}) %collective-permute-start.36) | collective-permute-done | bytes 1048608 | tf_op jit(solution)/shard_map/ppermute | solution.py:149
  265.7 1.6 collective-permute-start.39
  267.9 5.7 %shard_map.267.do_ref = bf16[960,1024]{1,0:T(8,128)(2,1)} custom-call(bf16[960,1024]{1,0:T(8,128)(2,1)} %get-tuple-element.224.d_ref.refs_3_, bf16[1024,1024]{1,0:T(8,128)(2,1)} %get-tuple-element.179.w_ref), custom_call_target="tpu_custom_call" | custom-call | tf_op jit(solution)/shard_map/pallas_call | solution.py:561
  273.6 5.0 %collective-permute-done.39.refs_1_ = bf16[2,512,256]{2,1,0:T(8,128)(2,1)S(1)} collective-permute-done((bf16[2,512,256]{2,1,0:T(8,128)(2,1)S(1)}, bf16[2,512,256]{2,1,0:T(8,128)(2,1)S(1)}, u32[]{:S(2)}, u32[]{:S(2)}) %collective-permute-start.39) | collective-permute-done | bytes 524320 | tf_op jit(solution)/shard_map/ppermute | solution.py:149
  278.6 1.2 collective-permute-done.40.refs_3_
  281.1 2.3 copy-done.4
  283.4 5.7 %shard_map.269 = (bf16[2,2,128,1024]{3,2,1,0:T(8,128)(2,1)S(1)}, bf16[2,2,128,1024]{3,2,1,0:T(8,128)(2,1)}, bf16[2,2,128,1024]{3,2,1,0:T(8,128)(2,1)S(1)}, bf16[2,2,128,1024]{3,2,1,0:T(8,128)(2,1)}) custom-call(s32[3]{0:T(128)S(1)} %copy-done.22, bf16[4,4,128,1024]{3,2,1,0:T(8,128)(2,1)S(1)} %copy-done.4, ...), custom_call_target="tpu_custom_call" | custom-call | tf_op jit(solution)/shard_map/pallas_call | solution.py:337
  291.4 24.0 %shard_map.270.refs_1_.d_ref = bf16[960,3072]{1,0:T(8,128)(2,1)} custom-call(s32[3]{0:T(128)S(1)} %fusion.12.counts_ref, bf16[960,3072]{1,0:T(8,128)(2,1)} %shard_map.255.qkv_ref, bf16[960,1024]{1,0:T(8,128)(2,1)S(1)} %copy-done.3), custom_call_target="tpu_custom_call" | custom-call | tf_op jit(solution)/shard_map/pallas_call | solution.py:85
  316.6 1.9 shard_map.271
  318.6 1.4 collective-permute-start.43
  319.9 1.5 collective-permute-start.44
  321.5 15.2 %shard_map.272 = (bf16[4,4,128,1024]{3,2,1,0:T(8,128)(2,1)}, bf16[4,4,128,1024]{3,2,1,0:T(8,128)(2,1)}) custom-call(s32[3]{0:T(128)} %copy-done.20, bf16[960,1024]{1,0:T(8,128)(2,1)} %add_convert_fusion.a_ref.refs_0_, bf16[960,3072]{1,0:T(8,128)(2,1)} %shard_map.270.refs_1_.d_ref, bf16[960,1024]{1,0:T(8,128)(2,1)} %copy-done.2, ...), custom_call_target="tpu_custom_call" | custom-call | tf_op jit(solution)/shard_map/pallas_call | solution.py:250
  338.6 6.8 %collective-permute-done.45.far_ref = bf16[4,4,128,1024]{3,2,1,0:T(8,128)(2,1)} collective-permute-done((bf16[4,4,128,1024]{3,2,1,0:T(8,128)(2,1)}, bf16[4,4,128,1024]{3,2,1,0:T(8,128)(2,1)}, u32[]{:S(2)}, u32[]{:S(2)}) %collective-permute-start.45) | collective-permute-done | bytes 4194336 | tf_op jit(solution)/shard_map/ppermute | solution.py:149
  345.4 2.2 copy-done.5
  347.6 5.5 %shard_map.274 = (bf16[2,2,128,1024]{3,2,1,0:T(8,128)(2,1)S(1)}, bf16[2,2,128,1024]{3,2,1,0:T(8,128)(2,1)}, bf16[2,2,128,1024]{3,2,1,0:T(8,128)(2,1)S(1)}, bf16[2,2,128,1024]{3,2,1,0:T(8,128)(2,1)}) custom-call(s32[3]{0:T(128)S(1)} %copy-done.23, bf16[4,4,128,1024]{3,2,1,0:T(8,128)(2,1)S(1)} %copy-done.5, ...), custom_call_target="tpu_custom_call" | custom-call | tf_op jit(solution)/shard_map/pallas_call | solution.py:337
  354.3 2.1 convert_reduce_fusion.1
  356.4 14.8 %shard_map.275 = (bf16[960,1024]{1,0:T(8,128)(2,1)}, f32[1,1024]{1,0:T(1,128)}, f32[1,1024]{1,0:T(1,128)}, f32[1,3072]{1,0:T(1,128)}) custom-call(bf16[960,3072]{1,0:T(8,128)(2,1)} %shard_map.270.refs_1_.d_ref, bf16[1024,3072]{1,0:T(8,128)(2,1)} %shard_map.254.w_ref, bf16[960,1024]{1,0:T(8,128)(2,1)} %bitcast.96, f32[960,1024]{1,0:T(8,128)} %get-tuple-element.217.dy_ref, ...), custom_call_target="tpu_custom_call" | custom-call | tf_op jit(solution)/shard_map/pallas_call | solution.py:561
  372.4 1.5 shard_map.276
  373.9 10.2 %collective-permute-done.46.ga_ref = bf16[2,2,128,1024]{3,2,1,0:T(8,128)(2,1)S(1)} collective-permute-done((bf16[2,2,128,1024]{3,2,1,0:T(8,128)(2,1)}, bf16[2,2,128,1024]{3,2,1,0:T(8,128)(2,1)S(1)}, u32[]{:S(2)}, u32[]{:S(2)}) %collective-permute-start.46) | collective-permute-done | bytes 1048608 | tf_op jit(solution)/shard_map/ppermute | solution.py:149
  384.4 2.6 shard_map.277
  390.7 14.2 %shard_map.278 = bf16[960,1024]{1,0:T(8,128)(2,1)} custom-call(bf16[960,4096]{1,0:T(8,128)(2,1)} %get-tuple-element.263.left_ref.h_ref, bf16[4096,1024]{1,0:T(8,128)(2,1)} %shard_map.261.w_ref, f32[960,1024]{1,0:T(8,128)} %get-tuple-element.215.y_ref, f32[1,1024]{1,0:T(1,128)} %bitcast.121), custom_call_target="tpu_custom_call" | custom-call | tf_op jit(solution)/shard_map/pallas_call | solution.py:561
  407.5 1.9 collective-permute-start.53
  409.4 7.8 %collective-permute-done.51 = bf16[144,1024]{1,0:T(8,128)(2,1)S(1)} collective-permute-done((bf16[144,1024]{1,0:T(8,128)(2,1)S(1)}, bf16[144,1024]{1,0:T(8,128)(2,1)S(1)}, u32[]{:S(2)}, u32[]{:S(2)}) %collective-permute-start.51) | collective-permute-done | bytes 294944 | tf_op jit(solution)/shard_map/ppermute | solution.py:149
  417.3 16.0 %collective-permute-done.52 = bf16[144,1024]{1,0:T(8,128)(2,1)S(1)} collective-permute-done((bf16[144,1024]{1,0:T(8,128)(2,1)S(1)}, bf16[144,1024]{1,0:T(8,128)(2,1)S(1)}, u32[]{:S(2)}, u32[]{:S(2)}) %collective-permute-start.52) | collective-permute-done | bytes 294944 | tf_op jit(solution)/shard_map/ppermute | solution.py:149
  434.3 1.3 collective-permute-start.55
  435.6 1.4 collective-permute-start.56
  437.0 6.4 %collective-permute-done.54.refs_1_ = bf16[144,1024]{1,0:T(8,128)(2,1)S(1)} collective-permute-done((bf16[144,1024]{1,0:T(8,128)(2,1)S(1)}, bf16[144,1024]{1,0:T(8,128)(2,1)S(1)}, u32[]{:S(2)}, u32[]{:S(2)}) %collective-permute-start.54) | collective-permute-done | bytes 294944 | tf_op jit(solution)/shard_map/ppermute | solution.py:149
  443.4 4.3 collective-permute-done.55.refs_2_
  447.8 1.7 collective-permute-done.56.refs_3_
  449.5 2.0 shard_map.280
  454.4 1.5 shard_map.281
  (227 shorter events, 56.0 us)
Async XLA Ops:
  7.2 102.6 %copy-start = (s32[3,4]{1,0:T(4,128)S(1)}, s32[3,4]{1,0:T(4,128)}, u32[]{:S(2)}) copy-start(s32[3,4]{1,0:T(4,128)} %param.16) | copy-start | bytes 148
  7.2 61.7 %all-gather.9.cloned.1.call-start = ((), (), s32[]{:S(2)}) async-start(), calls=%async_computation.4 | async-start | bytes 1843200 | tf_op jit(solution)/shard_map/all_gather | solution.py:514
  11.8 98.2 %all-gather.11.cloned.1.call-start = ((), (), s32[]{:S(2)}) async-start(), calls=%async_computation.5 | async-start | bytes 1310720 | tf_op jit(solution)/shard_map/all_gather | solution.py:514
  11.8 16.7 %collective-permute-start = (bf16[128,768]{1,0:T(8,128)(2,1)S(1)}, bf16[128,768]{1,0:T(8,128)(2,1)S(1)}, u32[]{:S(2)}, u32[]{:S(2)}) collective-permute-start(bf16[128,768]{1,0:T(8,128)(2,1)S(1)} %constant_dynamic-slice_fusion.9), channel_id=1, source_target_pairs={{0,8},{1,9},{2,10},{3,11},{4,12},{5,13},{6,14},{7,15},{8,16},{9,17... | collective-permute-start | bytes 589832 | tf_op jit(solution)/shard_map/ppermute | solution.py:149
  13.4 30.6 %collective-permute-start.1 = (bf16[128,768]{1,0:T(8,128)(2,1)S(1)}, bf16[128,768]{1,0:T(8,128)(2,1)S(1)}, u32[]{:S(2)}, u32[]{:S(2)}) collective-permute-start(bf16[128,768]{1,0:T(8,128)(2,1)S(1)} %constant_dynamic-slice_fusion.9), channel_id=1, source_target_pairs={{0,16},{1,17},{2,18},{3,19},{4,20},{5,21},{6,22},{7,23},{8,24},{9,... | collective-permute-start | bytes 589832 | tf_op jit(solution)/shard_map/ppermute | solution.py:149
  14.5 34.5 %collective-permute-start.2 = (bf16[128,768]{1,0:T(8,128)(2,1)S(1)}, bf16[128,768]{1,0:T(8,128)(2,1)S(1)}, u32[]{:S(2)}, u32[]{:S(2)}) collective-permute-start(bf16[128,768]{1,0:T(8,128)(2,1)S(1)} %constant_dynamic-slice_fusion.9), channel_id=1, source_target_pairs={{0,24},{1,25},{2,26},{3,27},{4,28},{5,29},{6,30},{7,31},{8,0},{9,1... | collective-permute-start | bytes 589832 | tf_op jit(solution)/shard_map/ppermute | solution.py:149
  49.1 15.2 %collective-permute-start.3 = (bf16[3,128,768]{2,1,0:T(8,128)(2,1)S(1)}, bf16[3,128,768]{2,1,0:T(8,128)(2,1)}, u32[]{:S(2)}, u32[]{:S(2)}) collective-permute-start(bf16[3,128,768]{2,1,0:T(8,128)(2,1)S(1)} %pad_maximum_fusion.2.refs_1_), channel_id=1, source_target_pairs={{0,1},{1,0},{2,3},{3,2},{4,5},{5,4},{6,7},{7,6},{8,9},{9,8},{10,11... | collective-permute-start | bytes 1769480 | tf_op jit(solution)/shard_map/ppermute | solution.py:149
  50.5 14.8 %collective-permute-start.4 = (bf16[3,128,768]{2,1,0:T(8,128)(2,1)S(1)}, bf16[3,128,768]{2,1,0:T(8,128)(2,1)S(1)}, u32[]{:S(2)}, u32[]{:S(2)}) collective-permute-start(bf16[3,128,768]{2,1,0:T(8,128)(2,1)S(1)} %pad_maximum_fusion.2.refs_1_), channel_id=1, source_target_pairs={{0,2},{1,3},{2,0},{3,1},{4,6},{5,7},{6,4},{7,5},{8,10},{9,11},{10,... | collective-permute-start | bytes 1769480 | tf_op jit(solution)/shard_map/ppermute | solution.py:149
  53.7 261.7 %reduce-scatter.3.cloned.1.call-start = ((), (), s32[]{:S(2)}) async-start(), calls=%async_computation.2 | async-start | bytes 1310720 | tf_op jit(solution)/shard_map/reduce_scatter | solution.py:436
  54.0 18.7 %collective-permute-start.9 = (bf16[3,128,768]{2,1,0:T(8,128)(2,1)S(1)}, bf16[3,128,768]{2,1,0:T(8,128)(2,1)S(1)}, u32[]{:S(2)}, u32[]{:S(2)}) collective-permute-start(bf16[3,128,768]{2,1,0:T(8,128)(2,1)S(1)} %pad_maximum_fusion.2.refs_1_), channel_id=1, source_target_pairs={{0,4},{1,5},{2,6},{3,7},{4,0},{5,1},{6,2},{7,3},{8,12},{9,13},{10,... | collective-permute-start | bytes 1769480 | tf_op jit(solution)/shard_map/ppermute | solution.py:149
  54.0 31.1 %collective-permute-start.8 = (bf16[128,3072]{1,0:T(8,128)(2,1)}, bf16[128,3072]{1,0:T(8,128)(2,1)}, u32[]{:S(2)}, u32[]{:S(2)}) collective-permute-start(bf16[128,3072]{1,0:T(8,128)(2,1)} %refs_0_.1), channel_id=1, source_target_pairs={{0,4},{1,5},{2,6},{3,7},{4,0},{5,1},{6,2},{7,3},{8,12},{9,13},{10,... | collective-permute-start | bytes 2359304 | tf_op jit(solution)/shard_map/ppermute | solution.py:149
  66.4 19.2 %collective-permute-start.10 = (bf16[3,128,768]{2,1,0:T(8,128)(2,1)}, bf16[3,128,768]{2,1,0:T(8,128)(2,1)}, u32[]{:S(2)}, u32[]{:S(2)}) collective-permute-start(bf16[3,128,768]{2,1,0:T(8,128)(2,1)} %collective-permute-done.3.refs_2_), channel_id=1, source_target_pairs={{0,4},{1,5},{2,6},{3,7},{4,0},{5,1},{6,2},{7,3},{8,12},{9,13},{10,... | collective-permute-start | bytes 1769480 | tf_op jit(solution)/shard_map/ppermute | solution.py:149
  66.5 9.5 %collective-permute-start.6 = (bf16[3,64,768]{2,1,0:T(8,128)(2,1)S(1)}, bf16[3,64,768]{2,1,0:T(8,128)(2,1)}, u32[]{:S(2)}, u32[]{:S(2)}) collective-permute-start(bf16[3,64,768]{2,1,0:T(8,128)(2,1)S(1)} %slice.102), channel_id=1, source_target_pairs={{0,2},{1,3},{2,0},{3,1},{4,6},{5,7},{6,4},{7,5},{8,10},{9,11},{10,... | collective-permute-start | bytes 884744 | tf_op jit(solution)/shard_map/ppermute | solution.py:149
  69.7 1.6 collective-permute-start.5
  71.3 10.2 %collective-permute-start.7 = (bf16[3,64,768]{2,1,0:T(8,128)(2,1)}, bf16[3,64,768]{2,1,0:T(8,128)(2,1)}, u32[]{:S(2)}, u32[]{:S(2)}) collective-permute-start(bf16[3,64,768]{2,1,0:T(8,128)(2,1)} %slice.103), channel_id=1, source_target_pairs={{0,1},{1,0},{2,3},{3,2},{4,5},{5,4},{6,7},{7,6},{8,9},{9,8},{10,11... | collective-permute-start | bytes 884744 | tf_op jit(solution)/shard_map/ppermute | solution.py:149
  73.5 33.0 %collective-permute-start.14 = (bf16[3,128,1280]{2,1,0:T(8,128)(2,1)S(1)}, bf16[3,128,1280]{2,1,0:T(8,128)(2,1)S(1)}, u32[]{:S(2)}, u32[]{:S(2)}) collective-permute-start(bf16[3,128,1280]{2,1,0:T(8,128)(2,1)S(1)} %pad_maximum_fusion.refs_2_), channel_id=1, source_target_pairs={{0,1},{1,0},{2,3},{3,2},{4,5},{5,4},{6,7},{7,6},{8,9},{9,8},{10,11... | collective-permute-start | bytes 2949128 | tf_op jit(solution)/shard_map/ppermute | solution.py:149
  76.1 30.4 %collective-permute-start.15 = (bf16[3,128,1280]{2,1,0:T(8,128)(2,1)S(1)}, bf16[3,128,1280]{2,1,0:T(8,128)(2,1)S(1)}, u32[]{:S(2)}, u32[]{:S(2)}) collective-permute-start(bf16[3,128,1280]{2,1,0:T(8,128)(2,1)S(1)} %pad_maximum_fusion.refs_2_), channel_id=1, source_target_pairs={{0,2},{1,3},{2,0},{3,1},{4,6},{5,7},{6,4},{7,5},{8,10},{9,11},{10,... | collective-permute-start | bytes 2949128 | tf_op jit(solution)/shard_map/ppermute | solution.py:149
  81.6 4.8 %collective-permute-start.11 = (bf16[3,128,768]{2,1,0:T(8,128)(2,1)}, bf16[3,128,768]{2,1,0:T(8,128)(2,1)S(1)}, u32[]{:S(2)}, u32[]{:S(2)}) collective-permute-start(bf16[3,128,768]{2,1,0:T(8,128)(2,1)} %copy-done.7), channel_id=1, source_target_pairs={{0,4},{1,5},{2,6},{3,7},{4,0},{5,1},{6,2},{7,3},{8,12},{9,13},{10,... | collective-permute-start | bytes 1769480 | tf_op jit(solution)/shard_map/ppermute | solution.py:149
  85.2 1.9 collective-permute-start.12
  85.7 1.8 collective-permute-start.13
  107.3 13.7 %collective-permute-start.16 = (bf16[3,64,1280]{2,1,0:T(8,128)(2,1)}, bf16[3,64,1280]{2,1,0:T(8,128)(2,1)S(1)}, u32[]{:S(2)}, u32[]{:S(2)}) collective-permute-start(bf16[3,64,1280]{2,1,0:T(8,128)(2,1)} %slice.112), channel_id=1, source_target_pairs={{0,2},{1,3},{2,0},{3,1},{4,6},{5,7},{6,4},{7,5},{8,10},{9,11},{10,... | collective-permute-start | bytes 1474568 | tf_op jit(solution)/shard_map/ppermute | solution.py:149
  107.7 29.5 %collective-permute-start.18 = (bf16[128,4096]{1,0:T(8,128)(2,1)}, bf16[128,4096]{1,0:T(8,128)(2,1)}, u32[]{:S(2)}, u32[]{:S(2)}) collective-permute-start(bf16[128,4096]{1,0:T(8,128)(2,1)} %refs_0_.2), channel_id=1, source_target_pairs={{0,4},{1,5},{2,6},{3,7},{4,0},{5,1},{6,2},{7,3},{8,12},{9,13},{10,... | collective-permute-start | bytes 3145736 | tf_op jit(solution)/shard_map/ppermute | solution.py:149
  107.9 28.9 %collective-permute-start.20 = (bf16[3,128,1280]{2,1,0:T(8,128)(2,1)S(1)}, bf16[3,128,1280]{2,1,0:T(8,128)(2,1)}, u32[]{:S(2)}, u32[]{:S(2)}) collective-permute-start(bf16[3,128,1280]{2,1,0:T(8,128)(2,1)S(1)} %pad_maximum_fusion.refs_2_), channel_id=1, source_target_pairs={{0,4},{1,5},{2,6},{3,7},{4,0},{5,1},{6,2},{7,3},{8,12},{9,13},{10,... | collective-permute-start | bytes 2949128 | tf_op jit(solution)/shard_map/ppermute | solution.py:149
  109.0 27.1 %collective-permute-start.17 = (bf16[3,64,1280]{2,1,0:T(8,128)(2,1)}, bf16[3,64,1280]{2,1,0:T(8,128)(2,1)}, u32[]{:S(2)}, u32[]{:S(2)}) collective-permute-start(bf16[3,64,1280]{2,1,0:T(8,128)(2,1)} %slice.113), channel_id=1, source_target_pairs={{0,1},{1,0},{2,3},{3,2},{4,5},{5,4},{6,7},{7,6},{8,9},{9,8},{10,11... | collective-permute-start | bytes 1474568 | tf_op jit(solution)/shard_map/ppermute | solution.py:149
  109.8 31.3 %collective-permute-start.21 = (bf16[3,128,1280]{2,1,0:T(8,128)(2,1)S(1)}, bf16[3,128,1280]{2,1,0:T(8,128)(2,1)}, u32[]{:S(2)}, u32[]{:S(2)}) collective-permute-start(bf16[3,128,1280]{2,1,0:T(8,128)(2,1)S(1)} %collective-permute-done.14.refs_3_), channel_id=1, source_target_pairs={{0,4},{1,5},{2,6},{3,7},{4,0},{5,1},{6,2},{7,3},{8,12},{9,13},{10,... | collective-permute-start | bytes 2949128 | tf_op jit(solution)/shard_map/ppermute | solution.py:149
  121.0 15.7 %collective-permute-start.19 = (bf16[128,1024]{1,0:T(8,128)(2,1)}, bf16[128,1024]{1,0:T(8,128)(2,1)S(1)}, u32[]{:S(2)}, u32[]{:S(2)}) collective-permute-start(bf16[128,1024]{1,0:T(8,128)(2,1)} %refs_1_), channel_id=1, source_target_pairs={{0,4},{1,5},{2,6},{3,7},{4,0},{5,1},{6,2},{7,3},{8,12},{9,13},{10,... | collective-permute-start | bytes 786440 | tf_op jit(solution)/shard_map/ppermute | solution.py:149
  136.2 2.0 collective-permute-start.23
  136.7 3.8 collective-permute-start.24
  136.8 23.6 %collective-permute-start.27 = (bf16[512,1024]{1,0:T(8,128)(2,1)}, bf16[512,1024]{1,0:T(8,128)(2,1)}, u32[]{:S(2)}, u32[]{:S(2)}) collective-permute-start(bf16[512,1024]{1,0:T(8,128)(2,1)} %refs_0_.3), channel_id=1, source_target_pairs={{0,4},{1,5},{2,6},{3,7},{4,0},{5,1},{6,2},{7,3},{8,12},{9,13},{10,... | collective-permute-start | bytes 3145736 | tf_op jit(solution)/shard_map/ppermute | solution.py:149
  137.2 4.5 collective-permute-start.22
  138.2 19.8 %collective-permute-start.25 = (bf16[3,512,256]{2,1,0:T(8,128)(2,1)S(1)}, bf16[3,512,256]{2,1,0:T(8,128)(2,1)S(1)}, u32[]{:S(2)}, u32[]{:S(2)}) collective-permute-start(bf16[3,512,256]{2,1,0:T(8,128)(2,1)S(1)} %pad_maximum_fusion.1.refs_1_), channel_id=1, source_target_pairs={{0,1},{1,0},{2,3},{3,2},{4,5},{5,4},{6,7},{7,6},{8,9},{9,8},{10,11... | collective-permute-start | bytes 2359304 | tf_op jit(solution)/shard_map/ppermute | solution.py:149
  140.5 19.8 %collective-permute-start.26 = (bf16[3,512,256]{2,1,0:T(8,128)(2,1)S(1)}, bf16[3,512,256]{2,1,0:T(8,128)(2,1)S(1)}, u32[]{:S(2)}, u32[]{:S(2)}) collective-permute-start(bf16[3,512,256]{2,1,0:T(8,128)(2,1)S(1)} %pad_maximum_fusion.1.refs_1_), channel_id=1, source_target_pairs={{0,2},{1,3},{2,0},{3,1},{4,6},{5,7},{6,4},{7,5},{8,10},{9,11},{10,... | collective-permute-start | bytes 2359304 | tf_op jit(solution)/shard_map/ppermute | solution.py:149
  141.0 19.3 %collective-permute-start.28 = (bf16[3,512,256]{2,1,0:T(8,128)(2,1)S(1)}, bf16[3,512,256]{2,1,0:T(8,128)(2,1)}, u32[]{:S(2)}, u32[]{:S(2)}) collective-permute-start(bf16[3,512,256]{2,1,0:T(8,128)(2,1)S(1)} %pad_maximum_fusion.1.refs_1_), channel_id=1, source_target_pairs={{0,4},{1,5},{2,6},{3,7},{4,0},{5,1},{6,2},{7,3},{8,12},{9,13},{10,... | collective-permute-start | bytes 2359304 | tf_op jit(solution)/shard_map/ppermute | solution.py:149
  160.3 22.5 %collective-permute-start.29 = (bf16[3,512,256]{2,1,0:T(8,128)(2,1)S(1)}, bf16[3,512,256]{2,1,0:T(8,128)(2,1)S(1)}, u32[]{:S(2)}, u32[]{:S(2)}) collective-permute-start(bf16[3,512,256]{2,1,0:T(8,128)(2,1)S(1)} %collective-permute-done.25.refs_2_), channel_id=1, source_target_pairs={{0,4},{1,5},{2,6},{3,7},{4,0},{5,1},{6,2},{7,3},{8,12},{9,13},{10,... | collective-permute-start | bytes 2359304 | tf_op jit(solution)/shard_map/ppermute | solution.py:149
  160.4 22.5 %collective-permute-start.30 = (bf16[3,512,256]{2,1,0:T(8,128)(2,1)S(1)}, bf16[3,512,256]{2,1,0:T(8,128)(2,1)S(1)}, u32[]{:S(2)}, u32[]{:S(2)}) collective-permute-start(bf16[3,512,256]{2,1,0:T(8,128)(2,1)S(1)} %collective-permute-done.26.refs_3_), channel_id=1, source_target_pairs={{0,4},{1,5},{2,6},{3,7},{4,0},{5,1},{6,2},{7,3},{8,12},{9,13},{10,... | collective-permute-start | bytes 2359304 | tf_op jit(solution)/shard_map/ppermute | solution.py:149
  160.9 21.9 %collective-permute-start.31 = (bf16[3,256,256]{2,1,0:T(8,128)(2,1)S(1)}, bf16[3,256,256]{2,1,0:T(8,128)(2,1)S(1)}, u32[]{:S(2)}, u32[]{:S(2)}) collective-permute-start(bf16[3,256,256]{2,1,0:T(8,128)(2,1)S(1)} %slice.118), channel_id=1, source_target_pairs={{0,2},{1,3},{2,0},{3,1},{4,6},{5,7},{6,4},{7,5},{8,10},{9,11},{10,... | collective-permute-start | bytes 1179656 | tf_op jit(solution)/shard_map/ppermute | solution.py:149
  161.5 21.3 %collective-permute-start.32 = (bf16[3,256,256]{2,1,0:T(8,128)(2,1)S(1)}, bf16[3,256,256]{2,1,0:T(8,128)(2,1)S(1)}, u32[]{:S(2)}, u32[]{:S(2)}) collective-permute-start(bf16[3,256,256]{2,1,0:T(8,128)(2,1)S(1)} %slice.119), channel_id=1, source_target_pairs={{0,1},{1,0},{2,3},{3,2},{4,5},{5,4},{6,7},{7,6},{8,9},{9,8},{10,11... | collective-permute-start | bytes 1179656 | tf_op jit(solution)/shard_map/ppermute | solution.py:149
  182.8 14.9 %collective-permute-start.33 = (bf16[3,256,256]{2,1,0:T(8,128)(2,1)S(1)}, bf16[3,256,256]{2,1,0:T(8,128)(2,1)S(1)}, u32[]{:S(2)}, u32[]{:S(2)}) collective-permute-start(bf16[3,256,256]{2,1,0:T(8,128)(2,1)S(1)} %collective-permute-done.31.refs_4_), channel_id=1, source_target_pairs={{0,4},{1,5},{2,6},{3,7},{4,0},{5,1},{6,2},{7,3},{8,12},{9,13},{10,... | collective-permute-start | bytes 1179656 | tf_op jit(solution)/shard_map/ppermute | solution.py:149
  182.9 14.8 %collective-permute-start.34 = (bf16[3,256,256]{2,1,0:T(8,128)(2,1)S(1)}, bf16[3,256,256]{2,1,0:T(8,128)(2,1)S(1)}, u32[]{:S(2)}, u32[]{:S(2)}) collective-permute-start(bf16[3,256,256]{2,1,0:T(8,128)(2,1)S(1)} %collective-permute-done.32.refs_5_), channel_id=1, source_target_pairs={{0,4},{1,5},{2,6},{3,7},{4,0},{5,1},{6,2},{7,3},{8,12},{9,13},{10,... | collective-permute-start | bytes 1179656 | tf_op jit(solution)/shard_map/ppermute | solution.py:149
  197.7 22.0 %collective-permute-start.35 = (bf16[4,4,512,256]{3,2,1,0:T(8,128)(2,1)}, bf16[4,4,512,256]{3,2,1,0:T(8,128)(2,1)}, u32[]{:S(2)}, u32[]{:S(2)}) collective-permute-start(bf16[4,4,512,256]{3,2,1,0:T(8,128)(2,1)} %get-tuple-element.205), channel_id=1, source_target_pairs={{0,4},{1,5},{2,6},{3,7},{4,0},{5,1},{6,2},{7,3},{8,12},{9,13},{10,... | collective-permute-start | bytes 12582920 | tf_op jit(solution)/shard_map/ppermute | solution.py:149
  238.6 42.5 %collective-permute-start.38 = (bf16[4,4,128,1024]{3,2,1,0:T(8,128)(2,1)}, bf16[4,4,128,1024]{3,2,1,0:T(8,128)(2,1)}, u32[]{:S(2)}, u32[]{:S(2)}) collective-permute-start(bf16[4,4,128,1024]{3,2,1,0:T(8,128)(2,1)} %get-tuple-element.225), channel_id=1, source_target_pairs={{0,4},{1,5},{2,6},{3,7},{4,0},{5,1},{6,2},{7,3},{8,12},{9,13},{10,... | collective-permute-start | bytes 12582920 | tf_op jit(solution)/shard_map/ppermute | solution.py:149
  239.0 25.2 %collective-permute-start.36 = (bf16[2,2,512,256]{3,2,1,0:T(8,128)(2,1)S(1)}, bf16[2,2,512,256]{3,2,1,0:T(8,128)(2,1)S(1)}, u32[]{:S(2)}, u32[]{:S(2)}) collective-permute-start(bf16[2,2,512,256]{3,2,1,0:T(8,128)(2,1)S(1)} %copy-done.25), channel_id=1, source_target_pairs={{0,1},{1,0},{2,3},{3,2},{4,5},{5,4},{6,7},{7,6},{8,9},{9,8},{10,11... | collective-permute-start | bytes 3145736 | tf_op jit(solution)/shard_map/ppermute | solution.py:149
  240.3 24.9 %collective-permute-start.37 = (bf16[2,2,512,256]{3,2,1,0:T(8,128)(2,1)S(1)}, bf16[2,2,512,256]{3,2,1,0:T(8,128)(2,1)S(1)}, u32[]{:S(2)}, u32[]{:S(2)}) collective-permute-start(bf16[2,2,512,256]{3,2,1,0:T(8,128)(2,1)S(1)} %get-tuple-element.211), channel_id=1, source_target_pairs={{0,2},{1,3},{2,0},{3,1},{4,6},{5,7},{6,4},{7,5},{8,10},{9,11},{10,... | collective-permute-start | bytes 3145736 | tf_op jit(solution)/shard_map/ppermute | solution.py:149
  265.7 12.8 %collective-permute-start.39 = (bf16[2,512,256]{2,1,0:T(8,128)(2,1)S(1)}, bf16[2,512,256]{2,1,0:T(8,128)(2,1)S(1)}, u32[]{:S(2)}, u32[]{:S(2)}) collective-permute-start(bf16[2,512,256]{2,1,0:T(8,128)(2,1)S(1)} %get-tuple-element.221), channel_id=1, source_target_pairs={{0,2},{1,3},{2,0},{3,1},{4,6},{5,7},{6,4},{7,5},{8,10},{9,11},{10,... | collective-permute-start | bytes 1572872 | tf_op jit(solution)/shard_map/ppermute | solution.py:149
  267.3 12.5 %collective-permute-start.40 = (bf16[2,512,256]{2,1,0:T(8,128)(2,1)S(1)}, bf16[2,512,256]{2,1,0:T(8,128)(2,1)S(1)}, u32[]{:S(2)}, u32[]{:S(2)}) collective-permute-start(bf16[2,512,256]{2,1,0:T(8,128)(2,1)S(1)} %get-tuple-element.223), channel_id=1, source_target_pairs={{0,1},{1,0},{2,3},{3,2},{4,5},{5,4},{6,7},{7,6},{8,9},{9,8},{10,11... | collective-permute-start | bytes 1572872 | tf_op jit(solution)/shard_map/ppermute | solution.py:149
  281.1 90.1 %all-gather.13.cloned.1.call-start = ((), (), s32[]{:S(2)}) async-start(), calls=%async_computation.6 | async-start | bytes 1310720 | tf_op jit(solution)/shard_map/all_gather | solution.py:442
  290.2 25.2 %collective-permute-start.41 = (bf16[2,2,128,1024]{3,2,1,0:T(8,128)(2,1)}, bf16[2,2,128,1024]{3,2,1,0:T(8,128)(2,1)}, u32[]{:S(2)}, u32[]{:S(2)}) collective-permute-start(bf16[2,2,128,1024]{3,2,1,0:T(8,128)(2,1)} %get-tuple-element.231), channel_id=1, source_target_pairs={{0,1},{1,0},{2,3},{3,2},{4,5},{5,4},{6,7},{7,6},{8,9},{9,8},{10,11... | collective-permute-start | bytes 3145736 | tf_op jit(solution)/shard_map/ppermute | solution.py:149
  290.7 24.7 %collective-permute-start.42 = (bf16[2,2,128,1024]{3,2,1,0:T(8,128)(2,1)}, bf16[2,2,128,1024]{3,2,1,0:T(8,128)(2,1)}, u32[]{:S(2)}, u32[]{:S(2)}) collective-permute-start(bf16[2,2,128,1024]{3,2,1,0:T(8,128)(2,1)} %get-tuple-element.233), channel_id=1, source_target_pairs={{0,2},{1,3},{2,0},{3,1},{4,6},{5,7},{6,4},{7,5},{8,10},{9,11},{10,... | collective-permute-start | bytes 3145736 | tf_op jit(solution)/shard_map/ppermute | solution.py:149
  318.6 18.1 %collective-permute-start.43 = (bf16[2,128,1024]{2,1,0:T(8,128)(2,1)S(1)}, bf16[2,128,1024]{2,1,0:T(8,128)(2,1)S(1)}, u32[]{:S(2)}, u32[]{:S(2)}) collective-permute-start(bf16[2,128,1024]{2,1,0:T(8,128)(2,1)S(1)} %get-tuple-element.239), channel_id=1, source_target_pairs={{0,2},{1,3},{2,0},{3,1},{4,6},{5,7},{6,4},{7,5},{8,10},{9,11},{10,... | collective-permute-start | bytes 1572872 | tf_op jit(solution)/shard_map/ppermute | solution.py:149
  319.9 16.8 %collective-permute-start.44 = (bf16[2,128,1024]{2,1,0:T(8,128)(2,1)S(1)}, bf16[2,128,1024]{2,1,0:T(8,128)(2,1)S(1)}, u32[]{:S(2)}, u32[]{:S(2)}) collective-permute-start(bf16[2,128,1024]{2,1,0:T(8,128)(2,1)S(1)} %get-tuple-element.241), channel_id=1, source_target_pairs={{0,1},{1,0},{2,3},{3,2},{4,5},{5,4},{6,7},{7,6},{8,9},{9,8},{10,11... | collective-permute-start | bytes 1572872 | tf_op jit(solution)/shard_map/ppermute | solution.py:149
  337.9 7.5 %collective-permute-start.45 = (bf16[4,4,128,1024]{3,2,1,0:T(8,128)(2,1)}, bf16[4,4,128,1024]{3,2,1,0:T(8,128)(2,1)}, u32[]{:S(2)}, u32[]{:S(2)}) collective-permute-start(bf16[4,4,128,1024]{3,2,1,0:T(8,128)(2,1)} %get-tuple-element.247), channel_id=1, source_target_pairs={{0,4},{1,5},{2,6},{3,7},{4,0},{5,1},{6,2},{7,3},{8,12},{9,13},{10,... | collective-permute-start | bytes 12582920 | tf_op jit(solution)/shard_map/ppermute | solution.py:149
  338.0 67.0 %reduce-scatter.5.cloned.1.call-start = ((), (), s32[]{:S(2)}) async-start(), calls=%async_computation.3 | async-start | bytes 1310720 | tf_op jit(solution)/shard_map/reduce_scatter | solution.py:436
  338.5 114.7 %all-gather.15.cloned.1.call-start = ((), (), s32[]{:S(2)}) async-start(), calls=%async_computation.7 | async-start | bytes 1310720 | tf_op jit(solution)/shard_map/all_gather | solution.py:442
  353.1 31.0 %collective-permute-start.46 = (bf16[2,2,128,1024]{3,2,1,0:T(8,128)(2,1)}, bf16[2,2,128,1024]{3,2,1,0:T(8,128)(2,1)S(1)}, u32[]{:S(2)}, u32[]{:S(2)}) collective-permute-start(bf16[2,2,128,1024]{3,2,1,0:T(8,128)(2,1)} %get-tuple-element.251), channel_id=1, source_target_pairs={{0,1},{1,0},{2,3},{3,2},{4,5},{5,4},{6,7},{7,6},{8,9},{9,8},{10,11... | collective-permute-start | bytes 3145736 | tf_op jit(solution)/shard_map/ppermute | solution.py:149
  353.6 30.9 %collective-permute-start.47 = (bf16[2,2,128,1024]{3,2,1,0:T(8,128)(2,1)}, bf16[2,2,128,1024]{3,2,1,0:T(8,128)(2,1)}, u32[]{:S(2)}, u32[]{:S(2)}) collective-permute-start(bf16[2,2,128,1024]{3,2,1,0:T(8,128)(2,1)} %get-tuple-element.252), channel_id=1, source_target_pairs={{0,2},{1,3},{2,0},{3,1},{4,6},{5,7},{6,4},{7,5},{8,10},{9,11},{10,... | collective-permute-start | bytes 3145736 | tf_op jit(solution)/shard_map/ppermute | solution.py:149
  388.7 17.8 %collective-permute-start.48 = (bf16[2,128,1024]{2,1,0:T(8,128)(2,1)}, bf16[2,128,1024]{2,1,0:T(8,128)(2,1)S(1)}, u32[]{:S(2)}, u32[]{:S(2)}) collective-permute-start(bf16[2,128,1024]{2,1,0:T(8,128)(2,1)} %get-tuple-element.260), channel_id=1, source_target_pairs={{0,2},{1,3},{2,0},{3,1},{4,6},{5,7},{6,4},{7,5},{8,10},{9,11},{10,... | collective-permute-start | bytes 1572872 | tf_op jit(solution)/shard_map/ppermute | solution.py:149
  389.4 17.0 %collective-permute-start.49 = (bf16[2,128,1024]{2,1,0:T(8,128)(2,1)}, bf16[2,128,1024]{2,1,0:T(8,128)(2,1)S(1)}, u32[]{:S(2)}, u32[]{:S(2)}) collective-permute-start(bf16[2,128,1024]{2,1,0:T(8,128)(2,1)} %get-tuple-element.262), channel_id=1, source_target_pairs={{0,1},{1,0},{2,3},{3,2},{4,5},{5,4},{6,7},{7,6},{8,9},{9,8},{10,11... | collective-permute-start | bytes 1572872 | tf_op jit(solution)/shard_map/ppermute | solution.py:149
  405.1 1.3 collective-permute-start.50
  407.4 9.9 %collective-permute-start.51 = (bf16[144,1024]{1,0:T(8,128)(2,1)S(1)}, bf16[144,1024]{1,0:T(8,128)(2,1)S(1)}, u32[]{:S(2)}, u32[]{:S(2)}) collective-permute-start(bf16[144,1024]{1,0:T(8,128)(2,1)S(1)} %get-tuple-element.274), channel_id=1, source_target_pairs={{0,8},{1,9},{2,10},{3,11},{4,12},{5,13},{6,14},{7,15},{8,16},{9,17... | collective-permute-start | bytes 884744 | tf_op jit(solution)/shard_map/ppermute | solution.py:149
  407.4 25.8 %collective-permute-start.52 = (bf16[144,1024]{1,0:T(8,128)(2,1)S(1)}, bf16[144,1024]{1,0:T(8,128)(2,1)S(1)}, u32[]{:S(2)}, u32[]{:S(2)}) collective-permute-start(bf16[144,1024]{1,0:T(8,128)(2,1)S(1)} %get-tuple-element.275), channel_id=1, source_target_pairs={{0,16},{1,17},{2,18},{3,19},{4,20},{5,21},{6,22},{7,23},{8,24},{9,... | collective-permute-start | bytes 884744 | tf_op jit(solution)/shard_map/ppermute | solution.py:149
  407.5 25.7 %collective-permute-start.53 = (bf16[144,1024]{1,0:T(8,128)(2,1)S(1)}, bf16[144,1024]{1,0:T(8,128)(2,1)S(1)}, u32[]{:S(2)}, u32[]{:S(2)}) collective-permute-start(bf16[144,1024]{1,0:T(8,128)(2,1)S(1)} %get-tuple-element.276), channel_id=1, source_target_pairs={{0,24},{1,25},{2,26},{3,27},{4,28},{5,29},{6,30},{7,31},{8,0},{9,1... | collective-permute-start | bytes 884744 | tf_op jit(solution)/shard_map/ppermute | solution.py:149
  433.5 10.0 %collective-permute-start.54 = (bf16[144,1024]{1,0:T(8,128)(2,1)S(1)}, bf16[144,1024]{1,0:T(8,128)(2,1)S(1)}, u32[]{:S(2)}, u32[]{:S(2)}) collective-permute-start(bf16[144,1024]{1,0:T(8,128)(2,1)S(1)} %add_convert_fusion.1.refs_0_), channel_id=1, source_target_pairs={{0,1},{1,0},{2,3},{3,2},{4,5},{5,4},{6,7},{7,6},{8,9},{9,8},{10,11... | collective-permute-start | bytes 884744 | tf_op jit(solution)/shard_map/ppermute | solution.py:149
  434.3 13.4 %collective-permute-start.55 = (bf16[144,1024]{1,0:T(8,128)(2,1)S(1)}, bf16[144,1024]{1,0:T(8,128)(2,1)S(1)}, u32[]{:S(2)}, u32[]{:S(2)}) collective-permute-start(bf16[144,1024]{1,0:T(8,128)(2,1)S(1)} %add_convert_fusion.1.refs_0_), channel_id=1, source_target_pairs={{0,2},{1,3},{2,0},{3,1},{4,6},{5,7},{6,4},{7,5},{8,10},{9,11},{10,... | collective-permute-start | bytes 884744 | tf_op jit(solution)/shard_map/ppermute | solution.py:149
  435.6 13.8 %collective-permute-start.56 = (bf16[144,1024]{1,0:T(8,128)(2,1)S(1)}, bf16[144,1024]{1,0:T(8,128)(2,1)S(1)}, u32[]{:S(2)}, u32[]{:S(2)}) collective-permute-start(bf16[144,1024]{1,0:T(8,128)(2,1)S(1)} %add_convert_fusion.1.refs_0_), channel_id=1, source_target_pairs={{0,3},{1,2},{2,1},{3,0},{4,7},{5,6},{6,5},{7,4},{8,11},{9,10},{10,... | collective-permute-start | bytes 884744 | tf_op jit(solution)/shard_map/ppermute | solution.py:149
  (36 other events, 454.5 us)
Sparse Core Ops, SparseCore 0:
  11.9 44.5 all-gather.8
  58.6 27.6 all-gather.10
  281.2 22.4 reduce-scatter.2
  338.1 30.2 all-gather.12
  371.2 25.1 reduce-scatter.4
  405.1 24.9 all-gather.14

commit v3 on v2

--- a/solution.py
+++ b/solution.py
@@ -234,7 +234,7 @@
             pltpu.SemaphoreType.DMA((total,)),
             pltpu.SemaphoreType.DMA((total,)),
         ],
-        compiler_params=pltpu.CompilerParams(vmem_limit_bytes=48 * 2**20),
+        compiler_params=pltpu.CompilerParams(vmem_limit_bytes=58 * 2**20),
     )(where, *flat)
 
 
@@ -246,50 +246,47 @@
         yield n, jnp.where(first, low, high), jnp.where(first, high, low)
 
 
-def wgrad_call(kernel, where, grid, specs, out, shape, arrays):
+def wgrad_call(kernel, where, grid, specs, outs, shapes, arrays):
     return pl.pallas_call(
         kernel,
         grid_spec=pltpu.PrefetchScalarGridSpec(
-            num_scalar_prefetch=1, grid=grid, in_specs=specs, out_specs=[out, out]
+            num_scalar_prefetch=1, grid=grid, in_specs=specs, out_specs=outs
         ),
-        out_shape=[jax.ShapeDtypeStruct(shape, BF)] * 2,
+        out_shape=[jax.ShapeDtypeStruct(shape, BF) for shape in shapes],
         compiler_params=pltpu.CompilerParams(vmem_limit_bytes=56 * 2**20),
     )(where, *arrays)
 
 
-def wgrad_units(where, left, right, extra=None):
+def wgrad_units(where, left, right, extra=()):
     rows, width = left.shape
     shards = lax.axis_size("fsdp")
-    depth, wide = width // shards, right.shape[1] // (3 if extra else 4)
+    planes, depth, wide = shards // 2, width // shards, right.shape[1] // 4
+    count = 2 + len(extra)
 
     def kernel(place_ref, *refs):
-        mine_ref, far_ref = refs[-2:]
-
-        def store(left_ref, right_ref):
-            total = tn(left_ref[...], right_ref[...])
-            for n, mine, far in halves(place_ref, total, depth):
-                mine_ref[n] = mine
-                far_ref[n] = far
-
+        ins, outs = refs[:count], refs[count:]
+        for n, mine, far in halves(place_ref, tn(ins[0][...], ins[1][...]), depth):
+            outs[0][n] = mine
+            outs[1][n] = far
         if extra:
-            pl.when(pl.program_id(0) < 3)(lambda: store(refs[0], refs[1]))
-            pl.when(pl.program_id(0) == 3)(lambda: store(refs[2], refs[3]))
-        else:
-            store(refs[0], refs[1])
-
-    one = pl.Buffered(1)
-    arrays = [left, right]
-    specs = [
-        pl.BlockSpec((rows, width), lambda j, c: (0, 0), pipeline_mode=one),
-        pl.BlockSpec((rows, wide), lambda j, c: (0, jnp.minimum(j, 2) if extra else j)),
-    ]
+
+            @pl.when(pl.program_id(0) == 0)
+            def _():
+                part = width // 4
+                for n, mine, far in halves(place_ref, tn(ins[2][...], ins[3][...]), depth):
+                    for j in range(4):
+                        outs[2][j, n] = mine[:, j * part : (j + 1) * part]
+                        outs[3][j, n] = far[:, j * part : (j + 1) * part]
+
+    one = pl.BlockSpec((rows, width), lambda j, c: (0, 0), pipeline_mode=pl.Buffered(1))
+    specs = [one, pl.BlockSpec((rows, wide), lambda j, c: (0, j))] + [one] * len(extra)
+    outs = [pl.BlockSpec((None, planes, depth, wide), lambda j, c: (j, 0, 0, 0))] * 2
+    shapes = [(4, planes, depth, wide)] * 2
     if extra:
-        arrays += list(extra)
-        specs.append(pl.BlockSpec((rows, width), lambda j, c: (0, 0), pipeline_mode=one))
-        specs.append(pl.BlockSpec((rows, wide), lambda j, c: (0, 0), pipeline_mode=one))
-    out = pl.BlockSpec((None, shards // 2, depth, wide), lambda j, c: (j, 0, 0, 0))
-    shape = (4, shards // 2, depth, wide)
-    return wgrad_call(kernel, where, (4,), specs, out, shape, arrays)
+        shape = (4, planes, depth, width // 4)
+        outs += [pl.BlockSpec(shape, lambda j, c: (0, 0, 0, 0), pipeline_mode=pl.Buffered(1))] * 2
+        shapes += [shape] * 2
+    return wgrad_call(kernel, where, (4,), specs, outs, shapes, (left, right, *extra))
 
 
 def wgrad_planes(where, left, right):
@@ -298,8 +295,7 @@
     depth, wide = left.shape[1] // (2 * planes), width // 4
 
     def kernel(place_ref, left_ref, right_ref, mine_ref, far_ref):
-        total = tn(left_ref[...], right_ref[...])
-        for _, mine, far in halves(place_ref, total, depth):
+        for _, mine, far in halves(place_ref, tn(left_ref[...], right_ref[...]), depth):
             for j in range(4):
                 mine_ref[j] = mine[:, j * wide : (j + 1) * wide]
                 far_ref[j] = far[:, j * wide : (j + 1) * wide]
@@ -310,7 +306,7 @@
     ]
     out = pl.BlockSpec((4, None, depth, wide), lambda z, c: (0, z, 0, 0))
     shape = (4, planes, depth, wide)
-    return wgrad_call(kernel, where, (planes,), specs, out, shape, (left, right))
+    return wgrad_call(kernel, where, (planes,), specs, [out] * 2, [shape] * 2, (left, right))
 
 
 def add(*parts):
@@ -321,30 +317,38 @@
 
 
 def chip_sum(where, mine, far):
-    planes, depth, wide = mine.shape[1:]
+    planes, depth = mine[0].shape[1:3]
+    wides = [part.shape[3] for part in mine]
     half = planes // 2
 
-    def kernel(place_ref, mine_ref, far_ref, *outs):
+    def kernel(place_ref, *refs):
+        ins, outs = refs[: 2 * len(wides)], refs[2 * len(wides) :]
         for flip, (first, second) in enumerate(((0, 2), (1, 2), (0, 3), (1, 3))):
 
             @pl.when(pl.program_id(0) == flip)
             def _():
-                total = add(mine_ref[...], far_ref[...])
-                outs[first][flip // 2] = total[:half]
-                outs[second][flip % 2] = total[half:]
-
-    piece = (2, half, depth, wide)
+                for n, wide in enumerate(wides):
+                    columns = pl.ds(sum(wides[:n]), wide)
+                    total = add(ins[n][...], ins[len(wides) + n][...])
+                    outs[first][flip // 2, :, :, columns] = total[:half]
+                    outs[second][flip % 2, :, :, columns] = total[half:]
+
+    piece = (2, half, depth, sum(wides))
     return pl.pallas_call(
         kernel,
         grid_spec=pltpu.PrefetchScalarGridSpec(
             num_scalar_prefetch=1,
             grid=(4,),
-            in_specs=[pl.BlockSpec((None, planes, depth, wide), lambda f, c: (c[2] ^ f, 0, 0, 0))] * 2,
+            in_specs=[
+                pl.BlockSpec((None, planes, depth, wide), lambda f, c: (c[2] ^ f, 0, 0, 0))
+                for wide in wides
+            ]
+            * 2,
             out_specs=[pl.BlockSpec(piece, lambda f, c: (0, 0, 0, 0))] * 4,
         ),
         out_shape=[jax.ShapeDtypeStruct(piece, BF)] * 4,
-        compiler_params=pltpu.CompilerParams(vmem_limit_bytes=32 * 2**20),
-    )(where, mine, far)
+        compiler_params=pltpu.CompilerParams(vmem_limit_bytes=40 * 2**20),
+    )(where, *mine, *far)
 
 
 def sides(chip):
@@ -442,18 +446,20 @@
     return lax.all_gather(share, "seq", axis=0, tiled=False)
 
 
-def joined(units):
-    count, depth, wide = units.shape
-
-    def kernel(in_ref, out_ref):
-        for j in range(count):
-            out_ref[:, pl.ds(j * wide, wide)] = in_ref[j].astype(F32)
+def joined(units, widths):
+    count, depth, _ = units.shape
+
+    def kernel(in_ref, *outs):
+        for n, (wide, out_ref) in enumerate(zip(widths, outs)):
+            for j in range(count):
+                value = in_ref[j, :, pl.ds(sum(widths[:n]), wide)].astype(F32)
+                out_ref[:, pl.ds(j * wide, wide)] = value
 
     return pl.pallas_call(
         kernel,
         in_specs=[pl.BlockSpec(memory_space=pltpu.VMEM)],
-        out_specs=pl.BlockSpec(memory_space=pltpu.VMEM),
-        out_shape=jax.ShapeDtypeStruct((depth, count * wide), F32),
+        out_specs=[pl.BlockSpec(memory_space=pltpu.VMEM)] * len(widths),
+        out_shape=[jax.ShapeDtypeStruct((depth, count * wide), F32) for wide in widths],
         compiler_params=pltpu.CompilerParams(vmem_limit_bytes=24 * 2**20),
     )(units)
 
@@ -462,38 +468,29 @@
     return [total] + over_plane(total)
 
 
-def spread(where, parts, shapes, more=0):
-    wide = parts[0].shape[1]
-    depth = shapes[0][0]
+def spread(where, parts, widths, more=0):
+    depth = parts[0].shape[0] - (16 if more else 0)
 
     def kernel(place_ref, *refs):
         ins, outs = refs[: len(parts)], refs[len(parts) :]
         me = place_ref[2]
         for spot, ref in zip([me, me + 1 - 2 * (me % 2), (me + 2) % 4, 3 - me], ins):
-            value = ref[pl.ds(0, depth), :].astype(F32)
-            column = pl.ds(pl.multiple_of(spot * wide, wide), wide)
-            if len(shapes) == 1:
-                outs[0][:, column] = value
-            else:
-
-                @pl.when(spot < 3)
-                def _():
-                    outs[0][:, column] = value
-
-                @pl.when(spot == 3)
-                def _():
-                    outs[1][...] = value
-
+            for n, wide in enumerate(widths):
+                column = pl.ds(pl.multiple_of(spot * wide, wide), wide)
+                value = ref[pl.ds(0, depth), pl.ds(sum(widths[:n]), wide)]
+                outs[n][:, column] = value.astype(F32)
         if more:
             rows = [ref[pl.ds(depth, 16), :].astype(F32) for ref in ins]
             outs[-1][...] = (rows[0] + rows[1] + rows[2] + rows[3])[:more]
 
-    out = [jax.ShapeDtypeStruct(shape, F32) for shape in shapes]
+    shapes = [struct(depth, 4 * wide, dtype=F32) for wide in widths]
+    if more:
+        shapes.append(struct(more, parts[0].shape[1], dtype=F32))
     return pl.pallas_call(
         kernel,
         in_specs=[pl.BlockSpec(memory_space=pltpu.SMEM)]
         + [pl.BlockSpec(memory_space=pltpu.VMEM)] * len(parts),
-        out_shape=out + ([jax.ShapeDtypeStruct((more, wide), F32)] if more else []),
+        out_shape=shapes,
         compiler_params=pltpu.CompilerParams(vmem_limit_bytes=24 * 2**20),
     )(where, *parts)
 
@@ -523,9 +520,13 @@
     )
 
 
-def across(along_x, along_y):
-    half = along_x.shape[1] // 2
-    return [send(along_x[:, :half], 0, 0, 2), send(along_y[:, half:], 0, 0, 1)]
+def edges(two):
+    half = two[0].shape[1] // 2
+    return [two[0][:, :half], two[1][:, half:]]
+
+
+def across(parts):
+    return [send(parts[0], 0, 0, 2), send(parts[1], 0, 0, 1)]
 
 
 def plain_sum(left, right):
@@ -557,7 +558,7 @@
     return hid, half + hid * (1.0 - t) * (c + (3 * 0.044715 * c) * square)
 
 
-def call(kernel, grid, in_specs, out_specs, out_shape, scratch, args):
+def call(kernel, grid, in_specs, out_specs, out_shape, scratch, args, room=56):
     return pl.pallas_call(
         kernel,
         grid=grid,
@@ -565,7 +566,7 @@
         out_specs=out_specs,
         out_shape=out_shape,
         scratch_shapes=scratch,
-        compiler_params=pltpu.CompilerParams(vmem_limit_bytes=56 * 2**20),
+        compiler_params=pltpu.CompilerParams(vmem_limit_bytes=room * 2**20),
     )(*args)
 
 
@@ -647,26 +648,6 @@
     )
 
 
-def back_down(g, w, slope):
-    rows, wide = slope.shape
-
-    def kernel(g_ref, w_ref, slope_ref, du_ref, sum_ref):
-        du = (nt(g_ref[...], w_ref[...]) * slope_ref[...].astype(F32)).astype(BF)
-        du_ref[...] = du
-        sum_ref[...] = jnp.sum(du.astype(F32), axis=0, keepdims=True)
-
-    tile = columns_of(rows, TILE)
-    return call(
-        kernel,
-        (wide // TILE,),
-        [whole(g), rows_of(TILE, w.shape[1]), tile],
-        [tile, columns_of(1, TILE)],
-        [struct(rows, wide), struct(1, wide, dtype=F32)],
-        [],
-        (g, w, slope),
-    )
-
-
 def back_norm(total, values, gain):
     unit, inverse = normal(values)
     sums = (
@@ -688,13 +669,45 @@
             ref[...] += value
 
 
-def back_up(du, w, y1, g, gain):
-    rows, wide = du.shape
+def back_ffn(g, w_down, slope, w_up, y1, gain):
+    rows, wide = slope.shape
     width = y1.shape[1]
-    height = rows // HEIGHTS
-
-    def kernel(du_ref, w_ref, y_ref, g_ref, gain_ref, dy_ref, d1_ref, s1_ref, s2_ref, s3_ref):
-        back, sums = back_norm(nt(du_ref[...], w_ref[...]), y_ref[...], gain_ref[...])
+    height, part = rows // HEIGHTS, wide // 4
+
+    def kernel(g_ref, down_ref, slope_ref, up_ref, y_ref, gain_ref, *refs):
+        du_ref, sum_ref, dy_ref, d1_ref, s1_ref, s2_ref, s3_ref, down, up, sems = refs
+        first = pl.program_id(0) == 0
+
+        def bring(n):
+            at = pl.ds(n * part, part)
+            return (
+                pltpu.make_async_copy(down_ref.at[at, :], down.at[at, :], sems.at[2 * n]),
+                pltpu.make_async_copy(up_ref.at[:, at], up.at[:, at], sems.at[2 * n + 1]),
+            )
+
+        @pl.when(first)
+        def _():
+            sum_ref[...] = jnp.zeros_like(sum_ref)
+            for n in range(4):
+                for copy in bring(n):
+                    copy.start()
+
+        total = None
+        for n in range(4):
+            at = pl.ds(n * part, part)
+
+            @pl.when(first)
+            def _():
+                for copy in bring(n):
+                    copy.wait()
+
+            dh = nt(g_ref[...], down[at, :])
+            du = (dh * slope_ref[:, at].astype(F32)).astype(BF)
+            du_ref[:, at] = du
+            sum_ref[:, at] += jnp.sum(du.astype(F32), axis=0, keepdims=True)
+            more = nt(du, up[:, at])
+            total = more if total is None else total + more
+        back, sums = back_norm(total, y_ref[...], gain_ref[...])
         dy = g_ref[...].astype(F32) + back
         dy_ref[...] = dy
         d1 = dy.astype(BF)
@@ -702,16 +715,30 @@
         sums += (jnp.sum(d1.astype(F32), axis=0, keepdims=True),)
         gather_sums((s1_ref, s2_ref, s3_ref), sums)
 
-    row, tile = pl.BlockSpec((1, width), lambda i: (0, 0)), rows_of(height, width)
+    tile, long = rows_of(height, width), rows_of(height, wide)
+    row = pl.BlockSpec((1, width), lambda i: (0, 0))
+    far = pl.BlockSpec(memory_space=pl.ANY)
     vector = struct(1, width, dtype=F32)
     return call(
         kernel,
         (rows // height,),
-        [rows_of(height, wide), whole(w), tile, tile, whole(gain[None])],
-        [tile, tile, row, row, row],
-        [struct(rows, width, dtype=F32), struct(rows, width), vector, vector, vector],
-        [],
-        (du, w, y1, g, gain[None]),
+        [tile, far, long, far, tile, whole(gain[None])],
+        [long, pl.BlockSpec((1, wide), lambda i: (0, 0)), tile, tile, row, row, row],
+        [
+            struct(rows, wide),
+            struct(1, wide, dtype=F32),
+            struct(rows, width, dtype=F32),
+            struct(rows, width),
+            vector,
+            vector,
+            vector,
+        ],
+        [
+            pltpu.VMEM(w_down.shape, BF),
+            pltpu.VMEM(w_up.shape, BF),
+            pltpu.SemaphoreType.DMA((8,)),
+        ],
+        (g, w_down, slope, w_up, y1, gain[None]),
     )
 
 
@@ -723,9 +750,9 @@
 
     return call(
         kernel,
-        (width // TILE,),
-        [whole(d1), rows_of(TILE, width)],
-        columns_of(rows, TILE),
+        (width // 512,),
+        [whole(d1), rows_of(512, width)],
+        columns_of(rows, 512),
         struct(rows, width),
         [],
         (d1, w),
@@ -844,24 +871,24 @@
     depth = w_qkv.shape[0]
     first = unit(w_qkv)
     z_first = along_z(first)
-    w_up, w_out, w_down, vectors = after((w_up, w_out, w_down, vectors), first)
     packed = jnp.pad(packed_rows(vectors), ((0, 4), (0, 0))).reshape(2, width)
     packed = jnp.pad(packed, ((0, 14), (0, width // 4)))
-    z_second = column(
-        jnp.concatenate([jnp.concatenate([unit(w_up), unit(w_out)], axis=1), packed])
-    )
+    packed = jnp.concatenate([jnp.concatenate([unit(w_up), unit(w_out)], axis=1), packed])
+    z_second = column(after(packed, z_first))
     z_third = column(unit(w_down))
     unit1, _ = normal(x)
     sum_down = jnp.sum(g_low.astype(F32), axis=0)
 
-    col_first = jnp.stack(after(z_first, unit1))
+    far_own = to_partner(after([w_qkv, w_out], unit1))
+    col_first = jnp.stack(after(z_first, far_own))
+    far_own = far_own + to_partner(after([w_up, w_down], col_first))
     two_first = [send(col_first, 0, 0, flip) for flip in (1, 2)]
-    far_own_first = to_partner(after([w_qkv, w_out], col_first))
     far_first = to_partner([col_first])
-    two_first = after(two_first, unit1)
-    cross_first = across(*two_first)
-    far_first += to_partner(two_first)
-    z_second = after(z_second, two_first)
+    two_first, far_own, far_first = after((two_first, far_own, far_first), col_first)
+    edges_first = edges(two_first)
+    cross_first = across(edges_first)
+    far_first = far_first + to_partner(two_first)
+    z_second = after(z_second, edges_first)
     small = complete(small_table(where, z_second[:, depth : depth + 2, :width], vectors), width)
     gain1, shift1, bias_qkv, bias_out, gain2, shift2, bias_up, bias_down = small
     a1 = (unit1 * gain1 + shift1).astype(BF)
@@ -869,79 +896,78 @@
     two_second = [send(col_second, 0, 0, flip) for flip in (1, 2)]
     cross_first = after(cross_first, col_second, a1)
     near_first = [col_first] + two_first + cross_first
-    far_first += to_partner(cross_first)
+    far_first = far_first + to_partner(cross_first)
     (qkv_w,) = assemble(
         where,
-        [[w_qkv], far_own_first[:1]],
+        [[w_qkv], far_own[:1]],
         [near_first, far_first],
         [(width, 3 * width)],
     )
+    far_second = to_partner(after([col_second], qkv_w))
     qkv = project(a1, qkv_w, bias_qkv)
-    two_second = after(two_second, qkv)
-    cross_second = across(*two_second)
-    col_third = others(where, after(z_third, two_second), w_down.shape[0])
-    two_third = [send(col_third, 0, 0, flip) for flip in (1, 2)]
-    far_own_second = to_partner(after([w_up], qkv_w)) + far_own_first[1:]
-    far_second = to_partner(after([col_second], qkv_w)) + to_partner(two_second)
-    o = per_image(attention_forward, live, slots, [after(qkv, col_third)], width)
-    cross_second = after(cross_second, o)
+    two_second, far_second = after((two_second, far_second), qkv)
+    cross_second = across(edges(two_second))
+    far_second = far_second + to_partner(two_second)
+    o = per_image(attention_forward, live, slots, [after(qkv, two_second, sum_down)], width)
+    cross_second, far_second = after((cross_second, far_second), o)
     near_second = [col_second] + two_second + cross_second
-    far_second += to_partner(cross_second)
+    far_second = far_second + to_partner(cross_second)
     up_w, out_w = assemble(
         where,
-        [[w_up, w_out], far_own_second],
+        [[w_up, w_out], [far_own[2], far_own[1]]],
         [near_second, far_second],
         [(width, wide), (width, width)],
     )
     y1, a2 = middle(o, out_w, x_low, bias_out, gain2, shift2)
-    far_own_third = to_partner(after([w_down], cross_second))
-    far_third = to_partner(after([col_third], cross_second))
-    two_third, far_own_third, far_third = after((two_third, far_own_third, far_third), a2)
-    cross_third = across(*two_third)
+    col_third = others(where, after(z_third, up_w), w_down.shape[0])
+    two_third = [send(col_third, 0, 0, flip) for flip in (1, 2)]
+    far_third = to_partner([col_third])
+    hid, slope = expand(after(a2, col_third), up_w, bias_up)
+    two_third, far_third = after((two_third, far_third), hid)
+    edges_third = edges(two_third)
+    cross_third = across(edges_third)
     far_third = far_third + to_partner(two_third)
-    hid, slope = expand(a2, after(up_w, two_third), bias_up)
-    far_third, cross_third = after((far_third, cross_third), hid)
+
+    mine_down, far_down = wgrad_planes(where, after(hid, edges_third), g_low)
+    cross_third, far_third = after((cross_third, far_third), mine_down)
     near_third = [col_third] + two_third + cross_third
     far_third = far_third + to_partner(cross_third)
-
-    mine_down, far_down = wgrad_planes(where, after(hid, far_third[:3]), g_low)
-    far_third = after(far_third, mine_down)
     got_down = send(after(far_down, far_third), 0, 1, 0)
     (down_w,) = assemble(
         where,
-        [[w_down], far_own_third],
+        [[w_down], far_own[3:]],
         [near_third, far_third],
         [(wide, width)],
     )
-    du, sum_up = back_down(g_low, down_w, slope)
-    chip_down = chip_sum(where, *after((mine_down, got_down), du))
+    chip_down = chip_sum(where, *after(([mine_down], [got_down]), down_w))
     sides_down = sides(chip_down)
-    mine_up, far_up = wgrad_units(where, a2, after(du, chip_down))
-    got_up = send(far_up, 0, 1, 0)
-    dy1, d1, sum_gain2, sum_shift2, sum_out = back_up(after(du, mine_up), up_w, y1, g_low, gain2)
+    du, sum_up, dy1, d1, sum_gain2, sum_shift2, sum_out = back_ffn(
+        after(g_low, chip_down), down_w, slope, up_w, y1, gain2
+    )
     side_down = side_sum(chip_down, after(sides_down, dy1))
     ends_down = ends(side_down)
-    do = back_out(after(d1, side_down), out_w)
-    total_down = plane_sum(side_down, after(ends_down, do))
+    up_out = wgrad_units(where, a2, after(du, side_down), (o, d1))
+    mine_up, far_up = up_out[::2], up_out[1::2]
+    total_down = plane_sum(side_down, after(ends_down, mine_up))
+    got_up = to_partner(after(far_up, total_down))
     share_down = column_sum(total_down)
-    chip_up = chip_sum(where, *after((mine_up, got_up), total_down))
+    do = back_out(after(d1, total_down), out_w)
+    chip_up = chip_sum(where, *after((mine_up, got_up), do))
     sides_up = sides(chip_up)
     dqkv = per_image(attention_backward, live, slots, [qkv, after(do, chip_up)], 3 * width)
     share_down = after(share_down, dqkv)
     side_up = side_sum(chip_up, after(sides_up, share_down))
     ends_up = ends(side_up)
-    mine_qkv, far_qkv = wgrad_units(where, a1, after(dqkv, side_up), extra=(o, d1))
+    mine_qkv, far_qkv = wgrad_units(where, a1, after(dqkv, side_up))
     total_up = plane_sum(side_up, after(ends_up, mine_qkv))
     got_qkv = send(after(far_qkv, total_up), 0, 1, 0)
     share_up = column_sum(total_up)
-    from_down = from_plane(share_down)
-    chip_qkv = chip_sum(where, *after((mine_qkv, got_qkv), total_up))
+    chip_qkv = chip_sum(where, *after(([mine_qkv], [got_qkv]), total_up))
     sides_qkv = sides(chip_qkv)
     input_grad, sum_gain1, sum_shift1, sum_qkv = back_qkv(
         after(dqkv, chip_qkv), qkv_w, x_low, dy1, gain1
     )
-    s_down = joined(after(from_down, input_grad))
-    side_qkv = side_sum(chip_qkv, after(sides_qkv, s_down))
+    side_qkv = side_sum(chip_qkv, after(sides_qkv, input_grad))
     ends_qkv = ends(side_qkv)
 
     sum_qv = jnp.concatenate([sum_qkv[0, :width], sum_qkv[0, 2 * width :]])
@@ -957,18 +983,22 @@
     )
     planes = lax.axis_size("fsdp") // 2
     rows = packed_rows([part.reshape(planes, 2, -1) for part in sums])
+    hid = after(hid, rows, side_qkv)
     rows = pick(rows, where[1], 1) + send(pick(rows, 1 - where[1], 1), 0, 1, 0)
-    rows = jnp.pad(rows, ((0, 0), (0, 4), (0, 0))).reshape(planes, 2, width).astype(BF)
+    rows = rows.reshape(planes, 2, -1).astype(BF)
     rows = jnp.pad(rows, ((0, 0), (0, 14), (0, 0)))
 
-    activations = contract(after(hid, side_qkv), down_w, y1, bias_down)
+    activations = contract(hid, down_w, y1, bias_down)
+    from_down = from_plane(after(share_down, chip_qkv))
     column_qkv = column_parts(
         plane_columns(where, side_qkv, after(ends_qkv, activations), rows)
     )
-    from_up = from_plane(after(share_up, activations))
-    share_qkv = add(*after(column_qkv, column_qkv[0]))
-    s_up = joined(after(from_up, share_qkv))
-    s_qkv, s_out, own = spread(where, shares(share_qkv), [w_qkv.shape, w_out.shape], more=2)
+    shares_up = shares(after(share_up, column_qkv[0]))
+    (s_down,) = joined(after(from_down, column_qkv[0]), [width // 4])
+    share_qkv = add(*after(column_qkv, s_down, shares_up))
+    shares_qkv = shares(share_qkv)
+    s_up, s_out = spread(where, after(shares_up, share_qkv), [wide // 4, width // 4])
+    s_qkv, own = spread(where, after(shares_qkv, s_up), [width * 3 // 4], 2)
     own = own.reshape(-1)
     return activations, input_grad, s_qkv, s_out, s_up, s_down, own_parts(own, sums)
 

time: 469 us -> 420 us (0.90)
  waiting for transfers between devices: 131 us -> 76.8 us
  starting transfers between devices: 39.3 us -> 51 us
    ppermute x57 -> x61, waiting for transfers between devices: 131 us -> 71 us  [send(): return lax.ppermute(value, ('fsdp', 'seq'), pairs)]
    ppermute x57 -> x61, starting transfers between devices: 39.1 us -> 50.6 us  [send(): return lax.ppermute(value, ('fsdp', 'seq'), pairs)]
    all_gather x2, waiting for transfers between devices: 0.02 us -> 5.78 us  [column(): lax.all_gather(mine, 'fsdp', axis=0, tiled=False, axis_index_groups=colum...]
    pallas_call x8 -> x7, Pallas kernels: 105 us -> 102 us  [call(): pl.pallas_call(kernel, grid=grid, in_specs=in_specs, out_specs=out_specs,...]
    unnamed x80 -> x97, local copies, waits for them, and re-layouts: 15.5 us -> 13 us
  transfers between devices with their start and end apart: 63 -> 66, of which waited for: 28 -> 27; matrix products, arithmetic and copies ran while one was open for 5% -> 5% of each run, Pallas kernels for 46% -> 53%
where the time goes in v3:
time: 420 us; the launch traced here: 415 us
  Pallas kernels  233 us (55%)
  waiting for transfers between devices  76.8 us (18%)
  starting transfers between devices  51 us (12%)
  local copies, waits for them, and re-layouts  29.9 us (7%)
  between operations  14.8 us (4%)
  other arithmetic  9.17 us (2%)
    pallas_call x7, Pallas kernels, call(): pl.pallas_call(kernel, grid=grid, in_specs=in_specs, out_specs=out_specs,...  102 us
    ppermute x61, waiting for transfers between devices, send(): return lax.ppermute(value, ('fsdp', 'seq'), pairs)  71 us
    ppermute x61, starting transfers between devices, send(): return lax.ppermute(value, ('fsdp', 'seq'), pairs)  50.6 us
    pallas_call x3, Pallas kernels, wgrad_call(): pl.pallas_call(kernel, grid_spec=pltpu.PrefetchScalarGridSpec(num_scalar_...  43.6 us
    pallas_call x2, Pallas kernels, per_image(): pl.pallas_call(kernel, grid_spec=pltpu.PrefetchScalarGridSpec(num_scalar_...  36.6 us
    pallas_call x3, Pallas kernels, assemble(): pl.pallas_call(kernel, in_specs=[pl.BlockSpec(memory_space=pltpu.SMEM)] +...  24.3 us
    pallas_call x3, Pallas kernels, chip_sum(): pl.pallas_call(kernel, grid_spec=pltpu.PrefetchScalarGridSpec(num_scalar_...  15.2 us
    unnamed x97, local copies, waits for them, and re-layouts  13 us
  transfers between devices with their start and end apart: 66, of which 27 were waited for; matrix products, arithmetic and copies ran while one was open for 5% of the time, Pallas kernels for 53%

profile of v3, /device:TPU:8, one launch (start us, length us, event | category | flops | bytes accessed | tf_op | source)
XLA Modules:
  0.0 414.9 jit_solution(1550157138323325528)
XLA Ops:
  8.3 1.6 collective-permute-start
  11.1 1.9 collective-permute-start.2
  16.4 7.3 %collective-permute-done = bf16[128,768]{1,0:T(8,128)(2,1)S(1)} collective-permute-done((bf16[128,768]{1,0:T(8,128)(2,1)S(1)}, bf16[128,768]{1,0:T(8,128)(2,1)S(1)}, u32[]{:S(2)}, u32[]{:S(2)}) %collective-permute-start) | collective-permute-done | bytes 196640 | tf_op jit(solution)/shard_map/ppermute | solution.py:149
  23.7 3.1 collective-permute-done.1
  26.8 1.8 collective-permute-done.2
  29.7 2.4 collective-permute-done.4.refs_8_
  35.0 1.5 collective-permute-start.5
  36.5 1.5 collective-permute-start.6
  38.8 11.7 %collective-permute-done.5.refs_2_ = bf16[3,128,768]{2,1,0:T(8,128)(2,1)} collective-permute-done((bf16[3,128,768]{2,1,0:T(8,128)(2,1)S(1)}, bf16[3,128,768]{2,1,0:T(8,128)(2,1)}, u32[]{:S(2)}, u32[]{:S(2)}) %collective-permute-start.5) | collective-permute-done | bytes 589856 | tf_op jit(solution)/shard_map/ppermute | solution.py:149
  51.7 1.7 slice.99
  53.4 1.7 slice.100
  55.6 1.5 collective-permute-start.11
  57.7 5.8 %all-gather.7.cloned.1.call-done = bf16[576,1280]{1,0:T(8,128)(2,1)} async-done(((bf16[144,1280]{1,0:T(8,128)(2,1)}), bf16[576,1280]{1,0:T(8,128)(2,1)}) %all-gather.7.cloned.1.call-update) | async-done | bytes 1474576 | tf_op jit(solution)/shard_map/all_gather | solution.py:511
  67.1 2.1 add_convert_fusion.a_ref.refs_0_
  70.4 1.5 collective-permute-start.17
  71.8 1.5 collective-permute-start.18
  74.8 6.4 %shard_map.254.w_ref = bf16[1024,3072]{1,0:T(8,128)(2,1)} custom-call(s32[3]{0:T(128)} %pad_add_fusion.1.place_ref, bf16[128,3072]{1,0:T(8,128)(2,1)} %refs_0_.3, bf16[3,128,768]{2,1,0:T(8,128)(2,1)} %copy-done.23, bf16[3,128,768]{2,1,0:T(8,128)(2,1)} %collective-permute-done.5.refs_2_, bf16[3,128,768]{2,1,0:T(8,128)(2,1)} %collective-permute-done.6.refs_3_, ...), custom_call_target="tpu_custom_call" | custom-call | tf_op jit(solution)/shard_map/pallas_call | solution.py:226
  81.3 1.7 constant_dynamic-slice_fusion.3
  83.9 11.0 %shard_map.255.qkv_ref = bf16[960,3072]{1,0:T(8,128)(2,1)} custom-call(bf16[960,1024]{1,0:T(8,128)(2,1)} %add_convert_fusion.a_ref.refs_0_, bf16[1024,3072]{1,0:T(8,128)(2,1)} %shard_map.254.w_ref, f32[1,3072]{1,0:T(1,128)} %bitcast.110), custom_call_target="tpu_custom_call" | custom-call | tf_op jit(solution)/shard_map/pallas_call | solution.py:562
  98.4 1.5 collective-permute-start.20
  101.1 12.6 %shard_map.256.o_ref.refs_2_ = bf16[960,1024]{1,0:T(8,128)(2,1)S(1)} custom-call(s32[3]{0:T(128)S(1)} %fusion.12.counts_ref, bf16[960,3072]{1,0:T(8,128)(2,1)} %shard_map.255.qkv_ref), custom_call_target="tpu_custom_call" | custom-call | tf_op jit(solution)/shard_map/pallas_call | solution.py:85
  115.6 1.6 collective-permute-done.24.refs_12_
  118.7 9.6 %shard_map.257 = (bf16[1024,4096]{1,0:T(8,128)(2,1)}, bf16[1024,1024]{1,0:T(8,128)(2,1)}) custom-call(s32[3]{0:T(128)} %pad_add_fusion.1.place_ref, bf16[128,4096]{1,0:T(8,128)(2,1)} %refs_0_.4, bf16[128,1024]{1,0:T(8,128)(2,1)} %refs_1_.1, bf16[3,128,1280]{2,1,0:T(8,128)(2,1)} %copy-done.21, bf16[3,128,1280]{2,1,0:T(8,128)(2,1)} %collective-permute-done.17.refs_3_, ...), custom_call_target="tpu_custom_call" | custom-call | tf_op jit(solution)/shard_map/pallas_call | solution.py:226
  129.6 1.5 collective-permute-start.26
  132.3 7.2 %shard_map.258 = (f32[960,1024]{1,0:T(8,128)}, bf16[960,1024]{1,0:T(8,128)(2,1)}) custom-call(bf16[960,1024]{1,0:T(8,128)(2,1)} %copy-done.2, bf16[1024,1024]{1,0:T(8,128)(2,1)} %get-tuple-element.184.w_ref, bf16[960,1024]{1,0:T(8,128)(2,1)} %bitcast.92, f32[1,1024]{1,0:T(1,128)} %bitcast.117, f32[1,1024]{1,0:T(1,128)} %bitcast.111, f32[1,1024]{1,0:T(1,128)} %bitcast.116), custom_call_target="tpu_custom_call" | custom-call | tf_op jit(solution)/shard_map/pallas_call | solution.py:562
  139.5 19.4 %shard_map.259 = (bf16[960,4096]{1,0:T(8,128)(2,1)}, bf16[960,4096]{1,0:T(8,128)(2,1)}) custom-call(bf16[960,1024]{1,0:T(8,128)(2,1)} %get-tuple-element.188.a_ref.refs_0_, bf16[1024,4096]{1,0:T(8,128)(2,1)} %get-tuple-element.186.w_ref.up_ref, f32[1,4096]{1,0:T(1,128)} %bitcast.109), custom_call_target="tpu_custom_call" | custom-call | tf_op jit(solution)/shard_map/pallas_call | solution.py:562
  159.7 1.5 collective-permute-start.29
  161.7 14.1 %shard_map.260 = (bf16[4,4,512,256]{3,2,1,0:T(8,128)(2,1)}, bf16[4,4,512,256]{3,2,1,0:T(8,128)(2,1)}) custom-call(s32[3]{0:T(128)} %pad_add_fusion.1.place_ref, bf16[960,4096]{1,0:T(8,128)(2,1)} %get-tuple-element.274.left_ref.h_ref, bf16[960,1024]{1,0:T(8,128)(2,1)} %bitcast.94), custom_call_target="tpu_custom_call" | custom-call | tf_op jit(solution)/shard_map/pallas_call | solution.py:250
  179.4 8.3 %shard_map.261.down_ref.w_ref = bf16[4096,1024]{1,0:T(8,128)(2,1)} custom-call(s32[3]{0:T(128)} %pad_add_fusion.1.place_ref, bf16[512,1024]{1,0:T(8,128)(2,1)} %refs_0_.5, bf16[3,512,256]{2,1,0:T(8,128)(2,1)} %copy-done.22, bf16[3,512,256]{2,1,0:T(8,128)(2,1)} %copy-done.24, bf16[3,512,256]{2,1,0:T(8,128)(2,1)} %copy-done.25, ...), custom_call_target="tpu_custom_call" | custom-call | tf_op jit(solution)/shard_map/pallas_call | solution.py:226
  187.7 4.9 %shard_map.262 = (bf16[2,2,512,256]{3,2,1,0:T(8,128)(2,1)S(1)}, bf16[2,2,512,256]{3,2,1,0:T(8,128)(2,1)}, bf16[2,2,512,256]{3,2,1,0:T(8,128)(2,1)S(1)}, bf16[2,2,512,256]{3,2,1,0:T(8,128)(2,1)S(1)}) custom-call(s32[3]{0:T(128)S(1)} %copy-done.16, bf16[4,4,512,256]{3,2,1,0:T(8,128)(2,1)S(1)} %copy-done.4, bf16[4,4,512,256]{3,2,1,0:T(8,128)(2,1)} %collective-permute-done.35.refs_1_), custom_call_target="tpu_custom_call" | custom-call | tf_op jit(solution)/shard_map/pallas_call | solution.py:337
  192.6 1.5 collective-permute-start.36
  194.7 29.3 %shard_map.263 = (bf16[960,4096]{1,0:T(8,128)(2,1)}, f32[1,4096]{1,0:T(1,128)}, f32[960,1024]{1,0:T(8,128)}, bf16[960,1024]{1,0:T(8,128)(2,1)}, f32[1,1024]{1,0:...) custom-call(bf16[960,1024]{1,0:T(8,128)(2,1)} %bitcast.95, bf16[4096,1024]{1,0:T(8,128)(2,1)} %shard_map.261.down_ref.w_ref, ...), custom_call_target="tpu_custom_call" | custom-call | tf_op jit(solution)/shard_map/pallas_call | solution.py:562
  224.6 1.5 collective-permute-start.38
  226.6 18.0 %shard_map.265 = (bf16[4,4,128,1024]{3,2,1,0:T(8,128)(2,1)}, bf16[4,4,128,1024]{3,2,1,0:T(8,128)(2,1)}, bf16[4,4,128,256]{3,2,1,0:T(8,128)(2,1)}, bf16[4,4,128,256]{3,2,1,0:T(8,128)(2,1)}) custom-call(s32[3]{0:T(128)} %pad_add_fusion.1.place_ref, bf16[960,1024]{1,0:T(8,128)(2,1)} %get-tuple-element.188.a_ref.refs_0_, ...), custom_call_target="tpu_custom_call" | custom-call | tf_op jit(solution)/shard_map/pallas_call | solution.py:250
  246.4 5.6 %shard_map.267.do_ref = bf16[960,1024]{1,0:T(8,128)(2,1)} custom-call(bf16[960,1024]{1,0:T(8,128)(2,1)} %get-tuple-element.226.refs_3_.d_ref, bf16[1024,1024]{1,0:T(8,128)(2,1)} %get-tuple-element.184.w_ref), custom_call_target="tpu_custom_call" | custom-call | tf_op jit(solution)/shard_map/pallas_call | solution.py:562
  252.0 2.3 collective-permute-done.41.refs_3_
  257.8 5.5 %shard_map.268 = (bf16[2,2,128,1280]{3,2,1,0:T(8,128)(2,1)S(1)}, bf16[2,2,128,1280]{3,2,1,0:T(8,128)(2,1)}, bf16[2,2,128,1280]{3,2,1,0:T(8,128)(2,1)S(1)}, bf16[2,2,128,1280]{3,2,1,0:T(8,128)(2,1)}) custom-call(s32[3]{0:T(128)S(1)} %copy-done.17, bf16[4,4,128,1024]{3,2,1,0:T(8,128)(2,1)S(1)} %copy-done.5, bf16[4,4,128,256]{3,2,1,0:T(8,128)(2,1)S(1)} %copy-done.8, ...), custom_call_target="tpu_custom_call" | custom-call | tf_op jit(solution)/shard_map/pallas_call | solution.py:337
  263.3 1.5 collective-permute-start.42
  265.4 24.0 %shard_map.269.refs_1_.d_ref = bf16[960,3072]{1,0:T(8,128)(2,1)} custom-call(s32[3]{0:T(128)S(1)} %fusion.12.counts_ref, bf16[960,3072]{1,0:T(8,128)(2,1)} %shard_map.255.qkv_ref, bf16[960,1024]{1,0:T(8,128)(2,1)S(1)} %copy-done.3), custom_call_target="tpu_custom_call" | custom-call | tf_op jit(solution)/shard_map/pallas_call | solution.py:85
  289.4 5.3 %collective-permute-done.42.ga_ref = bf16[2,2,128,1280]{3,2,1,0:T(8,128)(2,1)} collective-permute-done((bf16[2,2,128,1280]{3,2,1,0:T(8,128)(2,1)}, bf16[2,2,128,1280]{3,2,1,0:T(8,128)(2,1)}, u32[]{:S(2)}, u32[]{:S(2)}) %collective-permute-start.42) | collective-permute-done | bytes 1310752 | tf_op jit(solution)/shard_map/ppermute | solution.py:149
  295.9 2.0 shard_map.270
  299.1 11.5 %shard_map.271 = (bf16[4,4,128,768]{3,2,1,0:T(8,128)(2,1)}, bf16[4,4,128,768]{3,2,1,0:T(8,128)(2,1)}) custom-call(s32[3]{0:T(128)} %pad_add_fusion.1.place_ref, bf16[960,1024]{1,0:T(8,128)(2,1)} %add_convert_fusion.a_ref.refs_0_, bf16[960,3072]{1,0:T(8,128)(2,1)} %shard_map.269.refs_1_.d_ref), custom_call_target="tpu_custom_call" | custom-call | tf_op jit(solution)/shard_map/pallas_call | solution.py:250
  310.6 3.3 collective-permute-done.44.refs_1_
  315.6 5.9 %collective-permute-done.46.refs_1_ = bf16[4,4,128,768]{3,2,1,0:T(8,128)(2,1)} collective-permute-done((bf16[4,4,128,768]{3,2,1,0:T(8,128)(2,1)}, bf16[4,4,128,768]{3,2,1,0:T(8,128)(2,1)}, u32[]{:S(2)}, u32[]{:S(2)}) %collective-permute-start.46) | collective-permute-done | bytes 3145760 | tf_op jit(solution)/shard_map/ppermute | solution.py:149
  321.5 4.8 %shard_map.273 = (bf16[2,2,128,768]{3,2,1,0:T(8,128)(2,1)S(1)}, bf16[2,2,128,768]{3,2,1,0:T(8,128)(2,1)}, bf16[2,2,128,768]{3,2,1,0:T(8,128)(2,1)S(1)}, bf16[2,2,128,768]{3,2,1,0:T(8,128)(2,1)}) custom-call(s32[3]{0:T(128)S(1)} %copy-done.18, bf16[4,4,128,768]{3,2,1,0:T(8,128)(2,1)S(1)} %copy-done.6, bf16[4,4,128,768]{3,2,1,0:T(8,128)(2,1)} %collective-permute-done.46.refs_1_), custom_call_target="tpu_custom_call" | custom-call | tf_op jit(solution)/shard_map/pallas_call | solution.py:337
  328.7 1.4 collective-permute-start.48
  330.3 15.0 %shard_map.274 = (bf16[960,1024]{1,0:T(8,128)(2,1)}, f32[1,1024]{1,0:T(1,128)}, f32[1,1024]{1,0:T(1,128)}, f32[1,3072]{1,0:T(1,128)}) custom-call(bf16[960,3072]{1,0:T(8,128)(2,1)} %shard_map.269.refs_1_.d_ref, bf16[1024,3072]{1,0:T(8,128)(2,1)} %shard_map.254.w_ref, bf16[960,1024]{1,0:T(8,128)(2,1)} %bitcast.93, f32[960,1024]{1,0:T(8,128)} %get-tuple-element.213.dy_ref, ...), custom_call_target="tpu_custom_call" | custom-call | tf_op jit(solution)/shard_map/pallas_call | solution.py:562
  345.9 2.0 collective-permute-done.47.ga_ref
  348.7 1.5 collective-permute-start.49
  350.2 1.4 collective-permute-start.50
  353.7 14.2 %shard_map.276 = bf16[960,1024]{1,0:T(8,128)(2,1)} custom-call(bf16[960,4096]{1,0:T(8,128)(2,1)} %get-tuple-element.274.left_ref.h_ref, bf16[4096,1024]{1,0:T(8,128)(2,1)} %shard_map.261.down_ref.w_ref, f32[960,1024]{1,0:T(8,128)} %get-tuple-element.211.y_ref, f32[1,1024]{1,0:T(1,128)} %bitcast.113), custom_call_target="tpu_custom_call" | custom-call | tf_op jit(solution)/shard_map/pallas_call | solution.py:562
  368.8 1.4 collective-permute-start.52
  371.5 2.2 collective-permute-start.57
  373.6 2.4 collective-permute-start.53
  377.1 3.2 collective-permute-start.54
  381.6 1.5 shard_map.278
  383.0 6.4 %collective-permute-done.53 = bf16[144,768]{1,0:T(8,128)(2,1)S(1)} collective-permute-done((bf16[144,768]{1,0:T(8,128)(2,1)S(1)}, bf16[144,768]{1,0:T(8,128)(2,1)S(1)}, u32[]{:S(2)}, u32[]{:S(2)}) %collective-permute-start.53) | collective-permute-done | bytes 221216 | tf_op jit(solution)/shard_map/ppermute | solution.py:149
  389.4 2.9 collective-permute-done.54
  393.8 2.1 collective-permute-start.60
  396.0 2.2 shard_map.279
  398.1 2.6 collective-permute-done.58.refs_1_
  400.8 2.3 collective-permute-done.59.refs_2_
  403.1 1.5 collective-permute-done.60.refs_3_
  404.6 1.8 shard_map.280
  (248 shorter events, 60.2 us)
Async XLA Ops:
  7.2 56.2 %all-gather.7.cloned.1.call-start = ((), (), s32[]{:S(2)}) async-start(), calls=%async_computation.4 | async-start | bytes 1843200 | tf_op jit(solution)/shard_map/all_gather | solution.py:511
  8.3 15.4 %collective-permute-start = (bf16[128,768]{1,0:T(8,128)(2,1)S(1)}, bf16[128,768]{1,0:T(8,128)(2,1)S(1)}, u32[]{:S(2)}, u32[]{:S(2)}) collective-permute-start(bf16[128,768]{1,0:T(8,128)(2,1)S(1)} %constant_dynamic-slice_fusion.7), channel_id=1, source_target_pairs={{0,8},{1,9},{2,10},{3,11},{4,12},{5,13},{6,14},{7,15},{8,16},{9,17... | collective-permute-start | bytes 589832 | tf_op jit(solution)/shard_map/ppermute | solution.py:149
  10.0 16.8 %collective-permute-start.1 = (bf16[128,768]{1,0:T(8,128)(2,1)S(1)}, bf16[128,768]{1,0:T(8,128)(2,1)S(1)}, u32[]{:S(2)}, u32[]{:S(2)}) collective-permute-start(bf16[128,768]{1,0:T(8,128)(2,1)S(1)} %constant_dynamic-slice_fusion.7), channel_id=1, source_target_pairs={{0,16},{1,17},{2,18},{3,19},{4,20},{5,21},{6,22},{7,23},{8,24},{9,... | collective-permute-start | bytes 589832 | tf_op jit(solution)/shard_map/ppermute | solution.py:149
  11.1 17.5 %collective-permute-start.2 = (bf16[128,768]{1,0:T(8,128)(2,1)S(1)}, bf16[128,768]{1,0:T(8,128)(2,1)S(1)}, u32[]{:S(2)}, u32[]{:S(2)}) collective-permute-start(bf16[128,768]{1,0:T(8,128)(2,1)S(1)} %constant_dynamic-slice_fusion.7), channel_id=1, source_target_pairs={{0,24},{1,25},{2,26},{3,27},{4,28},{5,29},{6,30},{7,31},{8,0},{9,1... | collective-permute-start | bytes 589832 | tf_op jit(solution)/shard_map/ppermute | solution.py:149
  29.2 99.1 %all-gather.9.cloned.1.call-start = ((), (), s32[]{:S(2)}) async-start(), calls=%async_computation.5 | async-start | bytes 1310720 | tf_op jit(solution)/shard_map/all_gather | solution.py:511
  29.2 2.9 collective-permute-start.3
  29.2 2.9 collective-permute-start.4
  34.0 17.7 %collective-permute-start.7 = (bf16[128,4096]{1,0:T(8,128)(2,1)}, bf16[128,4096]{1,0:T(8,128)(2,1)}, u32[]{:S(2)}, u32[]{:S(2)}) collective-permute-start(bf16[128,4096]{1,0:T(8,128)(2,1)} %refs_0_.4), channel_id=1, source_target_pairs={{0,4},{1,5},{2,6},{3,7},{4,0},{5,1},{6,2},{7,3},{8,12},{9,13},{10,... | collective-permute-start | bytes 3145736 | tf_op jit(solution)/shard_map/ppermute | solution.py:149
  34.2 17.5 %collective-permute-start.8 = (bf16[512,1024]{1,0:T(8,128)(2,1)}, bf16[512,1024]{1,0:T(8,128)(2,1)}, u32[]{:S(2)}, u32[]{:S(2)}) collective-permute-start(bf16[512,1024]{1,0:T(8,128)(2,1)} %refs_0_.5), channel_id=1, source_target_pairs={{0,4},{1,5},{2,6},{3,7},{4,0},{5,1},{6,2},{7,3},{8,12},{9,13},{10,... | collective-permute-start | bytes 3145736 | tf_op jit(solution)/shard_map/ppermute | solution.py:149
  35.0 15.5 %collective-permute-start.5 = (bf16[3,128,768]{2,1,0:T(8,128)(2,1)S(1)}, bf16[3,128,768]{2,1,0:T(8,128)(2,1)}, u32[]{:S(2)}, u32[]{:S(2)}) collective-permute-start(bf16[3,128,768]{2,1,0:T(8,128)(2,1)S(1)} %pad_maximum_fusion.2.refs_1_), channel_id=1, source_target_pairs={{0,1},{1,0},{2,3},{3,2},{4,5},{5,4},{6,7},{7,6},{8,9},{9,8},{10,11... | collective-permute-start | bytes 1769480 | tf_op jit(solution)/shard_map/ppermute | solution.py:149
  36.5 15.2 %collective-permute-start.6 = (bf16[3,128,768]{2,1,0:T(8,128)(2,1)S(1)}, bf16[3,128,768]{2,1,0:T(8,128)(2,1)}, u32[]{:S(2)}, u32[]{:S(2)}) collective-permute-start(bf16[3,128,768]{2,1,0:T(8,128)(2,1)S(1)} %pad_maximum_fusion.2.refs_1_), channel_id=1, source_target_pairs={{0,2},{1,3},{2,0},{3,1},{4,6},{5,7},{6,4},{7,5},{8,10},{9,11},{10,... | collective-permute-start | bytes 1769480 | tf_op jit(solution)/shard_map/ppermute | solution.py:149
  38.0 13.7 %collective-permute-start.9 = (bf16[3,128,768]{2,1,0:T(8,128)(2,1)S(1)}, bf16[3,128,768]{2,1,0:T(8,128)(2,1)}, u32[]{:S(2)}, u32[]{:S(2)}) collective-permute-start(bf16[3,128,768]{2,1,0:T(8,128)(2,1)S(1)} %pad_maximum_fusion.2.refs_1_), channel_id=1, source_target_pairs={{0,4},{1,5},{2,6},{3,7},{4,0},{5,1},{6,2},{7,3},{8,12},{9,13},{10,... | collective-permute-start | bytes 1769480 | tf_op jit(solution)/shard_map/ppermute | solution.py:149
  53.4 18.4 %collective-permute-start.13 = (bf16[3,128,768]{2,1,0:T(8,128)(2,1)}, bf16[3,128,768]{2,1,0:T(8,128)(2,1)}, u32[]{:S(2)}, u32[]{:S(2)}) collective-permute-start(bf16[3,128,768]{2,1,0:T(8,128)(2,1)} %collective-permute-done.5.refs_2_), channel_id=1, source_target_pairs={{0,4},{1,5},{2,6},{3,7},{4,0},{5,1},{6,2},{7,3},{8,12},{9,13},{10,... | collective-permute-start | bytes 1769480 | tf_op jit(solution)/shard_map/ppermute | solution.py:149
  55.1 18.2 %collective-permute-start.14 = (bf16[3,128,768]{2,1,0:T(8,128)(2,1)}, bf16[3,128,768]{2,1,0:T(8,128)(2,1)}, u32[]{:S(2)}, u32[]{:S(2)}) collective-permute-start(bf16[3,128,768]{2,1,0:T(8,128)(2,1)} %collective-permute-done.6.refs_3_), channel_id=1, source_target_pairs={{0,4},{1,5},{2,6},{3,7},{4,0},{5,1},{6,2},{7,3},{8,12},{9,13},{10,... | collective-permute-start | bytes 1769480 | tf_op jit(solution)/shard_map/ppermute | solution.py:149
  55.6 13.6 %collective-permute-start.11 = (bf16[3,64,768]{2,1,0:T(8,128)(2,1)}, bf16[3,64,768]{2,1,0:T(8,128)(2,1)}, u32[]{:S(2)}, u32[]{:S(2)}) collective-permute-start(bf16[3,64,768]{2,1,0:T(8,128)(2,1)} %slice.99), channel_id=1, source_target_pairs={{0,2},{1,3},{2,0},{3,1},{4,6},{5,7},{6,4},{7,5},{8,10},{9,11},{10,... | collective-permute-start | bytes 884744 | tf_op jit(solution)/shard_map/ppermute | solution.py:149
  57.2 12.1 %collective-permute-start.12 = (bf16[3,64,768]{2,1,0:T(8,128)(2,1)}, bf16[3,64,768]{2,1,0:T(8,128)(2,1)}, u32[]{:S(2)}, u32[]{:S(2)}) collective-permute-start(bf16[3,64,768]{2,1,0:T(8,128)(2,1)} %slice.100), channel_id=1, source_target_pairs={{0,1},{1,0},{2,3},{3,2},{4,5},{5,4},{6,7},{7,6},{8,9},{9,8},{10,11... | collective-permute-start | bytes 884744 | tf_op jit(solution)/shard_map/ppermute | solution.py:149
  69.2 4.1 collective-permute-start.15
  69.7 3.6 collective-permute-start.16
  70.4 24.6 %collective-permute-start.17 = (bf16[3,128,1280]{2,1,0:T(8,128)(2,1)S(1)}, bf16[3,128,1280]{2,1,0:T(8,128)(2,1)}, u32[]{:S(2)}, u32[]{:S(2)}) collective-permute-start(bf16[3,128,1280]{2,1,0:T(8,128)(2,1)S(1)} %pad_maximum_fusion.refs_2_), channel_id=1, source_target_pairs={{0,1},{1,0},{2,3},{3,2},{4,5},{5,4},{6,7},{7,6},{8,9},{9,8},{10,11... | collective-permute-start | bytes 2949128 | tf_op jit(solution)/shard_map/ppermute | solution.py:149
  71.8 23.9 %collective-permute-start.18 = (bf16[3,128,1280]{2,1,0:T(8,128)(2,1)S(1)}, bf16[3,128,1280]{2,1,0:T(8,128)(2,1)}, u32[]{:S(2)}, u32[]{:S(2)}) collective-permute-start(bf16[3,128,1280]{2,1,0:T(8,128)(2,1)S(1)} %pad_maximum_fusion.refs_2_), channel_id=1, source_target_pairs={{0,2},{1,3},{2,0},{3,1},{4,6},{5,7},{6,4},{7,5},{8,10},{9,11},{10,... | collective-permute-start | bytes 2949128 | tf_op jit(solution)/shard_map/ppermute | solution.py:149
  81.2 14.6 %collective-permute-start.19 = (bf16[3,128,1280]{2,1,0:T(8,128)(2,1)S(1)}, bf16[3,128,1280]{2,1,0:T(8,128)(2,1)}, u32[]{:S(2)}, u32[]{:S(2)}) collective-permute-start(bf16[3,128,1280]{2,1,0:T(8,128)(2,1)S(1)} %pad_maximum_fusion.refs_2_), channel_id=1, source_target_pairs={{0,4},{1,5},{2,6},{3,7},{4,0},{5,1},{6,2},{7,3},{8,12},{9,13},{10,... | collective-permute-start | bytes 2949128 | tf_op jit(solution)/shard_map/ppermute | solution.py:149
  83.0 206.4 %reduce-scatter.3.cloned.1.call-start = ((), (), s32[]{:S(2)}) async-start(), calls=%async_computation.2 | async-start | bytes 1310720 | tf_op jit(solution)/shard_map/reduce_scatter | solution.py:440
  95.8 19.2 %collective-permute-start.22 = (bf16[3,128,1280]{2,1,0:T(8,128)(2,1)}, bf16[3,128,1280]{2,1,0:T(8,128)(2,1)}, u32[]{:S(2)}, u32[]{:S(2)}) collective-permute-start(bf16[3,128,1280]{2,1,0:T(8,128)(2,1)} %collective-permute-done.17.refs_3_), channel_id=1, source_target_pairs={{0,4},{1,5},{2,6},{3,7},{4,0},{5,1},{6,2},{7,3},{8,12},{9,13},{10,... | collective-permute-start | bytes 2949128 | tf_op jit(solution)/shard_map/ppermute | solution.py:149
  95.8 19.2 %collective-permute-start.23 = (bf16[3,128,1280]{2,1,0:T(8,128)(2,1)}, bf16[3,128,1280]{2,1,0:T(8,128)(2,1)}, u32[]{:S(2)}, u32[]{:S(2)}) collective-permute-start(bf16[3,128,1280]{2,1,0:T(8,128)(2,1)} %collective-permute-done.18.refs_4_), channel_id=1, source_target_pairs={{0,4},{1,5},{2,6},{3,7},{4,0},{5,1},{6,2},{7,3},{8,12},{9,13},{10,... | collective-permute-start | bytes 2949128 | tf_op jit(solution)/shard_map/ppermute | solution.py:149
  98.4 16.6 %collective-permute-start.20 = (bf16[3,64,1280]{2,1,0:T(8,128)(2,1)S(1)}, bf16[3,64,1280]{2,1,0:T(8,128)(2,1)}, u32[]{:S(2)}, u32[]{:S(2)}) collective-permute-start(bf16[3,64,1280]{2,1,0:T(8,128)(2,1)S(1)} %slice.112), channel_id=1, source_target_pairs={{0,2},{1,3},{2,0},{3,1},{4,6},{5,7},{6,4},{7,5},{8,10},{9,11},{10,... | collective-permute-start | bytes 1474568 | tf_op jit(solution)/shard_map/ppermute | solution.py:149
  100.0 15.0 %collective-permute-start.21 = (bf16[3,64,1280]{2,1,0:T(8,128)(2,1)S(1)}, bf16[3,64,1280]{2,1,0:T(8,128)(2,1)}, u32[]{:S(2)}, u32[]{:S(2)}) collective-permute-start(bf16[3,64,1280]{2,1,0:T(8,128)(2,1)S(1)} %slice.113), channel_id=1, source_target_pairs={{0,1},{1,0},{2,3},{3,2},{4,5},{5,4},{6,7},{7,6},{8,9},{9,8},{10,11... | collective-permute-start | bytes 1474568 | tf_op jit(solution)/shard_map/ppermute | solution.py:149
  115.0 2.1 collective-permute-start.24
  115.1 2.8 collective-permute-start.25
  129.6 29.3 %collective-permute-start.26 = (bf16[3,512,256]{2,1,0:T(8,128)(2,1)S(1)}, bf16[3,512,256]{2,1,0:T(8,128)(2,1)S(1)}, u32[]{:S(2)}, u32[]{:S(2)}) collective-permute-start(bf16[3,512,256]{2,1,0:T(8,128)(2,1)S(1)} %pad_maximum_fusion.1.refs_1_), channel_id=1, source_target_pairs={{0,1},{1,0},{2,3},{3,2},{4,5},{5,4},{6,7},{7,6},{8,9},{9,8},{10,11... | collective-permute-start | bytes 2359304 | tf_op jit(solution)/shard_map/ppermute | solution.py:149
  131.1 27.8 %collective-permute-start.27 = (bf16[3,512,256]{2,1,0:T(8,128)(2,1)S(1)}, bf16[3,512,256]{2,1,0:T(8,128)(2,1)S(1)}, u32[]{:S(2)}, u32[]{:S(2)}) collective-permute-start(bf16[3,512,256]{2,1,0:T(8,128)(2,1)S(1)} %pad_maximum_fusion.1.refs_1_), channel_id=1, source_target_pairs={{0,2},{1,3},{2,0},{3,1},{4,6},{5,7},{6,4},{7,5},{8,10},{9,11},{10,... | collective-permute-start | bytes 2359304 | tf_op jit(solution)/shard_map/ppermute | solution.py:149
  131.7 27.2 %collective-permute-start.28 = (bf16[3,512,256]{2,1,0:T(8,128)(2,1)S(1)}, bf16[3,512,256]{2,1,0:T(8,128)(2,1)S(1)}, u32[]{:S(2)}, u32[]{:S(2)}) collective-permute-start(bf16[3,512,256]{2,1,0:T(8,128)(2,1)S(1)} %pad_maximum_fusion.1.refs_1_), channel_id=1, source_target_pairs={{0,4},{1,5},{2,6},{3,7},{4,0},{5,1},{6,2},{7,3},{8,12},{9,13},{10,... | collective-permute-start | bytes 2359304 | tf_op jit(solution)/shard_map/ppermute | solution.py:149
  159.0 16.9 %collective-permute-start.31 = (bf16[3,512,256]{2,1,0:T(8,128)(2,1)S(1)}, bf16[3,512,256]{2,1,0:T(8,128)(2,1)S(1)}, u32[]{:S(2)}, u32[]{:S(2)}) collective-permute-start(bf16[3,512,256]{2,1,0:T(8,128)(2,1)S(1)} %collective-permute-done.26.refs_2_), channel_id=1, source_target_pairs={{0,4},{1,5},{2,6},{3,7},{4,0},{5,1},{6,2},{7,3},{8,12},{9,13},{10,... | collective-permute-start | bytes 2359304 | tf_op jit(solution)/shard_map/ppermute | solution.py:149
  159.5 16.4 %collective-permute-start.32 = (bf16[3,512,256]{2,1,0:T(8,128)(2,1)S(1)}, bf16[3,512,256]{2,1,0:T(8,128)(2,1)S(1)}, u32[]{:S(2)}, u32[]{:S(2)}) collective-permute-start(bf16[3,512,256]{2,1,0:T(8,128)(2,1)S(1)} %collective-permute-done.27.refs_3_), channel_id=1, source_target_pairs={{0,4},{1,5},{2,6},{3,7},{4,0},{5,1},{6,2},{7,3},{8,12},{9,13},{10,... | collective-permute-start | bytes 2359304 | tf_op jit(solution)/shard_map/ppermute | solution.py:149
  159.7 16.2 %collective-permute-start.29 = (bf16[3,256,256]{2,1,0:T(8,128)(2,1)S(1)}, bf16[3,256,256]{2,1,0:T(8,128)(2,1)S(1)}, u32[]{:S(2)}, u32[]{:S(2)}) collective-permute-start(bf16[3,256,256]{2,1,0:T(8,128)(2,1)S(1)} %slice.118), channel_id=1, source_target_pairs={{0,2},{1,3},{2,0},{3,1},{4,6},{5,7},{6,4},{7,5},{8,10},{9,11},{10,... | collective-permute-start | bytes 1179656 | tf_op jit(solution)/shard_map/ppermute | solution.py:149
  161.2 14.7 %collective-permute-start.30 = (bf16[3,256,256]{2,1,0:T(8,128)(2,1)S(1)}, bf16[3,256,256]{2,1,0:T(8,128)(2,1)S(1)}, u32[]{:S(2)}, u32[]{:S(2)}) collective-permute-start(bf16[3,256,256]{2,1,0:T(8,128)(2,1)S(1)} %slice.119), channel_id=1, source_target_pairs={{0,1},{1,0},{2,3},{3,2},{4,5},{5,4},{6,7},{7,6},{8,9},{9,8},{10,11... | collective-permute-start | bytes 1179656 | tf_op jit(solution)/shard_map/ppermute | solution.py:149
  175.9 1.8 collective-permute-start.33
  176.0 2.3 collective-permute-start.34
  179.2 8.5 %collective-permute-start.35 = (bf16[4,4,512,256]{3,2,1,0:T(8,128)(2,1)}, bf16[4,4,512,256]{3,2,1,0:T(8,128)(2,1)}, u32[]{:S(2)}, u32[]{:S(2)}) collective-permute-start(bf16[4,4,512,256]{3,2,1,0:T(8,128)(2,1)} %get-tuple-element.201), channel_id=1, source_target_pairs={{0,4},{1,5},{2,6},{3,7},{4,0},{5,1},{6,2},{7,3},{8,12},{9,13},{10,... | collective-permute-start | bytes 12582920 | tf_op jit(solution)/shard_map/ppermute | solution.py:149
  192.6 31.4 %collective-permute-start.36 = (bf16[2,2,512,256]{3,2,1,0:T(8,128)(2,1)}, bf16[2,2,512,256]{3,2,1,0:T(8,128)(2,1)S(1)}, u32[]{:S(2)}, u32[]{:S(2)}) collective-permute-start(bf16[2,2,512,256]{3,2,1,0:T(8,128)(2,1)} %get-tuple-element.206), channel_id=1, source_target_pairs={{0,1},{1,0},{2,3},{3,2},{4,5},{5,4},{6,7},{7,6},{8,9},{9,8},{10,11... | collective-permute-start | bytes 3145736 | tf_op jit(solution)/shard_map/ppermute | solution.py:149
  194.1 29.9 %collective-permute-start.37 = (bf16[2,2,512,256]{3,2,1,0:T(8,128)(2,1)S(1)}, bf16[2,2,512,256]{3,2,1,0:T(8,128)(2,1)S(1)}, u32[]{:S(2)}, u32[]{:S(2)}) collective-permute-start(bf16[2,2,512,256]{3,2,1,0:T(8,128)(2,1)S(1)} %get-tuple-element.208), channel_id=1, source_target_pairs={{0,2},{1,3},{2,0},{3,1},{4,6},{5,7},{6,4},{7,5},{8,10},{9,11},{10,... | collective-permute-start | bytes 3145736 | tf_op jit(solution)/shard_map/ppermute | solution.py:149
  224.6 20.1 %collective-permute-start.38 = (bf16[2,512,256]{2,1,0:T(8,128)(2,1)S(1)}, bf16[2,512,256]{2,1,0:T(8,128)(2,1)S(1)}, u32[]{:S(2)}, u32[]{:S(2)}) collective-permute-start(bf16[2,512,256]{2,1,0:T(8,128)(2,1)S(1)} %get-tuple-element.217), channel_id=1, source_target_pairs={{0,2},{1,3},{2,0},{3,1},{4,6},{5,7},{6,4},{7,5},{8,10},{9,11},{10,... | collective-permute-start | bytes 1572872 | tf_op jit(solution)/shard_map/ppermute | solution.py:149
  226.0 18.6 %collective-permute-start.39 = (bf16[2,512,256]{2,1,0:T(8,128)(2,1)S(1)}, bf16[2,512,256]{2,1,0:T(8,128)(2,1)S(1)}, u32[]{:S(2)}, u32[]{:S(2)}) collective-permute-start(bf16[2,512,256]{2,1,0:T(8,128)(2,1)S(1)} %get-tuple-element.218), channel_id=1, source_target_pairs={{0,1},{1,0},{2,3},{3,2},{4,5},{5,4},{6,7},{7,6},{8,9},{9,8},{10,11... | collective-permute-start | bytes 1572872 | tf_op jit(solution)/shard_map/ppermute | solution.py:149
  245.8 9.5 %collective-permute-start.40 = (bf16[4,4,128,1024]{3,2,1,0:T(8,128)(2,1)}, bf16[4,4,128,1024]{3,2,1,0:T(8,128)(2,1)}, u32[]{:S(2)}, u32[]{:S(2)}) collective-permute-start(bf16[4,4,128,1024]{3,2,1,0:T(8,128)(2,1)} %get-tuple-element.229), channel_id=1, source_target_pairs={{0,4},{1,5},{2,6},{3,7},{4,0},{5,1},{6,2},{7,3},{8,12},{9,13},{10,... | collective-permute-start | bytes 12582920 | tf_op jit(solution)/shard_map/ppermute | solution.py:149
  245.8 8.5 %collective-permute-start.41 = (bf16[4,4,128,256]{3,2,1,0:T(8,128)(2,1)}, bf16[4,4,128,256]{3,2,1,0:T(8,128)(2,1)S(1)}, u32[]{:S(2)}, u32[]{:S(2)}) collective-permute-start(bf16[4,4,128,256]{3,2,1,0:T(8,128)(2,1)} %get-tuple-element.230), channel_id=1, source_target_pairs={{0,4},{1,5},{2,6},{3,7},{4,0},{5,1},{6,2},{7,3},{8,12},{9,13},{10,... | collective-permute-start | bytes 3145736 | tf_op jit(solution)/shard_map/ppermute | solution.py:149
  246.4 123.8 %reduce-scatter.5.cloned.1.call-start = ((), (), s32[]{:S(2)}) async-start(), calls=%async_computation.3 | async-start | bytes 1638400 | tf_op jit(solution)/shard_map/reduce_scatter | solution.py:440
  263.3 31.4 %collective-permute-start.42 = (bf16[2,2,128,1280]{3,2,1,0:T(8,128)(2,1)}, bf16[2,2,128,1280]{3,2,1,0:T(8,128)(2,1)}, u32[]{:S(2)}, u32[]{:S(2)}) collective-permute-start(bf16[2,2,128,1280]{3,2,1,0:T(8,128)(2,1)} %get-tuple-element.236), channel_id=1, source_target_pairs={{0,1},{1,0},{2,3},{3,2},{4,5},{5,4},{6,7},{7,6},{8,9},{9,8},{10,11... | collective-permute-start | bytes 3932168 | tf_op jit(solution)/shard_map/ppermute | solution.py:149
  264.8 31.1 %collective-permute-start.43 = (bf16[2,2,128,1280]{3,2,1,0:T(8,128)(2,1)}, bf16[2,2,128,1280]{3,2,1,0:T(8,128)(2,1)}, u32[]{:S(2)}, u32[]{:S(2)}) collective-permute-start(bf16[2,2,128,1280]{3,2,1,0:T(8,128)(2,1)} %get-tuple-element.238), channel_id=1, source_target_pairs={{0,2},{1,3},{2,0},{3,1},{4,6},{5,7},{6,4},{7,5},{8,10},{9,11},{10,... | collective-permute-start | bytes 3932168 | tf_op jit(solution)/shard_map/ppermute | solution.py:149
  297.9 15.9 %collective-permute-start.44 = (bf16[2,128,1280]{2,1,0:T(8,128)(2,1)S(1)}, bf16[2,128,1280]{2,1,0:T(8,128)(2,1)S(1)}, u32[]{:S(2)}, u32[]{:S(2)}) collective-permute-start(bf16[2,128,1280]{2,1,0:T(8,128)(2,1)S(1)} %get-tuple-element.244), channel_id=1, source_target_pairs={{0,2},{1,3},{2,0},{3,1},{4,6},{5,7},{6,4},{7,5},{8,10},{9,11},{10,... | collective-permute-start | bytes 1966088 | tf_op jit(solution)/shard_map/ppermute | solution.py:149
  298.6 15.6 %collective-permute-start.45 = (bf16[2,128,1280]{2,1,0:T(8,128)(2,1)S(1)}, bf16[2,128,1280]{2,1,0:T(8,128)(2,1)S(1)}, u32[]{:S(2)}, u32[]{:S(2)}) collective-permute-start(bf16[2,128,1280]{2,1,0:T(8,128)(2,1)S(1)} %get-tuple-element.246), channel_id=1, source_target_pairs={{0,1},{1,0},{2,3},{3,2},{4,5},{5,4},{6,7},{7,6},{8,9},{9,8},{10,11... | collective-permute-start | bytes 1966088 | tf_op jit(solution)/shard_map/ppermute | solution.py:149
  315.5 6.0 %collective-permute-start.46 = (bf16[4,4,128,768]{3,2,1,0:T(8,128)(2,1)}, bf16[4,4,128,768]{3,2,1,0:T(8,128)(2,1)}, u32[]{:S(2)}, u32[]{:S(2)}) collective-permute-start(bf16[4,4,128,768]{3,2,1,0:T(8,128)(2,1)} %get-tuple-element.252), channel_id=1, source_target_pairs={{0,4},{1,5},{2,6},{3,7},{4,0},{5,1},{6,2},{7,3},{8,12},{9,13},{10,... | collective-permute-start | bytes 9437192 | tf_op jit(solution)/shard_map/ppermute | solution.py:149
  315.5 64.8 %all-gather.11.cloned.1.call-start = ((), (), s32[]{:S(2)}) async-start(), calls=%async_computation.6 | async-start | bytes 1310720 | tf_op jit(solution)/shard_map/all_gather | solution.py:446
  328.1 19.8 %collective-permute-start.47 = (bf16[2,2,128,768]{3,2,1,0:T(8,128)(2,1)}, bf16[2,2,128,768]{3,2,1,0:T(8,128)(2,1)S(1)}, u32[]{:S(2)}, u32[]{:S(2)}) collective-permute-start(bf16[2,2,128,768]{3,2,1,0:T(8,128)(2,1)} %get-tuple-element.256), channel_id=1, source_target_pairs={{0,1},{1,0},{2,3},{3,2},{4,5},{5,4},{6,7},{7,6},{8,9},{9,8},{10,11... | collective-permute-start | bytes 2359304 | tf_op jit(solution)/shard_map/ppermute | solution.py:149
  328.7 19.5 %collective-permute-start.48 = (bf16[2,2,128,768]{3,2,1,0:T(8,128)(2,1)}, bf16[2,2,128,768]{3,2,1,0:T(8,128)(2,1)S(1)}, u32[]{:S(2)}, u32[]{:S(2)}) collective-permute-start(bf16[2,2,128,768]{3,2,1,0:T(8,128)(2,1)} %get-tuple-element.258), channel_id=1, source_target_pairs={{0,2},{1,3},{2,0},{3,1},{4,6},{5,7},{6,4},{7,5},{8,10},{9,11},{10,... | collective-permute-start | bytes 2359304 | tf_op jit(solution)/shard_map/ppermute | solution.py:149
  348.7 19.3 %collective-permute-start.49 = (bf16[2,128,768]{2,1,0:T(8,128)(2,1)S(1)}, bf16[2,128,768]{2,1,0:T(8,128)(2,1)S(1)}, u32[]{:S(2)}, u32[]{:S(2)}) collective-permute-start(bf16[2,128,768]{2,1,0:T(8,128)(2,1)S(1)} %get-tuple-element.271), channel_id=1, source_target_pairs={{0,2},{1,3},{2,0},{3,1},{4,6},{5,7},{6,4},{7,5},{8,10},{9,11},{10,... | collective-permute-start | bytes 1179656 | tf_op jit(solution)/shard_map/ppermute | solution.py:149
  350.2 17.8 %collective-permute-start.50 = (bf16[2,128,768]{2,1,0:T(8,128)(2,1)S(1)}, bf16[2,128,768]{2,1,0:T(8,128)(2,1)S(1)}, u32[]{:S(2)}, u32[]{:S(2)}) collective-permute-start(bf16[2,128,768]{2,1,0:T(8,128)(2,1)S(1)} %get-tuple-element.273), channel_id=1, source_target_pairs={{0,1},{1,0},{2,3},{3,2},{4,5},{5,4},{6,7},{7,6},{8,9},{9,8},{10,11... | collective-permute-start | bytes 1179656 | tf_op jit(solution)/shard_map/ppermute | solution.py:149
  368.8 8.3 %collective-permute-start.52 = (bf16[144,768]{1,0:T(8,128)(2,1)S(1)}, bf16[144,768]{1,0:T(8,128)(2,1)S(1)}, u32[]{:S(2)}, u32[]{:S(2)}) collective-permute-start(bf16[144,768]{1,0:T(8,128)(2,1)S(1)} %get-tuple-element.278), channel_id=1, source_target_pairs={{0,8},{1,9},{2,10},{3,11},{4,12},{5,13},{6,14},{7,15},{8,16},{9,17... | collective-permute-start | bytes 663560 | tf_op jit(solution)/shard_map/ppermute | solution.py:149
  370.2 22.1 %collective-permute-start.55 = (bf16[128,1280]{1,0:T(8,128)(2,1)}, bf16[128,1280]{1,0:T(8,128)(2,1)S(1)}, u32[]{:S(2)}, u32[]{:S(2)}) collective-permute-start(bf16[128,1280]{1,0:T(8,128)(2,1)} %bitcast.88), channel_id=1, source_target_pairs={{0,1},{1,0},{2,3},{3,2},{4,5},{5,4},{6,7},{7,6},{8,9},{9,8},{10,11... | collective-permute-start | bytes 983048 | tf_op jit(solution)/shard_map/ppermute | solution.py:149
  370.9 21.4 %collective-permute-start.56 = (bf16[128,1280]{1,0:T(8,128)(2,1)}, bf16[128,1280]{1,0:T(8,128)(2,1)S(1)}, u32[]{:S(2)}, u32[]{:S(2)}) collective-permute-start(bf16[128,1280]{1,0:T(8,128)(2,1)} %bitcast.89), channel_id=1, source_target_pairs={{0,2},{1,3},{2,0},{3,1},{4,6},{5,7},{6,4},{7,5},{8,10},{9,11},{10,... | collective-permute-start | bytes 983048 | tf_op jit(solution)/shard_map/ppermute | solution.py:149
  371.5 20.8 %collective-permute-start.57 = (bf16[128,1280]{1,0:T(8,128)(2,1)}, bf16[128,1280]{1,0:T(8,128)(2,1)S(1)}, u32[]{:S(2)}, u32[]{:S(2)}) collective-permute-start(bf16[128,1280]{1,0:T(8,128)(2,1)} %bitcast.90), channel_id=1, source_target_pairs={{0,3},{1,2},{2,1},{3,0},{4,7},{5,6},{6,5},{7,4},{8,11},{9,10},{10,... | collective-permute-start | bytes 983048 | tf_op jit(solution)/shard_map/ppermute | solution.py:149
  373.6 15.7 %collective-permute-start.53 = (bf16[144,768]{1,0:T(8,128)(2,1)S(1)}, bf16[144,768]{1,0:T(8,128)(2,1)S(1)}, u32[]{:S(2)}, u32[]{:S(2)}) collective-permute-start(bf16[144,768]{1,0:T(8,128)(2,1)S(1)} %get-tuple-element.279), channel_id=1, source_target_pairs={{0,16},{1,17},{2,18},{3,19},{4,20},{5,21},{6,22},{7,23},{8,24},{9,... | collective-permute-start | bytes 663560 | tf_op jit(solution)/shard_map/ppermute | solution.py:149
  377.1 15.2 %collective-permute-start.54 = (bf16[144,768]{1,0:T(8,128)(2,1)S(1)}, bf16[144,768]{1,0:T(8,128)(2,1)S(1)}, u32[]{:S(2)}, u32[]{:S(2)}) collective-permute-start(bf16[144,768]{1,0:T(8,128)(2,1)S(1)} %get-tuple-element.280), channel_id=1, source_target_pairs={{0,24},{1,25},{2,26},{3,27},{4,28},{5,29},{6,30},{7,31},{8,0},{9,1... | collective-permute-start | bytes 663560 | tf_op jit(solution)/shard_map/ppermute | solution.py:149
  392.4 8.4 %collective-permute-start.58 = (bf16[144,768]{1,0:T(8,128)(2,1)S(1)}, bf16[144,768]{1,0:T(8,128)(2,1)S(1)}, u32[]{:S(2)}, u32[]{:S(2)}) collective-permute-start(bf16[144,768]{1,0:T(8,128)(2,1)S(1)} %add_convert_fusion.1.refs_0_), channel_id=1, source_target_pairs={{0,1},{1,0},{2,3},{3,2},{4,5},{5,4},{6,7},{7,6},{8,9},{9,8},{10,11... | collective-permute-start | bytes 663560 | tf_op jit(solution)/shard_map/ppermute | solution.py:149
  393.2 10.0 %collective-permute-start.59 = (bf16[144,768]{1,0:T(8,128)(2,1)S(1)}, bf16[144,768]{1,0:T(8,128)(2,1)S(1)}, u32[]{:S(2)}, u32[]{:S(2)}) collective-permute-start(bf16[144,768]{1,0:T(8,128)(2,1)S(1)} %add_convert_fusion.1.refs_0_), channel_id=1, source_target_pairs={{0,2},{1,3},{2,0},{3,1},{4,6},{5,7},{6,4},{7,5},{8,10},{9,11},{10,... | collective-permute-start | bytes 663560 | tf_op jit(solution)/shard_map/ppermute | solution.py:149
  393.8 10.8 %collective-permute-start.60 = (bf16[144,768]{1,0:T(8,128)(2,1)S(1)}, bf16[144,768]{1,0:T(8,128)(2,1)S(1)}, u32[]{:S(2)}, u32[]{:S(2)}) collective-permute-start(bf16[144,768]{1,0:T(8,128)(2,1)S(1)} %add_convert_fusion.1.refs_0_), channel_id=1, source_target_pairs={{0,3},{1,2},{2,1},{3,0},{4,7},{5,6},{6,5},{7,4},{8,11},{9,10},{10,... | collective-permute-start | bytes 663560 | tf_op jit(solution)/shard_map/ppermute | solution.py:149
  (48 other events, 602.3 us)
Sparse Core Ops, SparseCore 0:
  28.7 34.7 all-gather.6
  83.1 26.0 all-gather.8
  246.5 23.9 reduce-scatter.2
  315.7 28.3 reduce-scatter.4
  345.9 30.2 all-gather.10

commit v4 on v3

--- a/solution.py
+++ b/solution.py
@@ -246,11 +246,164 @@
         yield n, jnp.where(first, low, high), jnp.where(first, high, low)
 
 
-def wgrad_call(kernel, where, grid, specs, outs, shapes, arrays):
+def pieces_to(place_ref, ins, widths, held, sems):
+    each = len(ins) // 2
+    planes, depth = ins[each - 5].shape[0] + 1, ins[each - 5].shape[1]
+    half = depth // 2
+    z, core, me = place_ref[0], place_ref[1], place_ref[2]
+    places = [me, me + 1 - 2 * (me % 2), (me + 2) % 4, 3 - me, 3 - me]
+    parts = [(0, depth), (0, depth), (0, depth), (0, half), (half, half)]
+    lists, count = [], 0
+    for target, wide in enumerate(widths):
+        copies = []
+        for flip_core in range(2):
+            side = (core + flip_core) % 2
+            mine = ins[flip_core * each : (flip_core + 1) * each]
+            sources = [
+                (mine[target].at[:, pl.ds(unit * wide, wide)], 2 * z + side, unit, 0, depth)
+                for unit in range(4)
+            ]
+            for step in range(1, planes):
+                shard = 2 * ((z + planes - step) % planes) + side
+                for other, spot, part in zip(mine[each - 5 :], places, parts):
+                    source = other.at[step - 1, :, pl.ds(sum(widths[:target]), wide)]
+                    sources.append((source, shard, spot, *part))
+            for source, shard, unit, first, size in sources:
+                row = pl.multiple_of(shard * depth + first, half)
+                column = pl.multiple_of(jnp.int32(unit) * wide, wide)
+                spot = held[target].at[pl.ds(row, size), pl.ds(column, wide)]
+                copies.append(pltpu.make_async_copy(source, spot, sems.at[count]))
+                count += 1
+        lists.append(copies)
+    return lists
+
+
+def piece_count(pieces, targets):
+    return targets * 2 * (4 + pieces[0][0].shape[0] * 5)
+
+
+def assembled_project(where, owns, pieces, a, bias):
+    flat = [*owns[0], *pieces[0], *owns[1], *pieces[1]]
+    rows, width = a.shape
+    wide = owns[0][0].shape[1]
+    steps = wide // TILE
+    unit = wide // 4
+
+    def kernel(place_ref, *refs):
+        ins, (a_ref, b_ref, out_ref, w_ref, held, sems, done) = refs[: len(flat)], refs[len(flat) :]
+        step = pl.program_id(0)
+        (copies,) = pieces_to(place_ref, ins, [unit], [held], sems)
+        whole_copy = pltpu.make_async_copy(held, w_ref, done.at[0])
+
+        @pl.when(step == 0)
+        def _():
+            for copy in copies:
+                copy.start()
+            for copy in copies:
+                copy.wait()
+            whole_copy.start()
+
+        w = held[:, pl.ds(pl.multiple_of(step * TILE, TILE), TILE)]
+        out_ref[...] = (nn(a_ref[...], w) + b_ref[...]).astype(BF)
+
+        @pl.when(step == steps - 1)
+        def _():
+            whole_copy.wait()
+
+    return call(
+        kernel,
+        (steps,),
+        [pl.BlockSpec(memory_space=pltpu.SMEM)]
+        + [pl.BlockSpec(memory_space=pl.ANY)] * len(flat)
+        + [whole(a), columns_of(1, TILE)],
+        [columns_of(rows, TILE), pl.BlockSpec(memory_space=pltpu.HBM)],
+        [struct(rows, wide), struct(width, wide)],
+        [
+            pltpu.VMEM((width, wide), BF),
+            pltpu.SemaphoreType.DMA((piece_count(pieces, 1),)),
+            pltpu.SemaphoreType.DMA((1,)),
+        ],
+        (where, *flat, a, bias[None]),
+    )
+
+
+def assembled_middle(where, owns, pieces, o, x, bias, gain, shift):
+    flat = [*owns[0], *pieces[0], *owns[1], *pieces[1]]
+    rows, width = x.shape
+    wide = owns[0][0].shape[1]
+    height = rows // 4
+
+    def kernel(place_ref, *refs):
+        ins, refs = refs[: len(flat)], refs[len(flat) :]
+        o_ref, x_ref, b_ref, gain_ref, shift_ref, y_ref, a_ref, up_ref, out_ref = refs[:9]
+        up, out, sems, done = refs[9:]
+        step = pl.program_id(0)
+        up_copies, out_copies = pieces_to(
+            place_ref, ins, [wide // 4, width // 4], [up, out], sems
+        )
+        up_whole = pltpu.make_async_copy(up, up_ref, done.at[0])
+        out_whole = pltpu.make_async_copy(out, out_ref, done.at[1])
+
+        @pl.when(step == 0)
+        def _():
+            for copy in out_copies + up_copies:
+                copy.start()
+            for copy in out_copies:
+                copy.wait()
+            out_whole.start()
+
+        @pl.when(step == 1)
+        def _():
+            for copy in up_copies:
+                copy.wait()
+            up_whole.start()
+
+        y = nn(o_ref[...], out[...]) + x_ref[...].astype(F32) + b_ref[...]
+        y_ref[...] = y
+        unit, _ = normal(y)
+        a_ref[...] = (unit * gain_ref[...] + shift_ref[...]).astype(BF)
+
+        @pl.when(step == 3)
+        def _():
+            out_whole.wait()
+            up_whole.wait()
+
+    tile = rows_of(height, width)
+    vectors = [bias[None], gain[None], shift[None]]
+    far = pl.BlockSpec(memory_space=pltpu.HBM)
+    return call(
+        kernel,
+        (4,),
+        [pl.BlockSpec(memory_space=pltpu.SMEM)]
+        + [pl.BlockSpec(memory_space=pl.ANY)] * len(flat)
+        + [tile, tile]
+        + [whole(v) for v in vectors],
+        [tile, tile, far, far],
+        [
+            struct(rows, width, dtype=F32),
+            struct(rows, width),
+            struct(width, wide),
+            struct(width, width),
+        ],
+        [
+            pltpu.VMEM((width, wide), BF),
+            pltpu.VMEM((width, width), BF),
+            pltpu.SemaphoreType.DMA((piece_count(pieces, 2),)),
+            pltpu.SemaphoreType.DMA((2,)),
+        ],
+        (where, *flat, o, x, *vectors),
+    )
+
+
+def wgrad_call(kernel, where, grid, specs, outs, shapes, arrays, scratch=()):
     return pl.pallas_call(
         kernel,
         grid_spec=pltpu.PrefetchScalarGridSpec(
-            num_scalar_prefetch=1, grid=grid, in_specs=specs, out_specs=outs
+            num_scalar_prefetch=1,
+            grid=grid,
+            in_specs=specs,
+            out_specs=outs,
+            scratch_shapes=scratch,
         ),
         out_shape=[jax.ShapeDtypeStruct(shape, BF) for shape in shapes],
         compiler_params=pltpu.CompilerParams(vmem_limit_bytes=56 * 2**20),
@@ -261,32 +414,35 @@
     rows, width = left.shape
     shards = lax.axis_size("fsdp")
     planes, depth, wide = shards // 2, width // shards, right.shape[1] // 4
+    part = extra[1].shape[1] // 4 if extra else 0
     count = 2 + len(extra)
 
     def kernel(place_ref, *refs):
-        ins, outs = refs[:count], refs[count:]
-        for n, mine, far in halves(place_ref, tn(ins[0][...], ins[1][...]), depth):
-            outs[0][n] = mine
-            outs[1][n] = far
+        ins, outs, held = refs[:count], refs[count : count + 2], refs[count + 2 :]
+        step = pl.program_id(0)
         if extra:
 
-            @pl.when(pl.program_id(0) == 0)
+            @pl.when(step == 0)
             def _():
-                part = width // 4
                 for n, mine, far in halves(place_ref, tn(ins[2][...], ins[3][...]), depth):
                     for j in range(4):
-                        outs[2][j, n] = mine[:, j * part : (j + 1) * part]
-                        outs[3][j, n] = far[:, j * part : (j + 1) * part]
+                        held[0][j, n] = mine[:, j * part : (j + 1) * part]
+                        held[1][j, n] = far[:, j * part : (j + 1) * part]
+
+        for n, mine, far in halves(place_ref, tn(ins[0][...], ins[1][...]), depth):
+            outs[0][n, :, pl.ds(0, wide)] = mine
+            outs[1][n, :, pl.ds(0, wide)] = far
+        if extra:
+            for out, kept in zip(outs, held):
+                out[:, :, pl.ds(wide, part)] = kept[step]
 
     one = pl.BlockSpec((rows, width), lambda j, c: (0, 0), pipeline_mode=pl.Buffered(1))
     specs = [one, pl.BlockSpec((rows, wide), lambda j, c: (0, j))] + [one] * len(extra)
-    outs = [pl.BlockSpec((None, planes, depth, wide), lambda j, c: (j, 0, 0, 0))] * 2
-    shapes = [(4, planes, depth, wide)] * 2
-    if extra:
-        shape = (4, planes, depth, width // 4)
-        outs += [pl.BlockSpec(shape, lambda j, c: (0, 0, 0, 0), pipeline_mode=pl.Buffered(1))] * 2
-        shapes += [shape] * 2
-    return wgrad_call(kernel, where, (4,), specs, outs, shapes, (left, right, *extra))
+    out = pl.BlockSpec((None, planes, depth, wide + part), lambda j, c: (j, 0, 0, 0))
+    shape = (4, planes, depth, wide + part)
+    scratch = [pltpu.VMEM((4, planes, depth, part), BF)] * 2 if extra else []
+    arrays = (left, right, *extra)
+    return wgrad_call(kernel, where, (4,), specs, [out] * 2, [shape] * 2, arrays, scratch)
 
 
 def wgrad_planes(where, left, right):
@@ -310,6 +466,8 @@
 
 
 def add(*parts):
+    if len(parts) == 2:
+        return parts[0] + parts[1]
     total = parts[0].astype(F32)
     for part in parts[1:]:
         total += part.astype(F32)
@@ -897,14 +1055,10 @@
     cross_first = after(cross_first, col_second, a1)
     near_first = [col_first] + two_first + cross_first
     far_first = far_first + to_partner(cross_first)
-    (qkv_w,) = assemble(
-        where,
-        [[w_qkv], far_own[:1]],
-        [near_first, far_first],
-        [(width, 3 * width)],
-    )
-    far_second = to_partner(after([col_second], qkv_w))
-    qkv = project(a1, qkv_w, bias_qkv)
+    far_second = to_partner(after([col_second], far_first))
+    qkv, qkv_w = assembled_project(
+        where, [[w_qkv], far_own[:1]], [near_first, far_first], a1, bias_qkv
+    )
     two_second, far_second = after((two_second, far_second), qkv)
     cross_second = across(edges(two_second))
     far_second = far_second + to_partner(two_second)
@@ -912,14 +1066,17 @@
     cross_second, far_second = after((cross_second, far_second), o)
     near_second = [col_second] + two_second + cross_second
     far_second = far_second + to_partner(cross_second)
-    up_w, out_w = assemble(
+    y1, a2, up_w, out_w = assembled_middle(
         where,
         [[w_up, w_out], [far_own[2], far_own[1]]],
         [near_second, far_second],
-        [(width, wide), (width, width)],
-    )
-    y1, a2 = middle(o, out_w, x_low, bias_out, gain2, shift2)
-    col_third = others(where, after(z_third, up_w), w_down.shape[0])
+        o,
+        x_low,
+        bias_out,
+        gain2,
+        shift2,
+    )
+    col_third = others(where, after(z_third, far_second), w_down.shape[0])
     two_third = [send(col_third, 0, 0, flip) for flip in (1, 2)]
     far_third = to_partner([col_third])
     hid, slope = expand(after(a2, col_third), up_w, bias_up)
@@ -946,13 +1103,12 @@
     )
     side_down = side_sum(chip_down, after(sides_down, dy1))
     ends_down = ends(side_down)
-    up_out = wgrad_units(where, a2, after(du, side_down), (o, d1))
-    mine_up, far_up = up_out[::2], up_out[1::2]
+    mine_up, far_up = wgrad_units(where, a2, after(du, side_down), (o, d1))
     total_down = plane_sum(side_down, after(ends_down, mine_up))
-    got_up = to_partner(after(far_up, total_down))
+    got_up = send(after(far_up, total_down), 0, 1, 0)
     share_down = column_sum(total_down)
     do = back_out(after(d1, total_down), out_w)
-    chip_up = chip_sum(where, *after((mine_up, got_up), do))
+    chip_up = chip_sum(where, *after(([mine_up], [got_up]), do))
     sides_up = sides(chip_up)
     dqkv = per_image(attention_backward, live, slots, [qkv, after(do, chip_up)], 3 * width)
     share_down = after(share_down, dqkv)
@@ -983,22 +1139,19 @@
     )
     planes = lax.axis_size("fsdp") // 2
     rows = packed_rows([part.reshape(planes, 2, -1) for part in sums])
-    hid = after(hid, rows, side_qkv)
     rows = pick(rows, where[1], 1) + send(pick(rows, 1 - where[1], 1), 0, 1, 0)
     rows = rows.reshape(planes, 2, -1).astype(BF)
     rows = jnp.pad(rows, ((0, 0), (0, 14), (0, 0)))
 
-    activations = contract(hid, down_w, y1, bias_down)
     from_down = from_plane(after(share_down, chip_qkv))
-    column_qkv = column_parts(
-        plane_columns(where, side_qkv, after(ends_qkv, activations), rows)
-    )
+    column_qkv = column_parts(plane_columns(where, side_qkv, ends_qkv, rows))
+    activations = contract(after(hid, column_qkv[0]), down_w, y1, bias_down)
     shares_up = shares(after(share_up, column_qkv[0]))
-    (s_down,) = joined(after(from_down, column_qkv[0]), [width // 4])
-    share_qkv = add(*after(column_qkv, s_down, shares_up))
+    share_qkv = add(*after(column_qkv, activations))
     shares_qkv = shares(share_qkv)
+    (s_down,) = joined(after(from_down, share_qkv), [width // 4])
     s_up, s_out = spread(where, after(shares_up, share_qkv), [wide // 4, width // 4])
-    s_qkv, own = spread(where, after(shares_qkv, s_up), [width * 3 // 4], 2)
+    s_qkv, own = spread(where, after(shares_qkv, s_up, s_down), [width * 3 // 4], 2)
     own = own.reshape(-1)
     return activations, input_grad, s_qkv, s_out, s_up, s_down, own_parts(own, sums)
 

time: 420 us -> 410 us (0.976)
  Pallas kernels: 233 us -> 223 us
    pallas_call x3 -> x1, Pallas kernels: 24.3 us -> 8 us  [assemble(): pl.pallas_call(kernel, in_specs=[pl.BlockSpec(memory_space=pltpu.SMEM)] +...]
    pallas_call x7, Pallas kernels: 102 us -> 110 us  [call(): pl.pallas_call(kernel, grid=grid, in_specs=in_specs, out_specs=out_specs,...]
    unnamed x97 -> x95, local copies, waits for them, and re-layouts: 13 us -> 7.55 us
    ppermute x61 -> x60, starting transfers between devices: 50.6 us -> 47.2 us  [send(): return lax.ppermute(value, ('fsdp', 'seq'), pairs)]
    ppermute x61 -> x60, waiting for transfers between devices: 71 us -> 74.2 us  [send(): return lax.ppermute(value, ('fsdp', 'seq'), pairs)]
  transfers between devices with their start and end apart: 66 -> 65, of which waited for: 27 -> 25; matrix products, arithmetic and copies ran while one was open for 5% -> 6% of each run, Pallas kernels for 53% -> 53%
where the time goes in v4:
time: 410 us; the launch traced here: 402 us
  Pallas kernels  223 us (54%)
  waiting for transfers between devices  80.1 us (20%)
  starting transfers between devices  47.5 us (12%)
  local copies, waits for them, and re-layouts  26.2 us (6%)
  between operations  14.7 us (4%)
  other arithmetic  10.5 us (3%)
    pallas_call x7, Pallas kernels, call(): pl.pallas_call(kernel, grid=grid, in_specs=in_specs, out_specs=out_specs,...  110 us
    ppermute x60, waiting for transfers between devices, send(): return lax.ppermute(value, ('fsdp', 'seq'), pairs)  74.2 us
    ppermute x60, starting transfers between devices, send(): return lax.ppermute(value, ('fsdp', 'seq'), pairs)  47.2 us
    pallas_call x3, Pallas kernels, wgrad_call(): pl.pallas_call(kernel, grid_spec=pltpu.PrefetchScalarGridSpec(num_scalar_...  42.9 us
    pallas_call x2, Pallas kernels, per_image(): pl.pallas_call(kernel, grid_spec=pltpu.PrefetchScalarGridSpec(num_scalar_...  36.6 us
    pallas_call x3, Pallas kernels, chip_sum(): pl.pallas_call(kernel, grid_spec=pltpu.PrefetchScalarGridSpec(num_scalar_...  14.6 us
  transfers between devices with their start and end apart: 65, of which 25 were waited for; matrix products, arithmetic and copies ran while one was open for 6% of the time, Pallas kernels for 53%

profile of v4, /device:TPU:8, one launch (start us, length us, event | category | flops | bytes accessed | tf_op | source)
XLA Modules:
  0.0 401.9 jit_solution(16279864046022357019)
XLA Ops:
  8.3 1.6 collective-permute-start
  11.1 1.9 collective-permute-start.2
  16.4 7.3 %collective-permute-done = bf16[128,768]{1,0:T(8,128)(2,1)S(1)} collective-permute-done((bf16[128,768]{1,0:T(8,128)(2,1)S(1)}, bf16[128,768]{1,0:T(8,128)(2,1)S(1)}, u32[]{:S(2)}, u32[]{:S(2)}) %collective-permute-start) | collective-permute-done | bytes 196640 | tf_op jit(solution)/shard_map/ppermute | solution.py:149
  23.7 3.1 collective-permute-done.1
  26.8 1.8 collective-permute-done.2
  29.7 2.4 collective-permute-done.4.refs_8_
  35.0 1.5 collective-permute-start.5
  36.5 1.5 collective-permute-start.6
  38.8 11.7 %collective-permute-done.5.refs_2_ = bf16[3,128,768]{2,1,0:T(8,128)(2,1)} collective-permute-done((bf16[3,128,768]{2,1,0:T(8,128)(2,1)S(1)}, bf16[3,128,768]{2,1,0:T(8,128)(2,1)}, u32[]{:S(2)}, u32[]{:S(2)}) %collective-permute-start.5) | collective-permute-done | bytes 589856 | tf_op jit(solution)/shard_map/ppermute | solution.py:149
  51.7 1.7 slice.99
  53.4 1.7 slice.100
  55.6 1.5 collective-permute-start.14
  57.6 5.8 %all-gather.7.cloned.1.call-done = bf16[576,1280]{1,0:T(8,128)(2,1)} async-done(((bf16[144,1280]{1,0:T(8,128)(2,1)}), bf16[576,1280]{1,0:T(8,128)(2,1)}) %all-gather.7.cloned.1.call-update) | async-done | bytes 1474576 | tf_op jit(solution)/shard_map/all_gather | solution.py:669
  67.7 2.1 add_convert_fusion.refs_12_.refs_0_
  70.4 1.5 collective-permute-start.10
  71.9 1.5 collective-permute-start.11
  73.4 1.8 constant_dynamic-slice_fusion.3
  77.4 13.2 %shard_map.254 = (bf16[960,3072]{1,0:T(8,128)(2,1)}, bf16[1024,3072]{1,0:T(8,128)(2,1)}) custom-call(s32[3]{0:T(128)} %pad_add_fusion.1.place_ref, bf16[128,3072]{1,0:T(8,128)(2,1)} %refs_0_.3, bf16[3,128,768]{2,1,0:T(8,128)(2,1)} %copy-done.20, bf16[3,128,768]{2,1,0:T(8,128)(2,1)} %collective-permute-done.5.refs_2_, ...), custom_call_target="tpu_custom_call" | custom-call | tf_op jit(solution)/shard_map/pallas_call | solution.py:720
  90.6 4.0 collective-permute-done.10.refs_3_
  96.3 1.8 slice.112
  98.1 1.8 slice.113
  100.0 1.5 collective-permute-start.20
  102.5 12.6 %shard_map.255.refs_14_.refs_2_ = bf16[960,1024]{1,0:T(8,128)(2,1)S(1)} custom-call(s32[3]{0:T(128)S(1)} %fusion.12.counts_ref, bf16[960,3072]{1,0:T(8,128)(2,1)} %get-tuple-element.172.qkv_ref), custom_call_target="tpu_custom_call" | custom-call | tf_op jit(solution)/shard_map/pallas_call | solution.py:85
  117.1 1.6 collective-permute-done.24.refs_12_
  119.3 1.3 constant_dynamic-slice_fusion.2
  120.8 1.5 collective-permute-start.26
  124.2 13.2 %shard_map.256 = (f32[960,1024]{1,0:T(8,128)}, bf16[960,1024]{1,0:T(8,128)(2,1)}, bf16[1024,4096]{1,0:T(8,128)(2,1)}, bf16[1024,1024]{1,0:T(8,128)(2,1)}) custom-call(s32[3]{0:T(128)} %pad_add_fusion.1.place_ref, bf16[128,4096]{1,0:T(8,128)(2,1)} %refs_0_.4, bf16[128,1024]{1,0:T(8,128)(2,1)} %refs_1_.1, bf16[3,128,1280]{2,1,0:T(8,128)(2,1)} %copy-done.18, ...), custom_call_target="tpu_custom_call" | custom-call | tf_op jit(solution)/shard_map/pallas_call | solution.py:720
  137.5 19.3 %shard_map.257 = (bf16[960,4096]{1,0:T(8,128)(2,1)}, bf16[960,4096]{1,0:T(8,128)(2,1)}) custom-call(bf16[960,1024]{1,0:T(8,128)(2,1)} %get-tuple-element.182.a_ref.refs_0_, bf16[1024,4096]{1,0:T(8,128)(2,1)} %get-tuple-element.183.w_ref.up_ref, f32[1,4096]{1,0:T(1,128)} %bitcast.109), custom_call_target="tpu_custom_call" | custom-call | tf_op jit(solution)/shard_map/pallas_call | solution.py:720
  157.5 1.5 collective-permute-start.29
  159.6 13.9 %shard_map.258 = (bf16[4,4,512,256]{3,2,1,0:T(8,128)(2,1)}, bf16[4,4,512,256]{3,2,1,0:T(8,128)(2,1)}) custom-call(s32[3]{0:T(128)} %pad_add_fusion.1.place_ref, bf16[960,4096]{1,0:T(8,128)(2,1)} %get-tuple-element.267.left_ref.h_ref, bf16[960,1024]{1,0:T(8,128)(2,1)} %bitcast.94), custom_call_target="tpu_custom_call" | custom-call | tf_op jit(solution)/shard_map/pallas_call | solution.py:399
  176.7 8.0 %shard_map.259.down_ref.w_ref = bf16[4096,1024]{1,0:T(8,128)(2,1)} custom-call(s32[3]{0:T(128)} %pad_add_fusion.1.place_ref, bf16[512,1024]{1,0:T(8,128)(2,1)} %refs_0_.5, bf16[3,512,256]{2,1,0:T(8,128)(2,1)} %copy-done.19, bf16[3,512,256]{2,1,0:T(8,128)(2,1)} %copy-done.21, bf16[3,512,256]{2,1,0:T(8,128)(2,1)} %copy-done.22, ...), custom_call_target="tpu_custom_call" | custom-call | tf_op jit(solution)/shard_map/pallas_call | solution.py:226
  184.8 4.6 %shard_map.260 = (bf16[2,2,512,256]{3,2,1,0:T(8,128)(2,1)S(1)}, bf16[2,2,512,256]{3,2,1,0:T(8,128)(2,1)}, bf16[2,2,512,256]{3,2,1,0:T(8,128)(2,1)S(1)}, bf16[2,2,512,256]{3,2,1,0:T(8,128)(2,1)S(1)}) custom-call(s32[3]{0:T(128)S(1)} %copy-done.13, bf16[4,4,512,256]{3,2,1,0:T(8,128)(2,1)S(1)} %copy-done.5, bf16[4,4,512,256]{3,2,1,0:T(8,128)(2,1)} %collective-permute-done.35.refs_1_), custom_call_target="tpu_custom_call" | custom-call | tf_op jit(solution)/shard_map/pallas_call | solution.py:495
  189.4 1.5 collective-permute-start.36
  191.4 29.3 %shard_map.261 = (bf16[960,4096]{1,0:T(8,128)(2,1)}, f32[1,4096]{1,0:T(1,128)}, f32[960,1024]{1,0:T(8,128)}, bf16[960,1024]{1,0:T(8,128)(2,1)}, f32[1,1024]{1,0:...) custom-call(bf16[960,1024]{1,0:T(8,128)(2,1)} %bitcast.95, bf16[4096,1024]{1,0:T(8,128)(2,1)} %shard_map.259.down_ref.w_ref, ...), custom_call_target="tpu_custom_call" | custom-call | tf_op jit(solution)/shard_map/pallas_call | solution.py:720
  221.0 1.5 collective-permute-start.38
  223.1 17.5 %shard_map.263 = (bf16[4,4,128,1280]{3,2,1,0:T(8,128)(2,1)}, bf16[4,4,128,1280]{3,2,1,0:T(8,128)(2,1)}) custom-call(s32[3]{0:T(128)} %pad_add_fusion.1.place_ref, bf16[960,1024]{1,0:T(8,128)(2,1)} %get-tuple-element.182.a_ref.refs_0_, bf16[960,4096]{1,0:T(8,128)(2,1)} %get-tuple-element.216.refs_1_, bf16[960,1024]{1,0:T(8,128)(2,1)} %copy-done.2, ...), custom_call_target="tpu_custom_call" | custom-call | tf_op jit(solution)/shard_map/pallas_call | solution.py:399
  241.8 5.9 %shard_map.265.do_ref = bf16[960,1024]{1,0:T(8,128)(2,1)} custom-call(bf16[960,1024]{1,0:T(8,128)(2,1)} %get-tuple-element.220.refs_3_.d_ref, bf16[1024,1024]{1,0:T(8,128)(2,1)} %get-tuple-element.221.w_ref), custom_call_target="tpu_custom_call" | custom-call | tf_op jit(solution)/shard_map/pallas_call | solution.py:720
  247.7 3.0 collective-permute-done.40.refs_1_
  250.7 5.5 %shard_map.266 = (bf16[2,2,128,1280]{3,2,1,0:T(8,128)(2,1)S(1)}, bf16[2,2,128,1280]{3,2,1,0:T(8,128)(2,1)}, bf16[2,2,128,1280]{3,2,1,0:T(8,128)(2,1)S(1)}, bf16[2,2,128,1280]{3,2,1,0:T(8,128)(2,1)}) custom-call(s32[3]{0:T(128)S(1)} %copy-done.14, bf16[4,4,128,1280]{3,2,1,0:T(8,128)(2,1)S(1)} %copy-done.4, ...), custom_call_target="tpu_custom_call" | custom-call | tf_op jit(solution)/shard_map/pallas_call | solution.py:495
  256.2 1.5 collective-permute-start.41
  258.2 24.0 %shard_map.267.refs_1_.d_ref = bf16[960,3072]{1,0:T(8,128)(2,1)} custom-call(s32[3]{0:T(128)S(1)} %fusion.12.counts_ref, bf16[960,3072]{1,0:T(8,128)(2,1)} %get-tuple-element.172.qkv_ref, bf16[960,1024]{1,0:T(8,128)(2,1)S(1)} %copy-done.3), custom_call_target="tpu_custom_call" | custom-call | tf_op jit(solution)/shard_map/pallas_call | solution.py:85
  282.2 5.1 %collective-permute-done.41.ga_ref = bf16[2,2,128,1280]{3,2,1,0:T(8,128)(2,1)} collective-permute-done((bf16[2,2,128,1280]{3,2,1,0:T(8,128)(2,1)}, bf16[2,2,128,1280]{3,2,1,0:T(8,128)(2,1)}, u32[]{:S(2)}, u32[]{:S(2)}) %collective-permute-start.41) | collective-permute-done | bytes 1310752 | tf_op jit(solution)/shard_map/ppermute | solution.py:149
  288.5 1.8 shard_map.268
  291.5 11.5 %shard_map.269 = (bf16[4,4,128,768]{3,2,1,0:T(8,128)(2,1)}, bf16[4,4,128,768]{3,2,1,0:T(8,128)(2,1)}) custom-call(s32[3]{0:T(128)} %pad_add_fusion.1.place_ref, bf16[960,1024]{1,0:T(8,128)(2,1)} %add_convert_fusion.refs_12_.refs_0_, bf16[960,3072]{1,0:T(8,128)(2,1)} %shard_map.267.refs_1_.d_ref), custom_call_target="tpu_custom_call" | custom-call | tf_op jit(solution)/shard_map/pallas_call | solution.py:399
  303.0 3.1 collective-permute-done.43.refs_1_
  307.6 5.9 %collective-permute-done.45.refs_1_ = bf16[4,4,128,768]{3,2,1,0:T(8,128)(2,1)} collective-permute-done((bf16[4,4,128,768]{3,2,1,0:T(8,128)(2,1)}, bf16[4,4,128,768]{3,2,1,0:T(8,128)(2,1)}, u32[]{:S(2)}, u32[]{:S(2)}) %collective-permute-start.45) | collective-permute-done | bytes 3145760 | tf_op jit(solution)/shard_map/ppermute | solution.py:149
  313.5 4.6 %shard_map.271 = (bf16[2,2,128,768]{3,2,1,0:T(8,128)(2,1)S(1)}, bf16[2,2,128,768]{3,2,1,0:T(8,128)(2,1)}, bf16[2,2,128,768]{3,2,1,0:T(8,128)(2,1)S(1)}, bf16[2,2,128,768]{3,2,1,0:T(8,128)(2,1)}) custom-call(s32[3]{0:T(128)S(1)} %copy-done.15, bf16[4,4,128,768]{3,2,1,0:T(8,128)(2,1)S(1)} %copy-done.6, bf16[4,4,128,768]{3,2,1,0:T(8,128)(2,1)} %collective-permute-done.45.refs_1_), custom_call_target="tpu_custom_call" | custom-call | tf_op jit(solution)/shard_map/pallas_call | solution.py:495
  320.5 1.5 collective-permute-start.47
  322.1 15.0 %shard_map.272 = (bf16[960,1024]{1,0:T(8,128)(2,1)}, f32[1,1024]{1,0:T(1,128)}, f32[1,1024]{1,0:T(1,128)}, f32[1,3072]{1,0:T(1,128)}) custom-call(bf16[960,3072]{1,0:T(8,128)(2,1)} %shard_map.267.refs_1_.d_ref, bf16[1024,3072]{1,0:T(8,128)(2,1)} %get-tuple-element.251.w_ref, bf16[960,1024]{1,0:T(8,128)(2,1)} %bitcast.93, ...), custom_call_target="tpu_custom_call" | custom-call | tf_op jit(solution)/shard_map/pallas_call | solution.py:720
  337.8 1.9 collective-permute-done.46.ga_ref
  340.2 1.6 collective-permute-start.48
  341.8 1.4 collective-permute-start.49
  345.4 7.7 %collective-permute-done.48.refs_1_ = bf16[2,128,768]{2,1,0:T(8,128)(2,1)S(1)} collective-permute-done((bf16[2,128,768]{2,1,0:T(8,128)(2,1)S(1)}, bf16[2,128,768]{2,1,0:T(8,128)(2,1)S(1)}, u32[]{:S(2)}, u32[]{:S(2)}) %collective-permute-start.48) | collective-permute-done | bytes 393248 | tf_op jit(solution)/shard_map/ppermute | solution.py:149
  355.1 1.3 collective-permute-start.51
  356.4 2.6 collective-permute-start.52
  359.0 1.4 collective-permute-start.57
  361.0 14.1 %shard_map.275 = bf16[960,1024]{1,0:T(8,128)(2,1)} custom-call(bf16[960,4096]{1,0:T(8,128)(2,1)} %get-tuple-element.267.left_ref.h_ref, bf16[4096,1024]{1,0:T(8,128)(2,1)} %shard_map.259.down_ref.w_ref, f32[960,1024]{1,0:T(8,128)} %get-tuple-element.206.y_ref, f32[1,1024]{1,0:T(1,128)} %bitcast.113), custom_call_target="tpu_custom_call" | custom-call | tf_op jit(solution)/shard_map/pallas_call | solution.py:720
  375.1 1.6 collective-permute-start.59
  376.8 1.5 collective-permute-start.54
  378.9 1.5 collective-permute-start.56
  380.4 6.5 %collective-permute-done.59.refs_3_ = bf16[128,1280]{1,0:T(8,128)(2,1)S(1)} collective-permute-done((bf16[128,1280]{1,0:T(8,128)(2,1)S(1)}, bf16[128,1280]{1,0:T(8,128)(2,1)S(1)}, u32[]{:S(2)}, u32[]{:S(2)}) %collective-permute-start.59) | collective-permute-done | bytes 327712 | tf_op jit(solution)/shard_map/ppermute | solution.py:149
  386.8 2.2 shard_map.276
  390.3 1.5 shard_map.277
  391.7 1.8 shard_map.278
  (242 shorter events, 50.3 us)
Async XLA Ops:
  7.2 56.2 %all-gather.7.cloned.1.call-start = ((), (), s32[]{:S(2)}) async-start(), calls=%async_computation.4 | async-start | bytes 1843200 | tf_op jit(solution)/shard_map/all_gather | solution.py:669
  8.3 15.4 %collective-permute-start = (bf16[128,768]{1,0:T(8,128)(2,1)S(1)}, bf16[128,768]{1,0:T(8,128)(2,1)S(1)}, u32[]{:S(2)}, u32[]{:S(2)}) collective-permute-start(bf16[128,768]{1,0:T(8,128)(2,1)S(1)} %constant_dynamic-slice_fusion.8), channel_id=1, source_target_pairs={{0,8},{1,9},{2,10},{3,11},{4,12},{5,13},{6,14},{7,15},{8,16},{9,17... | collective-permute-start | bytes 589832 | tf_op jit(solution)/shard_map/ppermute | solution.py:149
  10.0 16.8 %collective-permute-start.1 = (bf16[128,768]{1,0:T(8,128)(2,1)S(1)}, bf16[128,768]{1,0:T(8,128)(2,1)S(1)}, u32[]{:S(2)}, u32[]{:S(2)}) collective-permute-start(bf16[128,768]{1,0:T(8,128)(2,1)S(1)} %constant_dynamic-slice_fusion.8), channel_id=1, source_target_pairs={{0,16},{1,17},{2,18},{3,19},{4,20},{5,21},{6,22},{7,23},{8,24},{9,... | collective-permute-start | bytes 589832 | tf_op jit(solution)/shard_map/ppermute | solution.py:149
  11.1 17.5 %collective-permute-start.2 = (bf16[128,768]{1,0:T(8,128)(2,1)S(1)}, bf16[128,768]{1,0:T(8,128)(2,1)S(1)}, u32[]{:S(2)}, u32[]{:S(2)}) collective-permute-start(bf16[128,768]{1,0:T(8,128)(2,1)S(1)} %constant_dynamic-slice_fusion.8), channel_id=1, source_target_pairs={{0,24},{1,25},{2,26},{3,27},{4,28},{5,29},{6,30},{7,31},{8,0},{9,1... | collective-permute-start | bytes 589832 | tf_op jit(solution)/shard_map/ppermute | solution.py:149
  29.2 87.8 %all-gather.9.cloned.1.call-start = ((), (), s32[]{:S(2)}) async-start(), calls=%async_computation.5 | async-start | bytes 1310720 | tf_op jit(solution)/shard_map/all_gather | solution.py:669
  29.2 2.9 collective-permute-start.3
  29.2 2.9 collective-permute-start.4
  34.0 17.7 %collective-permute-start.7 = (bf16[128,4096]{1,0:T(8,128)(2,1)}, bf16[128,4096]{1,0:T(8,128)(2,1)}, u32[]{:S(2)}, u32[]{:S(2)}) collective-permute-start(bf16[128,4096]{1,0:T(8,128)(2,1)} %refs_0_.4), channel_id=1, source_target_pairs={{0,4},{1,5},{2,6},{3,7},{4,0},{5,1},{6,2},{7,3},{8,12},{9,13},{10,... | collective-permute-start | bytes 3145736 | tf_op jit(solution)/shard_map/ppermute | solution.py:149
  34.2 17.5 %collective-permute-start.8 = (bf16[512,1024]{1,0:T(8,128)(2,1)}, bf16[512,1024]{1,0:T(8,128)(2,1)}, u32[]{:S(2)}, u32[]{:S(2)}) collective-permute-start(bf16[512,1024]{1,0:T(8,128)(2,1)} %refs_0_.5), channel_id=1, source_target_pairs={{0,4},{1,5},{2,6},{3,7},{4,0},{5,1},{6,2},{7,3},{8,12},{9,13},{10,... | collective-permute-start | bytes 3145736 | tf_op jit(solution)/shard_map/ppermute | solution.py:149
  35.0 15.5 %collective-permute-start.5 = (bf16[3,128,768]{2,1,0:T(8,128)(2,1)S(1)}, bf16[3,128,768]{2,1,0:T(8,128)(2,1)}, u32[]{:S(2)}, u32[]{:S(2)}) collective-permute-start(bf16[3,128,768]{2,1,0:T(8,128)(2,1)S(1)} %pad_maximum_fusion.2.refs_1_), channel_id=1, source_target_pairs={{0,1},{1,0},{2,3},{3,2},{4,5},{5,4},{6,7},{7,6},{8,9},{9,8},{10,11... | collective-permute-start | bytes 1769480 | tf_op jit(solution)/shard_map/ppermute | solution.py:149
  36.5 15.2 %collective-permute-start.6 = (bf16[3,128,768]{2,1,0:T(8,128)(2,1)S(1)}, bf16[3,128,768]{2,1,0:T(8,128)(2,1)}, u32[]{:S(2)}, u32[]{:S(2)}) collective-permute-start(bf16[3,128,768]{2,1,0:T(8,128)(2,1)S(1)} %pad_maximum_fusion.2.refs_1_), channel_id=1, source_target_pairs={{0,2},{1,3},{2,0},{3,1},{4,6},{5,7},{6,4},{7,5},{8,10},{9,11},{10,... | collective-permute-start | bytes 1769480 | tf_op jit(solution)/shard_map/ppermute | solution.py:149
  38.0 13.7 %collective-permute-start.9 = (bf16[3,128,768]{2,1,0:T(8,128)(2,1)S(1)}, bf16[3,128,768]{2,1,0:T(8,128)(2,1)}, u32[]{:S(2)}, u32[]{:S(2)}) collective-permute-start(bf16[3,128,768]{2,1,0:T(8,128)(2,1)S(1)} %pad_maximum_fusion.2.refs_1_), channel_id=1, source_target_pairs={{0,4},{1,5},{2,6},{3,7},{4,0},{5,1},{6,2},{7,3},{8,12},{9,13},{10,... | collective-permute-start | bytes 1769480 | tf_op jit(solution)/shard_map/ppermute | solution.py:149
  53.4 18.5 %collective-permute-start.12 = (bf16[3,128,768]{2,1,0:T(8,128)(2,1)}, bf16[3,128,768]{2,1,0:T(8,128)(2,1)}, u32[]{:S(2)}, u32[]{:S(2)}) collective-permute-start(bf16[3,128,768]{2,1,0:T(8,128)(2,1)} %collective-permute-done.5.refs_2_), channel_id=1, source_target_pairs={{0,4},{1,5},{2,6},{3,7},{4,0},{5,1},{6,2},{7,3},{8,12},{9,13},{10,... | collective-permute-start | bytes 1769480 | tf_op jit(solution)/shard_map/ppermute | solution.py:149
  55.1 18.2 %collective-permute-start.13 = (bf16[3,128,768]{2,1,0:T(8,128)(2,1)}, bf16[3,128,768]{2,1,0:T(8,128)(2,1)}, u32[]{:S(2)}, u32[]{:S(2)}) collective-permute-start(bf16[3,128,768]{2,1,0:T(8,128)(2,1)} %collective-permute-done.6.refs_3_), channel_id=1, source_target_pairs={{0,4},{1,5},{2,6},{3,7},{4,0},{5,1},{6,2},{7,3},{8,12},{9,13},{10,... | collective-permute-start | bytes 1769480 | tf_op jit(solution)/shard_map/ppermute | solution.py:149
  55.6 14.2 %collective-permute-start.14 = (bf16[3,64,768]{2,1,0:T(8,128)(2,1)}, bf16[3,64,768]{2,1,0:T(8,128)(2,1)}, u32[]{:S(2)}, u32[]{:S(2)}) collective-permute-start(bf16[3,64,768]{2,1,0:T(8,128)(2,1)} %slice.99), channel_id=1, source_target_pairs={{0,2},{1,3},{2,0},{3,1},{4,6},{5,7},{6,4},{7,5},{8,10},{9,11},{10,... | collective-permute-start | bytes 884744 | tf_op jit(solution)/shard_map/ppermute | solution.py:149
  57.1 12.7 %collective-permute-start.15 = (bf16[3,64,768]{2,1,0:T(8,128)(2,1)}, bf16[3,64,768]{2,1,0:T(8,128)(2,1)}, u32[]{:S(2)}, u32[]{:S(2)}) collective-permute-start(bf16[3,64,768]{2,1,0:T(8,128)(2,1)} %slice.100), channel_id=1, source_target_pairs={{0,1},{1,0},{2,3},{3,2},{4,5},{5,4},{6,7},{7,6},{8,9},{9,8},{10,11... | collective-permute-start | bytes 884744 | tf_op jit(solution)/shard_map/ppermute | solution.py:149
  64.3 1.5 collective-permute-start.16
  69.8 3.5 collective-permute-start.17
  70.3 3.0 collective-permute-start.18
  70.4 24.2 %collective-permute-start.10 = (bf16[3,128,1280]{2,1,0:T(8,128)(2,1)S(1)}, bf16[3,128,1280]{2,1,0:T(8,128)(2,1)}, u32[]{:S(2)}, u32[]{:S(2)}) collective-permute-start(bf16[3,128,1280]{2,1,0:T(8,128)(2,1)S(1)} %pad_maximum_fusion.refs_2_), channel_id=1, source_target_pairs={{0,1},{1,0},{2,3},{3,2},{4,5},{5,4},{6,7},{7,6},{8,9},{9,8},{10,11... | collective-permute-start | bytes 2949128 | tf_op jit(solution)/shard_map/ppermute | solution.py:149
  71.9 23.9 %collective-permute-start.11 = (bf16[3,128,1280]{2,1,0:T(8,128)(2,1)S(1)}, bf16[3,128,1280]{2,1,0:T(8,128)(2,1)}, u32[]{:S(2)}, u32[]{:S(2)}) collective-permute-start(bf16[3,128,1280]{2,1,0:T(8,128)(2,1)S(1)} %pad_maximum_fusion.refs_2_), channel_id=1, source_target_pairs={{0,2},{1,3},{2,0},{3,1},{4,6},{5,7},{6,4},{7,5},{8,10},{9,11},{10,... | collective-permute-start | bytes 2949128 | tf_op jit(solution)/shard_map/ppermute | solution.py:149
  73.4 22.4 %collective-permute-start.19 = (bf16[3,128,1280]{2,1,0:T(8,128)(2,1)S(1)}, bf16[3,128,1280]{2,1,0:T(8,128)(2,1)}, u32[]{:S(2)}, u32[]{:S(2)}) collective-permute-start(bf16[3,128,1280]{2,1,0:T(8,128)(2,1)S(1)} %pad_maximum_fusion.refs_2_), channel_id=1, source_target_pairs={{0,4},{1,5},{2,6},{3,7},{4,0},{5,1},{6,2},{7,3},{8,12},{9,13},{10,... | collective-permute-start | bytes 2949128 | tf_op jit(solution)/shard_map/ppermute | solution.py:149
  75.3 207.0 %reduce-scatter.3.cloned.1.call-start = ((), (), s32[]{:S(2)}) async-start(), calls=%async_computation.2 | async-start | bytes 1310720 | tf_op jit(solution)/shard_map/reduce_scatter | solution.py:598
  95.8 20.7 %collective-permute-start.22 = (bf16[3,128,1280]{2,1,0:T(8,128)(2,1)}, bf16[3,128,1280]{2,1,0:T(8,128)(2,1)S(1)}, u32[]{:S(2)}, u32[]{:S(2)}) collective-permute-start(bf16[3,128,1280]{2,1,0:T(8,128)(2,1)} %collective-permute-done.10.refs_3_), channel_id=1, source_target_pairs={{0,4},{1,5},{2,6},{3,7},{4,0},{5,1},{6,2},{7,3},{8,12},{9,13},{10,... | collective-permute-start | bytes 2949128 | tf_op jit(solution)/shard_map/ppermute | solution.py:149
  95.8 20.7 %collective-permute-start.23 = (bf16[3,128,1280]{2,1,0:T(8,128)(2,1)}, bf16[3,128,1280]{2,1,0:T(8,128)(2,1)}, u32[]{:S(2)}, u32[]{:S(2)}) collective-permute-start(bf16[3,128,1280]{2,1,0:T(8,128)(2,1)} %collective-permute-done.11.refs_4_), channel_id=1, source_target_pairs={{0,4},{1,5},{2,6},{3,7},{4,0},{5,1},{6,2},{7,3},{8,12},{9,13},{10,... | collective-permute-start | bytes 2949128 | tf_op jit(solution)/shard_map/ppermute | solution.py:149
  100.0 16.5 %collective-permute-start.20 = (bf16[3,64,1280]{2,1,0:T(8,128)(2,1)}, bf16[3,64,1280]{2,1,0:T(8,128)(2,1)}, u32[]{:S(2)}, u32[]{:S(2)}) collective-permute-start(bf16[3,64,1280]{2,1,0:T(8,128)(2,1)} %slice.112), channel_id=1, source_target_pairs={{0,2},{1,3},{2,0},{3,1},{4,6},{5,7},{6,4},{7,5},{8,10},{9,11},{10,... | collective-permute-start | bytes 1474568 | tf_op jit(solution)/shard_map/ppermute | solution.py:149
  101.4 15.0 %collective-permute-start.21 = (bf16[3,64,1280]{2,1,0:T(8,128)(2,1)}, bf16[3,64,1280]{2,1,0:T(8,128)(2,1)}, u32[]{:S(2)}, u32[]{:S(2)}) collective-permute-start(bf16[3,64,1280]{2,1,0:T(8,128)(2,1)} %slice.113), channel_id=1, source_target_pairs={{0,1},{1,0},{2,3},{3,2},{4,5},{5,4},{6,7},{7,6},{8,9},{9,8},{10,11... | collective-permute-start | bytes 1474568 | tf_op jit(solution)/shard_map/ppermute | solution.py:149
  116.5 2.1 collective-permute-start.24
  116.6 2.8 collective-permute-start.25
  120.8 35.9 %collective-permute-start.26 = (bf16[3,512,256]{2,1,0:T(8,128)(2,1)S(1)}, bf16[3,512,256]{2,1,0:T(8,128)(2,1)S(1)}, u32[]{:S(2)}, u32[]{:S(2)}) collective-permute-start(bf16[3,512,256]{2,1,0:T(8,128)(2,1)S(1)} %pad_maximum_fusion.1.refs_1_), channel_id=1, source_target_pairs={{0,1},{1,0},{2,3},{3,2},{4,5},{5,4},{6,7},{7,6},{8,9},{9,8},{10,11... | collective-permute-start | bytes 2359304 | tf_op jit(solution)/shard_map/ppermute | solution.py:149
  122.3 34.4 %collective-permute-start.27 = (bf16[3,512,256]{2,1,0:T(8,128)(2,1)S(1)}, bf16[3,512,256]{2,1,0:T(8,128)(2,1)S(1)}, u32[]{:S(2)}, u32[]{:S(2)}) collective-permute-start(bf16[3,512,256]{2,1,0:T(8,128)(2,1)S(1)} %pad_maximum_fusion.1.refs_1_), channel_id=1, source_target_pairs={{0,2},{1,3},{2,0},{3,1},{4,6},{5,7},{6,4},{7,5},{8,10},{9,11},{10,... | collective-permute-start | bytes 2359304 | tf_op jit(solution)/shard_map/ppermute | solution.py:149
  122.9 33.9 %collective-permute-start.28 = (bf16[3,512,256]{2,1,0:T(8,128)(2,1)S(1)}, bf16[3,512,256]{2,1,0:T(8,128)(2,1)S(1)}, u32[]{:S(2)}, u32[]{:S(2)}) collective-permute-start(bf16[3,512,256]{2,1,0:T(8,128)(2,1)S(1)} %pad_maximum_fusion.1.refs_1_), channel_id=1, source_target_pairs={{0,4},{1,5},{2,6},{3,7},{4,0},{5,1},{6,2},{7,3},{8,12},{9,13},{10,... | collective-permute-start | bytes 2359304 | tf_op jit(solution)/shard_map/ppermute | solution.py:149
  156.8 16.8 %collective-permute-start.31 = (bf16[3,512,256]{2,1,0:T(8,128)(2,1)S(1)}, bf16[3,512,256]{2,1,0:T(8,128)(2,1)S(1)}, u32[]{:S(2)}, u32[]{:S(2)}) collective-permute-start(bf16[3,512,256]{2,1,0:T(8,128)(2,1)S(1)} %collective-permute-done.26.refs_2_), channel_id=1, source_target_pairs={{0,4},{1,5},{2,6},{3,7},{4,0},{5,1},{6,2},{7,3},{8,12},{9,13},{10,... | collective-permute-start | bytes 2359304 | tf_op jit(solution)/shard_map/ppermute | solution.py:149
  157.3 16.3 %collective-permute-start.32 = (bf16[3,512,256]{2,1,0:T(8,128)(2,1)S(1)}, bf16[3,512,256]{2,1,0:T(8,128)(2,1)S(1)}, u32[]{:S(2)}, u32[]{:S(2)}) collective-permute-start(bf16[3,512,256]{2,1,0:T(8,128)(2,1)S(1)} %collective-permute-done.27.refs_3_), channel_id=1, source_target_pairs={{0,4},{1,5},{2,6},{3,7},{4,0},{5,1},{6,2},{7,3},{8,12},{9,13},{10,... | collective-permute-start | bytes 2359304 | tf_op jit(solution)/shard_map/ppermute | solution.py:149
  157.5 16.1 %collective-permute-start.29 = (bf16[3,256,256]{2,1,0:T(8,128)(2,1)S(1)}, bf16[3,256,256]{2,1,0:T(8,128)(2,1)S(1)}, u32[]{:S(2)}, u32[]{:S(2)}) collective-permute-start(bf16[3,256,256]{2,1,0:T(8,128)(2,1)S(1)} %slice.118), channel_id=1, source_target_pairs={{0,2},{1,3},{2,0},{3,1},{4,6},{5,7},{6,4},{7,5},{8,10},{9,11},{10,... | collective-permute-start | bytes 1179656 | tf_op jit(solution)/shard_map/ppermute | solution.py:149
  159.0 14.5 %collective-permute-start.30 = (bf16[3,256,256]{2,1,0:T(8,128)(2,1)S(1)}, bf16[3,256,256]{2,1,0:T(8,128)(2,1)S(1)}, u32[]{:S(2)}, u32[]{:S(2)}) collective-permute-start(bf16[3,256,256]{2,1,0:T(8,128)(2,1)S(1)} %slice.119), channel_id=1, source_target_pairs={{0,1},{1,0},{2,3},{3,2},{4,5},{5,4},{6,7},{7,6},{8,9},{9,8},{10,11... | collective-permute-start | bytes 1179656 | tf_op jit(solution)/shard_map/ppermute | solution.py:149
  173.6 1.8 collective-permute-start.33
  173.7 2.3 collective-permute-start.34
  176.0 8.7 %collective-permute-start.35 = (bf16[4,4,512,256]{3,2,1,0:T(8,128)(2,1)}, bf16[4,4,512,256]{3,2,1,0:T(8,128)(2,1)}, u32[]{:S(2)}, u32[]{:S(2)}) collective-permute-start(bf16[4,4,512,256]{3,2,1,0:T(8,128)(2,1)} %get-tuple-element.196), channel_id=1, source_target_pairs={{0,4},{1,5},{2,6},{3,7},{4,0},{5,1},{6,2},{7,3},{8,12},{9,13},{10,... | collective-permute-start | bytes 12582920 | tf_op jit(solution)/shard_map/ppermute | solution.py:149
  189.4 31.3 %collective-permute-start.36 = (bf16[2,2,512,256]{3,2,1,0:T(8,128)(2,1)}, bf16[2,2,512,256]{3,2,1,0:T(8,128)(2,1)S(1)}, u32[]{:S(2)}, u32[]{:S(2)}) collective-permute-start(bf16[2,2,512,256]{3,2,1,0:T(8,128)(2,1)} %get-tuple-element.201), channel_id=1, source_target_pairs={{0,1},{1,0},{2,3},{3,2},{4,5},{5,4},{6,7},{7,6},{8,9},{9,8},{10,11... | collective-permute-start | bytes 3145736 | tf_op jit(solution)/shard_map/ppermute | solution.py:149
  190.8 29.9 %collective-permute-start.37 = (bf16[2,2,512,256]{3,2,1,0:T(8,128)(2,1)S(1)}, bf16[2,2,512,256]{3,2,1,0:T(8,128)(2,1)S(1)}, u32[]{:S(2)}, u32[]{:S(2)}) collective-permute-start(bf16[2,2,512,256]{3,2,1,0:T(8,128)(2,1)S(1)} %get-tuple-element.203), channel_id=1, source_target_pairs={{0,2},{1,3},{2,0},{3,1},{4,6},{5,7},{6,4},{7,5},{8,10},{9,11},{10,... | collective-permute-start | bytes 3145736 | tf_op jit(solution)/shard_map/ppermute | solution.py:149
  221.0 19.6 %collective-permute-start.38 = (bf16[2,512,256]{2,1,0:T(8,128)(2,1)S(1)}, bf16[2,512,256]{2,1,0:T(8,128)(2,1)S(1)}, u32[]{:S(2)}, u32[]{:S(2)}) collective-permute-start(bf16[2,512,256]{2,1,0:T(8,128)(2,1)S(1)} %get-tuple-element.212), channel_id=1, source_target_pairs={{0,2},{1,3},{2,0},{3,1},{4,6},{5,7},{6,4},{7,5},{8,10},{9,11},{10,... | collective-permute-start | bytes 1572872 | tf_op jit(solution)/shard_map/ppermute | solution.py:149
  222.5 18.1 %collective-permute-start.39 = (bf16[2,512,256]{2,1,0:T(8,128)(2,1)S(1)}, bf16[2,512,256]{2,1,0:T(8,128)(2,1)S(1)}, u32[]{:S(2)}, u32[]{:S(2)}) collective-permute-start(bf16[2,512,256]{2,1,0:T(8,128)(2,1)S(1)} %get-tuple-element.213), channel_id=1, source_target_pairs={{0,1},{1,0},{2,3},{3,2},{4,5},{5,4},{6,7},{7,6},{8,9},{9,8},{10,11... | collective-permute-start | bytes 1572872 | tf_op jit(solution)/shard_map/ppermute | solution.py:149
  241.7 9.0 %collective-permute-start.40 = (bf16[4,4,128,1280]{3,2,1,0:T(8,128)(2,1)}, bf16[4,4,128,1280]{3,2,1,0:T(8,128)(2,1)}, u32[]{:S(2)}, u32[]{:S(2)}) collective-permute-start(bf16[4,4,128,1280]{3,2,1,0:T(8,128)(2,1)} %get-tuple-element.223), channel_id=1, source_target_pairs={{0,4},{1,5},{2,6},{3,7},{4,0},{5,1},{6,2},{7,3},{8,12},{9,13},{10,... | collective-permute-start | bytes 15728648 | tf_op jit(solution)/shard_map/ppermute | solution.py:149
  241.8 117.2 %reduce-scatter.5.cloned.1.call-start = ((), (), s32[]{:S(2)}) async-start(), calls=%async_computation.3 | async-start | bytes 1638400 | tf_op jit(solution)/shard_map/reduce_scatter | solution.py:598
  256.2 31.1 %collective-permute-start.41 = (bf16[2,2,128,1280]{3,2,1,0:T(8,128)(2,1)}, bf16[2,2,128,1280]{3,2,1,0:T(8,128)(2,1)}, u32[]{:S(2)}, u32[]{:S(2)}) collective-permute-start(bf16[2,2,128,1280]{3,2,1,0:T(8,128)(2,1)} %get-tuple-element.227), channel_id=1, source_target_pairs={{0,1},{1,0},{2,3},{3,2},{4,5},{5,4},{6,7},{7,6},{8,9},{9,8},{10,11... | collective-permute-start | bytes 3932168 | tf_op jit(solution)/shard_map/ppermute | solution.py:149
  257.7 30.9 %collective-permute-start.42 = (bf16[2,2,128,1280]{3,2,1,0:T(8,128)(2,1)}, bf16[2,2,128,1280]{3,2,1,0:T(8,128)(2,1)}, u32[]{:S(2)}, u32[]{:S(2)}) collective-permute-start(bf16[2,2,128,1280]{3,2,1,0:T(8,128)(2,1)} %get-tuple-element.229), channel_id=1, source_target_pairs={{0,2},{1,3},{2,0},{3,1},{4,6},{5,7},{6,4},{7,5},{8,10},{9,11},{10,... | collective-permute-start | bytes 3932168 | tf_op jit(solution)/shard_map/ppermute | solution.py:149
  290.4 15.7 %collective-permute-start.43 = (bf16[2,128,1280]{2,1,0:T(8,128)(2,1)S(1)}, bf16[2,128,1280]{2,1,0:T(8,128)(2,1)S(1)}, u32[]{:S(2)}, u32[]{:S(2)}) collective-permute-start(bf16[2,128,1280]{2,1,0:T(8,128)(2,1)S(1)} %get-tuple-element.235), channel_id=1, source_target_pairs={{0,2},{1,3},{2,0},{3,1},{4,6},{5,7},{6,4},{7,5},{8,10},{9,11},{10,... | collective-permute-start | bytes 1966088 | tf_op jit(solution)/shard_map/ppermute | solution.py:149
  291.0 15.3 %collective-permute-start.44 = (bf16[2,128,1280]{2,1,0:T(8,128)(2,1)S(1)}, bf16[2,128,1280]{2,1,0:T(8,128)(2,1)S(1)}, u32[]{:S(2)}, u32[]{:S(2)}) collective-permute-start(bf16[2,128,1280]{2,1,0:T(8,128)(2,1)S(1)} %get-tuple-element.237), channel_id=1, source_target_pairs={{0,1},{1,0},{2,3},{3,2},{4,5},{5,4},{6,7},{7,6},{8,9},{9,8},{10,11... | collective-permute-start | bytes 1966088 | tf_op jit(solution)/shard_map/ppermute | solution.py:149
  307.5 6.0 %collective-permute-start.45 = (bf16[4,4,128,768]{3,2,1,0:T(8,128)(2,1)}, bf16[4,4,128,768]{3,2,1,0:T(8,128)(2,1)}, u32[]{:S(2)}, u32[]{:S(2)}) collective-permute-start(bf16[4,4,128,768]{3,2,1,0:T(8,128)(2,1)} %get-tuple-element.243), channel_id=1, source_target_pairs={{0,4},{1,5},{2,6},{3,7},{4,0},{5,1},{6,2},{7,3},{8,12},{9,13},{10,... | collective-permute-start | bytes 9437192 | tf_op jit(solution)/shard_map/ppermute | solution.py:149
  307.5 81.5 %all-gather.11.cloned.1.call-start = ((), (), s32[]{:S(2)}) async-start(), calls=%async_computation.6 | async-start | bytes 1310720 | tf_op jit(solution)/shard_map/all_gather | solution.py:604
  319.9 19.8 %collective-permute-start.46 = (bf16[2,2,128,768]{3,2,1,0:T(8,128)(2,1)}, bf16[2,2,128,768]{3,2,1,0:T(8,128)(2,1)S(1)}, u32[]{:S(2)}, u32[]{:S(2)}) collective-permute-start(bf16[2,2,128,768]{3,2,1,0:T(8,128)(2,1)} %get-tuple-element.247), channel_id=1, source_target_pairs={{0,1},{1,0},{2,3},{3,2},{4,5},{5,4},{6,7},{7,6},{8,9},{9,8},{10,11... | collective-permute-start | bytes 2359304 | tf_op jit(solution)/shard_map/ppermute | solution.py:149
  320.5 19.5 %collective-permute-start.47 = (bf16[2,2,128,768]{3,2,1,0:T(8,128)(2,1)}, bf16[2,2,128,768]{3,2,1,0:T(8,128)(2,1)S(1)}, u32[]{:S(2)}, u32[]{:S(2)}) collective-permute-start(bf16[2,2,128,768]{3,2,1,0:T(8,128)(2,1)} %get-tuple-element.248), channel_id=1, source_target_pairs={{0,2},{1,3},{2,0},{3,1},{4,6},{5,7},{6,4},{7,5},{8,10},{9,11},{10,... | collective-permute-start | bytes 2359304 | tf_op jit(solution)/shard_map/ppermute | solution.py:149
  340.2 12.9 %collective-permute-start.48 = (bf16[2,128,768]{2,1,0:T(8,128)(2,1)S(1)}, bf16[2,128,768]{2,1,0:T(8,128)(2,1)S(1)}, u32[]{:S(2)}, u32[]{:S(2)}) collective-permute-start(bf16[2,128,768]{2,1,0:T(8,128)(2,1)S(1)} %get-tuple-element.256), channel_id=1, source_target_pairs={{0,2},{1,3},{2,0},{3,1},{4,6},{5,7},{6,4},{7,5},{8,10},{9,11},{10,... | collective-permute-start | bytes 1179656 | tf_op jit(solution)/shard_map/ppermute | solution.py:149
  341.8 12.6 %collective-permute-start.49 = (bf16[2,128,768]{2,1,0:T(8,128)(2,1)S(1)}, bf16[2,128,768]{2,1,0:T(8,128)(2,1)S(1)}, u32[]{:S(2)}, u32[]{:S(2)}) collective-permute-start(bf16[2,128,768]{2,1,0:T(8,128)(2,1)S(1)} %get-tuple-element.258), channel_id=1, source_target_pairs={{0,1},{1,0},{2,3},{3,2},{4,5},{5,4},{6,7},{7,6},{8,9},{9,8},{10,11... | collective-permute-start | bytes 1179656 | tf_op jit(solution)/shard_map/ppermute | solution.py:149
  355.1 20.0 %collective-permute-start.51 = (bf16[144,768]{1,0:T(8,128)(2,1)S(1)}, bf16[144,768]{1,0:T(8,128)(2,1)S(1)}, u32[]{:S(2)}, u32[]{:S(2)}) collective-permute-start(bf16[144,768]{1,0:T(8,128)(2,1)S(1)} %get-tuple-element.268), channel_id=1, source_target_pairs={{0,8},{1,9},{2,10},{3,11},{4,12},{5,13},{6,14},{7,15},{8,16},{9,17... | collective-permute-start | bytes 663560 | tf_op jit(solution)/shard_map/ppermute | solution.py:149
  356.4 20.3 %collective-permute-start.52 = (bf16[144,768]{1,0:T(8,128)(2,1)S(1)}, bf16[144,768]{1,0:T(8,128)(2,1)S(1)}, u32[]{:S(2)}, u32[]{:S(2)}) collective-permute-start(bf16[144,768]{1,0:T(8,128)(2,1)S(1)} %get-tuple-element.269), channel_id=1, source_target_pairs={{0,16},{1,17},{2,18},{3,19},{4,20},{5,21},{6,22},{7,23},{8,24},{9,... | collective-permute-start | bytes 663560 | tf_op jit(solution)/shard_map/ppermute | solution.py:149
  359.0 17.7 %collective-permute-start.53 = (bf16[144,768]{1,0:T(8,128)(2,1)S(1)}, bf16[144,768]{1,0:T(8,128)(2,1)S(1)}, u32[]{:S(2)}, u32[]{:S(2)}) collective-permute-start(bf16[144,768]{1,0:T(8,128)(2,1)S(1)} %get-tuple-element.270), channel_id=1, source_target_pairs={{0,24},{1,25},{2,26},{3,27},{4,28},{5,29},{6,30},{7,31},{8,0},{9,1... | collective-permute-start | bytes 663560 | tf_op jit(solution)/shard_map/ppermute | solution.py:149
  359.0 19.9 %collective-permute-start.57 = (bf16[128,1280]{1,0:T(8,128)(2,1)}, bf16[128,1280]{1,0:T(8,128)(2,1)S(1)}, u32[]{:S(2)}, u32[]{:S(2)}) collective-permute-start(bf16[128,1280]{1,0:T(8,128)(2,1)} %bitcast.88), channel_id=1, source_target_pairs={{0,1},{1,0},{2,3},{3,2},{4,5},{5,4},{6,7},{7,6},{8,9},{9,8},{10,11... | collective-permute-start | bytes 983048 | tf_op jit(solution)/shard_map/ppermute | solution.py:149
  360.4 20.0 %collective-permute-start.58 = (bf16[128,1280]{1,0:T(8,128)(2,1)}, bf16[128,1280]{1,0:T(8,128)(2,1)S(1)}, u32[]{:S(2)}, u32[]{:S(2)}) collective-permute-start(bf16[128,1280]{1,0:T(8,128)(2,1)} %bitcast.89), channel_id=1, source_target_pairs={{0,2},{1,3},{2,0},{3,1},{4,6},{5,7},{6,4},{7,5},{8,10},{9,11},{10,... | collective-permute-start | bytes 983048 | tf_op jit(solution)/shard_map/ppermute | solution.py:149
  375.1 11.7 %collective-permute-start.59 = (bf16[128,1280]{1,0:T(8,128)(2,1)S(1)}, bf16[128,1280]{1,0:T(8,128)(2,1)S(1)}, u32[]{:S(2)}, u32[]{:S(2)}) collective-permute-start(bf16[128,1280]{1,0:T(8,128)(2,1)S(1)} %bitcast.90), channel_id=1, source_target_pairs={{0,3},{1,2},{2,1},{3,0},{4,7},{5,6},{6,5},{7,4},{8,11},{9,10},{10,... | collective-permute-start | bytes 983048 | tf_op jit(solution)/shard_map/ppermute | solution.py:149
  376.8 14.9 %collective-permute-start.54 = (bf16[144,768]{1,0:T(8,128)(2,1)S(1)}, bf16[144,768]{1,0:T(8,128)(2,1)S(1)}, u32[]{:S(2)}, u32[]{:S(2)}) collective-permute-start(bf16[144,768]{1,0:T(8,128)(2,1)S(1)} %add_convert_fusion.1.refs_0_), channel_id=1, source_target_pairs={{0,1},{1,0},{2,3},{3,2},{4,5},{5,4},{6,7},{7,6},{8,9},{9,8},{10,11... | collective-permute-start | bytes 663560 | tf_op jit(solution)/shard_map/ppermute | solution.py:149
  378.3 13.4 %collective-permute-start.55 = (bf16[144,768]{1,0:T(8,128)(2,1)S(1)}, bf16[144,768]{1,0:T(8,128)(2,1)S(1)}, u32[]{:S(2)}, u32[]{:S(2)}) collective-permute-start(bf16[144,768]{1,0:T(8,128)(2,1)S(1)} %add_convert_fusion.1.refs_0_), channel_id=1, source_target_pairs={{0,2},{1,3},{2,0},{3,1},{4,6},{5,7},{6,4},{7,5},{8,10},{9,11},{10,... | collective-permute-start | bytes 663560 | tf_op jit(solution)/shard_map/ppermute | solution.py:149
  378.9 12.8 %collective-permute-start.56 = (bf16[144,768]{1,0:T(8,128)(2,1)S(1)}, bf16[144,768]{1,0:T(8,128)(2,1)S(1)}, u32[]{:S(2)}, u32[]{:S(2)}) collective-permute-start(bf16[144,768]{1,0:T(8,128)(2,1)S(1)} %add_convert_fusion.1.refs_0_), channel_id=1, source_target_pairs={{0,3},{1,2},{2,1},{3,0},{4,7},{5,6},{6,5},{7,4},{8,11},{9,10},{10,... | collective-permute-start | bytes 663560 | tf_op jit(solution)/shard_map/ppermute | solution.py:149
  (46 other events, 594.3 us)
Sparse Core Ops, SparseCore 0:
  28.7 34.7 all-gather.6
  75.4 26.6 all-gather.8
  241.9 24.1 reduce-scatter.2
  307.6 28.4 reduce-scatter.4
  338.0 33.0 all-gather.10

commit v5 on v4

--- a/solution.py
+++ b/solution.py
@@ -287,111 +287,109 @@
     rows, width = a.shape
     wide = owns[0][0].shape[1]
     steps = wide // TILE
-    unit = wide // 4
 
     def kernel(place_ref, *refs):
-        ins, (a_ref, b_ref, out_ref, w_ref, held, sems, done) = refs[: len(flat)], refs[len(flat) :]
+        ins, refs = refs[: len(flat)], refs[len(flat) :]
+        a_ref, b_ref, y_ref, qkv_ref, out_ref, qkv, out, sems, done = refs
         step = pl.program_id(0)
-        (copies,) = pieces_to(place_ref, ins, [unit], [held], sems)
-        whole_copy = pltpu.make_async_copy(held, w_ref, done.at[0])
+        qkv_copies, out_copies = pieces_to(
+            place_ref, ins, [wide // 4, width // 4], [qkv, out], sems
+        )
+        qkv_whole = pltpu.make_async_copy(qkv, qkv_ref, done.at[0])
+        out_whole = pltpu.make_async_copy(out, out_ref, done.at[1])
 
         @pl.when(step == 0)
         def _():
-            for copy in copies:
+            for copy in qkv_copies + out_copies:
                 copy.start()
-            for copy in copies:
+            for copy in qkv_copies:
                 copy.wait()
-            whole_copy.start()
-
-        w = held[:, pl.ds(pl.multiple_of(step * TILE, TILE), TILE)]
-        out_ref[...] = (nn(a_ref[...], w) + b_ref[...]).astype(BF)
+            qkv_whole.start()
+
+        @pl.when(step == 1)
+        def _():
+            for copy in out_copies:
+                copy.wait()
+            out_whole.start()
+
+        w = qkv[:, pl.ds(pl.multiple_of(step * TILE, TILE), TILE)]
+        y_ref[...] = (nn(a_ref[...], w) + b_ref[...]).astype(BF)
 
         @pl.when(step == steps - 1)
         def _():
-            whole_copy.wait()
-
+            qkv_whole.wait()
+            out_whole.wait()
+
+    far = pl.BlockSpec(memory_space=pltpu.HBM)
     return call(
         kernel,
         (steps,),
         [pl.BlockSpec(memory_space=pltpu.SMEM)]
         + [pl.BlockSpec(memory_space=pl.ANY)] * len(flat)
         + [whole(a), columns_of(1, TILE)],
-        [columns_of(rows, TILE), pl.BlockSpec(memory_space=pltpu.HBM)],
-        [struct(rows, wide), struct(width, wide)],
-        [
-            pltpu.VMEM((width, wide), BF),
-            pltpu.SemaphoreType.DMA((piece_count(pieces, 1),)),
-            pltpu.SemaphoreType.DMA((1,)),
-        ],
-        (where, *flat, a, bias[None]),
-    )
-
-
-def assembled_middle(where, owns, pieces, o, x, bias, gain, shift):
-    flat = [*owns[0], *pieces[0], *owns[1], *pieces[1]]
-    rows, width = x.shape
-    wide = owns[0][0].shape[1]
-    height = rows // 4
-
-    def kernel(place_ref, *refs):
-        ins, refs = refs[: len(flat)], refs[len(flat) :]
-        o_ref, x_ref, b_ref, gain_ref, shift_ref, y_ref, a_ref, up_ref, out_ref = refs[:9]
-        up, out, sems, done = refs[9:]
-        step = pl.program_id(0)
-        up_copies, out_copies = pieces_to(
-            place_ref, ins, [wide // 4, width // 4], [up, out], sems
-        )
-        up_whole = pltpu.make_async_copy(up, up_ref, done.at[0])
-        out_whole = pltpu.make_async_copy(out, out_ref, done.at[1])
-
-        @pl.when(step == 0)
-        def _():
-            for copy in out_copies + up_copies:
-                copy.start()
-            for copy in out_copies:
-                copy.wait()
-            out_whole.start()
-
-        @pl.when(step == 1)
-        def _():
-            for copy in up_copies:
-                copy.wait()
-            up_whole.start()
-
-        y = nn(o_ref[...], out[...]) + x_ref[...].astype(F32) + b_ref[...]
-        y_ref[...] = y
-        unit, _ = normal(y)
-        a_ref[...] = (unit * gain_ref[...] + shift_ref[...]).astype(BF)
-
-        @pl.when(step == 3)
-        def _():
-            out_whole.wait()
-            up_whole.wait()
-
-    tile = rows_of(height, width)
-    vectors = [bias[None], gain[None], shift[None]]
-    far = pl.BlockSpec(memory_space=pltpu.HBM)
-    return call(
-        kernel,
-        (4,),
-        [pl.BlockSpec(memory_space=pltpu.SMEM)]
-        + [pl.BlockSpec(memory_space=pl.ANY)] * len(flat)
-        + [tile, tile]
-        + [whole(v) for v in vectors],
-        [tile, tile, far, far],
-        [
-            struct(rows, width, dtype=F32),
-            struct(rows, width),
-            struct(width, wide),
-            struct(width, width),
-        ],
+        [columns_of(rows, TILE), far, far],
+        [struct(rows, wide), struct(width, wide), struct(width, width)],
         [
             pltpu.VMEM((width, wide), BF),
             pltpu.VMEM((width, width), BF),
             pltpu.SemaphoreType.DMA((piece_count(pieces, 2),)),
             pltpu.SemaphoreType.DMA((2,)),
         ],
-        (where, *flat, o, x, *vectors),
+        (where, *flat, a, bias[None]),
+    )
+
+
+def assembled_middle(where, owns, pieces, o, w, x, bias, gain, shift):
+    flat = [*owns[0], *pieces[0], *owns[1], *pieces[1]]
+    rows, width = x.shape
+    wide = owns[0][0].shape[1]
+    height = rows // 4
+
+    def kernel(place_ref, *refs):
+        ins, refs = refs[: len(flat)], refs[len(flat) :]
+        o_ref, w_ref, x_ref, b_ref, gain_ref, shift_ref, y_ref, a_ref, up_ref = refs[:9]
+        up, sems, done = refs[9:]
+        step = pl.program_id(0)
+        (copies,) = pieces_to(place_ref, ins, [wide // 4], [up], sems)
+        up_whole = pltpu.make_async_copy(up, up_ref, done.at[0])
+
+        @pl.when(step == 0)
+        def _():
+            for copy in copies:
+                copy.start()
+
+        @pl.when(step == 1)
+        def _():
+            for copy in copies:
+                copy.wait()
+            up_whole.start()
+
+        y = nn(o_ref[...], w_ref[...]) + x_ref[...].astype(F32) + b_ref[...]
+        y_ref[...] = y
+        unit, _ = normal(y)
+        a_ref[...] = (unit * gain_ref[...] + shift_ref[...]).astype(BF)
+
+        @pl.when(step == 3)
+        def _():
+            up_whole.wait()
+
+    tile = rows_of(height, width)
+    vectors = [bias[None], gain[None], shift[None]]
+    return call(
+        kernel,
+        (4,),
+        [pl.BlockSpec(memory_space=pltpu.SMEM)]
+        + [pl.BlockSpec(memory_space=pl.ANY)] * len(flat)
+        + [tile, whole(w), tile]
+        + [whole(v) for v in vectors],
+        [tile, tile, pl.BlockSpec(memory_space=pltpu.HBM)],
+        [struct(rows, width, dtype=F32), struct(rows, width), struct(width, wide)],
+        [
+            pltpu.VMEM((width, wide), BF),
+            pltpu.SemaphoreType.DMA((piece_count(pieces, 1),)),
+            pltpu.SemaphoreType.DMA((1,)),
+        ],
+        (where, *flat, o, w, x, *vectors),
     )
 
 
@@ -406,7 +404,7 @@
             scratch_shapes=scratch,
         ),
         out_shape=[jax.ShapeDtypeStruct(shape, BF) for shape in shapes],
-        compiler_params=pltpu.CompilerParams(vmem_limit_bytes=56 * 2**20),
+        compiler_params=pltpu.CompilerParams(vmem_limit_bytes=50 * 2**20),
     )(where, *arrays)
 
 
@@ -1027,13 +1025,14 @@
         return lax.dynamic_slice_in_dim(w, me * (w.shape[1] // 4), w.shape[1] // 4, axis=1)
 
     depth = w_qkv.shape[0]
-    first = unit(w_qkv)
+    first = jnp.concatenate([unit(w_qkv), unit(w_out)], axis=1)
     z_first = along_z(first)
     packed = jnp.pad(packed_rows(vectors), ((0, 4), (0, 0))).reshape(2, width)
-    packed = jnp.pad(packed, ((0, 14), (0, width // 4)))
-    packed = jnp.concatenate([jnp.concatenate([unit(w_up), unit(w_out)], axis=1), packed])
-    z_second = column(after(packed, z_first))
-    z_third = column(unit(w_down))
+    packed = jnp.pad(packed, ((0, 14), (0, 0)))
+    packed = jnp.concatenate([unit(w_up), packed])
+    third = unit(w_down)
+    z_second = column(after(packed, z_first, third))
+    z_third = column(third)
     unit1, _ = normal(x)
     sum_down = jnp.sum(g_low.astype(F32), axis=0)
 
@@ -1056,8 +1055,8 @@
     near_first = [col_first] + two_first + cross_first
     far_first = far_first + to_partner(cross_first)
     far_second = to_partner(after([col_second], far_first))
-    qkv, qkv_w = assembled_project(
-        where, [[w_qkv], far_own[:1]], [near_first, far_first], a1, bias_qkv
+    qkv, qkv_w, out_w = assembled_project(
+        where, [[w_qkv, w_out], far_own[:2]], [near_first, far_first], a1, bias_qkv
     )
     two_second, far_second = after((two_second, far_second), qkv)
     cross_second = across(edges(two_second))
@@ -1066,11 +1065,12 @@
     cross_second, far_second = after((cross_second, far_second), o)
     near_second = [col_second] + two_second + cross_second
     far_second = far_second + to_partner(cross_second)
-    y1, a2, up_w, out_w = assembled_middle(
+    y1, a2, up_w = assembled_middle(
         where,
-        [[w_up, w_out], [far_own[2], far_own[1]]],
+        [[w_up], far_own[2:3]],
         [near_second, far_second],
         o,
+        out_w,
         x_low,
         bias_out,
         gain2,
@@ -1150,8 +1150,8 @@
     share_qkv = add(*after(column_qkv, activations))
     shares_qkv = shares(share_qkv)
     (s_down,) = joined(after(from_down, share_qkv), [width // 4])
-    s_up, s_out = spread(where, after(shares_up, share_qkv), [wide // 4, width // 4])
-    s_qkv, own = spread(where, after(shares_qkv, s_up, s_down), [width * 3 // 4], 2)
+    s_up, s_out = spread(where, after(shares_up, s_down), [wide // 4, width // 4])
+    s_qkv, own = spread(where, after(shares_qkv, s_up), [width * 3 // 4], 2)
     own = own.reshape(-1)
     return activations, input_grad, s_qkv, s_out, s_up, s_down, own_parts(own, sums)
 

time: 410 us -> 408 us (level)
    ppermute x60, waiting for transfers between devices: 74.2 us -> 83.6 us  [send(): return lax.ppermute(value, ('fsdp', 'seq'), pairs)]
    all_gather x2, waiting for transfers between devices: 5.81 us -> 0.01 us  [column(): lax.all_gather(mine, 'fsdp', axis=0, tiled=False, axis_index_groups=colum...]
    unnamed x95 -> x101, local copies, waits for them, and re-layouts: 7.55 us -> 9.63 us
  transfers between devices with their start and end apart: 65 -> 65, of which waited for: 25 -> 30; matrix products, arithmetic and copies ran while one was open for 6% -> 6% of each run, Pallas kernels for 53% -> 52%
where the time goes in v5:
time: 408 us; the launch traced here: 400 us
  Pallas kernels  220 us (54%)
  waiting for transfers between devices  83.7 us (21%)
  starting transfers between devices  44.2 us (11%)
  local copies, waits for them, and re-layouts  27.2 us (7%)
  between operations  14.8 us (4%)
  other arithmetic  10.4 us (3%)
    pallas_call x7, Pallas kernels, call(): pl.pallas_call(kernel, grid=grid, in_specs=in_specs, out_specs=out_specs,...  109 us
    ppermute x60, waiting for transfers between devices, send(): return lax.ppermute(value, ('fsdp', 'seq'), pairs)  83.6 us
    ppermute x60, starting transfers between devices, send(): return lax.ppermute(value, ('fsdp', 'seq'), pairs)  43.8 us
    pallas_call x3, Pallas kernels, wgrad_call(): pl.pallas_call(kernel, grid_spec=pltpu.PrefetchScalarGridSpec(num_scalar_...  40.3 us
    pallas_call x2, Pallas kernels, per_image(): pl.pallas_call(kernel, grid_spec=pltpu.PrefetchScalarGridSpec(num_scalar_...  36.6 us
    pallas_call x3, Pallas kernels, chip_sum(): pl.pallas_call(kernel, grid_spec=pltpu.PrefetchScalarGridSpec(num_scalar_...  14.6 us
    unnamed x101, local copies, waits for them, and re-layouts  9.63 us
  transfers between devices with their start and end apart: 65, of which 30 were waited for; matrix products, arithmetic and copies ran while one was open for 6% of the time, Pallas kernels for 52%

profile of v5, /device:TPU:8, one launch (start us, length us, event | category | flops | bytes accessed | tf_op | source)
XLA Modules:
  0.0 399.9 jit_solution(6576552820804480912)
XLA Ops:
  9.2 1.6 collective-permute-start
  11.9 1.9 collective-permute-start.2
  13.9 1.7 constant_dynamic-slice_fusion.7
  18.1 10.7 %collective-permute-done = bf16[128,1024]{1,0:T(8,128)(2,1)S(1)} collective-permute-done((bf16[128,1024]{1,0:T(8,128)(2,1)S(1)}, bf16[128,1024]{1,0:T(8,128)(2,1)S(1)}, u32[]{:S(2)}, u32[]{:S(2)}) %collective-permute-start) | collective-permute-done | bytes 262176 | tf_op jit(solution)/shard_map/ppermute | solution.py:149
  28.8 4.5 %collective-permute-done.1 = bf16[128,1024]{1,0:T(8,128)(2,1)S(1)} collective-permute-done((bf16[128,1024]{1,0:T(8,128)(2,1)S(1)}, bf16[128,1024]{1,0:T(8,128)(2,1)S(1)}, u32[]{:S(2)}, u32[]{:S(2)}) %collective-permute-start.1) | collective-permute-done | bytes 262176 | tf_op jit(solution)/shard_map/ppermute | solution.py:149
  33.3 1.9 collective-permute-done.2
  35.3 1.7 collective-permute-done.4.refs_8_
  40.0 1.5 collective-permute-start.5
  41.5 1.5 collective-permute-start.6
  44.6 15.2 %collective-permute-done.5.refs_3_ = bf16[3,128,1024]{2,1,0:T(8,128)(2,1)} collective-permute-done((bf16[3,128,1024]{2,1,0:T(8,128)(2,1)S(1)}, bf16[3,128,1024]{2,1,0:T(8,128)(2,1)}, u32[]{:S(2)}, u32[]{:S(2)}) %collective-permute-start.5) | collective-permute-done | bytes 786464 | tf_op jit(solution)/shard_map/ppermute | solution.py:149
  61.0 2.1 slice.99
  63.0 1.8 slice.100
  65.3 1.5 collective-permute-start.14
  71.0 2.1 add_convert_fusion.refs_14_.refs_0_
  73.1 3.6 collective-permute-done.14.refs_5_
  76.6 1.2 collective-permute-done.15.refs_6_
  82.7 13.6 %shard_map.254 = (bf16[960,3072]{1,0:T(8,128)(2,1)}, bf16[1024,3072]{1,0:T(8,128)(2,1)}, bf16[1024,1024]{1,0:T(8,128)(2,1)}) custom-call(s32[3]{0:T(128)} %pad_add_fusion.1.place_ref, bf16[128,3072]{1,0:T(8,128)(2,1)} %refs_0_.3, bf16[128,1024]{1,0:T(8,128)(2,1)} %refs_1_.1, bf16[3,128,1024]{2,1,0:T(8,128)(2,1)} %copy-done.23, ...), custom_call_target="tpu_custom_call" | custom-call | tf_op jit(solution)/shard_map/pallas_call | solution.py:718
  96.3 1.5 collective-permute-done.10.refs_2_
  97.9 1.7 collective-permute-done.11.refs_3_
  103.5 12.6 %shard_map.255.refs_12_.refs_2_ = bf16[960,1024]{1,0:T(8,128)(2,1)S(1)} custom-call(s32[3]{0:T(128)S(1)} %fusion.12.counts_ref, bf16[960,3072]{1,0:T(8,128)(2,1)} %get-tuple-element.173.qkv_ref), custom_call_target="tpu_custom_call" | custom-call | tf_op jit(solution)/shard_map/pallas_call | solution.py:85
  116.1 1.3 copy-done.4
  118.0 1.4 collective-permute-done.24.refs_10_
  120.0 1.3 constant_dynamic-slice_fusion.2
  121.4 1.6 collective-permute-start.26
  123.0 1.5 collective-permute-start.27
  125.8 12.2 %shard_map.256 = (f32[960,1024]{1,0:T(8,128)}, bf16[960,1024]{1,0:T(8,128)(2,1)}, bf16[1024,4096]{1,0:T(8,128)(2,1)}) custom-call(s32[3]{0:T(128)} %pad_add_fusion.1.place_ref, bf16[128,4096]{1,0:T(8,128)(2,1)} %refs_0_.4, bf16[3,128,1024]{2,1,0:T(8,128)(2,1)} %copy-done.24, bf16[3,128,1024]{2,1,0:T(8,128)(2,1)} %copy-done.27, ...), custom_call_target="tpu_custom_call" | custom-call | tf_op jit(solution)/shard_map/pallas_call | solution.py:718
  138.0 19.3 %shard_map.257 = (bf16[960,4096]{1,0:T(8,128)(2,1)}, bf16[960,4096]{1,0:T(8,128)(2,1)}) custom-call(bf16[960,1024]{1,0:T(8,128)(2,1)} %get-tuple-element.183.a_ref.refs_0_, bf16[1024,4096]{1,0:T(8,128)(2,1)} %get-tuple-element.184.w_ref.up_ref, f32[1,4096]{1,0:T(1,128)} %bitcast.108), custom_call_target="tpu_custom_call" | custom-call | tf_op jit(solution)/shard_map/pallas_call | solution.py:718
  159.2 13.2 %shard_map.258 = (bf16[4,4,512,256]{3,2,1,0:T(8,128)(2,1)}, bf16[4,4,512,256]{3,2,1,0:T(8,128)(2,1)}) custom-call(s32[3]{0:T(128)S(1)} %copy-done.19, bf16[960,4096]{1,0:T(8,128)(2,1)} %get-tuple-element.267.left_ref.h_ref, bf16[960,1024]{1,0:T(8,128)(2,1)S(1)} %bitcast.88), custom_call_target="tpu_custom_call" | custom-call | tf_op jit(solution)/shard_map/pallas_call | solution.py:397
  175.7 8.0 %shard_map.259.down_ref.w_ref = bf16[4096,1024]{1,0:T(8,128)(2,1)} custom-call(s32[3]{0:T(128)} %pad_add_fusion.1.place_ref, bf16[512,1024]{1,0:T(8,128)(2,1)} %refs_0_.5, bf16[3,512,256]{2,1,0:T(8,128)(2,1)} %copy-done.22, bf16[3,512,256]{2,1,0:T(8,128)(2,1)} %copy-done.25, bf16[3,512,256]{2,1,0:T(8,128)(2,1)} %copy-done.26, ...), custom_call_target="tpu_custom_call" | custom-call | tf_op jit(solution)/shard_map/pallas_call | solution.py:226
  183.7 4.6 %shard_map.260 = (bf16[2,2,512,256]{3,2,1,0:T(8,128)(2,1)S(1)}, bf16[2,2,512,256]{3,2,1,0:T(8,128)(2,1)}, bf16[2,2,512,256]{3,2,1,0:T(8,128)(2,1)S(1)}, bf16[2,2,512,256]{3,2,1,0:T(8,128)(2,1)S(1)}) custom-call(s32[3]{0:T(128)S(1)} %copy-done.20, bf16[4,4,512,256]{3,2,1,0:T(8,128)(2,1)S(1)} %copy-done.9, bf16[4,4,512,256]{3,2,1,0:T(8,128)(2,1)} %collective-permute-done.35.refs_1_), custom_call_target="tpu_custom_call" | custom-call | tf_op jit(solution)/shard_map/pallas_call | solution.py:493
  188.3 1.5 collective-permute-start.36
  189.8 1.5 collective-permute-start.37
  191.3 29.3 %shard_map.261 = (bf16[960,4096]{1,0:T(8,128)(2,1)}, f32[1,4096]{1,0:T(1,128)}, f32[960,1024]{1,0:T(8,128)}, bf16[960,1024]{1,0:T(8,128)(2,1)}, f32[1,1024]{1,0:...) custom-call(bf16[960,1024]{1,0:T(8,128)(2,1)} %bitcast.87, bf16[4096,1024]{1,0:T(8,128)(2,1)} %shard_map.259.down_ref.w_ref, ...), custom_call_target="tpu_custom_call" | custom-call | tf_op jit(solution)/shard_map/pallas_call | solution.py:718
  222.8 16.3 %shard_map.263 = (bf16[4,4,128,1280]{3,2,1,0:T(8,128)(2,1)}, bf16[4,4,128,1280]{3,2,1,0:T(8,128)(2,1)}) custom-call(s32[3]{0:T(128)S(1)} %copy-done.20, bf16[960,1024]{1,0:T(8,128)(2,1)S(1)} %copy-done.6, bf16[960,4096]{1,0:T(8,128)(2,1)} %get-tuple-element.217.refs_1_, bf16[960,1024]{1,0:T(8,128)(2,1)S(1)} %copy-done.5, ...), custom_call_target="tpu_custom_call" | custom-call | tf_op jit(solution)/shard_map/pallas_call | solution.py:397
  240.3 5.9 %shard_map.265.do_ref = bf16[960,1024]{1,0:T(8,128)(2,1)} custom-call(bf16[960,1024]{1,0:T(8,128)(2,1)} %get-tuple-element.221.refs_3_.d_ref, bf16[1024,1024]{1,0:T(8,128)(2,1)} %get-tuple-element.180.refs_13_.w_ref), custom_call_target="tpu_custom_call" | custom-call | tf_op jit(solution)/shard_map/pallas_call | solution.py:718
  246.2 3.0 collective-permute-done.40.refs_1_
  249.2 5.5 %shard_map.266 = (bf16[2,2,128,1280]{3,2,1,0:T(8,128)(2,1)S(1)}, bf16[2,2,128,1280]{3,2,1,0:T(8,128)(2,1)}, bf16[2,2,128,1280]{3,2,1,0:T(8,128)(2,1)S(1)}, bf16[2,2,128,1280]{3,2,1,0:T(8,128)(2,1)}) custom-call(s32[3]{0:T(128)S(1)} %copy-done.20, bf16[4,4,128,1280]{3,2,1,0:T(8,128)(2,1)S(1)} %copy-done.8, ...), custom_call_target="tpu_custom_call" | custom-call | tf_op jit(solution)/shard_map/pallas_call | solution.py:493
  256.6 1.5 collective-permute-start.42
  258.1 23.9 %shard_map.267.refs_1_.d_ref = bf16[960,3072]{1,0:T(8,128)(2,1)} custom-call(s32[3]{0:T(128)S(1)} %fusion.12.counts_ref, bf16[960,3072]{1,0:T(8,128)(2,1)} %get-tuple-element.173.qkv_ref, bf16[960,1024]{1,0:T(8,128)(2,1)S(1)} %copy-done.7), custom_call_target="tpu_custom_call" | custom-call | tf_op jit(solution)/shard_map/pallas_call | solution.py:85
  282.0 4.9 %collective-permute-done.41.ga_ref = bf16[2,2,128,1280]{3,2,1,0:T(8,128)(2,1)} collective-permute-done((bf16[2,2,128,1280]{3,2,1,0:T(8,128)(2,1)}, bf16[2,2,128,1280]{3,2,1,0:T(8,128)(2,1)}, u32[]{:S(2)}, u32[]{:S(2)}) %collective-permute-start.41) | collective-permute-done | bytes 1310752 | tf_op jit(solution)/shard_map/ppermute | solution.py:149
  287.4 1.3 copy-done.12
  288.7 1.8 shard_map.268
  290.6 1.6 collective-permute-start.43
  292.7 10.7 %shard_map.269 = (bf16[4,4,128,768]{3,2,1,0:T(8,128)(2,1)}, bf16[4,4,128,768]{3,2,1,0:T(8,128)(2,1)}) custom-call(s32[3]{0:T(128)S(1)} %copy-done.20, bf16[960,1024]{1,0:T(8,128)(2,1)S(1)} %copy-done.3, bf16[960,3072]{1,0:T(8,128)(2,1)} %shard_map.267.refs_1_.d_ref), custom_call_target="tpu_custom_call" | custom-call | tf_op jit(solution)/shard_map/pallas_call | solution.py:397
  303.4 2.8 collective-permute-done.43.refs_1_
  306.2 1.2 collective-permute-done.44.refs_3_
  308.7 5.9 %collective-permute-done.45.refs_1_ = bf16[4,4,128,768]{3,2,1,0:T(8,128)(2,1)} collective-permute-done((bf16[4,4,128,768]{3,2,1,0:T(8,128)(2,1)}, bf16[4,4,128,768]{3,2,1,0:T(8,128)(2,1)}, u32[]{:S(2)}, u32[]{:S(2)}) %collective-permute-start.45) | collective-permute-done | bytes 3145760 | tf_op jit(solution)/shard_map/ppermute | solution.py:149
  314.6 4.6 %shard_map.271 = (bf16[2,2,128,768]{3,2,1,0:T(8,128)(2,1)S(1)}, bf16[2,2,128,768]{3,2,1,0:T(8,128)(2,1)}, bf16[2,2,128,768]{3,2,1,0:T(8,128)(2,1)S(1)}, bf16[2,2,128,768]{3,2,1,0:T(8,128)(2,1)}) custom-call(s32[3]{0:T(128)S(1)} %copy-done.20, bf16[4,4,128,768]{3,2,1,0:T(8,128)(2,1)S(1)} %copy-done.10, bf16[4,4,128,768]{3,2,1,0:T(8,128)(2,1)} %collective-permute-done.45.refs_1_), custom_call_target="tpu_custom_call" | custom-call | tf_op jit(solution)/shard_map/pallas_call | solution.py:493
  322.9 15.0 %shard_map.272 = (bf16[960,1024]{1,0:T(8,128)(2,1)}, f32[1,1024]{1,0:T(1,128)}, f32[1,1024]{1,0:T(1,128)}, f32[1,3072]{1,0:T(1,128)}) custom-call(bf16[960,3072]{1,0:T(8,128)(2,1)} %shard_map.267.refs_1_.d_ref, bf16[1024,3072]{1,0:T(8,128)(2,1)} %get-tuple-element.251.w_ref, bf16[960,1024]{1,0:T(8,128)(2,1)} %bitcast.95, ...), custom_call_target="tpu_custom_call" | custom-call | tf_op jit(solution)/shard_map/pallas_call | solution.py:718
  338.6 2.3 collective-permute-done.46.ga_ref
  341.4 1.3 collective-permute-start.48
  345.5 8.8 %collective-permute-done.48.refs_1_ = bf16[2,128,768]{2,1,0:T(8,128)(2,1)S(1)} collective-permute-done((bf16[2,128,768]{2,1,0:T(8,128)(2,1)S(1)}, bf16[2,128,768]{2,1,0:T(8,128)(2,1)S(1)}, u32[]{:S(2)}, u32[]{:S(2)}) %collective-permute-start.48) | collective-permute-done | bytes 393248 | tf_op jit(solution)/shard_map/ppermute | solution.py:149
  355.9 1.7 collective-permute-start.52
  357.6 1.9 collective-permute-start.53
  360.4 1.4 collective-permute-start.58
  361.8 14.1 %shard_map.275 = bf16[960,1024]{1,0:T(8,128)(2,1)} custom-call(bf16[960,4096]{1,0:T(8,128)(2,1)} %get-tuple-element.267.left_ref.h_ref, bf16[4096,1024]{1,0:T(8,128)(2,1)} %shard_map.259.down_ref.w_ref, f32[960,1024]{1,0:T(8,128)} %get-tuple-element.207.y_ref, f32[1,1024]{1,0:T(1,128)} %bitcast.112), custom_call_target="tpu_custom_call" | custom-call | tf_op jit(solution)/shard_map/pallas_call | solution.py:718
  375.9 1.4 collective-permute-start.59
  378.3 1.4 collective-permute-start.55
  379.7 1.3 collective-permute-start.56
  382.2 1.5 shard_map.276
  383.7 1.3 collective-permute-done.59.refs_3_
  385.0 2.2 shard_map.277
  387.2 2.4 collective-permute-done.56.refs_3_
  389.6 1.8 shard_map.278
  (249 shorter events, 53.8 us)
Async XLA Ops:
  7.2 60.2 %all-gather.7.cloned.1.call-start = ((), (), s32[]{:S(2)}) async-start(), calls=%async_computation.4 | async-start | bytes 1474560 | tf_op jit(solution)/shard_map/all_gather | solution.py:667
  9.2 19.6 %collective-permute-start = (bf16[128,1024]{1,0:T(8,128)(2,1)S(1)}, bf16[128,1024]{1,0:T(8,128)(2,1)S(1)}, u32[]{:S(2)}, u32[]{:S(2)}) collective-permute-start(bf16[128,1024]{1,0:T(8,128)(2,1)S(1)} %pad_maximum_fusion.3), channel_id=1, source_target_pairs={{0,8},{1,9},{2,10},{3,11},{4,12},{5,13},{6,14},{7,15},{8,16},{9,17... | collective-permute-start | bytes 786440 | tf_op jit(solution)/shard_map/ppermute | solution.py:149
  10.8 22.4 %collective-permute-start.1 = (bf16[128,1024]{1,0:T(8,128)(2,1)S(1)}, bf16[128,1024]{1,0:T(8,128)(2,1)S(1)}, u32[]{:S(2)}, u32[]{:S(2)}) collective-permute-start(bf16[128,1024]{1,0:T(8,128)(2,1)S(1)} %pad_maximum_fusion.3), channel_id=1, source_target_pairs={{0,16},{1,17},{2,18},{3,19},{4,20},{5,21},{6,22},{7,23},{8,24},{9,... | collective-permute-start | bytes 786440 | tf_op jit(solution)/shard_map/ppermute | solution.py:149
  11.9 23.2 %collective-permute-start.2 = (bf16[128,1024]{1,0:T(8,128)(2,1)S(1)}, bf16[128,1024]{1,0:T(8,128)(2,1)}, u32[]{:S(2)}, u32[]{:S(2)}) collective-permute-start(bf16[128,1024]{1,0:T(8,128)(2,1)S(1)} %pad_maximum_fusion.3), channel_id=1, source_target_pairs={{0,24},{1,25},{2,26},{3,27},{4,28},{5,29},{6,30},{7,31},{8,0},{9,1... | collective-permute-start | bytes 786440 | tf_op jit(solution)/shard_map/ppermute | solution.py:149
  13.9 23.2 %collective-permute-start.3 = (bf16[128,3072]{1,0:T(8,128)(2,1)}, bf16[128,3072]{1,0:T(8,128)(2,1)S(1)}, u32[]{:S(2)}, u32[]{:S(2)}) collective-permute-start(bf16[128,3072]{1,0:T(8,128)(2,1)} %refs_0_.3), channel_id=1, source_target_pairs={{0,4},{1,5},{2,6},{3,7},{4,0},{5,1},{6,2},{7,3},{8,12},{9,13},{10,... | collective-permute-start | bytes 2359304 | tf_op jit(solution)/shard_map/ppermute | solution.py:149
  35.2 82.8 %all-gather.9.cloned.1.call-start = ((), (), s32[]{:S(2)}) async-start(), calls=%async_computation.5 | async-start | bytes 1310720 | tf_op jit(solution)/shard_map/all_gather | solution.py:667
  35.2 1.8 collective-permute-start.4
  39.1 21.9 %collective-permute-start.7 = (bf16[128,4096]{1,0:T(8,128)(2,1)}, bf16[128,4096]{1,0:T(8,128)(2,1)}, u32[]{:S(2)}, u32[]{:S(2)}) collective-permute-start(bf16[128,4096]{1,0:T(8,128)(2,1)} %refs_0_.4), channel_id=1, source_target_pairs={{0,4},{1,5},{2,6},{3,7},{4,0},{5,1},{6,2},{7,3},{8,12},{9,13},{10,... | collective-permute-start | bytes 3145736 | tf_op jit(solution)/shard_map/ppermute | solution.py:149
  39.3 21.7 %collective-permute-start.8 = (bf16[512,1024]{1,0:T(8,128)(2,1)}, bf16[512,1024]{1,0:T(8,128)(2,1)}, u32[]{:S(2)}, u32[]{:S(2)}) collective-permute-start(bf16[512,1024]{1,0:T(8,128)(2,1)} %refs_0_.5), channel_id=1, source_target_pairs={{0,4},{1,5},{2,6},{3,7},{4,0},{5,1},{6,2},{7,3},{8,12},{9,13},{10,... | collective-permute-start | bytes 3145736 | tf_op jit(solution)/shard_map/ppermute | solution.py:149
  40.0 19.7 %collective-permute-start.5 = (bf16[3,128,1024]{2,1,0:T(8,128)(2,1)S(1)}, bf16[3,128,1024]{2,1,0:T(8,128)(2,1)}, u32[]{:S(2)}, u32[]{:S(2)}) collective-permute-start(bf16[3,128,1024]{2,1,0:T(8,128)(2,1)S(1)} %pad_maximum_fusion.refs_2_), channel_id=1, source_target_pairs={{0,1},{1,0},{2,3},{3,2},{4,5},{5,4},{6,7},{7,6},{8,9},{9,8},{10,11... | collective-permute-start | bytes 2359304 | tf_op jit(solution)/shard_map/ppermute | solution.py:149
  41.5 19.4 %collective-permute-start.6 = (bf16[3,128,1024]{2,1,0:T(8,128)(2,1)S(1)}, bf16[3,128,1024]{2,1,0:T(8,128)(2,1)}, u32[]{:S(2)}, u32[]{:S(2)}) collective-permute-start(bf16[3,128,1024]{2,1,0:T(8,128)(2,1)S(1)} %pad_maximum_fusion.refs_2_), channel_id=1, source_target_pairs={{0,2},{1,3},{2,0},{3,1},{4,6},{5,7},{6,4},{7,5},{8,10},{9,11},{10,... | collective-permute-start | bytes 2359304 | tf_op jit(solution)/shard_map/ppermute | solution.py:149
  43.1 17.9 %collective-permute-start.9 = (bf16[3,128,1024]{2,1,0:T(8,128)(2,1)S(1)}, bf16[3,128,1024]{2,1,0:T(8,128)(2,1)S(1)}, u32[]{:S(2)}, u32[]{:S(2)}) collective-permute-start(bf16[3,128,1024]{2,1,0:T(8,128)(2,1)S(1)} %pad_maximum_fusion.refs_2_), channel_id=1, source_target_pairs={{0,4},{1,5},{2,6},{3,7},{4,0},{5,1},{6,2},{7,3},{8,12},{9,13},{10,... | collective-permute-start | bytes 2359304 | tf_op jit(solution)/shard_map/ppermute | solution.py:149
  63.0 17.4 %collective-permute-start.12 = (bf16[3,128,1024]{2,1,0:T(8,128)(2,1)}, bf16[3,128,1024]{2,1,0:T(8,128)(2,1)}, u32[]{:S(2)}, u32[]{:S(2)}) collective-permute-start(bf16[3,128,1024]{2,1,0:T(8,128)(2,1)} %collective-permute-done.5.refs_3_), channel_id=1, source_target_pairs={{0,4},{1,5},{2,6},{3,7},{4,0},{5,1},{6,2},{7,3},{8,12},{9,13},{10,... | collective-permute-start | bytes 2359304 | tf_op jit(solution)/shard_map/ppermute | solution.py:149
  64.8 15.6 %collective-permute-start.13 = (bf16[3,128,1024]{2,1,0:T(8,128)(2,1)}, bf16[3,128,1024]{2,1,0:T(8,128)(2,1)}, u32[]{:S(2)}, u32[]{:S(2)}) collective-permute-start(bf16[3,128,1024]{2,1,0:T(8,128)(2,1)} %collective-permute-done.6.refs_4_), channel_id=1, source_target_pairs={{0,4},{1,5},{2,6},{3,7},{4,0},{5,1},{6,2},{7,3},{8,12},{9,13},{10,... | collective-permute-start | bytes 2359304 | tf_op jit(solution)/shard_map/ppermute | solution.py:149
  65.3 11.3 %collective-permute-start.14 = (bf16[3,64,1024]{2,1,0:T(8,128)(2,1)}, bf16[3,64,1024]{2,1,0:T(8,128)(2,1)}, u32[]{:S(2)}, u32[]{:S(2)}) collective-permute-start(bf16[3,64,1024]{2,1,0:T(8,128)(2,1)} %slice.99), channel_id=1, source_target_pairs={{0,2},{1,3},{2,0},{3,1},{4,6},{5,7},{6,4},{7,5},{8,10},{9,11},{10,... | collective-permute-start | bytes 1179656 | tf_op jit(solution)/shard_map/ppermute | solution.py:149
  66.8 11.1 %collective-permute-start.15 = (bf16[3,64,1024]{2,1,0:T(8,128)(2,1)}, bf16[3,64,1024]{2,1,0:T(8,128)(2,1)}, u32[]{:S(2)}, u32[]{:S(2)}) collective-permute-start(bf16[3,64,1024]{2,1,0:T(8,128)(2,1)} %slice.100), channel_id=1, source_target_pairs={{0,1},{1,0},{2,3},{3,2},{4,5},{5,4},{6,7},{7,6},{8,9},{9,8},{10,11... | collective-permute-start | bytes 1179656 | tf_op jit(solution)/shard_map/ppermute | solution.py:149
  68.2 1.4 collective-permute-start.16
  77.9 1.9 collective-permute-start.17
  77.9 2.5 collective-permute-start.18
  78.4 19.4 %collective-permute-start.10 = (bf16[3,128,1024]{2,1,0:T(8,128)(2,1)S(1)}, bf16[3,128,1024]{2,1,0:T(8,128)(2,1)S(1)}, u32[]{:S(2)}, u32[]{:S(2)}) collective-permute-start(bf16[3,128,1024]{2,1,0:T(8,128)(2,1)S(1)} %pad_maximum_fusion.1.refs_1_), channel_id=1, source_target_pairs={{0,1},{1,0},{2,3},{3,2},{4,5},{5,4},{6,7},{7,6},{8,9},{9,8},{10,11... | collective-permute-start | bytes 2359304 | tf_op jit(solution)/shard_map/ppermute | solution.py:149
  79.8 19.7 %collective-permute-start.11 = (bf16[3,128,1024]{2,1,0:T(8,128)(2,1)S(1)}, bf16[3,128,1024]{2,1,0:T(8,128)(2,1)}, u32[]{:S(2)}, u32[]{:S(2)}) collective-permute-start(bf16[3,128,1024]{2,1,0:T(8,128)(2,1)S(1)} %pad_maximum_fusion.1.refs_1_), channel_id=1, source_target_pairs={{0,2},{1,3},{2,0},{3,1},{4,6},{5,7},{6,4},{7,5},{8,10},{9,11},{10,... | collective-permute-start | bytes 2359304 | tf_op jit(solution)/shard_map/ppermute | solution.py:149
  80.4 19.1 %collective-permute-start.19 = (bf16[3,128,1024]{2,1,0:T(8,128)(2,1)S(1)}, bf16[3,128,1024]{2,1,0:T(8,128)(2,1)}, u32[]{:S(2)}, u32[]{:S(2)}) collective-permute-start(bf16[3,128,1024]{2,1,0:T(8,128)(2,1)S(1)} %pad_maximum_fusion.1.refs_1_), channel_id=1, source_target_pairs={{0,4},{1,5},{2,6},{3,7},{4,0},{5,1},{6,2},{7,3},{8,12},{9,13},{10,... | collective-permute-start | bytes 2359304 | tf_op jit(solution)/shard_map/ppermute | solution.py:149
  80.6 201.4 %reduce-scatter.3.cloned.1.call-start = ((), (), s32[]{:S(2)}) async-start(), calls=%async_computation.2 | async-start | bytes 1310720 | tf_op jit(solution)/shard_map/reduce_scatter | solution.py:596
  99.5 17.9 %collective-permute-start.22 = (bf16[3,128,1024]{2,1,0:T(8,128)(2,1)S(1)}, bf16[3,128,1024]{2,1,0:T(8,128)(2,1)}, u32[]{:S(2)}, u32[]{:S(2)}) collective-permute-start(bf16[3,128,1024]{2,1,0:T(8,128)(2,1)S(1)} %collective-permute-done.10.refs_2_), channel_id=1, source_target_pairs={{0,4},{1,5},{2,6},{3,7},{4,0},{5,1},{6,2},{7,3},{8,12},{9,13},{10,... | collective-permute-start | bytes 2359304 | tf_op jit(solution)/shard_map/ppermute | solution.py:149
  99.5 17.9 %collective-permute-start.23 = (bf16[3,128,1024]{2,1,0:T(8,128)(2,1)}, bf16[3,128,1024]{2,1,0:T(8,128)(2,1)}, u32[]{:S(2)}, u32[]{:S(2)}) collective-permute-start(bf16[3,128,1024]{2,1,0:T(8,128)(2,1)} %collective-permute-done.11.refs_3_), channel_id=1, source_target_pairs={{0,4},{1,5},{2,6},{3,7},{4,0},{5,1},{6,2},{7,3},{8,12},{9,13},{10,... | collective-permute-start | bytes 2359304 | tf_op jit(solution)/shard_map/ppermute | solution.py:149
  101.8 15.6 %collective-permute-start.20 = (bf16[3,64,1024]{2,1,0:T(8,128)(2,1)}, bf16[3,64,1024]{2,1,0:T(8,128)(2,1)}, u32[]{:S(2)}, u32[]{:S(2)}) collective-permute-start(bf16[3,64,1024]{2,1,0:T(8,128)(2,1)} %slice.112), channel_id=1, source_target_pairs={{0,2},{1,3},{2,0},{3,1},{4,6},{5,7},{6,4},{7,5},{8,10},{9,11},{10,... | collective-permute-start | bytes 1179656 | tf_op jit(solution)/shard_map/ppermute | solution.py:149
  102.4 15.0 %collective-permute-start.21 = (bf16[3,64,1024]{2,1,0:T(8,128)(2,1)S(1)}, bf16[3,64,1024]{2,1,0:T(8,128)(2,1)}, u32[]{:S(2)}, u32[]{:S(2)}) collective-permute-start(bf16[3,64,1024]{2,1,0:T(8,128)(2,1)S(1)} %slice.113), channel_id=1, source_target_pairs={{0,1},{1,0},{2,3},{3,2},{4,5},{5,4},{6,7},{7,6},{8,9},{9,8},{10,11... | collective-permute-start | bytes 1179656 | tf_op jit(solution)/shard_map/ppermute | solution.py:149
  117.4 2.0 collective-permute-start.24
  117.5 2.5 collective-permute-start.25
  121.4 35.9 %collective-permute-start.26 = (bf16[3,512,256]{2,1,0:T(8,128)(2,1)S(1)}, bf16[3,512,256]{2,1,0:T(8,128)(2,1)S(1)}, u32[]{:S(2)}, u32[]{:S(2)}) collective-permute-start(bf16[3,512,256]{2,1,0:T(8,128)(2,1)S(1)} %pad_maximum_fusion.2.refs_1_), channel_id=1, source_target_pairs={{0,1},{1,0},{2,3},{3,2},{4,5},{5,4},{6,7},{7,6},{8,9},{9,8},{10,11... | collective-permute-start | bytes 2359304 | tf_op jit(solution)/shard_map/ppermute | solution.py:149
  123.0 34.3 %collective-permute-start.27 = (bf16[3,512,256]{2,1,0:T(8,128)(2,1)S(1)}, bf16[3,512,256]{2,1,0:T(8,128)(2,1)S(1)}, u32[]{:S(2)}, u32[]{:S(2)}) collective-permute-start(bf16[3,512,256]{2,1,0:T(8,128)(2,1)S(1)} %pad_maximum_fusion.2.refs_1_), channel_id=1, source_target_pairs={{0,2},{1,3},{2,0},{3,1},{4,6},{5,7},{6,4},{7,5},{8,10},{9,11},{10,... | collective-permute-start | bytes 2359304 | tf_op jit(solution)/shard_map/ppermute | solution.py:149
  124.5 32.9 %collective-permute-start.28 = (bf16[3,512,256]{2,1,0:T(8,128)(2,1)S(1)}, bf16[3,512,256]{2,1,0:T(8,128)(2,1)S(1)}, u32[]{:S(2)}, u32[]{:S(2)}) collective-permute-start(bf16[3,512,256]{2,1,0:T(8,128)(2,1)S(1)} %pad_maximum_fusion.2.refs_1_), channel_id=1, source_target_pairs={{0,4},{1,5},{2,6},{3,7},{4,0},{5,1},{6,2},{7,3},{8,12},{9,13},{10,... | collective-permute-start | bytes 2359304 | tf_op jit(solution)/shard_map/ppermute | solution.py:149
  157.4 15.2 %collective-permute-start.31 = (bf16[3,512,256]{2,1,0:T(8,128)(2,1)S(1)}, bf16[3,512,256]{2,1,0:T(8,128)(2,1)S(1)}, u32[]{:S(2)}, u32[]{:S(2)}) collective-permute-start(bf16[3,512,256]{2,1,0:T(8,128)(2,1)S(1)} %collective-permute-done.26.refs_2_), channel_id=1, source_target_pairs={{0,4},{1,5},{2,6},{3,7},{4,0},{5,1},{6,2},{7,3},{8,12},{9,13},{10,... | collective-permute-start | bytes 2359304 | tf_op jit(solution)/shard_map/ppermute | solution.py:149
  157.9 14.6 %collective-permute-start.32 = (bf16[3,512,256]{2,1,0:T(8,128)(2,1)S(1)}, bf16[3,512,256]{2,1,0:T(8,128)(2,1)S(1)}, u32[]{:S(2)}, u32[]{:S(2)}) collective-permute-start(bf16[3,512,256]{2,1,0:T(8,128)(2,1)S(1)} %collective-permute-done.27.refs_3_), channel_id=1, source_target_pairs={{0,4},{1,5},{2,6},{3,7},{4,0},{5,1},{6,2},{7,3},{8,12},{9,13},{10,... | collective-permute-start | bytes 2359304 | tf_op jit(solution)/shard_map/ppermute | solution.py:149
  158.1 14.4 %collective-permute-start.29 = (bf16[3,256,256]{2,1,0:T(8,128)(2,1)S(1)}, bf16[3,256,256]{2,1,0:T(8,128)(2,1)S(1)}, u32[]{:S(2)}, u32[]{:S(2)}) collective-permute-start(bf16[3,256,256]{2,1,0:T(8,128)(2,1)S(1)} %slice.118), channel_id=1, source_target_pairs={{0,2},{1,3},{2,0},{3,1},{4,6},{5,7},{6,4},{7,5},{8,10},{9,11},{10,... | collective-permute-start | bytes 1179656 | tf_op jit(solution)/shard_map/ppermute | solution.py:149
  158.7 13.8 %collective-permute-start.30 = (bf16[3,256,256]{2,1,0:T(8,128)(2,1)S(1)}, bf16[3,256,256]{2,1,0:T(8,128)(2,1)S(1)}, u32[]{:S(2)}, u32[]{:S(2)}) collective-permute-start(bf16[3,256,256]{2,1,0:T(8,128)(2,1)S(1)} %slice.119), channel_id=1, source_target_pairs={{0,1},{1,0},{2,3},{3,2},{4,5},{5,4},{6,7},{7,6},{8,9},{9,8},{10,11... | collective-permute-start | bytes 1179656 | tf_op jit(solution)/shard_map/ppermute | solution.py:149
  172.6 1.8 collective-permute-start.33
  172.6 2.3 collective-permute-start.34
  174.9 8.7 %collective-permute-start.35 = (bf16[4,4,512,256]{3,2,1,0:T(8,128)(2,1)}, bf16[4,4,512,256]{3,2,1,0:T(8,128)(2,1)}, u32[]{:S(2)}, u32[]{:S(2)}) collective-permute-start(bf16[4,4,512,256]{3,2,1,0:T(8,128)(2,1)} %get-tuple-element.197), channel_id=1, source_target_pairs={{0,4},{1,5},{2,6},{3,7},{4,0},{5,1},{6,2},{7,3},{8,12},{9,13},{10,... | collective-permute-start | bytes 12582920 | tf_op jit(solution)/shard_map/ppermute | solution.py:149
  188.3 32.4 %collective-permute-start.36 = (bf16[2,2,512,256]{3,2,1,0:T(8,128)(2,1)}, bf16[2,2,512,256]{3,2,1,0:T(8,128)(2,1)S(1)}, u32[]{:S(2)}, u32[]{:S(2)}) collective-permute-start(bf16[2,2,512,256]{3,2,1,0:T(8,128)(2,1)} %get-tuple-element.202), channel_id=1, source_target_pairs={{0,1},{1,0},{2,3},{3,2},{4,5},{5,4},{6,7},{7,6},{8,9},{9,8},{10,11... | collective-permute-start | bytes 3145736 | tf_op jit(solution)/shard_map/ppermute | solution.py:149
  189.8 30.9 %collective-permute-start.37 = (bf16[2,2,512,256]{3,2,1,0:T(8,128)(2,1)S(1)}, bf16[2,2,512,256]{3,2,1,0:T(8,128)(2,1)S(1)}, u32[]{:S(2)}, u32[]{:S(2)}) collective-permute-start(bf16[2,2,512,256]{3,2,1,0:T(8,128)(2,1)S(1)} %get-tuple-element.204), channel_id=1, source_target_pairs={{0,2},{1,3},{2,0},{3,1},{4,6},{5,7},{6,4},{7,5},{8,10},{9,11},{10,... | collective-permute-start | bytes 3145736 | tf_op jit(solution)/shard_map/ppermute | solution.py:149
  221.0 18.1 %collective-permute-start.38 = (bf16[2,512,256]{2,1,0:T(8,128)(2,1)S(1)}, bf16[2,512,256]{2,1,0:T(8,128)(2,1)S(1)}, u32[]{:S(2)}, u32[]{:S(2)}) collective-permute-start(bf16[2,512,256]{2,1,0:T(8,128)(2,1)S(1)} %get-tuple-element.213), channel_id=1, source_target_pairs={{0,2},{1,3},{2,0},{3,1},{4,6},{5,7},{6,4},{7,5},{8,10},{9,11},{10,... | collective-permute-start | bytes 1572872 | tf_op jit(solution)/shard_map/ppermute | solution.py:149
  221.6 17.5 %collective-permute-start.39 = (bf16[2,512,256]{2,1,0:T(8,128)(2,1)S(1)}, bf16[2,512,256]{2,1,0:T(8,128)(2,1)S(1)}, u32[]{:S(2)}, u32[]{:S(2)}) collective-permute-start(bf16[2,512,256]{2,1,0:T(8,128)(2,1)S(1)} %get-tuple-element.214), channel_id=1, source_target_pairs={{0,1},{1,0},{2,3},{3,2},{4,5},{5,4},{6,7},{7,6},{8,9},{9,8},{10,11... | collective-permute-start | bytes 1572872 | tf_op jit(solution)/shard_map/ppermute | solution.py:149
  240.2 9.0 %collective-permute-start.40 = (bf16[4,4,128,1280]{3,2,1,0:T(8,128)(2,1)}, bf16[4,4,128,1280]{3,2,1,0:T(8,128)(2,1)}, u32[]{:S(2)}, u32[]{:S(2)}) collective-permute-start(bf16[4,4,128,1280]{3,2,1,0:T(8,128)(2,1)} %get-tuple-element.223), channel_id=1, source_target_pairs={{0,4},{1,5},{2,6},{3,7},{4,0},{5,1},{6,2},{7,3},{8,12},{9,13},{10,... | collective-permute-start | bytes 15728648 | tf_op jit(solution)/shard_map/ppermute | solution.py:149
  240.3 119.3 %reduce-scatter.5.cloned.1.call-start = ((), (), s32[]{:S(2)}) async-start(), calls=%async_computation.3 | async-start | bytes 1638400 | tf_op jit(solution)/shard_map/reduce_scatter | solution.py:596
  255.7 31.1 %collective-permute-start.41 = (bf16[2,2,128,1280]{3,2,1,0:T(8,128)(2,1)}, bf16[2,2,128,1280]{3,2,1,0:T(8,128)(2,1)}, u32[]{:S(2)}, u32[]{:S(2)}) collective-permute-start(bf16[2,2,128,1280]{3,2,1,0:T(8,128)(2,1)} %get-tuple-element.227), channel_id=1, source_target_pairs={{0,1},{1,0},{2,3},{3,2},{4,5},{5,4},{6,7},{7,6},{8,9},{9,8},{10,11... | collective-permute-start | bytes 3932168 | tf_op jit(solution)/shard_map/ppermute | solution.py:149
  256.6 30.8 %collective-permute-start.42 = (bf16[2,2,128,1280]{3,2,1,0:T(8,128)(2,1)}, bf16[2,2,128,1280]{3,2,1,0:T(8,128)(2,1)}, u32[]{:S(2)}, u32[]{:S(2)}) collective-permute-start(bf16[2,2,128,1280]{3,2,1,0:T(8,128)(2,1)} %get-tuple-element.229), channel_id=1, source_target_pairs={{0,2},{1,3},{2,0},{3,1},{4,6},{5,7},{6,4},{7,5},{8,10},{9,11},{10,... | collective-permute-start | bytes 3932168 | tf_op jit(solution)/shard_map/ppermute | solution.py:149
  290.6 15.7 %collective-permute-start.43 = (bf16[2,128,1280]{2,1,0:T(8,128)(2,1)S(1)}, bf16[2,128,1280]{2,1,0:T(8,128)(2,1)S(1)}, u32[]{:S(2)}, u32[]{:S(2)}) collective-permute-start(bf16[2,128,1280]{2,1,0:T(8,128)(2,1)S(1)} %get-tuple-element.235), channel_id=1, source_target_pairs={{0,2},{1,3},{2,0},{3,1},{4,6},{5,7},{6,4},{7,5},{8,10},{9,11},{10,... | collective-permute-start | bytes 1966088 | tf_op jit(solution)/shard_map/ppermute | solution.py:149
  292.1 15.3 %collective-permute-start.44 = (bf16[2,128,1280]{2,1,0:T(8,128)(2,1)S(1)}, bf16[2,128,1280]{2,1,0:T(8,128)(2,1)S(1)}, u32[]{:S(2)}, u32[]{:S(2)}) collective-permute-start(bf16[2,128,1280]{2,1,0:T(8,128)(2,1)S(1)} %get-tuple-element.237), channel_id=1, source_target_pairs={{0,1},{1,0},{2,3},{3,2},{4,5},{5,4},{6,7},{7,6},{8,9},{9,8},{10,11... | collective-permute-start | bytes 1966088 | tf_op jit(solution)/shard_map/ppermute | solution.py:149
  308.6 6.0 %collective-permute-start.45 = (bf16[4,4,128,768]{3,2,1,0:T(8,128)(2,1)}, bf16[4,4,128,768]{3,2,1,0:T(8,128)(2,1)}, u32[]{:S(2)}, u32[]{:S(2)}) collective-permute-start(bf16[4,4,128,768]{3,2,1,0:T(8,128)(2,1)} %get-tuple-element.243), channel_id=1, source_target_pairs={{0,4},{1,5},{2,6},{3,7},{4,0},{5,1},{6,2},{7,3},{8,12},{9,13},{10,... | collective-permute-start | bytes 9437192 | tf_op jit(solution)/shard_map/ppermute | solution.py:149
  308.7 72.3 %all-gather.11.cloned.1.call-start = ((), (), s32[]{:S(2)}) async-start(), calls=%async_computation.6 | async-start | bytes 1310720 | tf_op jit(solution)/shard_map/all_gather | solution.py:602
  321.0 19.8 %collective-permute-start.46 = (bf16[2,2,128,768]{3,2,1,0:T(8,128)(2,1)}, bf16[2,2,128,768]{3,2,1,0:T(8,128)(2,1)S(1)}, u32[]{:S(2)}, u32[]{:S(2)}) collective-permute-start(bf16[2,2,128,768]{3,2,1,0:T(8,128)(2,1)} %get-tuple-element.247), channel_id=1, source_target_pairs={{0,1},{1,0},{2,3},{3,2},{4,5},{5,4},{6,7},{7,6},{8,9},{9,8},{10,11... | collective-permute-start | bytes 2359304 | tf_op jit(solution)/shard_map/ppermute | solution.py:149
  321.6 19.5 %collective-permute-start.47 = (bf16[2,2,128,768]{3,2,1,0:T(8,128)(2,1)}, bf16[2,2,128,768]{3,2,1,0:T(8,128)(2,1)S(1)}, u32[]{:S(2)}, u32[]{:S(2)}) collective-permute-start(bf16[2,2,128,768]{3,2,1,0:T(8,128)(2,1)} %get-tuple-element.248), channel_id=1, source_target_pairs={{0,2},{1,3},{2,0},{3,1},{4,6},{5,7},{6,4},{7,5},{8,10},{9,11},{10,... | collective-permute-start | bytes 2359304 | tf_op jit(solution)/shard_map/ppermute | solution.py:149
  341.4 12.9 %collective-permute-start.48 = (bf16[2,128,768]{2,1,0:T(8,128)(2,1)S(1)}, bf16[2,128,768]{2,1,0:T(8,128)(2,1)S(1)}, u32[]{:S(2)}, u32[]{:S(2)}) collective-permute-start(bf16[2,128,768]{2,1,0:T(8,128)(2,1)S(1)} %get-tuple-element.256), channel_id=1, source_target_pairs={{0,2},{1,3},{2,0},{3,1},{4,6},{5,7},{6,4},{7,5},{8,10},{9,11},{10,... | collective-permute-start | bytes 1179656 | tf_op jit(solution)/shard_map/ppermute | solution.py:149
  342.6 12.5 %collective-permute-start.49 = (bf16[2,128,768]{2,1,0:T(8,128)(2,1)S(1)}, bf16[2,128,768]{2,1,0:T(8,128)(2,1)S(1)}, u32[]{:S(2)}, u32[]{:S(2)}) collective-permute-start(bf16[2,128,768]{2,1,0:T(8,128)(2,1)S(1)} %get-tuple-element.258), channel_id=1, source_target_pairs={{0,1},{1,0},{2,3},{3,2},{4,5},{5,4},{6,7},{7,6},{8,9},{9,8},{10,11... | collective-permute-start | bytes 1179656 | tf_op jit(solution)/shard_map/ppermute | solution.py:149
  355.9 20.0 %collective-permute-start.51 = (bf16[144,768]{1,0:T(8,128)(2,1)S(1)}, bf16[144,768]{1,0:T(8,128)(2,1)S(1)}, u32[]{:S(2)}, u32[]{:S(2)}) collective-permute-start(bf16[144,768]{1,0:T(8,128)(2,1)S(1)} %get-tuple-element.268), channel_id=1, source_target_pairs={{0,8},{1,9},{2,10},{3,11},{4,12},{5,13},{6,14},{7,15},{8,16},{9,17... | collective-permute-start | bytes 663560 | tf_op jit(solution)/shard_map/ppermute | solution.py:149
  355.9 21.3 %collective-permute-start.52 = (bf16[144,768]{1,0:T(8,128)(2,1)S(1)}, bf16[144,768]{1,0:T(8,128)(2,1)S(1)}, u32[]{:S(2)}, u32[]{:S(2)}) collective-permute-start(bf16[144,768]{1,0:T(8,128)(2,1)S(1)} %get-tuple-element.269), channel_id=1, source_target_pairs={{0,16},{1,17},{2,18},{3,19},{4,20},{5,21},{6,22},{7,23},{8,24},{9,... | collective-permute-start | bytes 663560 | tf_op jit(solution)/shard_map/ppermute | solution.py:149
  357.6 19.7 %collective-permute-start.53 = (bf16[144,768]{1,0:T(8,128)(2,1)S(1)}, bf16[144,768]{1,0:T(8,128)(2,1)S(1)}, u32[]{:S(2)}, u32[]{:S(2)}) collective-permute-start(bf16[144,768]{1,0:T(8,128)(2,1)S(1)} %get-tuple-element.270), channel_id=1, source_target_pairs={{0,24},{1,25},{2,26},{3,27},{4,28},{5,29},{6,30},{7,31},{8,0},{9,1... | collective-permute-start | bytes 663560 | tf_op jit(solution)/shard_map/ppermute | solution.py:149
  359.6 20.1 %collective-permute-start.57 = (bf16[128,1280]{1,0:T(8,128)(2,1)}, bf16[128,1280]{1,0:T(8,128)(2,1)S(1)}, u32[]{:S(2)}, u32[]{:S(2)}) collective-permute-start(bf16[128,1280]{1,0:T(8,128)(2,1)} %bitcast.90), channel_id=1, source_target_pairs={{0,1},{1,0},{2,3},{3,2},{4,5},{5,4},{6,7},{7,6},{8,9},{9,8},{10,11... | collective-permute-start | bytes 983048 | tf_op jit(solution)/shard_map/ppermute | solution.py:149
  360.4 23.3 %collective-permute-start.58 = (bf16[128,1280]{1,0:T(8,128)(2,1)}, bf16[128,1280]{1,0:T(8,128)(2,1)S(1)}, u32[]{:S(2)}, u32[]{:S(2)}) collective-permute-start(bf16[128,1280]{1,0:T(8,128)(2,1)} %bitcast.91), channel_id=1, source_target_pairs={{0,2},{1,3},{2,0},{3,1},{4,6},{5,7},{6,4},{7,5},{8,10},{9,11},{10,... | collective-permute-start | bytes 983048 | tf_op jit(solution)/shard_map/ppermute | solution.py:149
  375.9 9.0 %collective-permute-start.59 = (bf16[128,1280]{1,0:T(8,128)(2,1)S(1)}, bf16[128,1280]{1,0:T(8,128)(2,1)S(1)}, u32[]{:S(2)}, u32[]{:S(2)}) collective-permute-start(bf16[128,1280]{1,0:T(8,128)(2,1)S(1)} %bitcast.92), channel_id=1, source_target_pairs={{0,3},{1,2},{2,1},{3,0},{4,7},{5,6},{6,5},{7,4},{8,11},{9,10},{10,... | collective-permute-start | bytes 983048 | tf_op jit(solution)/shard_map/ppermute | solution.py:149
  377.4 9.7 %collective-permute-start.54 = (bf16[144,768]{1,0:T(8,128)(2,1)S(1)}, bf16[144,768]{1,0:T(8,128)(2,1)S(1)}, u32[]{:S(2)}, u32[]{:S(2)}) collective-permute-start(bf16[144,768]{1,0:T(8,128)(2,1)S(1)} %add_convert_fusion.1.refs_0_), channel_id=1, source_target_pairs={{0,1},{1,0},{2,3},{3,2},{4,5},{5,4},{6,7},{7,6},{8,9},{9,8},{10,11... | collective-permute-start | bytes 663560 | tf_op jit(solution)/shard_map/ppermute | solution.py:149
  378.3 9.0 %collective-permute-start.55 = (bf16[144,768]{1,0:T(8,128)(2,1)S(1)}, bf16[144,768]{1,0:T(8,128)(2,1)S(1)}, u32[]{:S(2)}, u32[]{:S(2)}) collective-permute-start(bf16[144,768]{1,0:T(8,128)(2,1)S(1)} %add_convert_fusion.1.refs_0_), channel_id=1, source_target_pairs={{0,2},{1,3},{2,0},{3,1},{4,6},{5,7},{6,4},{7,5},{8,10},{9,11},{10,... | collective-permute-start | bytes 663560 | tf_op jit(solution)/shard_map/ppermute | solution.py:149
  379.7 10.0 %collective-permute-start.56 = (bf16[144,768]{1,0:T(8,128)(2,1)S(1)}, bf16[144,768]{1,0:T(8,128)(2,1)S(1)}, u32[]{:S(2)}, u32[]{:S(2)}) collective-permute-start(bf16[144,768]{1,0:T(8,128)(2,1)S(1)} %add_convert_fusion.1.refs_0_), channel_id=1, source_target_pairs={{0,3},{1,2},{2,1},{3,0},{4,7},{5,6},{6,5},{7,4},{8,11},{9,10},{10,... | collective-permute-start | bytes 663560 | tf_op jit(solution)/shard_map/ppermute | solution.py:149
  (49 other events, 607.0 us)
Sparse Core Ops, SparseCore 0:
  35.3 29.9 all-gather.6
  80.7 27.0 all-gather.8
  240.4 24.5 reduce-scatter.2
  308.8 28.2 reduce-scatter.4
  339.0 30.7 all-gather.10

commit v6 on v5

--- a/solution.py
+++ b/solution.py
@@ -1146,7 +1146,7 @@
     from_down = from_plane(after(share_down, chip_qkv))
     column_qkv = column_parts(plane_columns(where, side_qkv, ends_qkv, rows))
     activations = contract(after(hid, column_qkv[0]), down_w, y1, bias_down)
-    shares_up = shares(after(share_up, column_qkv[0]))
+    shares_up = shares(after(share_up, side_qkv))
     share_qkv = add(*after(column_qkv, activations))
     shares_qkv = shares(share_qkv)
     (s_down,) = joined(after(from_down, share_qkv), [width // 4])

time: 408 us -> 408 us (level)
  no operation moved by 1% of the time
where the time goes in v6:
time: 408 us; the launch traced here: 400 us
  Pallas kernels  220 us (54%)
  waiting for transfers between devices  83.7 us (21%)
  starting transfers between devices  44.2 us (11%)
  local copies, waits for them, and re-layouts  27.2 us (7%)
  between operations  14.8 us (4%)
  other arithmetic  10.4 us (3%)
    pallas_call x7, Pallas kernels, call(): pl.pallas_call(kernel, grid=grid, in_specs=in_specs, out_specs=out_specs,...  109 us
    ppermute x60, waiting for transfers between devices, send(): return lax.ppermute(value, ('fsdp', 'seq'), pairs)  83.6 us
    ppermute x60, starting transfers between devices, send(): return lax.ppermute(value, ('fsdp', 'seq'), pairs)  43.8 us
    pallas_call x3, Pallas kernels, wgrad_call(): pl.pallas_call(kernel, grid_spec=pltpu.PrefetchScalarGridSpec(num_scalar_...  40.3 us
    pallas_call x2, Pallas kernels, per_image(): pl.pallas_call(kernel, grid_spec=pltpu.PrefetchScalarGridSpec(num_scalar_...  36.6 us
    pallas_call x3, Pallas kernels, chip_sum(): pl.pallas_call(kernel, grid_spec=pltpu.PrefetchScalarGridSpec(num_scalar_...  14.6 us
    unnamed x101, local copies, waits for them, and re-layouts  9.63 us
  transfers between devices with their start and end apart: 65, of which 30 were waited for; matrix products, arithmetic and copies ran while one was open for 6% of the time, Pallas kernels for 52%

profile of v6, /device:TPU:8, one launch (start us, length us, event | category | flops | bytes accessed | tf_op | source)
XLA Modules:
  0.0 399.9 jit_solution(6576552820804480912)
XLA Ops:
  9.2 1.6 collective-permute-start
  11.9 1.9 collective-permute-start.2
  13.9 1.7 constant_dynamic-slice_fusion.7
  18.1 10.7 %collective-permute-done = bf16[128,1024]{1,0:T(8,128)(2,1)S(1)} collective-permute-done((bf16[128,1024]{1,0:T(8,128)(2,1)S(1)}, bf16[128,1024]{1,0:T(8,128)(2,1)S(1)}, u32[]{:S(2)}, u32[]{:S(2)}) %collective-permute-start) | collective-permute-done | bytes 262176 | tf_op jit(solution)/shard_map/ppermute | solution.py:149
  28.8 4.5 %collective-permute-done.1 = bf16[128,1024]{1,0:T(8,128)(2,1)S(1)} collective-permute-done((bf16[128,1024]{1,0:T(8,128)(2,1)S(1)}, bf16[128,1024]{1,0:T(8,128)(2,1)S(1)}, u32[]{:S(2)}, u32[]{:S(2)}) %collective-permute-start.1) | collective-permute-done | bytes 262176 | tf_op jit(solution)/shard_map/ppermute | solution.py:149
  33.3 1.9 collective-permute-done.2
  35.3 1.7 collective-permute-done.4.refs_8_
  40.0 1.5 collective-permute-start.5
  41.5 1.5 collective-permute-start.6
  44.6 15.2 %collective-permute-done.5.refs_3_ = bf16[3,128,1024]{2,1,0:T(8,128)(2,1)} collective-permute-done((bf16[3,128,1024]{2,1,0:T(8,128)(2,1)S(1)}, bf16[3,128,1024]{2,1,0:T(8,128)(2,1)}, u32[]{:S(2)}, u32[]{:S(2)}) %collective-permute-start.5) | collective-permute-done | bytes 786464 | tf_op jit(solution)/shard_map/ppermute | solution.py:149
  61.0 2.1 slice.99
  63.0 1.8 slice.100
  65.3 1.5 collective-permute-start.14
  71.0 2.1 add_convert_fusion.refs_14_.refs_0_
  73.1 3.6 collective-permute-done.14.refs_5_
  76.6 1.2 collective-permute-done.15.refs_6_
  82.7 13.6 %shard_map.254 = (bf16[960,3072]{1,0:T(8,128)(2,1)}, bf16[1024,3072]{1,0:T(8,128)(2,1)}, bf16[1024,1024]{1,0:T(8,128)(2,1)}) custom-call(s32[3]{0:T(128)} %pad_add_fusion.1.place_ref, bf16[128,3072]{1,0:T(8,128)(2,1)} %refs_0_.3, bf16[128,1024]{1,0:T(8,128)(2,1)} %refs_1_.1, bf16[3,128,1024]{2,1,0:T(8,128)(2,1)} %copy-done.23, ...), custom_call_target="tpu_custom_call" | custom-call | tf_op jit(solution)/shard_map/pallas_call | solution.py:718
  96.3 1.5 collective-permute-done.10.refs_2_
  97.9 1.7 collective-permute-done.11.refs_3_
  103.5 12.6 %shard_map.255.refs_12_.refs_2_ = bf16[960,1024]{1,0:T(8,128)(2,1)S(1)} custom-call(s32[3]{0:T(128)S(1)} %fusion.12.counts_ref, bf16[960,3072]{1,0:T(8,128)(2,1)} %get-tuple-element.173.qkv_ref), custom_call_target="tpu_custom_call" | custom-call | tf_op jit(solution)/shard_map/pallas_call | solution.py:85
  116.1 1.3 copy-done.4
  118.0 1.4 collective-permute-done.24.refs_10_
  120.0 1.3 constant_dynamic-slice_fusion.2
  121.4 1.6 collective-permute-start.26
  123.0 1.5 collective-permute-start.27
  125.8 12.2 %shard_map.256 = (f32[960,1024]{1,0:T(8,128)}, bf16[960,1024]{1,0:T(8,128)(2,1)}, bf16[1024,4096]{1,0:T(8,128)(2,1)}) custom-call(s32[3]{0:T(128)} %pad_add_fusion.1.place_ref, bf16[128,4096]{1,0:T(8,128)(2,1)} %refs_0_.4, bf16[3,128,1024]{2,1,0:T(8,128)(2,1)} %copy-done.24, bf16[3,128,1024]{2,1,0:T(8,128)(2,1)} %copy-done.27, ...), custom_call_target="tpu_custom_call" | custom-call | tf_op jit(solution)/shard_map/pallas_call | solution.py:718
  138.0 19.3 %shard_map.257 = (bf16[960,4096]{1,0:T(8,128)(2,1)}, bf16[960,4096]{1,0:T(8,128)(2,1)}) custom-call(bf16[960,1024]{1,0:T(8,128)(2,1)} %get-tuple-element.183.a_ref.refs_0_, bf16[1024,4096]{1,0:T(8,128)(2,1)} %get-tuple-element.184.w_ref.up_ref, f32[1,4096]{1,0:T(1,128)} %bitcast.108), custom_call_target="tpu_custom_call" | custom-call | tf_op jit(solution)/shard_map/pallas_call | solution.py:718
  159.2 13.2 %shard_map.258 = (bf16[4,4,512,256]{3,2,1,0:T(8,128)(2,1)}, bf16[4,4,512,256]{3,2,1,0:T(8,128)(2,1)}) custom-call(s32[3]{0:T(128)S(1)} %copy-done.19, bf16[960,4096]{1,0:T(8,128)(2,1)} %get-tuple-element.267.left_ref.h_ref, bf16[960,1024]{1,0:T(8,128)(2,1)S(1)} %bitcast.88), custom_call_target="tpu_custom_call" | custom-call | tf_op jit(solution)/shard_map/pallas_call | solution.py:397
  175.7 8.0 %shard_map.259.down_ref.w_ref = bf16[4096,1024]{1,0:T(8,128)(2,1)} custom-call(s32[3]{0:T(128)} %pad_add_fusion.1.place_ref, bf16[512,1024]{1,0:T(8,128)(2,1)} %refs_0_.5, bf16[3,512,256]{2,1,0:T(8,128)(2,1)} %copy-done.22, bf16[3,512,256]{2,1,0:T(8,128)(2,1)} %copy-done.25, bf16[3,512,256]{2,1,0:T(8,128)(2,1)} %copy-done.26, ...), custom_call_target="tpu_custom_call" | custom-call | tf_op jit(solution)/shard_map/pallas_call | solution.py:226
  183.7 4.6 %shard_map.260 = (bf16[2,2,512,256]{3,2,1,0:T(8,128)(2,1)S(1)}, bf16[2,2,512,256]{3,2,1,0:T(8,128)(2,1)}, bf16[2,2,512,256]{3,2,1,0:T(8,128)(2,1)S(1)}, bf16[2,2,512,256]{3,2,1,0:T(8,128)(2,1)S(1)}) custom-call(s32[3]{0:T(128)S(1)} %copy-done.20, bf16[4,4,512,256]{3,2,1,0:T(8,128)(2,1)S(1)} %copy-done.9, bf16[4,4,512,256]{3,2,1,0:T(8,128)(2,1)} %collective-permute-done.35.refs_1_), custom_call_target="tpu_custom_call" | custom-call | tf_op jit(solution)/shard_map/pallas_call | solution.py:493
  188.3 1.5 collective-permute-start.36
  189.8 1.5 collective-permute-start.37
  191.3 29.3 %shard_map.261 = (bf16[960,4096]{1,0:T(8,128)(2,1)}, f32[1,4096]{1,0:T(1,128)}, f32[960,1024]{1,0:T(8,128)}, bf16[960,1024]{1,0:T(8,128)(2,1)}, f32[1,1024]{1,0:...) custom-call(bf16[960,1024]{1,0:T(8,128)(2,1)} %bitcast.87, bf16[4096,1024]{1,0:T(8,128)(2,1)} %shard_map.259.down_ref.w_ref, ...), custom_call_target="tpu_custom_call" | custom-call | tf_op jit(solution)/shard_map/pallas_call | solution.py:718
  222.8 16.3 %shard_map.263 = (bf16[4,4,128,1280]{3,2,1,0:T(8,128)(2,1)}, bf16[4,4,128,1280]{3,2,1,0:T(8,128)(2,1)}) custom-call(s32[3]{0:T(128)S(1)} %copy-done.20, bf16[960,1024]{1,0:T(8,128)(2,1)S(1)} %copy-done.6, bf16[960,4096]{1,0:T(8,128)(2,1)} %get-tuple-element.217.refs_1_, bf16[960,1024]{1,0:T(8,128)(2,1)S(1)} %copy-done.5, ...), custom_call_target="tpu_custom_call" | custom-call | tf_op jit(solution)/shard_map/pallas_call | solution.py:397
  240.3 5.9 %shard_map.265.do_ref = bf16[960,1024]{1,0:T(8,128)(2,1)} custom-call(bf16[960,1024]{1,0:T(8,128)(2,1)} %get-tuple-element.221.refs_3_.d_ref, bf16[1024,1024]{1,0:T(8,128)(2,1)} %get-tuple-element.180.refs_13_.w_ref), custom_call_target="tpu_custom_call" | custom-call | tf_op jit(solution)/shard_map/pallas_call | solution.py:718
  246.2 3.0 collective-permute-done.40.refs_1_
  249.2 5.5 %shard_map.266 = (bf16[2,2,128,1280]{3,2,1,0:T(8,128)(2,1)S(1)}, bf16[2,2,128,1280]{3,2,1,0:T(8,128)(2,1)}, bf16[2,2,128,1280]{3,2,1,0:T(8,128)(2,1)S(1)}, bf16[2,2,128,1280]{3,2,1,0:T(8,128)(2,1)}) custom-call(s32[3]{0:T(128)S(1)} %copy-done.20, bf16[4,4,128,1280]{3,2,1,0:T(8,128)(2,1)S(1)} %copy-done.8, ...), custom_call_target="tpu_custom_call" | custom-call | tf_op jit(solution)/shard_map/pallas_call | solution.py:493
  256.6 1.5 collective-permute-start.42
  258.1 23.9 %shard_map.267.refs_1_.d_ref = bf16[960,3072]{1,0:T(8,128)(2,1)} custom-call(s32[3]{0:T(128)S(1)} %fusion.12.counts_ref, bf16[960,3072]{1,0:T(8,128)(2,1)} %get-tuple-element.173.qkv_ref, bf16[960,1024]{1,0:T(8,128)(2,1)S(1)} %copy-done.7), custom_call_target="tpu_custom_call" | custom-call | tf_op jit(solution)/shard_map/pallas_call | solution.py:85
  282.0 4.9 %collective-permute-done.41.ga_ref = bf16[2,2,128,1280]{3,2,1,0:T(8,128)(2,1)} collective-permute-done((bf16[2,2,128,1280]{3,2,1,0:T(8,128)(2,1)}, bf16[2,2,128,1280]{3,2,1,0:T(8,128)(2,1)}, u32[]{:S(2)}, u32[]{:S(2)}) %collective-permute-start.41) | collective-permute-done | bytes 1310752 | tf_op jit(solution)/shard_map/ppermute | solution.py:149
  287.4 1.3 copy-done.12
  288.7 1.8 shard_map.268
  290.6 1.6 collective-permute-start.43
  292.7 10.7 %shard_map.269 = (bf16[4,4,128,768]{3,2,1,0:T(8,128)(2,1)}, bf16[4,4,128,768]{3,2,1,0:T(8,128)(2,1)}) custom-call(s32[3]{0:T(128)S(1)} %copy-done.20, bf16[960,1024]{1,0:T(8,128)(2,1)S(1)} %copy-done.3, bf16[960,3072]{1,0:T(8,128)(2,1)} %shard_map.267.refs_1_.d_ref), custom_call_target="tpu_custom_call" | custom-call | tf_op jit(solution)/shard_map/pallas_call | solution.py:397
  303.4 2.8 collective-permute-done.43.refs_1_
  306.2 1.2 collective-permute-done.44.refs_3_
  308.7 5.9 %collective-permute-done.45.refs_1_ = bf16[4,4,128,768]{3,2,1,0:T(8,128)(2,1)} collective-permute-done((bf16[4,4,128,768]{3,2,1,0:T(8,128)(2,1)}, bf16[4,4,128,768]{3,2,1,0:T(8,128)(2,1)}, u32[]{:S(2)}, u32[]{:S(2)}) %collective-permute-start.45) | collective-permute-done | bytes 3145760 | tf_op jit(solution)/shard_map/ppermute | solution.py:149
  314.6 4.6 %shard_map.271 = (bf16[2,2,128,768]{3,2,1,0:T(8,128)(2,1)S(1)}, bf16[2,2,128,768]{3,2,1,0:T(8,128)(2,1)}, bf16[2,2,128,768]{3,2,1,0:T(8,128)(2,1)S(1)}, bf16[2,2,128,768]{3,2,1,0:T(8,128)(2,1)}) custom-call(s32[3]{0:T(128)S(1)} %copy-done.20, bf16[4,4,128,768]{3,2,1,0:T(8,128)(2,1)S(1)} %copy-done.10, bf16[4,4,128,768]{3,2,1,0:T(8,128)(2,1)} %collective-permute-done.45.refs_1_), custom_call_target="tpu_custom_call" | custom-call | tf_op jit(solution)/shard_map/pallas_call | solution.py:493
  322.9 15.0 %shard_map.272 = (bf16[960,1024]{1,0:T(8,128)(2,1)}, f32[1,1024]{1,0:T(1,128)}, f32[1,1024]{1,0:T(1,128)}, f32[1,3072]{1,0:T(1,128)}) custom-call(bf16[960,3072]{1,0:T(8,128)(2,1)} %shard_map.267.refs_1_.d_ref, bf16[1024,3072]{1,0:T(8,128)(2,1)} %get-tuple-element.251.w_ref, bf16[960,1024]{1,0:T(8,128)(2,1)} %bitcast.95, ...), custom_call_target="tpu_custom_call" | custom-call | tf_op jit(solution)/shard_map/pallas_call | solution.py:718
  338.6 2.3 collective-permute-done.46.ga_ref
  341.4 1.3 collective-permute-start.48
  345.5 8.8 %collective-permute-done.48.refs_1_ = bf16[2,128,768]{2,1,0:T(8,128)(2,1)S(1)} collective-permute-done((bf16[2,128,768]{2,1,0:T(8,128)(2,1)S(1)}, bf16[2,128,768]{2,1,0:T(8,128)(2,1)S(1)}, u32[]{:S(2)}, u32[]{:S(2)}) %collective-permute-start.48) | collective-permute-done | bytes 393248 | tf_op jit(solution)/shard_map/ppermute | solution.py:149
  355.9 1.7 collective-permute-start.52
  357.6 1.9 collective-permute-start.53
  360.4 1.4 collective-permute-start.58
  361.8 14.1 %shard_map.275 = bf16[960,1024]{1,0:T(8,128)(2,1)} custom-call(bf16[960,4096]{1,0:T(8,128)(2,1)} %get-tuple-element.267.left_ref.h_ref, bf16[4096,1024]{1,0:T(8,128)(2,1)} %shard_map.259.down_ref.w_ref, f32[960,1024]{1,0:T(8,128)} %get-tuple-element.207.y_ref, f32[1,1024]{1,0:T(1,128)} %bitcast.112), custom_call_target="tpu_custom_call" | custom-call | tf_op jit(solution)/shard_map/pallas_call | solution.py:718
  375.9 1.4 collective-permute-start.59
  378.3 1.4 collective-permute-start.55
  379.7 1.3 collective-permute-start.56
  382.2 1.5 shard_map.276
  383.7 1.3 collective-permute-done.59.refs_3_
  385.0 2.2 shard_map.277
  387.2 2.4 collective-permute-done.56.refs_3_
  389.6 1.8 shard_map.278
  (249 shorter events, 53.8 us)
Async XLA Ops:
  7.2 60.2 %all-gather.7.cloned.1.call-start = ((), (), s32[]{:S(2)}) async-start(), calls=%async_computation.4 | async-start | bytes 1474560 | tf_op jit(solution)/shard_map/all_gather | solution.py:667
  9.2 19.6 %collective-permute-start = (bf16[128,1024]{1,0:T(8,128)(2,1)S(1)}, bf16[128,1024]{1,0:T(8,128)(2,1)S(1)}, u32[]{:S(2)}, u32[]{:S(2)}) collective-permute-start(bf16[128,1024]{1,0:T(8,128)(2,1)S(1)} %pad_maximum_fusion.3), channel_id=1, source_target_pairs={{0,8},{1,9},{2,10},{3,11},{4,12},{5,13},{6,14},{7,15},{8,16},{9,17... | collective-permute-start | bytes 786440 | tf_op jit(solution)/shard_map/ppermute | solution.py:149
  10.8 22.4 %collective-permute-start.1 = (bf16[128,1024]{1,0:T(8,128)(2,1)S(1)}, bf16[128,1024]{1,0:T(8,128)(2,1)S(1)}, u32[]{:S(2)}, u32[]{:S(2)}) collective-permute-start(bf16[128,1024]{1,0:T(8,128)(2,1)S(1)} %pad_maximum_fusion.3), channel_id=1, source_target_pairs={{0,16},{1,17},{2,18},{3,19},{4,20},{5,21},{6,22},{7,23},{8,24},{9,... | collective-permute-start | bytes 786440 | tf_op jit(solution)/shard_map/ppermute | solution.py:149
  11.9 23.2 %collective-permute-start.2 = (bf16[128,1024]{1,0:T(8,128)(2,1)S(1)}, bf16[128,1024]{1,0:T(8,128)(2,1)}, u32[]{:S(2)}, u32[]{:S(2)}) collective-permute-start(bf16[128,1024]{1,0:T(8,128)(2,1)S(1)} %pad_maximum_fusion.3), channel_id=1, source_target_pairs={{0,24},{1,25},{2,26},{3,27},{4,28},{5,29},{6,30},{7,31},{8,0},{9,1... | collective-permute-start | bytes 786440 | tf_op jit(solution)/shard_map/ppermute | solution.py:149
  13.9 23.2 %collective-permute-start.3 = (bf16[128,3072]{1,0:T(8,128)(2,1)}, bf16[128,3072]{1,0:T(8,128)(2,1)S(1)}, u32[]{:S(2)}, u32[]{:S(2)}) collective-permute-start(bf16[128,3072]{1,0:T(8,128)(2,1)} %refs_0_.3), channel_id=1, source_target_pairs={{0,4},{1,5},{2,6},{3,7},{4,0},{5,1},{6,2},{7,3},{8,12},{9,13},{10,... | collective-permute-start | bytes 2359304 | tf_op jit(solution)/shard_map/ppermute | solution.py:149
  35.2 82.8 %all-gather.9.cloned.1.call-start = ((), (), s32[]{:S(2)}) async-start(), calls=%async_computation.5 | async-start | bytes 1310720 | tf_op jit(solution)/shard_map/all_gather | solution.py:667
  35.2 1.8 collective-permute-start.4
  39.1 21.9 %collective-permute-start.7 = (bf16[128,4096]{1,0:T(8,128)(2,1)}, bf16[128,4096]{1,0:T(8,128)(2,1)}, u32[]{:S(2)}, u32[]{:S(2)}) collective-permute-start(bf16[128,4096]{1,0:T(8,128)(2,1)} %refs_0_.4), channel_id=1, source_target_pairs={{0,4},{1,5},{2,6},{3,7},{4,0},{5,1},{6,2},{7,3},{8,12},{9,13},{10,... | collective-permute-start | bytes 3145736 | tf_op jit(solution)/shard_map/ppermute | solution.py:149
  39.3 21.7 %collective-permute-start.8 = (bf16[512,1024]{1,0:T(8,128)(2,1)}, bf16[512,1024]{1,0:T(8,128)(2,1)}, u32[]{:S(2)}, u32[]{:S(2)}) collective-permute-start(bf16[512,1024]{1,0:T(8,128)(2,1)} %refs_0_.5), channel_id=1, source_target_pairs={{0,4},{1,5},{2,6},{3,7},{4,0},{5,1},{6,2},{7,3},{8,12},{9,13},{10,... | collective-permute-start | bytes 3145736 | tf_op jit(solution)/shard_map/ppermute | solution.py:149
  40.0 19.7 %collective-permute-start.5 = (bf16[3,128,1024]{2,1,0:T(8,128)(2,1)S(1)}, bf16[3,128,1024]{2,1,0:T(8,128)(2,1)}, u32[]{:S(2)}, u32[]{:S(2)}) collective-permute-start(bf16[3,128,1024]{2,1,0:T(8,128)(2,1)S(1)} %pad_maximum_fusion.refs_2_), channel_id=1, source_target_pairs={{0,1},{1,0},{2,3},{3,2},{4,5},{5,4},{6,7},{7,6},{8,9},{9,8},{10,11... | collective-permute-start | bytes 2359304 | tf_op jit(solution)/shard_map/ppermute | solution.py:149
  41.5 19.4 %collective-permute-start.6 = (bf16[3,128,1024]{2,1,0:T(8,128)(2,1)S(1)}, bf16[3,128,1024]{2,1,0:T(8,128)(2,1)}, u32[]{:S(2)}, u32[]{:S(2)}) collective-permute-start(bf16[3,128,1024]{2,1,0:T(8,128)(2,1)S(1)} %pad_maximum_fusion.refs_2_), channel_id=1, source_target_pairs={{0,2},{1,3},{2,0},{3,1},{4,6},{5,7},{6,4},{7,5},{8,10},{9,11},{10,... | collective-permute-start | bytes 2359304 | tf_op jit(solution)/shard_map/ppermute | solution.py:149
  43.1 17.9 %collective-permute-start.9 = (bf16[3,128,1024]{2,1,0:T(8,128)(2,1)S(1)}, bf16[3,128,1024]{2,1,0:T(8,128)(2,1)S(1)}, u32[]{:S(2)}, u32[]{:S(2)}) collective-permute-start(bf16[3,128,1024]{2,1,0:T(8,128)(2,1)S(1)} %pad_maximum_fusion.refs_2_), channel_id=1, source_target_pairs={{0,4},{1,5},{2,6},{3,7},{4,0},{5,1},{6,2},{7,3},{8,12},{9,13},{10,... | collective-permute-start | bytes 2359304 | tf_op jit(solution)/shard_map/ppermute | solution.py:149
  63.0 17.4 %collective-permute-start.12 = (bf16[3,128,1024]{2,1,0:T(8,128)(2,1)}, bf16[3,128,1024]{2,1,0:T(8,128)(2,1)}, u32[]{:S(2)}, u32[]{:S(2)}) collective-permute-start(bf16[3,128,1024]{2,1,0:T(8,128)(2,1)} %collective-permute-done.5.refs_3_), channel_id=1, source_target_pairs={{0,4},{1,5},{2,6},{3,7},{4,0},{5,1},{6,2},{7,3},{8,12},{9,13},{10,... | collective-permute-start | bytes 2359304 | tf_op jit(solution)/shard_map/ppermute | solution.py:149
  64.8 15.6 %collective-permute-start.13 = (bf16[3,128,1024]{2,1,0:T(8,128)(2,1)}, bf16[3,128,1024]{2,1,0:T(8,128)(2,1)}, u32[]{:S(2)}, u32[]{:S(2)}) collective-permute-start(bf16[3,128,1024]{2,1,0:T(8,128)(2,1)} %collective-permute-done.6.refs_4_), channel_id=1, source_target_pairs={{0,4},{1,5},{2,6},{3,7},{4,0},{5,1},{6,2},{7,3},{8,12},{9,13},{10,... | collective-permute-start | bytes 2359304 | tf_op jit(solution)/shard_map/ppermute | solution.py:149
  65.3 11.3 %collective-permute-start.14 = (bf16[3,64,1024]{2,1,0:T(8,128)(2,1)}, bf16[3,64,1024]{2,1,0:T(8,128)(2,1)}, u32[]{:S(2)}, u32[]{:S(2)}) collective-permute-start(bf16[3,64,1024]{2,1,0:T(8,128)(2,1)} %slice.99), channel_id=1, source_target_pairs={{0,2},{1,3},{2,0},{3,1},{4,6},{5,7},{6,4},{7,5},{8,10},{9,11},{10,... | collective-permute-start | bytes 1179656 | tf_op jit(solution)/shard_map/ppermute | solution.py:149
  66.8 11.1 %collective-permute-start.15 = (bf16[3,64,1024]{2,1,0:T(8,128)(2,1)}, bf16[3,64,1024]{2,1,0:T(8,128)(2,1)}, u32[]{:S(2)}, u32[]{:S(2)}) collective-permute-start(bf16[3,64,1024]{2,1,0:T(8,128)(2,1)} %slice.100), channel_id=1, source_target_pairs={{0,1},{1,0},{2,3},{3,2},{4,5},{5,4},{6,7},{7,6},{8,9},{9,8},{10,11... | collective-permute-start | bytes 1179656 | tf_op jit(solution)/shard_map/ppermute | solution.py:149
  68.2 1.4 collective-permute-start.16
  77.9 1.9 collective-permute-start.17
  77.9 2.5 collective-permute-start.18
  78.4 19.4 %collective-permute-start.10 = (bf16[3,128,1024]{2,1,0:T(8,128)(2,1)S(1)}, bf16[3,128,1024]{2,1,0:T(8,128)(2,1)S(1)}, u32[]{:S(2)}, u32[]{:S(2)}) collective-permute-start(bf16[3,128,1024]{2,1,0:T(8,128)(2,1)S(1)} %pad_maximum_fusion.1.refs_1_), channel_id=1, source_target_pairs={{0,1},{1,0},{2,3},{3,2},{4,5},{5,4},{6,7},{7,6},{8,9},{9,8},{10,11... | collective-permute-start | bytes 2359304 | tf_op jit(solution)/shard_map/ppermute | solution.py:149
  79.8 19.7 %collective-permute-start.11 = (bf16[3,128,1024]{2,1,0:T(8,128)(2,1)S(1)}, bf16[3,128,1024]{2,1,0:T(8,128)(2,1)}, u32[]{:S(2)}, u32[]{:S(2)}) collective-permute-start(bf16[3,128,1024]{2,1,0:T(8,128)(2,1)S(1)} %pad_maximum_fusion.1.refs_1_), channel_id=1, source_target_pairs={{0,2},{1,3},{2,0},{3,1},{4,6},{5,7},{6,4},{7,5},{8,10},{9,11},{10,... | collective-permute-start | bytes 2359304 | tf_op jit(solution)/shard_map/ppermute | solution.py:149
  80.4 19.1 %collective-permute-start.19 = (bf16[3,128,1024]{2,1,0:T(8,128)(2,1)S(1)}, bf16[3,128,1024]{2,1,0:T(8,128)(2,1)}, u32[]{:S(2)}, u32[]{:S(2)}) collective-permute-start(bf16[3,128,1024]{2,1,0:T(8,128)(2,1)S(1)} %pad_maximum_fusion.1.refs_1_), channel_id=1, source_target_pairs={{0,4},{1,5},{2,6},{3,7},{4,0},{5,1},{6,2},{7,3},{8,12},{9,13},{10,... | collective-permute-start | bytes 2359304 | tf_op jit(solution)/shard_map/ppermute | solution.py:149
  80.6 201.4 %reduce-scatter.3.cloned.1.call-start = ((), (), s32[]{:S(2)}) async-start(), calls=%async_computation.2 | async-start | bytes 1310720 | tf_op jit(solution)/shard_map/reduce_scatter | solution.py:596
  99.5 17.9 %collective-permute-start.22 = (bf16[3,128,1024]{2,1,0:T(8,128)(2,1)S(1)}, bf16[3,128,1024]{2,1,0:T(8,128)(2,1)}, u32[]{:S(2)}, u32[]{:S(2)}) collective-permute-start(bf16[3,128,1024]{2,1,0:T(8,128)(2,1)S(1)} %collective-permute-done.10.refs_2_), channel_id=1, source_target_pairs={{0,4},{1,5},{2,6},{3,7},{4,0},{5,1},{6,2},{7,3},{8,12},{9,13},{10,... | collective-permute-start | bytes 2359304 | tf_op jit(solution)/shard_map/ppermute | solution.py:149
  99.5 17.9 %collective-permute-start.23 = (bf16[3,128,1024]{2,1,0:T(8,128)(2,1)}, bf16[3,128,1024]{2,1,0:T(8,128)(2,1)}, u32[]{:S(2)}, u32[]{:S(2)}) collective-permute-start(bf16[3,128,1024]{2,1,0:T(8,128)(2,1)} %collective-permute-done.11.refs_3_), channel_id=1, source_target_pairs={{0,4},{1,5},{2,6},{3,7},{4,0},{5,1},{6,2},{7,3},{8,12},{9,13},{10,... | collective-permute-start | bytes 2359304 | tf_op jit(solution)/shard_map/ppermute | solution.py:149
  101.8 15.6 %collective-permute-start.20 = (bf16[3,64,1024]{2,1,0:T(8,128)(2,1)}, bf16[3,64,1024]{2,1,0:T(8,128)(2,1)}, u32[]{:S(2)}, u32[]{:S(2)}) collective-permute-start(bf16[3,64,1024]{2,1,0:T(8,128)(2,1)} %slice.112), channel_id=1, source_target_pairs={{0,2},{1,3},{2,0},{3,1},{4,6},{5,7},{6,4},{7,5},{8,10},{9,11},{10,... | collective-permute-start | bytes 1179656 | tf_op jit(solution)/shard_map/ppermute | solution.py:149
  102.4 15.0 %collective-permute-start.21 = (bf16[3,64,1024]{2,1,0:T(8,128)(2,1)S(1)}, bf16[3,64,1024]{2,1,0:T(8,128)(2,1)}, u32[]{:S(2)}, u32[]{:S(2)}) collective-permute-start(bf16[3,64,1024]{2,1,0:T(8,128)(2,1)S(1)} %slice.113), channel_id=1, source_target_pairs={{0,1},{1,0},{2,3},{3,2},{4,5},{5,4},{6,7},{7,6},{8,9},{9,8},{10,11... | collective-permute-start | bytes 1179656 | tf_op jit(solution)/shard_map/ppermute | solution.py:149
  117.4 2.0 collective-permute-start.24
  117.5 2.5 collective-permute-start.25
  121.4 35.9 %collective-permute-start.26 = (bf16[3,512,256]{2,1,0:T(8,128)(2,1)S(1)}, bf16[3,512,256]{2,1,0:T(8,128)(2,1)S(1)}, u32[]{:S(2)}, u32[]{:S(2)}) collective-permute-start(bf16[3,512,256]{2,1,0:T(8,128)(2,1)S(1)} %pad_maximum_fusion.2.refs_1_), channel_id=1, source_target_pairs={{0,1},{1,0},{2,3},{3,2},{4,5},{5,4},{6,7},{7,6},{8,9},{9,8},{10,11... | collective-permute-start | bytes 2359304 | tf_op jit(solution)/shard_map/ppermute | solution.py:149
  123.0 34.3 %collective-permute-start.27 = (bf16[3,512,256]{2,1,0:T(8,128)(2,1)S(1)}, bf16[3,512,256]{2,1,0:T(8,128)(2,1)S(1)}, u32[]{:S(2)}, u32[]{:S(2)}) collective-permute-start(bf16[3,512,256]{2,1,0:T(8,128)(2,1)S(1)} %pad_maximum_fusion.2.refs_1_), channel_id=1, source_target_pairs={{0,2},{1,3},{2,0},{3,1},{4,6},{5,7},{6,4},{7,5},{8,10},{9,11},{10,... | collective-permute-start | bytes 2359304 | tf_op jit(solution)/shard_map/ppermute | solution.py:149
  124.5 32.9 %collective-permute-start.28 = (bf16[3,512,256]{2,1,0:T(8,128)(2,1)S(1)}, bf16[3,512,256]{2,1,0:T(8,128)(2,1)S(1)}, u32[]{:S(2)}, u32[]{:S(2)}) collective-permute-start(bf16[3,512,256]{2,1,0:T(8,128)(2,1)S(1)} %pad_maximum_fusion.2.refs_1_), channel_id=1, source_target_pairs={{0,4},{1,5},{2,6},{3,7},{4,0},{5,1},{6,2},{7,3},{8,12},{9,13},{10,... | collective-permute-start | bytes 2359304 | tf_op jit(solution)/shard_map/ppermute | solution.py:149
  157.4 15.2 %collective-permute-start.31 = (bf16[3,512,256]{2,1,0:T(8,128)(2,1)S(1)}, bf16[3,512,256]{2,1,0:T(8,128)(2,1)S(1)}, u32[]{:S(2)}, u32[]{:S(2)}) collective-permute-start(bf16[3,512,256]{2,1,0:T(8,128)(2,1)S(1)} %collective-permute-done.26.refs_2_), channel_id=1, source_target_pairs={{0,4},{1,5},{2,6},{3,7},{4,0},{5,1},{6,2},{7,3},{8,12},{9,13},{10,... | collective-permute-start | bytes 2359304 | tf_op jit(solution)/shard_map/ppermute | solution.py:149
  157.9 14.6 %collective-permute-start.32 = (bf16[3,512,256]{2,1,0:T(8,128)(2,1)S(1)}, bf16[3,512,256]{2,1,0:T(8,128)(2,1)S(1)}, u32[]{:S(2)}, u32[]{:S(2)}) collective-permute-start(bf16[3,512,256]{2,1,0:T(8,128)(2,1)S(1)} %collective-permute-done.27.refs_3_), channel_id=1, source_target_pairs={{0,4},{1,5},{2,6},{3,7},{4,0},{5,1},{6,2},{7,3},{8,12},{9,13},{10,... | collective-permute-start | bytes 2359304 | tf_op jit(solution)/shard_map/ppermute | solution.py:149
  158.1 14.4 %collective-permute-start.29 = (bf16[3,256,256]{2,1,0:T(8,128)(2,1)S(1)}, bf16[3,256,256]{2,1,0:T(8,128)(2,1)S(1)}, u32[]{:S(2)}, u32[]{:S(2)}) collective-permute-start(bf16[3,256,256]{2,1,0:T(8,128)(2,1)S(1)} %slice.118), channel_id=1, source_target_pairs={{0,2},{1,3},{2,0},{3,1},{4,6},{5,7},{6,4},{7,5},{8,10},{9,11},{10,... | collective-permute-start | bytes 1179656 | tf_op jit(solution)/shard_map/ppermute | solution.py:149
  158.7 13.8 %collective-permute-start.30 = (bf16[3,256,256]{2,1,0:T(8,128)(2,1)S(1)}, bf16[3,256,256]{2,1,0:T(8,128)(2,1)S(1)}, u32[]{:S(2)}, u32[]{:S(2)}) collective-permute-start(bf16[3,256,256]{2,1,0:T(8,128)(2,1)S(1)} %slice.119), channel_id=1, source_target_pairs={{0,1},{1,0},{2,3},{3,2},{4,5},{5,4},{6,7},{7,6},{8,9},{9,8},{10,11... | collective-permute-start | bytes 1179656 | tf_op jit(solution)/shard_map/ppermute | solution.py:149
  172.6 1.8 collective-permute-start.33
  172.6 2.3 collective-permute-start.34
  174.9 8.7 %collective-permute-start.35 = (bf16[4,4,512,256]{3,2,1,0:T(8,128)(2,1)}, bf16[4,4,512,256]{3,2,1,0:T(8,128)(2,1)}, u32[]{:S(2)}, u32[]{:S(2)}) collective-permute-start(bf16[4,4,512,256]{3,2,1,0:T(8,128)(2,1)} %get-tuple-element.197), channel_id=1, source_target_pairs={{0,4},{1,5},{2,6},{3,7},{4,0},{5,1},{6,2},{7,3},{8,12},{9,13},{10,... | collective-permute-start | bytes 12582920 | tf_op jit(solution)/shard_map/ppermute | solution.py:149
  188.3 32.4 %collective-permute-start.36 = (bf16[2,2,512,256]{3,2,1,0:T(8,128)(2,1)}, bf16[2,2,512,256]{3,2,1,0:T(8,128)(2,1)S(1)}, u32[]{:S(2)}, u32[]{:S(2)}) collective-permute-start(bf16[2,2,512,256]{3,2,1,0:T(8,128)(2,1)} %get-tuple-element.202), channel_id=1, source_target_pairs={{0,1},{1,0},{2,3},{3,2},{4,5},{5,4},{6,7},{7,6},{8,9},{9,8},{10,11... | collective-permute-start | bytes 3145736 | tf_op jit(solution)/shard_map/ppermute | solution.py:149
  189.8 30.9 %collective-permute-start.37 = (bf16[2,2,512,256]{3,2,1,0:T(8,128)(2,1)S(1)}, bf16[2,2,512,256]{3,2,1,0:T(8,128)(2,1)S(1)}, u32[]{:S(2)}, u32[]{:S(2)}) collective-permute-start(bf16[2,2,512,256]{3,2,1,0:T(8,128)(2,1)S(1)} %get-tuple-element.204), channel_id=1, source_target_pairs={{0,2},{1,3},{2,0},{3,1},{4,6},{5,7},{6,4},{7,5},{8,10},{9,11},{10,... | collective-permute-start | bytes 3145736 | tf_op jit(solution)/shard_map/ppermute | solution.py:149
  221.0 18.1 %collective-permute-start.38 = (bf16[2,512,256]{2,1,0:T(8,128)(2,1)S(1)}, bf16[2,512,256]{2,1,0:T(8,128)(2,1)S(1)}, u32[]{:S(2)}, u32[]{:S(2)}) collective-permute-start(bf16[2,512,256]{2,1,0:T(8,128)(2,1)S(1)} %get-tuple-element.213), channel_id=1, source_target_pairs={{0,2},{1,3},{2,0},{3,1},{4,6},{5,7},{6,4},{7,5},{8,10},{9,11},{10,... | collective-permute-start | bytes 1572872 | tf_op jit(solution)/shard_map/ppermute | solution.py:149
  221.6 17.5 %collective-permute-start.39 = (bf16[2,512,256]{2,1,0:T(8,128)(2,1)S(1)}, bf16[2,512,256]{2,1,0:T(8,128)(2,1)S(1)}, u32[]{:S(2)}, u32[]{:S(2)}) collective-permute-start(bf16[2,512,256]{2,1,0:T(8,128)(2,1)S(1)} %get-tuple-element.214), channel_id=1, source_target_pairs={{0,1},{1,0},{2,3},{3,2},{4,5},{5,4},{6,7},{7,6},{8,9},{9,8},{10,11... | collective-permute-start | bytes 1572872 | tf_op jit(solution)/shard_map/ppermute | solution.py:149
  240.2 9.0 %collective-permute-start.40 = (bf16[4,4,128,1280]{3,2,1,0:T(8,128)(2,1)}, bf16[4,4,128,1280]{3,2,1,0:T(8,128)(2,1)}, u32[]{:S(2)}, u32[]{:S(2)}) collective-permute-start(bf16[4,4,128,1280]{3,2,1,0:T(8,128)(2,1)} %get-tuple-element.223), channel_id=1, source_target_pairs={{0,4},{1,5},{2,6},{3,7},{4,0},{5,1},{6,2},{7,3},{8,12},{9,13},{10,... | collective-permute-start | bytes 15728648 | tf_op jit(solution)/shard_map/ppermute | solution.py:149
  240.3 119.3 %reduce-scatter.5.cloned.1.call-start = ((), (), s32[]{:S(2)}) async-start(), calls=%async_computation.3 | async-start | bytes 1638400 | tf_op jit(solution)/shard_map/reduce_scatter | solution.py:596
  255.7 31.1 %collective-permute-start.41 = (bf16[2,2,128,1280]{3,2,1,0:T(8,128)(2,1)}, bf16[2,2,128,1280]{3,2,1,0:T(8,128)(2,1)}, u32[]{:S(2)}, u32[]{:S(2)}) collective-permute-start(bf16[2,2,128,1280]{3,2,1,0:T(8,128)(2,1)} %get-tuple-element.227), channel_id=1, source_target_pairs={{0,1},{1,0},{2,3},{3,2},{4,5},{5,4},{6,7},{7,6},{8,9},{9,8},{10,11... | collective-permute-start | bytes 3932168 | tf_op jit(solution)/shard_map/ppermute | solution.py:149
  256.6 30.8 %collective-permute-start.42 = (bf16[2,2,128,1280]{3,2,1,0:T(8,128)(2,1)}, bf16[2,2,128,1280]{3,2,1,0:T(8,128)(2,1)}, u32[]{:S(2)}, u32[]{:S(2)}) collective-permute-start(bf16[2,2,128,1280]{3,2,1,0:T(8,128)(2,1)} %get-tuple-element.229), channel_id=1, source_target_pairs={{0,2},{1,3},{2,0},{3,1},{4,6},{5,7},{6,4},{7,5},{8,10},{9,11},{10,... | collective-permute-start | bytes 3932168 | tf_op jit(solution)/shard_map/ppermute | solution.py:149
  290.6 15.7 %collective-permute-start.43 = (bf16[2,128,1280]{2,1,0:T(8,128)(2,1)S(1)}, bf16[2,128,1280]{2,1,0:T(8,128)(2,1)S(1)}, u32[]{:S(2)}, u32[]{:S(2)}) collective-permute-start(bf16[2,128,1280]{2,1,0:T(8,128)(2,1)S(1)} %get-tuple-element.235), channel_id=1, source_target_pairs={{0,2},{1,3},{2,0},{3,1},{4,6},{5,7},{6,4},{7,5},{8,10},{9,11},{10,... | collective-permute-start | bytes 1966088 | tf_op jit(solution)/shard_map/ppermute | solution.py:149
  292.1 15.3 %collective-permute-start.44 = (bf16[2,128,1280]{2,1,0:T(8,128)(2,1)S(1)}, bf16[2,128,1280]{2,1,0:T(8,128)(2,1)S(1)}, u32[]{:S(2)}, u32[]{:S(2)}) collective-permute-start(bf16[2,128,1280]{2,1,0:T(8,128)(2,1)S(1)} %get-tuple-element.237), channel_id=1, source_target_pairs={{0,1},{1,0},{2,3},{3,2},{4,5},{5,4},{6,7},{7,6},{8,9},{9,8},{10,11... | collective-permute-start | bytes 1966088 | tf_op jit(solution)/shard_map/ppermute | solution.py:149
  308.6 6.0 %collective-permute-start.45 = (bf16[4,4,128,768]{3,2,1,0:T(8,128)(2,1)}, bf16[4,4,128,768]{3,2,1,0:T(8,128)(2,1)}, u32[]{:S(2)}, u32[]{:S(2)}) collective-permute-start(bf16[4,4,128,768]{3,2,1,0:T(8,128)(2,1)} %get-tuple-element.243), channel_id=1, source_target_pairs={{0,4},{1,5},{2,6},{3,7},{4,0},{5,1},{6,2},{7,3},{8,12},{9,13},{10,... | collective-permute-start | bytes 9437192 | tf_op jit(solution)/shard_map/ppermute | solution.py:149
  308.7 72.3 %all-gather.11.cloned.1.call-start = ((), (), s32[]{:S(2)}) async-start(), calls=%async_computation.6 | async-start | bytes 1310720 | tf_op jit(solution)/shard_map/all_gather | solution.py:602
  321.0 19.8 %collective-permute-start.46 = (bf16[2,2,128,768]{3,2,1,0:T(8,128)(2,1)}, bf16[2,2,128,768]{3,2,1,0:T(8,128)(2,1)S(1)}, u32[]{:S(2)}, u32[]{:S(2)}) collective-permute-start(bf16[2,2,128,768]{3,2,1,0:T(8,128)(2,1)} %get-tuple-element.247), channel_id=1, source_target_pairs={{0,1},{1,0},{2,3},{3,2},{4,5},{5,4},{6,7},{7,6},{8,9},{9,8},{10,11... | collective-permute-start | bytes 2359304 | tf_op jit(solution)/shard_map/ppermute | solution.py:149
  321.6 19.5 %collective-permute-start.47 = (bf16[2,2,128,768]{3,2,1,0:T(8,128)(2,1)}, bf16[2,2,128,768]{3,2,1,0:T(8,128)(2,1)S(1)}, u32[]{:S(2)}, u32[]{:S(2)}) collective-permute-start(bf16[2,2,128,768]{3,2,1,0:T(8,128)(2,1)} %get-tuple-element.248), channel_id=1, source_target_pairs={{0,2},{1,3},{2,0},{3,1},{4,6},{5,7},{6,4},{7,5},{8,10},{9,11},{10,... | collective-permute-start | bytes 2359304 | tf_op jit(solution)/shard_map/ppermute | solution.py:149
  341.4 12.9 %collective-permute-start.48 = (bf16[2,128,768]{2,1,0:T(8,128)(2,1)S(1)}, bf16[2,128,768]{2,1,0:T(8,128)(2,1)S(1)}, u32[]{:S(2)}, u32[]{:S(2)}) collective-permute-start(bf16[2,128,768]{2,1,0:T(8,128)(2,1)S(1)} %get-tuple-element.256), channel_id=1, source_target_pairs={{0,2},{1,3},{2,0},{3,1},{4,6},{5,7},{6,4},{7,5},{8,10},{9,11},{10,... | collective-permute-start | bytes 1179656 | tf_op jit(solution)/shard_map/ppermute | solution.py:149
  342.6 12.5 %collective-permute-start.49 = (bf16[2,128,768]{2,1,0:T(8,128)(2,1)S(1)}, bf16[2,128,768]{2,1,0:T(8,128)(2,1)S(1)}, u32[]{:S(2)}, u32[]{:S(2)}) collective-permute-start(bf16[2,128,768]{2,1,0:T(8,128)(2,1)S(1)} %get-tuple-element.258), channel_id=1, source_target_pairs={{0,1},{1,0},{2,3},{3,2},{4,5},{5,4},{6,7},{7,6},{8,9},{9,8},{10,11... | collective-permute-start | bytes 1179656 | tf_op jit(solution)/shard_map/ppermute | solution.py:149
  355.9 20.0 %collective-permute-start.51 = (bf16[144,768]{1,0:T(8,128)(2,1)S(1)}, bf16[144,768]{1,0:T(8,128)(2,1)S(1)}, u32[]{:S(2)}, u32[]{:S(2)}) collective-permute-start(bf16[144,768]{1,0:T(8,128)(2,1)S(1)} %get-tuple-element.268), channel_id=1, source_target_pairs={{0,8},{1,9},{2,10},{3,11},{4,12},{5,13},{6,14},{7,15},{8,16},{9,17... | collective-permute-start | bytes 663560 | tf_op jit(solution)/shard_map/ppermute | solution.py:149
  355.9 21.3 %collective-permute-start.52 = (bf16[144,768]{1,0:T(8,128)(2,1)S(1)}, bf16[144,768]{1,0:T(8,128)(2,1)S(1)}, u32[]{:S(2)}, u32[]{:S(2)}) collective-permute-start(bf16[144,768]{1,0:T(8,128)(2,1)S(1)} %get-tuple-element.269), channel_id=1, source_target_pairs={{0,16},{1,17},{2,18},{3,19},{4,20},{5,21},{6,22},{7,23},{8,24},{9,... | collective-permute-start | bytes 663560 | tf_op jit(solution)/shard_map/ppermute | solution.py:149
  357.6 19.7 %collective-permute-start.53 = (bf16[144,768]{1,0:T(8,128)(2,1)S(1)}, bf16[144,768]{1,0:T(8,128)(2,1)S(1)}, u32[]{:S(2)}, u32[]{:S(2)}) collective-permute-start(bf16[144,768]{1,0:T(8,128)(2,1)S(1)} %get-tuple-element.270), channel_id=1, source_target_pairs={{0,24},{1,25},{2,26},{3,27},{4,28},{5,29},{6,30},{7,31},{8,0},{9,1... | collective-permute-start | bytes 663560 | tf_op jit(solution)/shard_map/ppermute | solution.py:149
  359.6 20.1 %collective-permute-start.57 = (bf16[128,1280]{1,0:T(8,128)(2,1)}, bf16[128,1280]{1,0:T(8,128)(2,1)S(1)}, u32[]{:S(2)}, u32[]{:S(2)}) collective-permute-start(bf16[128,1280]{1,0:T(8,128)(2,1)} %bitcast.90), channel_id=1, source_target_pairs={{0,1},{1,0},{2,3},{3,2},{4,5},{5,4},{6,7},{7,6},{8,9},{9,8},{10,11... | collective-permute-start | bytes 983048 | tf_op jit(solution)/shard_map/ppermute | solution.py:149
  360.4 23.3 %collective-permute-start.58 = (bf16[128,1280]{1,0:T(8,128)(2,1)}, bf16[128,1280]{1,0:T(8,128)(2,1)S(1)}, u32[]{:S(2)}, u32[]{:S(2)}) collective-permute-start(bf16[128,1280]{1,0:T(8,128)(2,1)} %bitcast.91), channel_id=1, source_target_pairs={{0,2},{1,3},{2,0},{3,1},{4,6},{5,7},{6,4},{7,5},{8,10},{9,11},{10,... | collective-permute-start | bytes 983048 | tf_op jit(solution)/shard_map/ppermute | solution.py:149
  375.9 9.0 %collective-permute-start.59 = (bf16[128,1280]{1,0:T(8,128)(2,1)S(1)}, bf16[128,1280]{1,0:T(8,128)(2,1)S(1)}, u32[]{:S(2)}, u32[]{:S(2)}) collective-permute-start(bf16[128,1280]{1,0:T(8,128)(2,1)S(1)} %bitcast.92), channel_id=1, source_target_pairs={{0,3},{1,2},{2,1},{3,0},{4,7},{5,6},{6,5},{7,4},{8,11},{9,10},{10,... | collective-permute-start | bytes 983048 | tf_op jit(solution)/shard_map/ppermute | solution.py:149
  377.4 9.7 %collective-permute-start.54 = (bf16[144,768]{1,0:T(8,128)(2,1)S(1)}, bf16[144,768]{1,0:T(8,128)(2,1)S(1)}, u32[]{:S(2)}, u32[]{:S(2)}) collective-permute-start(bf16[144,768]{1,0:T(8,128)(2,1)S(1)} %add_convert_fusion.1.refs_0_), channel_id=1, source_target_pairs={{0,1},{1,0},{2,3},{3,2},{4,5},{5,4},{6,7},{7,6},{8,9},{9,8},{10,11... | collective-permute-start | bytes 663560 | tf_op jit(solution)/shard_map/ppermute | solution.py:149
  378.3 9.0 %collective-permute-start.55 = (bf16[144,768]{1,0:T(8,128)(2,1)S(1)}, bf16[144,768]{1,0:T(8,128)(2,1)S(1)}, u32[]{:S(2)}, u32[]{:S(2)}) collective-permute-start(bf16[144,768]{1,0:T(8,128)(2,1)S(1)} %add_convert_fusion.1.refs_0_), channel_id=1, source_target_pairs={{0,2},{1,3},{2,0},{3,1},{4,6},{5,7},{6,4},{7,5},{8,10},{9,11},{10,... | collective-permute-start | bytes 663560 | tf_op jit(solution)/shard_map/ppermute | solution.py:149
  379.7 10.0 %collective-permute-start.56 = (bf16[144,768]{1,0:T(8,128)(2,1)S(1)}, bf16[144,768]{1,0:T(8,128)(2,1)S(1)}, u32[]{:S(2)}, u32[]{:S(2)}) collective-permute-start(bf16[144,768]{1,0:T(8,128)(2,1)S(1)} %add_convert_fusion.1.refs_0_), channel_id=1, source_target_pairs={{0,3},{1,2},{2,1},{3,0},{4,7},{5,6},{6,5},{7,4},{8,11},{9,10},{10,... | collective-permute-start | bytes 663560 | tf_op jit(solution)/shard_map/ppermute | solution.py:149
  (49 other events, 607.0 us)
Sparse Core Ops, SparseCore 0:
  35.3 29.9 all-gather.6
  80.7 27.0 all-gather.8
  240.4 24.5 reduce-scatter.2
  308.8 28.2 reduce-scatter.4
  339.0 30.7 all-gather.10
